TPU v7x, 128 devices: a whole 4x4x4 slice. The times are simulated.
128 devices in a mesh: replica: 8 (over x, core), tensor: 16 (over z, y).
Axes of the slice: x: 4, y: 4, z: 4, core: 2. Of those that a mesh axis runs over, the one named last changes fastest.
Arguments:
- gradient: bfloat16 [8, 2, 768, 4096], P(None, None, 'tensor', 'replica'), may hold values from -110 to 110
- momentum: float32 [8, 2, 768, 4096], P(None, None, 'tensor', 'replica'), may hold values from -110 to 110
Outputs:
- update: bfloat16 [8, 2, 768, 4096], P(None, None, 'tensor')
- new_momentum: float32 [8, 2, 768, 4096], P(None, None, 'tensor', 'replica')
All inputs are finite; a program needn't handle non-finite values.
Results may differ from a plain program's by a relative error of at most 0.019.
Values may be sent and summed in bfloat16 or wider, within the bound.
No kernel may reach another device: no remote copies, remote signals or barrier semaphores. Data moves between devices by JAX's collectives and lax.ppermute only.
A program may use at most 128 MiB of HBM per device.

v0:
```python
import math

import jax
import jax.numpy as jnp
from jax import lax
from jax.sharding import PartitionSpec as P

D = 4096
FF = 768
ITERS = 2


momentum_decay = 0.95
coef_linear = 3.4445
coef_gram = -4.775
coef_square = 2.0315
epsilon = 1e-07


def iterate_all(matrices, squares, gram_of):
    norm_value = jnp.sqrt(squares)[:, None, None]
    iterate = (matrices.astype(jnp.float32) / (norm_value + epsilon)).astype(jnp.bfloat16)
    for repeat in range(ITERS):
        gram_matrix = gram_of(iterate).astype(jnp.bfloat16)
        square_term = jnp.einsum(
            "kfg,kgh->kfh", gram_matrix, gram_matrix, preferred_element_type=jnp.float32
        )
        poly_term = (
            coef_gram * gram_matrix.astype(jnp.float32) + coef_square * square_term
        ).astype(jnp.bfloat16)
        product = jnp.einsum("kfg,kgd->kfd", poly_term, iterate, preferred_element_type=jnp.float32)
        iterate = (coef_linear * iterate.astype(jnp.float32) + product).astype(jnp.bfloat16)
    scale_factor = 0.2 * math.sqrt(max(FF, D))
    return (scale_factor * iterate.astype(jnp.float32)).astype(jnp.bfloat16)


def local_gram(iterate):
    return jnp.einsum("kfd,kgd->kfg", iterate, iterate, preferred_element_type=jnp.float32)


def local_update(matrices):
    squares = jnp.sum(jnp.square(matrices.astype(jnp.float32)), axis=(1, 2))
    return iterate_all(matrices, squares, local_gram)


def local(gradient, momentum):
    new_momentum = momentum_decay * momentum + gradient.astype(jnp.float32)
    look_ahead = (gradient.astype(jnp.float32) + momentum_decay * new_momentum).astype(jnp.bfloat16)
    expert_count, pair_count, row_count, col_count = look_ahead.shape
    flat_rows = look_ahead.reshape(expert_count * pair_count, row_count, col_count)
    col_blocks = lax.all_to_all(flat_rows, "tensor", split_axis=0, concat_axis=1, tiled=True)
    gathered = lax.all_gather(col_blocks, "replica", axis=2, tiled=True)
    finished = local_update(gathered)
    result = lax.all_to_all(finished, "tensor", split_axis=1, concat_axis=0, tiled=True)
    update = result.reshape(expert_count, pair_count, row_count, result.shape[2])
    return (update, new_momentum)


def solution(mesh):
    in_specs = (P(None, None, "tensor", "replica"), P(None, None, "tensor", "replica"))
    out_specs = (P(None, None, "tensor", None), P(None, None, "tensor", "replica"))
    return jax.shard_map(local, mesh=mesh, in_specs=in_specs, out_specs=out_specs, check_vma=False)
```

profile of v0, /device:TPU:1, one launch (start us, length us, event | category | flops | bytes accessed | tf_op | source)
XLA Modules:
  0.0 308.0 jit_solution(5275897478936816034)
XLA Ops:
  7.2 0.0 all-gather.2.cloned.1.call-start
  7.2 3.2 %fusion.12 = (bf16[8,2,48,512]{3,2,1,0:T(8,128)(2,1)S(1)}, f32[8,2,48,512]{3,2,1,0:T(8,128)}) fusion(bf16[8,2,48,512]{3,2,1,0:T(8,128)(2,1)} %param.2, f32[8,2,48,512]{3,2,1,0:T(8,128)} %param.3), kind=kLoop, calls=%fused_computation.19 | loop fusion | flops 2359296 | bytes 4718592 | tf_op jit(solution)/shard_map/convert_element_type | solution.py:48
  10.4 22.0 %all_to_all.21 = bf16[16,48,512]{2,1,0:T(8,128)(2,1)} all-to-all(bf16[16,48,512]{2,1,0:T(8,128)(2,1)S(1)} %bitcast.40), channel_id=1, replica_groups=mesh['replica'=8,'tensor'=16] {'tensor'}, dimensions={0} | all-to-all | bytes 1572864 | tf_op jit(solution)/shard_map/all_to_all | solution.py:51
  32.4 0.0 all-gather.2.cloned.1.call-update
  32.4 40.0 %all-gather.2.cloned.1.call-done = bf16[1,768,4096]{2,1,0:T(8,128)(2,1)} async-done(((bf16[1,768,512]{2,1,0:T(8,128)(2,1)}), bf16[1,768,4096]{2,1,0:T(8,128)(2,1)}) %all-gather.2.cloned.1.call-update) | async-done | bytes 6291472 | tf_op jit(solution)/shard_map/all_gather | solution.py:52
  72.4 6.6 %fusion = f32[]{:T(128)} fusion(bf16[1,768,4096]{2,1,0:T(8,128)(2,1)} %all-gather.2.cloned.1.call-done), kind=kLoop, calls=%fused_computation.2 | loop fusion | flops 9437183 | bytes 6291460 | tf_op jit(solution)/shard_map/reduce_sum | solution.py:42
  79.7 9.7 %fusion.13 = bf16[768,768]{1,0:T(8,128)(2,1)S(1)} fusion(bf16[1,768,4096]{2,1,0:T(8,128)(2,1)} %all-gather.2.cloned.1.call-done, f32[]{:T(128)S(6)} %add.27), kind=kOutput, calls=%fused_computation.20 | convolution fusion | flops 4841865216 | bytes 7471108 | tf_op jit(solution)/shard_map/kfd,kgd->kfg/dot_general | solution.py:38
  89.4 11.8 %fusion.3 = bf16[1,768,4096]{2,1,0:T(8,128)(2,1)} fusion(bf16[768,768]{1,0:T(8,128)(2,1)S(1)} %fusion.13, f32[]{:T(128)S(6)} %add.27, bf16[1,768,4096]{2,1,0:T(8,128)(2,1)} %all-gather.2.cloned.1.call-done), kind=kOutput, calls=%fused_computation.7 | convolution fusion | flops 5772214272 | bytes 13762564 | tf_op jit(solution)/shard_map/kfg,kgd->kfd/dot_general | solution.py:31
  101.3 9.9 %fusion.16 = bf16[768,768]{1,0:T(8,128)(2,1)S(1)} fusion(bf16[1,768,4096]{2,1,0:T(8,128)(2,1)} %fusion.3), kind=kOutput, calls=%fused_computation.21 | convolution fusion | flops 4832428032 | bytes 7471104 | tf_op jit(solution)/shard_map/kfd,kgd->kfg/dot_general | solution.py:38
  111.1 12.8 %multiply_convert_fusion = bf16[1,768,4096]{2,1,0:T(8,128)(2,1)} fusion(bf16[1,768,4096]{2,1,0:T(8,128)(2,1)} %fusion.3, bf16[768,768]{1,0:T(8,128)(2,1)S(1)} %fusion.16), kind=kOutput, calls=%fused_computation.8 | convolution fusion | flops 5762777088 | bytes 13762560 | tf_op jit(solution)/shard_map/kfg,kgd->kfd/dot_general | solution.py:31
  123.9 15.5 %copy.8 = bf16[1,768,4096]{2,0,1:T(2,128)(2,1)} copy(bf16[1,768,4096]{2,1,0:T(8,128)(2,1)} %multiply_convert_fusion) | data formatting | bytes 12582912 | tf_op jit(solution)/shard_map/convert_element_type | solution.py:34
  139.4 0.5 broadcast.45
  140.0 40.0 %reduce.1 = bf16[768,4096]{1,0:T(8,128)(2,1)} reduce(bf16[768,1,4096]{2,1,0:T(2,128)(2,1)} %bitcast.38, bf16[]{:T(256)} %broadcast.45), dimensions={1}, to_apply=%bitcast.36.reduce_sub_computation | reduce | bytes 12582914
  180.0 12.9 %reshape.71 = bf16[16,2,98304]{2,1,0:T(2,128)(2,1)} reshape(bf16[768,4096]{1,0:T(8,128)(2,1)} %reduce.1) | data formatting | bytes 12582912
  192.9 79.4 %all_to_all.22 = bf16[16,2,98304]{2,1,0:T(2,128)(2,1)} all-to-all(bf16[16,2,98304]{2,1,0:T(2,128)(2,1)} %reshape.71), channel_id=1, replica_groups=mesh['replica'=8,'tensor'=16] {'tensor'}, dimensions={0} | all-to-all | bytes 12582912 | tf_op jit(solution)/shard_map/all_to_all | solution.py:54
  272.3 14.3 %reshape.72 = bf16[768,1,4096]{2,1,0:T(2,128)(2,1)} reshape(bf16[16,2,98304]{2,1,0:T(2,128)(2,1)} %all_to_all.22) | data formatting | bytes 12582912
  286.7 14.5 %copy.6 = bf16[1,768,4096]{2,1,0:T(8,128)(2,1)} copy(bf16[1,768,4096]{2,0,1:T(2,128)(2,1)} %bitcast.37) | data formatting | bytes 12582912
Async XLA Ops:
  7.2 65.2 %all-gather.2.cloned.1.call-start = ((), (), s32[]{:S(2)}) async-start(), calls=%async_computation.2 | async-start | bytes 7077888 | tf_op jit(solution)/shard_map/all_gather | solution.py:52
Sparse Core Ops, SparseCore 0:
  32.5 39.8 all-gather.1
where the time goes:
time: 309 us; the launch traced here: 308 us
  blocking collectives  101 us (33%)
  local copies, waits for them, and re-layouts  57.7 us (19%)
  other arithmetic  49.8 us (16%)
  matrix products  44.2 us (14%)
  waiting for transfers between devices  40 us (13%)
  between operations  14.7 us (5%)
    all_to_all x1, blocking collectives, local(): lax.all_to_all(finished, 'tensor', split_axis=1, concat_axis=0, tiled=True)  79.4 us
    unnamed x4, local copies, waits for them, and re-layouts  42.2 us
    unnamed x1, other arithmetic  40 us
    all_gather x1, waiting for transfers between devices, local(): gathered = lax.all_gather(col_blocks, 'replica', axis=2, tiled=True)  40 us
    dot_general x2, matrix products, iterate_all(): jnp.einsum('kfg,kgd->kfd', poly_term, iterate, preferred_element_type=jnp...  24.6 us
    all_to_all x1, blocking collectives, local(): lax.all_to_all(flat_rows, 'tensor', split_axis=0, concat_axis=1, tiled=True)  22 us
    dot_general x2, matrix products, local_gram(): jnp.einsum('kfd,kgd->kfg', iterate, iterate, preferred_element_type=jnp.f...  19.6 us
    convert_element_type x1, local copies, waits for them, and re-layouts, iterate_all(): return (scale_factor * iterate.astype(jnp.float32)).astype(jnp.bfloat16)  15.5 us
  transfers between devices with their start and end apart: 1, of which 1 were waited for; matrix products, arithmetic and copies ran while one was open for 0% of the time, Pallas kernels for 0%

commit v1 on v0

v1 whole, which is shorter than its diff:
```python
import functools
import math

import jax
import jax.numpy as jnp
from jax import lax
from jax.experimental import pallas as pl
from jax.experimental.pallas import tpu as pltpu
from jax.sharding import PartitionSpec as P

D = 4096
FF = 768

momentum_decay = 0.95
coef_linear = 3.4445
coef_gram = -4.775
coef_square = 2.0315
epsilon = 1e-07
scale_factor = 0.2 * math.sqrt(max(FF, D))

BLOCK = 256
HALF = FF
VMEM = pl.BlockSpec(memory_space=pltpu.VMEM)
PARAMS = pltpu.CompilerParams(vmem_limit_bytes=48 * 1024 * 1024)
F32, BF16 = jnp.float32, jnp.bfloat16


def replica_place():
    index = lax.axis_index("replica")
    return index // 2, index % 2


def shift(value, steps, cross=0):
    pairs = [
        (chip * 2 + core, ((chip + steps) % 4) * 2 + (core ^ cross))
        for chip in range(4)
        for core in range(2)
    ]
    return lax.ppermute(value, "replica", pairs)


def dot_t(left, right):
    return lax.dot_general(left, right, (((1,), (1,)), ((), ())), preferred_element_type=F32)


def dot(left, right):
    return jnp.dot(left, right, preferred_element_type=F32)


def gram_kernel(rows_ref, keep_ref, send_ref):
    core = lax.axis_index("replica") % 2

    def rows(index):
        return rows_ref[pl.ds(index * BLOCK, BLOCK), :]

    halves = (((0, 0), (1, 0), (1, 1)), ((2, 0), (2, 1), (2, 2)))
    for mine in range(2):

        @pl.when(core == mine)
        def _():
            for place in range(3):
                kept, sent = halves[mine][place], halves[1 - mine][place]
                where = pl.ds(place * BLOCK, BLOCK)
                keep_ref[where, :] = dot_t(rows(kept[0]), rows(kept[1]))
                send_ref[where, :] = dot_t(rows(sent[0]), rows(sent[1])).astype(BF16)


def partial_gram(rows):
    return pl.pallas_call(
        gram_kernel,
        out_shape=(
            jax.ShapeDtypeStruct((HALF, BLOCK), F32),
            jax.ShapeDtypeStruct((HALF, BLOCK), BF16),
        ),
        in_specs=[VMEM],
        out_specs=(VMEM, VMEM),
        compiler_params=PARAMS,
    )(rows)


PIECE = HALF // 4


def chip_sum_kernel(keep_ref, got_ref, own_ref, next_ref, last_ref, far_ref):
    chip = lax.axis_index("replica") // 2

    def total(steps):
        where = pl.ds(pl.multiple_of(((chip + steps) % 4) * PIECE, PIECE), PIECE)
        return keep_ref[where, :] + got_ref[where, :].astype(F32)

    own_ref[...] = total(0)
    next_ref[...] = total(1).astype(BF16)
    last_ref[...] = total(3).astype(BF16)
    far_ref[...] = total(2).astype(BF16)


def chip_sum(keep, got):
    return pl.pallas_call(
        chip_sum_kernel,
        out_shape=(jax.ShapeDtypeStruct((PIECE, BLOCK), F32),)
        + (jax.ShapeDtypeStruct((PIECE, BLOCK), BF16),) * 3,
        in_specs=[VMEM, VMEM],
        out_specs=(VMEM,) * 4,
        compiler_params=PARAMS,
    )(keep, got)


def ring_sum_kernel(own_ref, a_ref, b_ref, c_ref, out_ref):
    total = own_ref[...] + a_ref[...].astype(F32) + b_ref[...].astype(F32) + c_ref[...].astype(F32)
    out_ref[...] = total.astype(BF16)


def ring_sum(own, first, second, third):
    return pl.pallas_call(
        ring_sum_kernel,
        out_shape=jax.ShapeDtypeStruct((PIECE, BLOCK), BF16),
        in_specs=[VMEM] * 4,
        out_specs=VMEM,
        compiler_params=PARAMS,
    )(own, first, second, third)


def chain_kernel(*refs):
    pieces, rows_ref, out_ref, packed, gram = refs[:8], refs[8], refs[9], refs[10], refs[11]
    index = lax.axis_index("replica")
    chip, core = index // 2, index % 2
    for steps in range(4):
        start = pl.multiple_of(((chip + steps) % 4) * PIECE, PIECE)
        packed[core, pl.ds(start, PIECE), :] = pieces[steps][...]
        packed[1 - core, pl.ds(start, PIECE), :] = pieces[4 + steps][...]
    row_id = lax.broadcasted_iota(jnp.int32, (BLOCK, BLOCK), 0)
    col_id = lax.broadcasted_iota(jnp.int32, (BLOCK, BLOCK), 1)
    diagonal = row_id == col_id
    places = ((0, 0), (1, 0), (1, 1), (2, 0), (2, 1), (2, 2))
    blocks = [packed[place // 3, pl.ds((place % 3) * BLOCK, BLOCK), :] for place in range(6)]
    squares = sum(
        jnp.sum(jnp.where(diagonal, block.astype(F32), 0.0))
        for block, (row, col) in zip(blocks, places)
        if row == col
    )
    squares = jnp.full((1, 1), squares, F32)
    scale = 1.0 / (jnp.sqrt(squares) + epsilon)
    for block, (row, col) in zip(blocks, places):
        scaled = (block.astype(F32) * scale) * scale
        gram[pl.ds(row * BLOCK, BLOCK), pl.ds(col * BLOCK, BLOCK)] = scaled.astype(BF16)
        if row != col:
            gram[pl.ds(col * BLOCK, BLOCK), pl.ds(row * BLOCK, BLOCK)] = scaled.T.astype(BF16)

    gram_0 = gram[...]
    poly_0 = (coef_gram * gram_0.astype(F32) + coef_square * dot(gram_0, gram_0)).astype(BF16)
    half_way = (coef_linear * gram_0.astype(F32) + dot(poly_0, gram_0)).astype(BF16)
    gram_1 = (coef_linear * half_way.astype(F32) + dot(half_way, poly_0)).astype(BF16)
    poly_1 = (coef_gram * gram_1.astype(F32) + coef_square * dot(gram_1, gram_1)).astype(BF16)
    rows = rows_ref[...]
    first = ((coef_linear * rows.astype(F32) + dot(poly_0, rows)) * scale).astype(BF16)
    second = coef_linear * first.astype(F32) + dot(poly_1, first)
    out_ref[...] = (scale_factor * second).astype(BF16)


def chain(pieces, rows):
    return pl.pallas_call(
        chain_kernel,
        out_shape=jax.ShapeDtypeStruct(rows.shape, BF16),
        in_specs=[VMEM] * 9,
        out_specs=VMEM,
        scratch_shapes=[pltpu.VMEM((2, HALF, BLOCK), BF16), pltpu.VMEM((FF, FF), BF16)],
        compiler_params=PARAMS,
    )(*pieces, rows)


def local(gradient, momentum):
    new_momentum = momentum_decay * momentum + gradient.astype(F32)
    look_ahead = (gradient.astype(F32) + momentum_decay * new_momentum).astype(BF16)
    experts, pairs, row_count, col_count = look_ahead.shape
    flat_rows = look_ahead.reshape(experts * pairs, row_count, col_count)
    rows = lax.all_to_all(flat_rows, "tensor", split_axis=0, concat_axis=0, tiled=True)
    rows = rows.reshape(FF, col_count)

    keep, send = partial_gram(rows)
    own, to_next, to_last, to_far = chip_sum(keep, shift(send, 0, 1))
    mine = ring_sum(own, shift(to_next, 1), shift(to_last, -1), shift(to_far, 2))
    here = (mine, shift(mine, -1), shift(mine, 2), shift(mine, 1))
    other = tuple(shift(piece, 0, 1) for piece in here)
    finished = chain(here + other, rows)

    finished = finished.reshape(experts * pairs, row_count, col_count)
    back = lax.all_to_all(finished, "tensor", split_axis=0, concat_axis=0, tiled=True)
    whole = lax.all_gather(back.reshape(FF, col_count), "replica", axis=1, tiled=True)
    update = whole.reshape(experts, pairs, row_count, whole.shape[1])
    return (update, new_momentum)


def solution(mesh):
    in_specs = (P(None, None, "tensor", "replica"), P(None, None, "tensor", "replica"))
    out_specs = (P(None, None, "tensor", None), P(None, None, "tensor", "replica"))
    return jax.shard_map(local, mesh=mesh, in_specs=in_specs, out_specs=out_specs, check_vma=False)
```

time: 309 us -> 130 us (0.42)
  blocking collectives: 101 us -> 39.3 us
  local copies, waits for them, and re-layouts: 57.7 us -> 6.28 us
  other arithmetic: 49.8 us -> 3.16 us
  matrix products: 44.2 us -> 0 us
  starting transfers between devices: 0.04 us -> 16.1 us
  Pallas kernels: 0 us -> 6.17 us
  waiting for transfers between devices: 40 us -> 44.8 us
    all_to_all x2, blocking collectives: 101 us -> 39.3 us  [the longest x1 21.9 us: local(): lax.all_to_all(flat_rows, 'tensor', split_axis=0, concat_axis=0, tiled=True)]
    dot_general x4 -> x0, matrix products: 44.2 us -> none  [the longest x2 24.6 us: iterate_all(): jnp.einsum('kfg,kgd->kfd', poly_term, iterate, preferred_element_type=jnp...]
    unnamed x1 -> x0, other arithmetic: 40 us -> none
    unnamed x4 -> x1, local copies, waits for them, and re-layouts: 42.2 us -> 6.28 us
    ppermute x0 -> x11, starting transfers between devices: none -> 16.1 us  [shift(): return lax.ppermute(value, 'replica', pairs)]
    convert_element_type x1 -> x0, local copies, waits for them, and re-layouts: 15.5 us -> none  [iterate_all(): return (scale_factor * iterate.astype(jnp.float32)).astype(jnp.bfloat16)]
    reduce_sum x1 -> x0, other arithmetic: 6.62 us -> none  [local_update(): squares = jnp.sum(jnp.square(matrices.astype(jnp.float32)), axis=(1, 2))]
    pallas_call x0 -> x4, Pallas kernels: none -> 6.17 us  [the longest x1 5.46 us: chain(): pl.pallas_call(chain_kernel, out_shape=jax.ShapeDtypeStruct(rows.shape, B...]
  transfers between devices with their start and end apart: 1 -> 12, of which waited for: 1 -> 6; matrix products, arithmetic and copies ran while one was open for 0% -> 0% of each run, Pallas kernels for 0% -> 0%
where the time goes in v1:
time: 130 us
  waiting for transfers between devices  44.8 us (34%)
  blocking collectives  39.3 us (30%)
  starting transfers between devices  16.1 us (12%)
  between operations  14.1 us (11%)
  local copies, waits for them, and re-layouts  6.28 us (5%)
  Pallas kernels  6.17 us (5%)
  other arithmetic  3.16 us (2%)
    all_gather x1, waiting for transfers between devices, local(): lax.all_gather(back.reshape(FF, col_count), 'replica', axis=1, tiled=True)  38.9 us
    all_to_all x1, blocking collectives, local(): lax.all_to_all(flat_rows, 'tensor', split_axis=0, concat_axis=0, tiled=True)  21.9 us
    all_to_all x1, blocking collectives, local(): lax.all_to_all(finished, 'tensor', split_axis=0, concat_axis=0, tiled=True)  17.4 us
    ppermute x11, starting transfers between devices, shift(): return lax.ppermute(value, 'replica', pairs)  16.1 us
    unnamed x1, local copies, waits for them, and re-layouts  6.28 us
    ppermute x11, waiting for transfers between devices, shift(): return lax.ppermute(value, 'replica', pairs)  5.86 us
    pallas_call x1, Pallas kernels, chain(): pl.pallas_call(chain_kernel, out_shape=jax.ShapeDtypeStruct(rows.shape, B...  5.46 us
    convert_element_type x1, other arithmetic, local(): (gradient.astype(F32) + momentum_decay * new_momentum).astype(BF16)  3.16 us
  transfers between devices with their start and end apart: 12, of which 6 were waited for; matrix products, arithmetic and copies ran while one was open for 0% of the time, Pallas kernels for 0%

profile of v1, /device:TPU:1, one launch (start us, length us, event | category | flops | bytes accessed | tf_op | source)
XLA Modules:
  0.0 129.8 jit_solution(8955998189817092485)
XLA Ops:
  7.2 0.0 all-gather.2.cloned.1.call-start
  7.2 3.2 %fusion = (bf16[8,2,48,512]{3,2,1,0:T(8,128)(2,1)S(1)}, f32[8,2,48,512]{3,2,1,0:T(8,128)}) fusion(bf16[8,2,48,512]{3,2,1,0:T(8,128)(2,1)} %param.2, f32[8,2,48,512]{3,2,1,0:T(8,128)} %param.3), kind=kLoop, calls=%fused_computation.2 | loop fusion | flops 2359296 | bytes 4718592 | tf_op jit(solution)/shard_map/convert_element_type | solution.py:173
  10.4 21.9 %all_to_all.10 = bf16[16,48,512]{2,1,0:T(8,128)(2,1)S(1)} all-to-all(bf16[16,48,512]{2,1,0:T(8,128)(2,1)S(1)} %bitcast.9), channel_id=1, replica_groups=mesh['replica'=8,'tensor'=16] {'tensor'}, dimensions={0} | all-to-all | bytes 1572864 | tf_op jit(solution)/shard_map/all_to_all | solution.py:176
  32.3 0.6 shard_map.41
  32.9 1.9 %collective-permute-start = (bf16[768,256]{1,0:T(8,128)(2,1)S(1)}, bf16[768,256]{1,0:T(8,128)(2,1)S(1)}, u32[]{:S(2)}, u32[]{:S(2)}) collective-permute-start(bf16[768,256]{1,0:T(8,128)(2,1)S(1)} %get-tuple-element.9), channel_id=1, source_target_pairs={{0,16},{16,0},{32,48},{48,32},{64,80},{80,64},{96,112},{112,96},{1... | collective-permute-start | bytes 1179656 | tf_op jit(solution)/shard_map/ppermute | solution.py:39
  34.8 1.3 %collective-permute-done.got_ref = bf16[768,256]{1,0:T(8,128)(2,1)S(1)} collective-permute-done((bf16[768,256]{1,0:T(8,128)(2,1)S(1)}, bf16[768,256]{1,0:T(8,128)(2,1)S(1)}, u32[]{:S(2)}, u32[]{:S(2)}) %collective-permute-start) | collective-permute-done | bytes 393248 | tf_op jit(solution)/shard_map/ppermute | solution.py:39
  36.1 0.1 shard_map.42
  36.2 1.3 collective-permute-start.1
  37.4 1.5 %collective-permute-start.2 = (bf16[192,256]{1,0:T(8,128)(2,1)S(1)}, bf16[192,256]{1,0:T(8,128)(2,1)S(1)}, u32[]{:S(2)}, u32[]{:S(2)}) collective-permute-start(bf16[192,256]{1,0:T(8,128)(2,1)S(1)} %get-tuple-element.12), channel_id=1, source_target_pairs={{0,96},{16,112},{32,0},{48,16},{64,32},{80,48},{96,64},{112,80},{1... | collective-permute-start | bytes 294920 | tf_op jit(solution)/shard_map/ppermute | solution.py:39
  38.9 1.5 %collective-permute-start.3 = (bf16[192,256]{1,0:T(8,128)(2,1)S(1)}, bf16[192,256]{1,0:T(8,128)(2,1)S(1)}, u32[]{:S(2)}, u32[]{:S(2)}) collective-permute-start(bf16[192,256]{1,0:T(8,128)(2,1)S(1)} %get-tuple-element.13), channel_id=1, source_target_pairs={{0,64},{16,80},{32,96},{48,112},{64,0},{80,16},{96,32},{112,48},{1... | collective-permute-start | bytes 294920 | tf_op jit(solution)/shard_map/ppermute | solution.py:39
  40.4 1.0 collective-permute-done.1.a_ref
  41.5 0.0 collective-permute-done.2.b_ref
  41.5 2.5 %collective-permute-done.3.c_ref = bf16[192,256]{1,0:T(8,128)(2,1)S(1)} collective-permute-done((bf16[192,256]{1,0:T(8,128)(2,1)S(1)}, bf16[192,256]{1,0:T(8,128)(2,1)S(1)}, u32[]{:S(2)}, u32[]{:S(2)}) %collective-permute-start.3) | collective-permute-done | bytes 98336 | tf_op jit(solution)/shard_map/ppermute | solution.py:39
  44.0 1.3 collective-permute-start.6
  45.3 1.5 %collective-permute-start.5 = (bf16[192,256]{1,0:T(8,128)(2,1)S(1)}, bf16[192,256]{1,0:T(8,128)(2,1)S(1)}, u32[]{:S(2)}, u32[]{:S(2)}) collective-permute-start(bf16[192,256]{1,0:T(8,128)(2,1)S(1)} %shard_map.43.refs_0_), channel_id=1, source_target_pairs={{0,64},{16,80},{32,96},{48,112},{64,0},{80,16},{96,32},{112,48},{1... | collective-permute-start | bytes 294920 | tf_op jit(solution)/shard_map/ppermute | solution.py:39
  46.8 1.0 collective-permute-start.4
  47.8 2.7 %collective-permute-start.7 = (bf16[192,256]{1,0:T(8,128)(2,1)S(1)}, bf16[192,256]{1,0:T(8,128)(2,1)S(1)}, u32[]{:S(2)}, u32[]{:S(2)}) collective-permute-start(bf16[192,256]{1,0:T(8,128)(2,1)S(1)} %shard_map.43.refs_0_), channel_id=1, source_target_pairs={{0,16},{16,0},{32,48},{48,32},{64,80},{80,64},{96,112},{112,96},{1... | collective-permute-start | bytes 294920 | tf_op jit(solution)/shard_map/ppermute | solution.py:39
  50.5 0.0 collective-permute-done.6.refs_3_
  50.5 1.5 %collective-permute-start.10 = (bf16[192,256]{1,0:T(8,128)(2,1)S(1)}, bf16[192,256]{1,0:T(8,128)(2,1)S(1)}, u32[]{:S(2)}, u32[]{:S(2)}) collective-permute-start(bf16[192,256]{1,0:T(8,128)(2,1)S(1)} %collective-permute-done.6.refs_3_), channel_id=1, source_target_pairs={{0,16},{16,0},{32,48},{48,32},{64,80},{80,64},{96,112},{112,96},{1... | collective-permute-start | bytes 294920 | tf_op jit(solution)/shard_map/ppermute | solution.py:39
  52.1 0.0 collective-permute-done.5.refs_2_
  52.1 1.1 collective-permute-start.9
  53.2 0.0 collective-permute-done.4.refs_1_
  53.2 0.8 collective-permute-start.8
  54.0 0.0 collective-permute-done.7.refs_4_
  54.0 0.0 collective-permute-done.10.refs_7_
  54.0 0.1 collective-permute-done.9.refs_6_
  54.1 0.8 collective-permute-done.8.refs_5_
  54.9 5.5 %shard_map.44 = bf16[768,512]{1,0:T(8,128)(2,1)S(1)} custom-call(bf16[192,256]{1,0:T(8,128)(2,1)S(1)} %shard_map.43.refs_0_, bf16[192,256]{1,0:T(8,128)(2,1)S(1)} %collective-permute-done.4.refs_1_, bf16[192,256]{1,0:T(8,128)(2,1)S(1)} %collective-permute-done.5.refs_2_, bf16[192,256]{1,0:T(8,128)(2,1)S(1)} %collective-permute-done.6.refs_3_, ...), custom_call_target="tpu_custom_call" | custom-call | tf_op jit(solution)/shard_map/pallas_call | solution.py:161
  60.4 17.4 %all_to_all.11 = bf16[16,48,512]{2,1,0:T(8,128)(2,1)} all-to-all(bf16[16,48,512]{2,1,0:T(8,128)(2,1)S(1)} %bitcast.7), channel_id=1, replica_groups=mesh['replica'=8,'tensor'=16] {'tensor'}, dimensions={0} | all-to-all | bytes 1572864 | tf_op jit(solution)/shard_map/all_to_all | solution.py:187
  77.8 0.0 all-gather.2.cloned.1.call-update
  77.8 38.9 %all-gather.2.cloned.1.call-done = bf16[768,4096]{1,0:T(8,128)(2,1)} async-done(((bf16[768,512]{1,0:T(8,128)(2,1)}), bf16[768,4096]{1,0:T(8,128)(2,1)}) %all-gather.2.cloned.1.call-update) | async-done | bytes 6291472 | tf_op jit(solution)/shard_map/all_gather | solution.py:188
  116.7 6.3 %copy.5 = bf16[8,2,48,4096]{3,2,1,0:T(8,128)(2,1)} copy(bf16[8,2,48,4096]{3,2,1,0:T(8,128)(2,1)} %bitcast.8) | data formatting | bytes 12582912
  (1 shorter events, 0.0 us)
Async XLA Ops:
  7.2 109.5 %all-gather.2.cloned.1.call-start = ((), (), s32[]{:S(2)}) async-start(), calls=%async_computation.2 | async-start | bytes 7077888 | tf_op jit(solution)/shard_map/all_gather | solution.py:188
  32.9 3.2 %collective-permute-start = (bf16[768,256]{1,0:T(8,128)(2,1)S(1)}, bf16[768,256]{1,0:T(8,128)(2,1)S(1)}, u32[]{:S(2)}, u32[]{:S(2)}) collective-permute-start(bf16[768,256]{1,0:T(8,128)(2,1)S(1)} %get-tuple-element.9), channel_id=1, source_target_pairs={{0,16},{16,0},{32,48},{48,32},{64,80},{80,64},{96,112},{112,96},{1... | collective-permute-start | bytes 1179656 | tf_op jit(solution)/shard_map/ppermute | solution.py:39
  36.2 5.3 %collective-permute-start.1 = (bf16[192,256]{1,0:T(8,128)(2,1)S(1)}, bf16[192,256]{1,0:T(8,128)(2,1)S(1)}, u32[]{:S(2)}, u32[]{:S(2)}) collective-permute-start(bf16[192,256]{1,0:T(8,128)(2,1)S(1)} %get-tuple-element.11), channel_id=1, source_target_pairs={{0,32},{16,48},{32,64},{48,80},{64,96},{80,112},{96,0},{112,16},{1... | collective-permute-start | bytes 294920 | tf_op jit(solution)/shard_map/ppermute | solution.py:39
  37.4 4.0 %collective-permute-start.2 = (bf16[192,256]{1,0:T(8,128)(2,1)S(1)}, bf16[192,256]{1,0:T(8,128)(2,1)S(1)}, u32[]{:S(2)}, u32[]{:S(2)}) collective-permute-start(bf16[192,256]{1,0:T(8,128)(2,1)S(1)} %get-tuple-element.12), channel_id=1, source_target_pairs={{0,96},{16,112},{32,0},{48,16},{64,32},{80,48},{96,64},{112,80},{1... | collective-permute-start | bytes 294920 | tf_op jit(solution)/shard_map/ppermute | solution.py:39
  38.9 5.1 %collective-permute-start.3 = (bf16[192,256]{1,0:T(8,128)(2,1)S(1)}, bf16[192,256]{1,0:T(8,128)(2,1)S(1)}, u32[]{:S(2)}, u32[]{:S(2)}) collective-permute-start(bf16[192,256]{1,0:T(8,128)(2,1)S(1)} %get-tuple-element.13), channel_id=1, source_target_pairs={{0,64},{16,80},{32,96},{48,112},{64,0},{80,16},{96,32},{112,48},{1... | collective-permute-start | bytes 294920 | tf_op jit(solution)/shard_map/ppermute | solution.py:39
  44.0 6.5 %collective-permute-start.6 = (bf16[192,256]{1,0:T(8,128)(2,1)S(1)}, bf16[192,256]{1,0:T(8,128)(2,1)S(1)}, u32[]{:S(2)}, u32[]{:S(2)}) collective-permute-start(bf16[192,256]{1,0:T(8,128)(2,1)S(1)} %shard_map.43.refs_0_), channel_id=1, source_target_pairs={{0,32},{16,48},{32,64},{48,80},{64,96},{80,112},{96,0},{112,16},{1... | collective-permute-start | bytes 294920 | tf_op jit(solution)/shard_map/ppermute | solution.py:39
  45.3 6.7 %collective-permute-start.5 = (bf16[192,256]{1,0:T(8,128)(2,1)S(1)}, bf16[192,256]{1,0:T(8,128)(2,1)S(1)}, u32[]{:S(2)}, u32[]{:S(2)}) collective-permute-start(bf16[192,256]{1,0:T(8,128)(2,1)S(1)} %shard_map.43.refs_0_), channel_id=1, source_target_pairs={{0,64},{16,80},{32,96},{48,112},{64,0},{80,16},{96,32},{112,48},{1... | collective-permute-start | bytes 294920 | tf_op jit(solution)/shard_map/ppermute | solution.py:39
  46.8 6.4 %collective-permute-start.4 = (bf16[192,256]{1,0:T(8,128)(2,1)S(1)}, bf16[192,256]{1,0:T(8,128)(2,1)S(1)}, u32[]{:S(2)}, u32[]{:S(2)}) collective-permute-start(bf16[192,256]{1,0:T(8,128)(2,1)S(1)} %shard_map.43.refs_0_), channel_id=1, source_target_pairs={{0,96},{16,112},{32,0},{48,16},{64,32},{80,48},{96,64},{112,80},{1... | collective-permute-start | bytes 294920 | tf_op jit(solution)/shard_map/ppermute | solution.py:39
  47.8 6.2 %collective-permute-start.7 = (bf16[192,256]{1,0:T(8,128)(2,1)S(1)}, bf16[192,256]{1,0:T(8,128)(2,1)S(1)}, u32[]{:S(2)}, u32[]{:S(2)}) collective-permute-start(bf16[192,256]{1,0:T(8,128)(2,1)S(1)} %shard_map.43.refs_0_), channel_id=1, source_target_pairs={{0,16},{16,0},{32,48},{48,32},{64,80},{80,64},{96,112},{112,96},{1... | collective-permute-start | bytes 294920 | tf_op jit(solution)/shard_map/ppermute | solution.py:39
  50.5 3.5 %collective-permute-start.10 = (bf16[192,256]{1,0:T(8,128)(2,1)S(1)}, bf16[192,256]{1,0:T(8,128)(2,1)S(1)}, u32[]{:S(2)}, u32[]{:S(2)}) collective-permute-start(bf16[192,256]{1,0:T(8,128)(2,1)S(1)} %collective-permute-done.6.refs_3_), channel_id=1, source_target_pairs={{0,16},{16,0},{32,48},{48,32},{64,80},{80,64},{96,112},{112,96},{1... | collective-permute-start | bytes 294920 | tf_op jit(solution)/shard_map/ppermute | solution.py:39
  52.1 2.1 %collective-permute-start.9 = (bf16[192,256]{1,0:T(8,128)(2,1)S(1)}, bf16[192,256]{1,0:T(8,128)(2,1)S(1)}, u32[]{:S(2)}, u32[]{:S(2)}) collective-permute-start(bf16[192,256]{1,0:T(8,128)(2,1)S(1)} %collective-permute-done.5.refs_2_), channel_id=1, source_target_pairs={{0,16},{16,0},{32,48},{48,32},{64,80},{80,64},{96,112},{112,96},{1... | collective-permute-start | bytes 294920 | tf_op jit(solution)/shard_map/ppermute | solution.py:39
  53.2 1.7 %collective-permute-start.8 = (bf16[192,256]{1,0:T(8,128)(2,1)S(1)}, bf16[192,256]{1,0:T(8,128)(2,1)S(1)}, u32[]{:S(2)}, u32[]{:S(2)}) collective-permute-start(bf16[192,256]{1,0:T(8,128)(2,1)S(1)} %collective-permute-done.4.refs_1_), channel_id=1, source_target_pairs={{0,16},{16,0},{32,48},{48,32},{64,80},{80,64},{96,112},{112,96},{1... | collective-permute-start | bytes 294920 | tf_op jit(solution)/shard_map/ppermute | solution.py:39
Sparse Core Ops, SparseCore 0:
  77.9 38.7 all-gather.1

commit v2 on v1

--- a/solution.py
+++ b/solution.py
@@ -18,6 +18,9 @@
 epsilon = 1e-07
 scale_factor = 0.2 * math.sqrt(max(FF, D))
 
+WIDTH = 512
+EARLY = 128
+LATE = WIDTH - EARLY
 BLOCK = 256
 HALF = FF
 VMEM = pl.BlockSpec(memory_space=pltpu.VMEM)
@@ -47,7 +50,7 @@
     return jnp.dot(left, right, preferred_element_type=F32)
 
 
-def gram_kernel(rows_ref, keep_ref, send_ref):
+def gram_kernel(rows_ref, keep_ref, send_ref, early_ref):
     core = lax.axis_index("replica") % 2
 
     def rows(index):
@@ -64,6 +67,8 @@
                 keep_ref[where, :] = dot_t(rows(kept[0]), rows(kept[1]))
                 send_ref[where, :] = dot_t(rows(sent[0]), rows(sent[1])).astype(BF16)
 
+    early_ref[...] = rows_ref[:, LATE:]
+
 
 def partial_gram(rows):
     return pl.pallas_call(
@@ -71,9 +76,10 @@
         out_shape=(
             jax.ShapeDtypeStruct((HALF, BLOCK), F32),
             jax.ShapeDtypeStruct((HALF, BLOCK), BF16),
+            jax.ShapeDtypeStruct((FF, EARLY), BF16),
         ),
         in_specs=[VMEM],
-        out_specs=(VMEM, VMEM),
+        out_specs=(VMEM,) * 3,
         compiler_params=PARAMS,
     )(rows)
 
@@ -121,7 +127,8 @@
 
 
 def chain_kernel(*refs):
-    pieces, rows_ref, out_ref, packed, gram = refs[:8], refs[8], refs[9], refs[10], refs[11]
+    pieces, rows_ref, early_refs = refs[:8], refs[8], refs[9:13]
+    late_out, early_out, packed, gram = refs[13:]
     index = lax.axis_index("replica")
     chip, core = index // 2, index % 2
     for steps in range(4):
@@ -151,21 +158,68 @@
     half_way = (coef_linear * gram_0.astype(F32) + dot(poly_0, gram_0)).astype(BF16)
     gram_1 = (coef_linear * half_way.astype(F32) + dot(half_way, poly_0)).astype(BF16)
     poly_1 = (coef_gram * gram_1.astype(F32) + coef_square * dot(gram_1, gram_1)).astype(BF16)
-    rows = rows_ref[...]
-    first = ((coef_linear * rows.astype(F32) + dot(poly_0, rows)) * scale).astype(BF16)
-    second = coef_linear * first.astype(F32) + dot(poly_1, first)
-    out_ref[...] = (scale_factor * second).astype(BF16)
-
-
-def chain(pieces, rows):
+
+    def apply(rows):
+        first = ((coef_linear * rows.astype(F32) + dot(poly_0, rows)) * scale).astype(BF16)
+        second = coef_linear * first.astype(F32) + dot(poly_1, first)
+        return (scale_factor * second).astype(BF16)
+
+    late_out[...] = apply(rows_ref[:, :LATE])
+    early_out[...] = apply(jnp.concatenate([ref[...] for ref in early_refs], axis=1))
+
+
+def chain(pieces, rows, early):
     return pl.pallas_call(
         chain_kernel,
-        out_shape=jax.ShapeDtypeStruct(rows.shape, BF16),
-        in_specs=[VMEM] * 9,
-        out_specs=VMEM,
+        out_shape=(
+            jax.ShapeDtypeStruct((FF, LATE), BF16),
+            jax.ShapeDtypeStruct((FF, 4 * EARLY), BF16),
+        ),
+        in_specs=[VMEM] * 13,
+        out_specs=(VMEM, VMEM),
         scratch_shapes=[pltpu.VMEM((2, HALF, BLOCK), BF16), pltpu.VMEM((FF, FF), BF16)],
         compiler_params=PARAMS,
-    )(*pieces, rows)
+    )(*pieces, rows, *early)
+
+
+def place_kernel(where, aliased, *refs):
+    index = lax.axis_index("replica")
+    chip, core = index // 2, index % 2
+    count = len(where)
+    pieces, out_ref, sems = refs[:count], refs[count + aliased], refs[count + aliased + 1]
+    copies = []
+    for number, (steps, cross, first, width, source) in enumerate(where):
+        block = ((chip + steps) % 4) * 2 + (1 - core if cross else core)
+        column = pl.multiple_of(block * WIDTH + first, 128)
+        copies.append(
+            pltpu.make_async_copy(
+                pieces[number].at[:, :, pl.ds(source, width)],
+                out_ref.at[:, :, pl.ds(column, width)],
+                sems.at[number],
+            )
+        )
+    for copy in copies:
+        copy.start()
+    for copy in copies:
+        copy.wait()
+
+
+def place(output, shape, pieces):
+    arrays = [piece[0] for piece in pieces]
+    where = tuple(piece[1:] for piece in pieces)
+    aliased = output is not None
+    anywhere = pl.BlockSpec(memory_space=pl.ANY)
+    moved = sum(piece[4] for piece in pieces) * shape[0] * shape[1] * 4
+    return pl.pallas_call(
+        functools.partial(place_kernel, where, int(aliased)),
+        out_shape=jax.ShapeDtypeStruct(shape, BF16),
+        in_specs=[anywhere] * (len(arrays) + aliased),
+        out_specs=anywhere,
+        scratch_shapes=[pltpu.SemaphoreType.DMA((len(arrays),))],
+        input_output_aliases={len(arrays): 0} if aliased else {},
+        cost_estimate=pl.CostEstimate(flops=0, bytes_accessed=moved, transcendentals=0),
+        compiler_params=PARAMS,
+    )(*arrays, *([output] if aliased else []))
 
 
 def local(gradient, momentum):
@@ -176,18 +230,46 @@
     rows = lax.all_to_all(flat_rows, "tensor", split_axis=0, concat_axis=0, tiled=True)
     rows = rows.reshape(FF, col_count)
 
-    keep, send = partial_gram(rows)
+    keep, send, early = partial_gram(rows)
     own, to_next, to_last, to_far = chip_sum(keep, shift(send, 0, 1))
     mine = ring_sum(own, shift(to_next, 1), shift(to_last, -1), shift(to_far, 2))
     here = (mine, shift(mine, -1), shift(mine, 2), shift(mine, 1))
     other = tuple(shift(piece, 0, 1) for piece in here)
-    finished = chain(here + other, rows)
-
-    finished = finished.reshape(experts * pairs, row_count, col_count)
-    back = lax.all_to_all(finished, "tensor", split_axis=0, concat_axis=0, tiled=True)
-    whole = lax.all_gather(back.reshape(FF, col_count), "replica", axis=1, tiled=True)
-    update = whole.reshape(experts, pairs, row_count, whole.shape[1])
-    return (update, new_momentum)
+    early, _ = lax.optimization_barrier((early, mine))
+    early = (early, shift(early, -1), shift(early, 2), shift(early, 1))
+    late_rows, early_rows = chain(here + other, rows, early)
+
+    def back(value):
+        value = value.reshape(experts * pairs, row_count, value.shape[1])
+        return lax.all_to_all(value, "tensor", split_axis=0, concat_axis=0, tiled=True)
+
+    late = back(late_rows)
+    late, early_rows = lax.optimization_barrier((late, early_rows))
+    late_pieces = {0: late, 1: shift(late, -1), 3: shift(late, 1), 2: shift(late, 2)}
+    late_across = {steps: shift(piece, 0, 1) for steps, piece in late_pieces.items()}
+    early = back(early_rows)
+    early_across = shift(early, 0, 1)
+
+    shape = (experts * pairs, row_count, 8 * WIDTH)
+
+    def late_place(pieces, steps, cross):
+        return (pieces[steps], steps, cross, 0, LATE, 0)
+
+    def early_places(value, cross):
+        return [(value, steps, cross, LATE, EARLY, steps * EARLY) for steps in range(4)]
+
+    update = place(
+        None,
+        shape,
+        [late_place(late_pieces, 0, 0), late_place(late_across, 0, 1)] + early_places(early, 0),
+    )
+    update = place(
+        update,
+        shape,
+        [late_place(late_pieces, steps, 0) for steps in (1, 2, 3)] + early_places(early_across, 1),
+    )
+    update = place(update, shape, [late_place(late_across, steps, 1) for steps in (1, 2, 3)])
+    return (update.reshape(experts, pairs, row_count, 8 * WIDTH), new_momentum)
 
 
 def solution(mesh):

time: 130 us -> 119 us (0.915)
  starting transfers between devices: 16.1 us -> 36.7 us
  waiting for transfers between devices: 44.8 us -> 29.1 us
  between operations: 14.1 us -> 0.88 us
  local copies, waits for them, and re-layouts: 6.28 us -> 0 us
  Pallas kernels: 6.17 us -> 12.4 us
  blocking collectives: 39.3 us -> 36 us
    all_gather x1 -> x0, waiting for transfers between devices: 38.9 us -> none  [local(): lax.all_gather(back.reshape(FF, col_count), 'replica', axis=1, tiled=True)]
    ppermute x11 -> x22, starting transfers between devices: 16.1 us -> 33.1 us  [shift(): return lax.ppermute(value, 'replica', pairs)]
    ppermute x11 -> x22, waiting for transfers between devices: 5.86 us -> 18.7 us  [shift(): return lax.ppermute(value, 'replica', pairs)]
    all_to_all x0 -> x1, waiting for transfers between devices: none -> 10.3 us  [back(): lax.all_to_all(value, 'tensor', split_axis=0, concat_axis=0, tiled=True)]
    unnamed x1 -> x0, local copies, waits for them, and re-layouts: 6.28 us -> none
    pallas_call x1 -> x4, Pallas kernels: 5.46 us -> 11.7 us  [the longest x1 7.58 us: chain(): pl.pallas_call(chain_kernel, out_shape=(jax.ShapeDtypeStruct((FF, LATE),...]
    all_to_all x0 -> x1, starting transfers between devices: none -> 3.61 us  [back(): lax.all_to_all(value, 'tensor', split_axis=0, concat_axis=0, tiled=True)]
    all_to_all x1, blocking collectives: 17.4 us -> 14.1 us  [back(): lax.all_to_all(value, 'tensor', split_axis=0, concat_axis=0, tiled=True)]
  transfers between devices with their start and end apart: 12 -> 23, of which waited for: 6 -> 10; matrix products, arithmetic and copies ran while one was open for 0% -> 0% of each run, Pallas kernels for 0% -> 2%
where the time goes in v2:
time: 119 us; the launch traced here: 118 us
  starting transfers between devices  36.7 us (31%)
  blocking collectives  36 us (30%)
  waiting for transfers between devices  29.1 us (24%)
  Pallas kernels  12.4 us (10%)
  other arithmetic  3.16 us (3%)
    ppermute x22, starting transfers between devices, shift(): return lax.ppermute(value, 'replica', pairs)  33.1 us
    all_to_all x1, blocking collectives, local(): lax.all_to_all(flat_rows, 'tensor', split_axis=0, concat_axis=0, tiled=True)  21.9 us
    ppermute x22, waiting for transfers between devices, shift(): return lax.ppermute(value, 'replica', pairs)  18.7 us
    all_to_all x1, blocking collectives, back(): lax.all_to_all(value, 'tensor', split_axis=0, concat_axis=0, tiled=True)  14.1 us
    all_to_all x1, waiting for transfers between devices, back(): lax.all_to_all(value, 'tensor', split_axis=0, concat_axis=0, tiled=True)  10.3 us
    pallas_call x1, Pallas kernels, chain(): pl.pallas_call(chain_kernel, out_shape=(jax.ShapeDtypeStruct((FF, LATE),...  7.58 us
    pallas_call x3, Pallas kernels, place(): pl.pallas_call(functools.partial(place_kernel, where, int(aliased)), out_...  4.11 us
    all_to_all x1, starting transfers between devices, back(): lax.all_to_all(value, 'tensor', split_axis=0, concat_axis=0, tiled=True)  3.61 us
  transfers between devices with their start and end apart: 23, of which 10 were waited for; matrix products, arithmetic and copies ran while one was open for 0% of the time, Pallas kernels for 2%

profile of v2, /device:TPU:1, one launch (start us, length us, event | category | flops | bytes accessed | tf_op | source)
XLA Modules:
  0.0 118.3 jit_solution(13176091862977206758)
XLA Ops:
  0.6 3.2 %fusion = (bf16[8,2,48,512]{3,2,1,0:T(8,128)(2,1)S(1)}, f32[8,2,48,512]{3,2,1,0:T(8,128)}) fusion(bf16[8,2,48,512]{3,2,1,0:T(8,128)(2,1)} %param.2, f32[8,2,48,512]{3,2,1,0:T(8,128)} %param.3), kind=kLoop, calls=%fused_computation.2 | loop fusion | flops 2359296 | bytes 4718592 | tf_op jit(solution)/shard_map/convert_element_type | solution.py:227
  3.8 21.9 %all_to_all.15 = bf16[16,48,512]{2,1,0:T(8,128)(2,1)S(1)} all-to-all(bf16[16,48,512]{2,1,0:T(8,128)(2,1)S(1)} %bitcast.9), channel_id=1, replica_groups=mesh['replica'=8,'tensor'=16] {'tensor'}, dimensions={0} | all-to-all | bytes 1572864 | tf_op jit(solution)/shard_map/all_to_all | solution.py:230
  25.7 0.6 shard_map.41
  26.3 1.9 %collective-permute-start = (bf16[768,256]{1,0:T(8,128)(2,1)S(1)}, bf16[768,256]{1,0:T(8,128)(2,1)S(1)}, u32[]{:S(2)}, u32[]{:S(2)}) collective-permute-start(bf16[768,256]{1,0:T(8,128)(2,1)S(1)} %get-tuple-element.15), channel_id=1, source_target_pairs={{0,16},{16,0},{32,48},{48,32},{64,80},{80,64},{96,112},{112,96},{1... | collective-permute-start | bytes 1179656 | tf_op jit(solution)/shard_map/ppermute | solution.py:42
  28.2 1.3 %collective-permute-done.got_ref = bf16[768,256]{1,0:T(8,128)(2,1)S(1)} collective-permute-done((bf16[768,256]{1,0:T(8,128)(2,1)S(1)}, bf16[768,256]{1,0:T(8,128)(2,1)S(1)}, u32[]{:S(2)}, u32[]{:S(2)}) %collective-permute-start) | collective-permute-done | bytes 393248 | tf_op jit(solution)/shard_map/ppermute | solution.py:42
  29.6 0.1 shard_map.42
  29.6 1.3 %collective-permute-start.1 = (bf16[192,256]{1,0:T(8,128)(2,1)S(1)}, bf16[192,256]{1,0:T(8,128)(2,1)S(1)}, u32[]{:S(2)}, u32[]{:S(2)}) collective-permute-start(bf16[192,256]{1,0:T(8,128)(2,1)S(1)} %get-tuple-element.17), channel_id=1, source_target_pairs={{0,32},{16,48},{32,64},{48,80},{64,96},{80,112},{96,0},{112,16},{1... | collective-permute-start | bytes 294920 | tf_op jit(solution)/shard_map/ppermute | solution.py:42
  30.9 1.5 %collective-permute-start.2 = (bf16[192,256]{1,0:T(8,128)(2,1)S(1)}, bf16[192,256]{1,0:T(8,128)(2,1)S(1)}, u32[]{:S(2)}, u32[]{:S(2)}) collective-permute-start(bf16[192,256]{1,0:T(8,128)(2,1)S(1)} %get-tuple-element.18), channel_id=1, source_target_pairs={{0,96},{16,112},{32,0},{48,16},{64,32},{80,48},{96,64},{112,80},{1... | collective-permute-start | bytes 294920 | tf_op jit(solution)/shard_map/ppermute | solution.py:42
  32.4 1.5 %collective-permute-start.3 = (bf16[192,256]{1,0:T(8,128)(2,1)S(1)}, bf16[192,256]{1,0:T(8,128)(2,1)S(1)}, u32[]{:S(2)}, u32[]{:S(2)}) collective-permute-start(bf16[192,256]{1,0:T(8,128)(2,1)S(1)} %get-tuple-element.19), channel_id=1, source_target_pairs={{0,64},{16,80},{32,96},{48,112},{64,0},{80,16},{96,32},{112,48},{1... | collective-permute-start | bytes 294920 | tf_op jit(solution)/shard_map/ppermute | solution.py:42
  33.9 1.0 collective-permute-done.1.a_ref
  34.9 0.0 collective-permute-done.2.b_ref
  34.9 2.5 %collective-permute-done.3.c_ref = bf16[192,256]{1,0:T(8,128)(2,1)S(1)} collective-permute-done((bf16[192,256]{1,0:T(8,128)(2,1)S(1)}, bf16[192,256]{1,0:T(8,128)(2,1)S(1)}, u32[]{:S(2)}, u32[]{:S(2)}) %collective-permute-start.3) | collective-permute-done | bytes 98336 | tf_op jit(solution)/shard_map/ppermute | solution.py:42
  37.5 1.3 %collective-permute-start.6 = (bf16[192,256]{1,0:T(8,128)(2,1)S(1)}, bf16[192,256]{1,0:T(8,128)(2,1)S(1)}, u32[]{:S(2)}, u32[]{:S(2)}) collective-permute-start(bf16[192,256]{1,0:T(8,128)(2,1)S(1)} %shard_map.43.refs_0_), channel_id=1, source_target_pairs={{0,32},{16,48},{32,64},{48,80},{64,96},{80,112},{96,0},{112,16},{1... | collective-permute-start | bytes 294920 | tf_op jit(solution)/shard_map/ppermute | solution.py:42
  38.8 1.4 %collective-permute-start.4 = (bf16[192,256]{1,0:T(8,128)(2,1)S(1)}, bf16[192,256]{1,0:T(8,128)(2,1)S(1)}, u32[]{:S(2)}, u32[]{:S(2)}) collective-permute-start(bf16[192,256]{1,0:T(8,128)(2,1)S(1)} %shard_map.43.refs_0_), channel_id=1, source_target_pairs={{0,96},{16,112},{32,0},{48,16},{64,32},{80,48},{96,64},{112,80},{1... | collective-permute-start | bytes 294920 | tf_op jit(solution)/shard_map/ppermute | solution.py:42
  40.2 0.3 collective-permute-start.11
  40.6 1.5 %collective-permute-start.12 = (bf16[768,128]{1,0:T(8,128)(2,1)S(1)}, bf16[768,128]{1,0:T(8,128)(2,1)S(1)}, u32[]{:S(2)}, u32[]{:S(2)}) collective-permute-start(bf16[768,128]{1,0:T(8,128)(2,1)S(1)} %get-tuple-element.21.refs_9_), channel_id=1, source_target_pairs={{0,64},{16,80},{32,96},{48,112},{64,0},{80,16},{96,32},{112,48},{1... | collective-permute-start | bytes 589832 | tf_op jit(solution)/shard_map/ppermute | solution.py:42
  42.1 0.0 collective-permute-start.13
  42.1 0.2 collective-permute-done.6.refs_3_
  42.3 3.0 %collective-permute-start.5 = (bf16[192,256]{1,0:T(8,128)(2,1)S(1)}, bf16[192,256]{1,0:T(8,128)(2,1)S(1)}, u32[]{:S(2)}, u32[]{:S(2)}) collective-permute-start(bf16[192,256]{1,0:T(8,128)(2,1)S(1)} %shard_map.43.refs_0_), channel_id=1, source_target_pairs={{0,64},{16,80},{32,96},{48,112},{64,0},{80,16},{96,32},{112,48},{1... | collective-permute-start | bytes 294920 | tf_op jit(solution)/shard_map/ppermute | solution.py:42
  45.3 3.7 %collective-permute-start.7 = (bf16[192,256]{1,0:T(8,128)(2,1)S(1)}, bf16[192,256]{1,0:T(8,128)(2,1)S(1)}, u32[]{:S(2)}, u32[]{:S(2)}) collective-permute-start(bf16[192,256]{1,0:T(8,128)(2,1)S(1)} %shard_map.43.refs_0_), channel_id=1, source_target_pairs={{0,16},{16,0},{32,48},{48,32},{64,80},{80,64},{96,112},{112,96},{1... | collective-permute-start | bytes 294920 | tf_op jit(solution)/shard_map/ppermute | solution.py:42
  49.0 3.4 %collective-permute-done.5.refs_2_ = bf16[192,256]{1,0:T(8,128)(2,1)S(1)} collective-permute-done((bf16[192,256]{1,0:T(8,128)(2,1)S(1)}, bf16[192,256]{1,0:T(8,128)(2,1)S(1)}, u32[]{:S(2)}, u32[]{:S(2)}) %collective-permute-start.5) | collective-permute-done | bytes 98336 | tf_op jit(solution)/shard_map/ppermute | solution.py:42
  52.3 3.6 %collective-permute-start.10 = (bf16[192,256]{1,0:T(8,128)(2,1)S(1)}, bf16[192,256]{1,0:T(8,128)(2,1)S(1)}, u32[]{:S(2)}, u32[]{:S(2)}) collective-permute-start(bf16[192,256]{1,0:T(8,128)(2,1)S(1)} %collective-permute-done.6.refs_3_), channel_id=1, source_target_pairs={{0,16},{16,0},{32,48},{48,32},{64,80},{80,64},{96,112},{112,96},{1... | collective-permute-start | bytes 294920 | tf_op jit(solution)/shard_map/ppermute | solution.py:42
  55.9 0.0 collective-permute-done.7.refs_4_
  56.0 0.0 collective-permute-start.8
  56.0 0.5 collective-permute-start.9
  56.5 0.0 collective-permute-done.13.refs_12_
  56.5 0.4 collective-permute-done.10.refs_7_
  56.9 0.4 collective-permute-done.8.refs_5_
  57.3 0.3 collective-permute-done.9.refs_6_
  57.5 7.6 %shard_map.44 = (bf16[768,384]{1,0:T(8,128)(2,1)S(1)}, bf16[768,512]{1,0:T(8,128)(2,1)}) custom-call(bf16[192,256]{1,0:T(8,128)(2,1)S(1)} %shard_map.43.refs_0_, bf16[192,256]{1,0:T(8,128)(2,1)S(1)} %collective-permute-done.4.refs_1_, bf16[192,256]{1,0:T(8,128)(2,1)S(1)} %collective-permute-done.5.refs_2_, ...), custom_call_target="tpu_custom_call" | custom-call | tf_op jit(solution)/shard_map/pallas_call | solution.py:172
  65.1 14.1 %all_to_all.16.refs_0_ = bf16[16,48,384]{2,1,0:T(8,128)(2,1)S(1)} all-to-all(bf16[16,48,384]{2,1,0:T(8,128)(2,1)S(1)} %bitcast.7), channel_id=1, replica_groups=mesh['replica'=8,'tensor'=16] {'tensor'}, dimensions={0} | all-to-all | bytes 1179648 | tf_op jit(solution)/shard_map/all_to_all | solution.py:244
  79.2 3.6 %all-to-all-start.2 = ((bf16[16,48,512]{2,1,0:T(8,128)(2,1)}), bf16[16,48,512]{2,1,0:T(8,128)(2,1)S(1)}, u32[]{:S(2)}, u32[]{:S(2)}) async-start(bf16[16,48,512]{2,1,0:T(8,128)(2,1)} %bitcast.3), calls=%async_computation.2 | async-start | bytes 1572864 | tf_op jit(solution)/shard_map/all_to_all | solution.py:244
  82.9 1.5 %collective-permute-start.14 = (bf16[16,48,384]{2,1,0:T(8,128)(2,1)S(1)}, bf16[16,48,384]{2,1,0:T(8,128)(2,1)S(1)}, u32[]{:S(2)}, u32[]{:S(2)}) collective-permute-start(bf16[16,48,384]{2,1,0:T(8,128)(2,1)S(1)} %all_to_all.16.refs_0_), channel_id=1, source_target_pairs={{0,96},{16,112},{32,0},{48,16},{64,32},{80,48},{96,64},{112,80},{1... | collective-permute-start | bytes 1769480 | tf_op jit(solution)/shard_map/ppermute | solution.py:42
  84.3 0.1 collective-permute-start.16
  84.4 0.8 collective-permute-start.18
  85.1 10.3 %all-to-all-done.2.refs_2_.refs_3_.refs_4_.refs_5_ = bf16[16,48,512]{2,1,0:T(8,128)(2,1)S(1)} async-done(((bf16[16,48,512]{2,1,0:T(8,128)(2,1)}), bf16[16,48,512]{2,1,0:T(8,128)(2,1)S(1)}, u32[]{:S(2)}, u32[]{:S(2)}) %all-to-all-start.2) | async-done | bytes 786464 | tf_op jit(solution)/shard_map/all_to_all | solution.py:244
  95.5 2.7 %collective-permute-start.20 = (bf16[16,48,512]{2,1,0:T(8,128)(2,1)S(1)}, bf16[16,48,512]{2,1,0:T(8,128)(2,1)S(1)}, u32[]{:S(2)}, u32[]{:S(2)}) collective-permute-start(bf16[16,48,512]{2,1,0:T(8,128)(2,1)S(1)} %all-to-all-done.2.refs_2_.refs_3_.refs_4_.refs_5_), channel_id=1, source_target_pairs={{0,16},{16,0},{32,48},{48,32},{64,80},{80,64},{96,112},{112,96},{1... | collective-permute-start | bytes 2359304 | tf_op jit(solution)/shard_map/ppermute | solution.py:42
  98.2 0.0 collective-permute-start.21
  98.2 2.7 %collective-permute-start.15 = (bf16[16,48,384]{2,1,0:T(8,128)(2,1)S(1)}, bf16[16,48,384]{2,1,0:T(8,128)(2,1)S(1)}, u32[]{:S(2)}, u32[]{:S(2)}) collective-permute-start(bf16[16,48,384]{2,1,0:T(8,128)(2,1)S(1)} %collective-permute-done.14.refs_0_), channel_id=1, source_target_pairs={{0,16},{16,0},{32,48},{48,32},{64,80},{80,64},{96,112},{112,96},{1... | collective-permute-start | bytes 1769480 | tf_op jit(solution)/shard_map/ppermute | solution.py:42
  100.9 3.2 %collective-permute-start.17 = (bf16[16,48,384]{2,1,0:T(8,128)(2,1)S(1)}, bf16[16,48,384]{2,1,0:T(8,128)(2,1)S(1)}, u32[]{:S(2)}, u32[]{:S(2)}) collective-permute-start(bf16[16,48,384]{2,1,0:T(8,128)(2,1)S(1)} %collective-permute-done.16.refs_1_), channel_id=1, source_target_pairs={{0,16},{16,0},{32,48},{48,32},{64,80},{80,64},{96,112},{112,96},{1... | collective-permute-start | bytes 1769480 | tf_op jit(solution)/shard_map/ppermute | solution.py:42
  104.1 9.2 %collective-permute-done.18.refs_2_ = bf16[16,48,384]{2,1,0:T(8,128)(2,1)S(1)} collective-permute-done((bf16[16,48,384]{2,1,0:T(8,128)(2,1)S(1)}, bf16[16,48,384]{2,1,0:T(8,128)(2,1)S(1)}, u32[]{:S(2)}, u32[]{:S(2)}) %collective-permute-start.18) | collective-permute-done | bytes 589856 | tf_op jit(solution)/shard_map/ppermute | solution.py:42
  113.2 0.7 collective-permute-start.19
  114.0 1.3 %shard_map.45.refs_7_ = bf16[16,48,4096]{2,1,0:T(8,128)(2,1)} custom-call(bf16[16,48,384]{2,1,0:T(8,128)(2,1)S(1)} %all_to_all.16.refs_0_, bf16[16,48,384]{2,1,0:T(8,128)(2,1)S(1)} %collective-permute-done.21.refs_1_, bf16[16,48,512]{2,1,0:T(8,128)(2,1)S(1)} %all-to-all-done.2.refs_2_.refs_3_.refs_4_.refs_5_, ...), custom_call_target="tpu_custom_call" | custom-call | bytes 3932160 | tf_op jit(solution)/shard_map/pallas_call | solution.py:213
  115.3 0.0 collective-permute-done.20.refs_3_.refs_4_.refs_5_.refs_6_
  115.3 1.5 %shard_map.46.refs_3_ = bf16[16,48,4096]{2,1,0:T(8,128)(2,1)} custom-call(bf16[16,48,384]{2,1,0:T(8,128)(2,1)S(1)} %collective-permute-done.14.refs_0_, bf16[16,48,384]{2,1,0:T(8,128)(2,1)S(1)} %collective-permute-done.16.refs_1_, bf16[16,48,384]{2,1,0:T(8,128)(2,1)S(1)} %collective-permute-done.18.refs_2_, ...), custom_call_target="tpu_custom_call", output_to_operand_aliasing={{}: (7, {})} | custom-call | bytes 5111808 | tf_op jit(solution)/shard_map/pallas_call | solution.py:213
  116.9 0.0 collective-permute-done.17.refs_1_
  116.9 0.0 collective-permute-done.19.refs_2_
  116.9 1.3 %shard_map.47 = bf16[16,48,4096]{2,1,0:T(8,128)(2,1)} custom-call(bf16[16,48,384]{2,1,0:T(8,128)(2,1)S(1)} %collective-permute-done.15.refs_0_, bf16[16,48,384]{2,1,0:T(8,128)(2,1)S(1)} %collective-permute-done.17.refs_1_, bf16[16,48,384]{2,1,0:T(8,128)(2,1)S(1)} %collective-permute-done.19.refs_2_, ...), custom_call_target="tpu_custom_call", output_to_operand_aliasing={{}: (3, {})} | custom-call | bytes 3538944 | tf_op jit(solution)/shard_map/pallas_call | solution.py:213
  (8 shorter events, 0.1 us)
Async XLA Ops:
  26.3 3.2 %collective-permute-start = (bf16[768,256]{1,0:T(8,128)(2,1)S(1)}, bf16[768,256]{1,0:T(8,128)(2,1)S(1)}, u32[]{:S(2)}, u32[]{:S(2)}) collective-permute-start(bf16[768,256]{1,0:T(8,128)(2,1)S(1)} %get-tuple-element.15), channel_id=1, source_target_pairs={{0,16},{16,0},{32,48},{48,32},{64,80},{80,64},{96,112},{112,96},{1... | collective-permute-start | bytes 1179656 | tf_op jit(solution)/shard_map/ppermute | solution.py:42
  29.6 5.3 %collective-permute-start.1 = (bf16[192,256]{1,0:T(8,128)(2,1)S(1)}, bf16[192,256]{1,0:T(8,128)(2,1)S(1)}, u32[]{:S(2)}, u32[]{:S(2)}) collective-permute-start(bf16[192,256]{1,0:T(8,128)(2,1)S(1)} %get-tuple-element.17), channel_id=1, source_target_pairs={{0,32},{16,48},{32,64},{48,80},{64,96},{80,112},{96,0},{112,16},{1... | collective-permute-start | bytes 294920 | tf_op jit(solution)/shard_map/ppermute | solution.py:42
  30.9 4.0 %collective-permute-start.2 = (bf16[192,256]{1,0:T(8,128)(2,1)S(1)}, bf16[192,256]{1,0:T(8,128)(2,1)S(1)}, u32[]{:S(2)}, u32[]{:S(2)}) collective-permute-start(bf16[192,256]{1,0:T(8,128)(2,1)S(1)} %get-tuple-element.18), channel_id=1, source_target_pairs={{0,96},{16,112},{32,0},{48,16},{64,32},{80,48},{96,64},{112,80},{1... | collective-permute-start | bytes 294920 | tf_op jit(solution)/shard_map/ppermute | solution.py:42
  32.4 5.1 %collective-permute-start.3 = (bf16[192,256]{1,0:T(8,128)(2,1)S(1)}, bf16[192,256]{1,0:T(8,128)(2,1)S(1)}, u32[]{:S(2)}, u32[]{:S(2)}) collective-permute-start(bf16[192,256]{1,0:T(8,128)(2,1)S(1)} %get-tuple-element.19), channel_id=1, source_target_pairs={{0,64},{16,80},{32,96},{48,112},{64,0},{80,16},{96,32},{112,48},{1... | collective-permute-start | bytes 294920 | tf_op jit(solution)/shard_map/ppermute | solution.py:42
  37.5 4.7 %collective-permute-start.6 = (bf16[192,256]{1,0:T(8,128)(2,1)S(1)}, bf16[192,256]{1,0:T(8,128)(2,1)S(1)}, u32[]{:S(2)}, u32[]{:S(2)}) collective-permute-start(bf16[192,256]{1,0:T(8,128)(2,1)S(1)} %shard_map.43.refs_0_), channel_id=1, source_target_pairs={{0,32},{16,48},{32,64},{48,80},{64,96},{80,112},{96,0},{112,16},{1... | collective-permute-start | bytes 294920 | tf_op jit(solution)/shard_map/ppermute | solution.py:42
  38.8 6.5 %collective-permute-start.4 = (bf16[192,256]{1,0:T(8,128)(2,1)S(1)}, bf16[192,256]{1,0:T(8,128)(2,1)S(1)}, u32[]{:S(2)}, u32[]{:S(2)}) collective-permute-start(bf16[192,256]{1,0:T(8,128)(2,1)S(1)} %shard_map.43.refs_0_), channel_id=1, source_target_pairs={{0,96},{16,112},{32,0},{48,16},{64,32},{80,48},{96,64},{112,80},{1... | collective-permute-start | bytes 294920 | tf_op jit(solution)/shard_map/ppermute | solution.py:42
  40.2 15.7 %collective-permute-start.11 = (bf16[768,128]{1,0:T(8,128)(2,1)S(1)}, bf16[768,128]{1,0:T(8,128)(2,1)S(1)}, u32[]{:S(2)}, u32[]{:S(2)}) collective-permute-start(bf16[768,128]{1,0:T(8,128)(2,1)S(1)} %get-tuple-element.21.refs_9_), channel_id=1, source_target_pairs={{0,96},{16,112},{32,0},{48,16},{64,32},{80,48},{96,64},{112,80},{1... | collective-permute-start | bytes 589832 | tf_op jit(solution)/shard_map/ppermute | solution.py:42
  40.6 15.9 %collective-permute-start.12 = (bf16[768,128]{1,0:T(8,128)(2,1)S(1)}, bf16[768,128]{1,0:T(8,128)(2,1)S(1)}, u32[]{:S(2)}, u32[]{:S(2)}) collective-permute-start(bf16[768,128]{1,0:T(8,128)(2,1)S(1)} %get-tuple-element.21.refs_9_), channel_id=1, source_target_pairs={{0,64},{16,80},{32,96},{48,112},{64,0},{80,16},{96,32},{112,48},{1... | collective-permute-start | bytes 589832 | tf_op jit(solution)/shard_map/ppermute | solution.py:42
  42.1 14.4 %collective-permute-start.13 = (bf16[768,128]{1,0:T(8,128)(2,1)S(1)}, bf16[768,128]{1,0:T(8,128)(2,1)S(1)}, u32[]{:S(2)}, u32[]{:S(2)}) collective-permute-start(bf16[768,128]{1,0:T(8,128)(2,1)S(1)} %get-tuple-element.21.refs_9_), channel_id=1, source_target_pairs={{0,32},{16,48},{32,64},{48,80},{64,96},{80,112},{96,0},{112,16},{1... | collective-permute-start | bytes 589832 | tf_op jit(solution)/shard_map/ppermute | solution.py:42
  42.3 10.1 %collective-permute-start.5 = (bf16[192,256]{1,0:T(8,128)(2,1)S(1)}, bf16[192,256]{1,0:T(8,128)(2,1)S(1)}, u32[]{:S(2)}, u32[]{:S(2)}) collective-permute-start(bf16[192,256]{1,0:T(8,128)(2,1)S(1)} %shard_map.43.refs_0_), channel_id=1, source_target_pairs={{0,64},{16,80},{32,96},{48,112},{64,0},{80,16},{96,32},{112,48},{1... | collective-permute-start | bytes 294920 | tf_op jit(solution)/shard_map/ppermute | solution.py:42
  45.3 10.7 %collective-permute-start.7 = (bf16[192,256]{1,0:T(8,128)(2,1)S(1)}, bf16[192,256]{1,0:T(8,128)(2,1)S(1)}, u32[]{:S(2)}, u32[]{:S(2)}) collective-permute-start(bf16[192,256]{1,0:T(8,128)(2,1)S(1)} %shard_map.43.refs_0_), channel_id=1, source_target_pairs={{0,16},{16,0},{32,48},{48,32},{64,80},{80,64},{96,112},{112,96},{1... | collective-permute-start | bytes 294920 | tf_op jit(solution)/shard_map/ppermute | solution.py:42
  52.3 4.6 %collective-permute-start.10 = (bf16[192,256]{1,0:T(8,128)(2,1)S(1)}, bf16[192,256]{1,0:T(8,128)(2,1)S(1)}, u32[]{:S(2)}, u32[]{:S(2)}) collective-permute-start(bf16[192,256]{1,0:T(8,128)(2,1)S(1)} %collective-permute-done.6.refs_3_), channel_id=1, source_target_pairs={{0,16},{16,0},{32,48},{48,32},{64,80},{80,64},{96,112},{112,96},{1... | collective-permute-start | bytes 294920 | tf_op jit(solution)/shard_map/ppermute | solution.py:42
  56.0 1.3 %collective-permute-start.8 = (bf16[192,256]{1,0:T(8,128)(2,1)S(1)}, bf16[192,256]{1,0:T(8,128)(2,1)S(1)}, u32[]{:S(2)}, u32[]{:S(2)}) collective-permute-start(bf16[192,256]{1,0:T(8,128)(2,1)S(1)} %collective-permute-done.4.refs_1_), channel_id=1, source_target_pairs={{0,16},{16,0},{32,48},{48,32},{64,80},{80,64},{96,112},{112,96},{1... | collective-permute-start | bytes 294920 | tf_op jit(solution)/shard_map/ppermute | solution.py:42
  56.0 1.6 %collective-permute-start.9 = (bf16[192,256]{1,0:T(8,128)(2,1)S(1)}, bf16[192,256]{1,0:T(8,128)(2,1)S(1)}, u32[]{:S(2)}, u32[]{:S(2)}) collective-permute-start(bf16[192,256]{1,0:T(8,128)(2,1)S(1)} %collective-permute-done.5.refs_2_), channel_id=1, source_target_pairs={{0,16},{16,0},{32,48},{48,32},{64,80},{80,64},{96,112},{112,96},{1... | collective-permute-start | bytes 294920 | tf_op jit(solution)/shard_map/ppermute | solution.py:42
  79.2 16.2 %all-to-all-start.2 = ((bf16[16,48,512]{2,1,0:T(8,128)(2,1)}), bf16[16,48,512]{2,1,0:T(8,128)(2,1)S(1)}, u32[]{:S(2)}, u32[]{:S(2)}) async-start(bf16[16,48,512]{2,1,0:T(8,128)(2,1)} %bitcast.3), calls=%async_computation.2 | async-start | bytes 1572864 | tf_op jit(solution)/shard_map/all_to_all | solution.py:244
  82.9 15.3 %collective-permute-start.14 = (bf16[16,48,384]{2,1,0:T(8,128)(2,1)S(1)}, bf16[16,48,384]{2,1,0:T(8,128)(2,1)S(1)}, u32[]{:S(2)}, u32[]{:S(2)}) collective-permute-start(bf16[16,48,384]{2,1,0:T(8,128)(2,1)S(1)} %all_to_all.16.refs_0_), channel_id=1, source_target_pairs={{0,96},{16,112},{32,0},{48,16},{64,32},{80,48},{96,64},{112,80},{1... | collective-permute-start | bytes 1769480 | tf_op jit(solution)/shard_map/ppermute | solution.py:42
  84.3 16.6 %collective-permute-start.16 = (bf16[16,48,384]{2,1,0:T(8,128)(2,1)S(1)}, bf16[16,48,384]{2,1,0:T(8,128)(2,1)S(1)}, u32[]{:S(2)}, u32[]{:S(2)}) collective-permute-start(bf16[16,48,384]{2,1,0:T(8,128)(2,1)S(1)} %all_to_all.16.refs_0_), channel_id=1, source_target_pairs={{0,64},{16,80},{32,96},{48,112},{64,0},{80,16},{96,32},{112,48},{1... | collective-permute-start | bytes 1769480 | tf_op jit(solution)/shard_map/ppermute | solution.py:42
  84.4 28.9 %collective-permute-start.18 = (bf16[16,48,384]{2,1,0:T(8,128)(2,1)S(1)}, bf16[16,48,384]{2,1,0:T(8,128)(2,1)S(1)}, u32[]{:S(2)}, u32[]{:S(2)}) collective-permute-start(bf16[16,48,384]{2,1,0:T(8,128)(2,1)S(1)} %all_to_all.16.refs_0_), channel_id=1, source_target_pairs={{0,32},{16,48},{32,64},{48,80},{64,96},{80,112},{96,0},{112,16},{1... | collective-permute-start | bytes 1769480 | tf_op jit(solution)/shard_map/ppermute | solution.py:42
  95.5 19.8 %collective-permute-start.20 = (bf16[16,48,512]{2,1,0:T(8,128)(2,1)S(1)}, bf16[16,48,512]{2,1,0:T(8,128)(2,1)S(1)}, u32[]{:S(2)}, u32[]{:S(2)}) collective-permute-start(bf16[16,48,512]{2,1,0:T(8,128)(2,1)S(1)} %all-to-all-done.2.refs_2_.refs_3_.refs_4_.refs_5_), channel_id=1, source_target_pairs={{0,16},{16,0},{32,48},{48,32},{64,80},{80,64},{96,112},{112,96},{1... | collective-permute-start | bytes 2359304 | tf_op jit(solution)/shard_map/ppermute | solution.py:42
  98.2 15.8 %collective-permute-start.21 = (bf16[16,48,384]{2,1,0:T(8,128)(2,1)S(1)}, bf16[16,48,384]{2,1,0:T(8,128)(2,1)S(1)}, u32[]{:S(2)}, u32[]{:S(2)}) collective-permute-start(bf16[16,48,384]{2,1,0:T(8,128)(2,1)S(1)} %all_to_all.16.refs_0_), channel_id=1, source_target_pairs={{0,16},{16,0},{32,48},{48,32},{64,80},{80,64},{96,112},{112,96},{1... | collective-permute-start | bytes 1769480 | tf_op jit(solution)/shard_map/ppermute | solution.py:42
  98.2 18.7 %collective-permute-start.15 = (bf16[16,48,384]{2,1,0:T(8,128)(2,1)S(1)}, bf16[16,48,384]{2,1,0:T(8,128)(2,1)S(1)}, u32[]{:S(2)}, u32[]{:S(2)}) collective-permute-start(bf16[16,48,384]{2,1,0:T(8,128)(2,1)S(1)} %collective-permute-done.14.refs_0_), channel_id=1, source_target_pairs={{0,16},{16,0},{32,48},{48,32},{64,80},{80,64},{96,112},{112,96},{1... | collective-permute-start | bytes 1769480 | tf_op jit(solution)/shard_map/ppermute | solution.py:42
  100.9 16.0 %collective-permute-start.17 = (bf16[16,48,384]{2,1,0:T(8,128)(2,1)S(1)}, bf16[16,48,384]{2,1,0:T(8,128)(2,1)S(1)}, u32[]{:S(2)}, u32[]{:S(2)}) collective-permute-start(bf16[16,48,384]{2,1,0:T(8,128)(2,1)S(1)} %collective-permute-done.16.refs_1_), channel_id=1, source_target_pairs={{0,16},{16,0},{32,48},{48,32},{64,80},{80,64},{96,112},{112,96},{1... | collective-permute-start | bytes 1769480 | tf_op jit(solution)/shard_map/ppermute | solution.py:42
  113.2 3.6 %collective-permute-start.19 = (bf16[16,48,384]{2,1,0:T(8,128)(2,1)S(1)}, bf16[16,48,384]{2,1,0:T(8,128)(2,1)S(1)}, u32[]{:S(2)}, u32[]{:S(2)}) collective-permute-start(bf16[16,48,384]{2,1,0:T(8,128)(2,1)S(1)} %collective-permute-done.18.refs_2_), channel_id=1, source_target_pairs={{0,16},{16,0},{32,48},{48,32},{64,80},{80,64},{96,112},{112,96},{1... | collective-permute-start | bytes 1769480 | tf_op jit(solution)/shard_map/ppermute | solution.py:42

commit v3 on v2

--- a/solution.py
+++ b/solution.py
@@ -19,12 +19,14 @@
 scale_factor = 0.2 * math.sqrt(max(FF, D))
 
 WIDTH = 512
-EARLY = 128
+EARLY = 256
 LATE = WIDTH - EARLY
 BLOCK = 256
 HALF = FF
 VMEM = pl.BlockSpec(memory_space=pltpu.VMEM)
-PARAMS = pltpu.CompilerParams(vmem_limit_bytes=48 * 1024 * 1024)
+HBM = pl.BlockSpec(memory_space=pltpu.HBM)
+PARAMS = pltpu.CompilerParams(vmem_limit_bytes=16 * 1024 * 1024)
+LARGE = pltpu.CompilerParams(vmem_limit_bytes=32 * 1024 * 1024)
 F32, BF16 = jnp.float32, jnp.bfloat16
 
 
@@ -127,8 +129,8 @@
 
 
 def chain_kernel(*refs):
-    pieces, rows_ref, early_refs = refs[:8], refs[8], refs[9:13]
-    late_out, early_out, packed, gram = refs[13:]
+    pieces, rows_ref = refs[:8], refs[8]
+    out_ref, polys_out, scale_ref, packed, gram, polys, sems = refs[9:]
     index = lax.axis_index("replica")
     chip, core = index // 2, index % 2
     for steps in range(4):
@@ -158,28 +160,71 @@
     half_way = (coef_linear * gram_0.astype(F32) + dot(poly_0, gram_0)).astype(BF16)
     gram_1 = (coef_linear * half_way.astype(F32) + dot(half_way, poly_0)).astype(BF16)
     poly_1 = (coef_gram * gram_1.astype(F32) + coef_square * dot(gram_1, gram_1)).astype(BF16)
-
-    def apply(rows):
-        first = ((coef_linear * rows.astype(F32) + dot(poly_0, rows)) * scale).astype(BF16)
-        second = coef_linear * first.astype(F32) + dot(poly_1, first)
-        return (scale_factor * second).astype(BF16)
-
-    late_out[...] = apply(rows_ref[:, :LATE])
-    early_out[...] = apply(jnp.concatenate([ref[...] for ref in early_refs], axis=1))
-
-
-def chain(pieces, rows, early):
+    polys[0] = poly_0
+    polys[1] = poly_1
+    scale_ref[...] = jnp.broadcast_to(scale, scale_ref.shape)
+    keep = pltpu.make_async_copy(polys, polys_out, sems.at[0])
+    keep.start()
+    out_ref[...] = both_steps(poly_0, poly_1, scale, rows_ref[:, :LATE])
+    keep.wait()
+
+
+def both_steps(poly_0, poly_1, scale, rows):
+    first = ((coef_linear * rows.astype(F32) + dot(poly_0, rows)) * scale).astype(BF16)
+    second = coef_linear * first.astype(F32) + dot(poly_1, first)
+    return (scale_factor * second).astype(BF16)
+
+
+def chain(pieces, rows):
     return pl.pallas_call(
         chain_kernel,
         out_shape=(
             jax.ShapeDtypeStruct((FF, LATE), BF16),
-            jax.ShapeDtypeStruct((FF, 4 * EARLY), BF16),
+            jax.ShapeDtypeStruct((2, FF, FF), BF16),
+            jax.ShapeDtypeStruct((8, 128), F32),
         ),
-        in_specs=[VMEM] * 13,
-        out_specs=(VMEM, VMEM),
-        scratch_shapes=[pltpu.VMEM((2, HALF, BLOCK), BF16), pltpu.VMEM((FF, FF), BF16)],
-        compiler_params=PARAMS,
-    )(*pieces, rows, *early)
+        in_specs=[VMEM] * 9,
+        out_specs=(VMEM, HBM, VMEM),
+        scratch_shapes=[
+            pltpu.VMEM((2, HALF, BLOCK), BF16),
+            pltpu.VMEM((FF, FF), BF16),
+            pltpu.VMEM((2, FF, FF), BF16),
+            pltpu.SemaphoreType.DMA((1,)),
+        ],
+        compiler_params=LARGE,
+    )(*pieces, rows)
+
+
+def early_kernel(polys_in, scale_ref, *refs):
+    early_in, out_ref, polys, early, sems = refs[:4], refs[4], refs[5], refs[6], refs[7]
+    copies = [pltpu.make_async_copy(polys_in, polys, sems.at[4])]
+    for steps in range(4):
+        copies.append(pltpu.make_async_copy(early_in[steps], early.at[steps], sems.at[steps]))
+    for copy in copies:
+        copy.start()
+    copies[0].wait()
+    for steps in range(4):
+        copies[1 + steps].wait()
+        out_ref[:, pl.ds(steps * EARLY, EARLY)] = both_steps(
+            polys[0], polys[1], scale_ref[:1, :1], early[steps]
+        )
+
+
+def early_products(polys, scale, early):
+    flops = 2 * 2 * FF * FF * 4 * EARLY
+    return pl.pallas_call(
+        early_kernel,
+        out_shape=jax.ShapeDtypeStruct((FF, 4 * EARLY), BF16),
+        in_specs=[HBM, VMEM] + [HBM] * 4,
+        out_specs=VMEM,
+        scratch_shapes=[
+            pltpu.VMEM((2, FF, FF), BF16),
+            pltpu.VMEM((4, FF, EARLY), BF16),
+            pltpu.SemaphoreType.DMA((5,)),
+        ],
+        cost_estimate=pl.CostEstimate(flops=flops, bytes_accessed=0, transcendentals=0),
+        compiler_params=LARGE,
+    )(polys, scale, *early)
 
 
 def place_kernel(where, aliased, *refs):
@@ -209,7 +254,6 @@
     where = tuple(piece[1:] for piece in pieces)
     aliased = output is not None
     anywhere = pl.BlockSpec(memory_space=pl.ANY)
-    moved = sum(piece[4] for piece in pieces) * shape[0] * shape[1] * 4
     return pl.pallas_call(
         functools.partial(place_kernel, where, int(aliased)),
         out_shape=jax.ShapeDtypeStruct(shape, BF16),
@@ -217,16 +261,18 @@
         out_specs=anywhere,
         scratch_shapes=[pltpu.SemaphoreType.DMA((len(arrays),))],
         input_output_aliases={len(arrays): 0} if aliased else {},
-        cost_estimate=pl.CostEstimate(flops=0, bytes_accessed=moved, transcendentals=0),
+        cost_estimate=pl.CostEstimate(flops=0, bytes_accessed=0, transcendentals=0),
         compiler_params=PARAMS,
     )(*arrays, *([output] if aliased else []))
 
 
 def local(gradient, momentum):
-    new_momentum = momentum_decay * momentum + gradient.astype(F32)
-    look_ahead = (gradient.astype(F32) + momentum_decay * new_momentum).astype(BF16)
-    experts, pairs, row_count, col_count = look_ahead.shape
-    flat_rows = look_ahead.reshape(experts * pairs, row_count, col_count)
+    def stepped(gradient, momentum):
+        return momentum_decay * momentum + gradient.astype(F32)
+
+    ahead = gradient.astype(F32) + momentum_decay * stepped(gradient, momentum)
+    experts, pairs, row_count, col_count = gradient.shape
+    flat_rows = ahead.astype(BF16).reshape(experts * pairs, row_count, col_count)
     rows = lax.all_to_all(flat_rows, "tensor", split_axis=0, concat_axis=0, tiled=True)
     rows = rows.reshape(FF, col_count)
 
@@ -235,40 +281,37 @@
     mine = ring_sum(own, shift(to_next, 1), shift(to_last, -1), shift(to_far, 2))
     here = (mine, shift(mine, -1), shift(mine, 2), shift(mine, 1))
     other = tuple(shift(piece, 0, 1) for piece in here)
-    early, _ = lax.optimization_barrier((early, mine))
-    early = (early, shift(early, -1), shift(early, 2), shift(early, 1))
-    late_rows, early_rows = chain(here + other, rows, early)
+    late_rows, polys, scale = chain(here + other, rows)
 
     def back(value):
         value = value.reshape(experts * pairs, row_count, value.shape[1])
         return lax.all_to_all(value, "tensor", split_axis=0, concat_axis=0, tiled=True)
 
+    gradient, momentum, late_rows = lax.optimization_barrier((gradient, momentum, late_rows))
+    new_momentum = stepped(gradient, momentum)
+    early, _ = lax.optimization_barrier((early, here[2]))
+    early = (early, shift(early, -1), shift(early, 2), shift(early, 1))
+    early_rows = early_products(polys, scale, early)
     late = back(late_rows)
-    late, early_rows = lax.optimization_barrier((late, early_rows))
+    late, early_rows, new_momentum = lax.optimization_barrier((late, early_rows, new_momentum))
     late_pieces = {0: late, 1: shift(late, -1), 3: shift(late, 1), 2: shift(late, 2)}
-    late_across = {steps: shift(piece, 0, 1) for steps, piece in late_pieces.items()}
     early = back(early_rows)
-    early_across = shift(early, 0, 1)
 
     shape = (experts * pairs, row_count, 8 * WIDTH)
 
     def late_place(pieces, steps, cross):
         return (pieces[steps], steps, cross, 0, LATE, 0)
 
-    def early_places(value, cross):
+    def early_place(value, cross):
         return [(value, steps, cross, LATE, EARLY, steps * EARLY) for steps in range(4)]
 
-    update = place(
-        None,
-        shape,
-        [late_place(late_pieces, 0, 0), late_place(late_across, 0, 1)] + early_places(early, 0),
-    )
-    update = place(
-        update,
-        shape,
-        [late_place(late_pieces, steps, 0) for steps in (1, 2, 3)] + early_places(early_across, 1),
-    )
+    late_across = {steps: shift(piece, 0, 1) for steps, piece in late_pieces.items()}
+    update = place(None, shape, [late_place(late_pieces, 0, 0), late_place(late_across, 0, 1)])
+    update = place(update, shape, [late_place(late_pieces, steps, 0) for steps in (1, 2, 3)])
     update = place(update, shape, [late_place(late_across, steps, 1) for steps in (1, 2, 3)])
+    early, update = lax.optimization_barrier((early, update))
+    update = place(update, shape, early_place(early, 0))
+    update = place(update, shape, early_place(shift(early, 0, 1), 1))
     return (update.reshape(experts, pairs, row_count, 8 * WIDTH), new_momentum)
 
 

time: 119 us -> 111 us (0.933)
  blocking collectives: 36 us -> 21.9 us
  Pallas kernels: 12.4 us -> 20.2 us
  waiting for transfers between devices: 29.1 us -> 25 us
  other arithmetic: 3.16 us -> 4.75 us
  local copies, waits for them, and re-layouts: 0 us -> 1.41 us
    all_to_all x1 -> x0, blocking collectives: 14.1 us -> none  [back(): lax.all_to_all(value, 'tensor', split_axis=0, concat_axis=0, tiled=True)]
    all_to_all x1 -> x2, waiting for transfers between devices: 10.3 us -> 0.01 us  [back(): lax.all_to_all(value, 'tensor', split_axis=0, concat_axis=0, tiled=True)]
    pallas_call x0 -> x1, Pallas kernels: none -> 7.57 us  [early_products(): pl.pallas_call(early_kernel, out_shape=jax.ShapeDtypeStruct((FF, 4 * EARL...]
    ppermute x22, waiting for transfers between devices: 18.7 us -> 25 us  [shift(): return lax.ppermute(value, 'replica', pairs)]
    ppermute x22, starting transfers between devices: 33.1 us -> 29.1 us  [shift(): return lax.ppermute(value, 'replica', pairs)]
    all_to_all x1 -> x2, starting transfers between devices: 3.61 us -> 7.45 us  [back(): lax.all_to_all(value, 'tensor', split_axis=0, concat_axis=0, tiled=True)]
    add x0 -> x1, other arithmetic: none -> 2.78 us  [stepped(): return momentum_decay * momentum + gradient.astype(F32)]
    unnamed x0 -> x6, local copies, waits for them, and re-layouts: none -> 1.41 us
  transfers between devices with their start and end apart: 23 -> 24, of which waited for: 10 -> 8; matrix products, arithmetic and copies ran while one was open for 0% -> 3% of each run, Pallas kernels for 2% -> 17%
where the time goes in v3:
time: 111 us
  starting transfers between devices  36.5 us (33%)
  waiting for transfers between devices  25 us (23%)
  blocking collectives  21.9 us (20%)
  Pallas kernels  20.2 us (18%)
  other arithmetic  4.75 us (4%)
  local copies, waits for them, and re-layouts  1.41 us (1%)
    ppermute x22, starting transfers between devices, shift(): return lax.ppermute(value, 'replica', pairs)  29.1 us
    ppermute x22, waiting for transfers between devices, shift(): return lax.ppermute(value, 'replica', pairs)  25 us
    all_to_all x1, blocking collectives, local(): lax.all_to_all(flat_rows, 'tensor', split_axis=0, concat_axis=0, tiled=True)  21.9 us
    pallas_call x1, Pallas kernels, early_products(): pl.pallas_call(early_kernel, out_shape=jax.ShapeDtypeStruct((FF, 4 * EARL...  7.57 us
    all_to_all x2, starting transfers between devices, back(): lax.all_to_all(value, 'tensor', split_axis=0, concat_axis=0, tiled=True)  7.45 us
    pallas_call x1, Pallas kernels, chain(): pl.pallas_call(chain_kernel, out_shape=(jax.ShapeDtypeStruct((FF, LATE),...  6.58 us
    pallas_call x5, Pallas kernels, place(): pl.pallas_call(functools.partial(place_kernel, where, int(aliased)), out_...  5.34 us
    add x1, other arithmetic, stepped(): return momentum_decay * momentum + gradient.astype(F32)  2.78 us
  transfers between devices with their start and end apart: 24, of which 8 were waited for; matrix products, arithmetic and copies ran while one was open for 3% of the time, Pallas kernels for 17%

profile of v3, /device:TPU:1, one launch (start us, length us, event | category | flops | bytes accessed | tf_op | source)
XLA Modules:
  0.0 110.8 jit_solution(7595003847968036722)
XLA Ops:
  0.6 2.0 %fusion.1 = bf16[8,2,48,512]{3,2,1,0:T(8,128)(2,1)S(1)} fusion(bf16[8,2,48,512]{3,2,1,0:T(8,128)(2,1)} %param.2, f32[8,2,48,512]{3,2,1,0:T(8,128)} %param.3), kind=kLoop, calls=%fused_computation.3 | loop fusion | flops 2359296 | bytes 3145728 | tf_op jit(solution)/shard_map/convert_element_type | solution.py:275
  2.6 21.9 %all_to_all.15 = bf16[16,48,512]{2,1,0:T(8,128)(2,1)S(1)} all-to-all(bf16[16,48,512]{2,1,0:T(8,128)(2,1)S(1)} %bitcast.8), channel_id=1, replica_groups=mesh['replica'=8,'tensor'=16] {'tensor'}, dimensions={0} | all-to-all | bytes 1572864 | tf_op jit(solution)/shard_map/all_to_all | solution.py:276
  24.5 0.6 shard_map.41
  25.1 1.9 %collective-permute-start = (bf16[768,256]{1,0:T(8,128)(2,1)S(1)}, bf16[768,256]{1,0:T(8,128)(2,1)S(1)}, u32[]{:S(2)}, u32[]{:S(2)}) collective-permute-start(bf16[768,256]{1,0:T(8,128)(2,1)S(1)} %get-tuple-element.22), channel_id=1, source_target_pairs={{0,16},{16,0},{32,48},{48,32},{64,80},{80,64},{96,112},{112,96},{1... | collective-permute-start | bytes 1179656 | tf_op jit(solution)/shard_map/ppermute | solution.py:44
  27.0 1.3 %collective-permute-done.got_ref = bf16[768,256]{1,0:T(8,128)(2,1)S(1)} collective-permute-done((bf16[768,256]{1,0:T(8,128)(2,1)S(1)}, bf16[768,256]{1,0:T(8,128)(2,1)S(1)}, u32[]{:S(2)}, u32[]{:S(2)}) %collective-permute-start) | collective-permute-done | bytes 393248 | tf_op jit(solution)/shard_map/ppermute | solution.py:44
  28.4 0.1 shard_map.42
  28.4 0.0 copy-start.2
  28.4 1.3 %collective-permute-start.1 = (bf16[192,256]{1,0:T(8,128)(2,1)S(1)}, bf16[192,256]{1,0:T(8,128)(2,1)S(1)}, u32[]{:S(2)}, u32[]{:S(2)}) collective-permute-start(bf16[192,256]{1,0:T(8,128)(2,1)S(1)} %get-tuple-element.24), channel_id=1, source_target_pairs={{0,32},{16,48},{32,64},{48,80},{64,96},{80,112},{96,0},{112,16},{1... | collective-permute-start | bytes 294920 | tf_op jit(solution)/shard_map/ppermute | solution.py:44
  29.7 1.5 %collective-permute-start.2 = (bf16[192,256]{1,0:T(8,128)(2,1)S(1)}, bf16[192,256]{1,0:T(8,128)(2,1)S(1)}, u32[]{:S(2)}, u32[]{:S(2)}) collective-permute-start(bf16[192,256]{1,0:T(8,128)(2,1)S(1)} %get-tuple-element.25), channel_id=1, source_target_pairs={{0,96},{16,112},{32,0},{48,16},{64,32},{80,48},{96,64},{112,80},{1... | collective-permute-start | bytes 294920 | tf_op jit(solution)/shard_map/ppermute | solution.py:44
  31.2 1.5 %collective-permute-start.3 = (bf16[192,256]{1,0:T(8,128)(2,1)S(1)}, bf16[192,256]{1,0:T(8,128)(2,1)S(1)}, u32[]{:S(2)}, u32[]{:S(2)}) collective-permute-start(bf16[192,256]{1,0:T(8,128)(2,1)S(1)} %get-tuple-element.26), channel_id=1, source_target_pairs={{0,64},{16,80},{32,96},{48,112},{64,0},{80,16},{96,32},{112,48},{1... | collective-permute-start | bytes 294920 | tf_op jit(solution)/shard_map/ppermute | solution.py:44
  32.7 1.0 collective-permute-done.1.a_ref
  33.7 2.6 %collective-permute-done.3.c_ref = bf16[192,256]{1,0:T(8,128)(2,1)S(1)} collective-permute-done((bf16[192,256]{1,0:T(8,128)(2,1)S(1)}, bf16[192,256]{1,0:T(8,128)(2,1)S(1)}, u32[]{:S(2)}, u32[]{:S(2)}) %collective-permute-start.3) | collective-permute-done | bytes 98336 | tf_op jit(solution)/shard_map/ppermute | solution.py:44
  36.3 1.5 %collective-permute-start.5 = (bf16[192,256]{1,0:T(8,128)(2,1)S(1)}, bf16[192,256]{1,0:T(8,128)(2,1)S(1)}, u32[]{:S(2)}, u32[]{:S(2)}) collective-permute-start(bf16[192,256]{1,0:T(8,128)(2,1)S(1)} %shard_map.43.refs_0_), channel_id=1, source_target_pairs={{0,64},{16,80},{32,96},{48,112},{64,0},{80,16},{96,32},{112,48},{1... | collective-permute-start | bytes 294920 | tf_op jit(solution)/shard_map/ppermute | solution.py:44
  37.8 0.7 collective-permute-start.6
  38.5 2.0 %collective-permute-start.4 = (bf16[192,256]{1,0:T(8,128)(2,1)S(1)}, bf16[192,256]{1,0:T(8,128)(2,1)S(1)}, u32[]{:S(2)}, u32[]{:S(2)}) collective-permute-start(bf16[192,256]{1,0:T(8,128)(2,1)S(1)} %shard_map.43.refs_0_), channel_id=1, source_target_pairs={{0,96},{16,112},{32,0},{48,16},{64,32},{80,48},{96,64},{112,80},{1... | collective-permute-start | bytes 294920 | tf_op jit(solution)/shard_map/ppermute | solution.py:44
  40.5 2.9 %collective-permute-start.7 = (bf16[192,256]{1,0:T(8,128)(2,1)S(1)}, bf16[192,256]{1,0:T(8,128)(2,1)S(1)}, u32[]{:S(2)}, u32[]{:S(2)}) collective-permute-start(bf16[192,256]{1,0:T(8,128)(2,1)S(1)} %shard_map.43.refs_0_), channel_id=1, source_target_pairs={{0,16},{16,0},{32,48},{48,32},{64,80},{80,64},{96,112},{112,96},{1... | collective-permute-start | bytes 294920 | tf_op jit(solution)/shard_map/ppermute | solution.py:44
  43.4 0.0 collective-permute-done.5.refs_2_
  43.4 1.2 %collective-permute-start.9 = (bf16[192,256]{1,0:T(8,128)(2,1)S(1)}, bf16[192,256]{1,0:T(8,128)(2,1)S(1)}, u32[]{:S(2)}, u32[]{:S(2)}) collective-permute-start(bf16[192,256]{1,0:T(8,128)(2,1)S(1)} %collective-permute-done.5.refs_2_), channel_id=1, source_target_pairs={{0,16},{16,0},{32,48},{48,32},{64,80},{80,64},{96,112},{112,96},{1... | collective-permute-start | bytes 294920 | tf_op jit(solution)/shard_map/ppermute | solution.py:44
  44.7 1.3 %collective-permute-start.10 = (bf16[192,256]{1,0:T(8,128)(2,1)S(1)}, bf16[192,256]{1,0:T(8,128)(2,1)S(1)}, u32[]{:S(2)}, u32[]{:S(2)}) collective-permute-start(bf16[192,256]{1,0:T(8,128)(2,1)S(1)} %collective-permute-done.6.refs_3_), channel_id=1, source_target_pairs={{0,16},{16,0},{32,48},{48,32},{64,80},{80,64},{96,112},{112,96},{1... | collective-permute-start | bytes 294920 | tf_op jit(solution)/shard_map/ppermute | solution.py:44
  46.0 0.0 collective-permute-start.8
  46.0 2.9 %collective-permute-start.11 = (bf16[768,256]{1,0:T(8,128)(2,1)S(1)}, bf16[768,256]{1,0:T(8,128)(2,1)S(1)}, u32[]{:S(2)}, u32[]{:S(2)}) collective-permute-start(bf16[768,256]{1,0:T(8,128)(2,1)S(1)} %get-tuple-element.32.refs_0_), channel_id=1, source_target_pairs={{0,96},{16,112},{32,0},{48,16},{64,32},{80,48},{96,64},{112,80},{1... | collective-permute-start | bytes 1179656 | tf_op jit(solution)/shard_map/ppermute | solution.py:44
  49.0 0.6 collective-permute-start.13
  49.6 6.6 %shard_map.44 = (bf16[768,256]{1,0:T(8,128)(2,1)}, bf16[2,768,768]{2,1,0:T(8,128)(2,1)S(1)}, f32[8,128]{1,0:T(8,128)S(1)}) custom-call(bf16[192,256]{1,0:T(8,128)(2,1)S(1)} %shard_map.43.refs_0_, bf16[192,256]{1,0:T(8,128)(2,1)S(1)} %collective-permute-done.4.refs_1_, bf16[192,256]{1,0:T(8,128)(2,1)S(1)} %collective-permute-done.5.refs_2_, ...), custom_call_target="tpu_custom_call" | custom-call | tf_op jit(solution)/shard_map/pallas_call | solution.py:179
  56.2 0.0 copy-start
  56.2 1.4 %copy-done = bf16[2,768,768]{2,1,0:T(8,128)(2,1)} copy-done((bf16[2,768,768]{2,1,0:T(8,128)(2,1)}, bf16[2,768,768]{2,1,0:T(8,128)(2,1)S(1)}, u32[]{:S(2)}) %copy-start) | copy-done | bytes 2359320
  57.6 3.7 %all-to-all-start.1 = ((bf16[16,48,256]{2,1,0:T(8,128)(2,1)}), bf16[16,48,256]{2,1,0:T(8,128)(2,1)S(1)}, u32[]{:S(2)}, u32[]{:S(2)}) async-start(bf16[16,48,256]{2,1,0:T(8,128)(2,1)} %bitcast.2), calls=%async_computation.1 | async-start | bytes 786432 | tf_op jit(solution)/shard_map/all_to_all | solution.py:288
  61.3 0.0 copy-start.1
  61.3 2.8 %convert_add_fusion.2 = f32[8,2,48,512]{3,2,1,0:T(8,128)} fusion(bf16[8,2,48,512]{3,2,1,0:T(8,128)(2,1)} %param.2, f32[8,2,48,512]{3,2,1,0:T(8,128)S(1)} %copy-done.2), kind=kLoop, calls=%fused_computation.4 | loop fusion | flops 1179648 | bytes 3932160 | tf_op jit(solution)/shard_map/add | solution.py:271
  64.1 1.7 %collective-permute-done.11.refs_1_ = bf16[768,256]{1,0:T(8,128)(2,1)S(1)} collective-permute-done((bf16[768,256]{1,0:T(8,128)(2,1)S(1)}, bf16[768,256]{1,0:T(8,128)(2,1)S(1)}, u32[]{:S(2)}, u32[]{:S(2)}) %collective-permute-start.11) | collective-permute-done | bytes 393248 | tf_op jit(solution)/shard_map/ppermute | solution.py:44
  65.8 3.7 %collective-permute-done.13.refs_3_ = bf16[768,256]{1,0:T(8,128)(2,1)S(1)} collective-permute-done((bf16[768,256]{1,0:T(8,128)(2,1)S(1)}, bf16[768,256]{1,0:T(8,128)(2,1)S(1)}, u32[]{:S(2)}, u32[]{:S(2)}) %collective-permute-start.13) | collective-permute-done | bytes 393248 | tf_op jit(solution)/shard_map/ppermute | solution.py:44
  69.5 7.6 %shard_map.45 = bf16[768,1024]{1,0:T(8,128)(2,1)} custom-call(bf16[2,768,768]{2,1,0:T(8,128)(2,1)S(1)} %copy-done.1, f32[8,128]{1,0:T(8,128)S(1)} %get-tuple-element.30.scale_ref, bf16[768,256]{1,0:T(8,128)(2,1)S(1)} %get-tuple-element.32.refs_0_, bf16[768,256]{1,0:T(8,128)(2,1)S(1)} %collective-permute-done.11.refs_1_, ...), custom_call_target="tpu_custom_call" | custom-call | flops 2415919104 | tf_op jit(solution)/shard_map/pallas_call | solution.py:215
  77.1 3.7 %all-to-all-start.2 = ((bf16[16,48,1024]{2,1,0:T(8,128)(2,1)}), bf16[16,48,1024]{2,1,0:T(8,128)(2,1)S(1)}, u32[]{:S(2)}, u32[]{:S(2)}) async-start(bf16[16,48,1024]{2,1,0:T(8,128)(2,1)} %bitcast.3), calls=%async_computation.2 | async-start | bytes 3145728 | tf_op jit(solution)/shard_map/all_to_all | solution.py:288
  80.8 0.2 collective-permute-start.14
  81.0 1.0 collective-permute-start.16
  82.1 0.3 collective-permute-start.18
  82.4 1.7 %collective-permute-start.20 = (bf16[16,48,256]{2,1,0:T(8,128)(2,1)S(1)}, bf16[16,48,256]{2,1,0:T(8,128)(2,1)S(1)}, u32[]{:S(2)}, u32[]{:S(2)}) collective-permute-start(bf16[16,48,256]{2,1,0:T(8,128)(2,1)S(1)} %all-to-all-done.1.refs_0_), channel_id=1, source_target_pairs={{0,16},{16,0},{32,48},{48,32},{64,80},{80,64},{96,112},{112,96},{1... | collective-permute-start | bytes 1179656 | tf_op jit(solution)/shard_map/ppermute | solution.py:44
  84.0 6.8 %collective-permute-done.14.refs_0_ = bf16[16,48,256]{2,1,0:T(8,128)(2,1)S(1)} collective-permute-done((bf16[16,48,256]{2,1,0:T(8,128)(2,1)S(1)}, bf16[16,48,256]{2,1,0:T(8,128)(2,1)S(1)}, u32[]{:S(2)}, u32[]{:S(2)}) %collective-permute-start.14) | collective-permute-done | bytes 393248 | tf_op jit(solution)/shard_map/ppermute | solution.py:44
  90.8 2.8 %collective-permute-start.15 = (bf16[16,48,256]{2,1,0:T(8,128)(2,1)S(1)}, bf16[16,48,256]{2,1,0:T(8,128)(2,1)S(1)}, u32[]{:S(2)}, u32[]{:S(2)}) collective-permute-start(bf16[16,48,256]{2,1,0:T(8,128)(2,1)S(1)} %collective-permute-done.14.refs_0_), channel_id=1, source_target_pairs={{0,16},{16,0},{32,48},{48,32},{64,80},{80,64},{96,112},{112,96},{1... | collective-permute-start | bytes 1179656 | tf_op jit(solution)/shard_map/ppermute | solution.py:44
  93.6 2.4 %collective-permute-start.17 = (bf16[16,48,256]{2,1,0:T(8,128)(2,1)S(1)}, bf16[16,48,256]{2,1,0:T(8,128)(2,1)S(1)}, u32[]{:S(2)}, u32[]{:S(2)}) collective-permute-start(bf16[16,48,256]{2,1,0:T(8,128)(2,1)S(1)} %collective-permute-done.16.refs_1_), channel_id=1, source_target_pairs={{0,16},{16,0},{32,48},{48,32},{64,80},{80,64},{96,112},{112,96},{1... | collective-permute-start | bytes 1179656 | tf_op jit(solution)/shard_map/ppermute | solution.py:44
  96.0 6.0 %collective-permute-done.18.refs_2_ = bf16[16,48,256]{2,1,0:T(8,128)(2,1)S(1)} collective-permute-done((bf16[16,48,256]{2,1,0:T(8,128)(2,1)S(1)}, bf16[16,48,256]{2,1,0:T(8,128)(2,1)S(1)}, u32[]{:S(2)}, u32[]{:S(2)}) %collective-permute-start.18) | collective-permute-done | bytes 393248 | tf_op jit(solution)/shard_map/ppermute | solution.py:44
  102.0 0.5 collective-permute-start.19
  102.5 0.9 shard_map.46.refs_3_
  103.4 1.1 shard_map.47.refs_3_
  104.5 1.1 shard_map.48.refs_4_
  105.6 0.8 collective-permute-start.21
  106.4 1.2 %shard_map.49.refs_4_ = bf16[16,48,4096]{2,1,0:T(8,128)(2,1)} custom-call(bf16[16,48,1024]{2,1,0:T(8,128)(2,1)S(1)} %all-to-all-done.2.refs_0_.refs_1_.refs_2_.refs_3_, bf16[16,48,1024]{2,1,0:T(8,128)(2,1)S(1)} %all-to-all-done.2.refs_0_.refs_1_.refs_2_.refs_3_, ...), custom_call_target="tpu_custom_call", output_to_operand_aliasing={{}: (4, {})} | custom-call | tf_op jit(solution)/shard_map/pallas_call | solution.py:257
  107.6 1.9 %collective-permute-done.21.refs_0_.refs_1_.refs_2_.refs_3_ = bf16[16,48,1024]{2,1,0:T(8,128)(2,1)S(1)} collective-permute-done((bf16[16,48,1024]{2,1,0:T(8,128)(2,1)S(1)}, bf16[16,48,1024]{2,1,0:T(8,128)(2,1)S(1)}, u32[]{:S(2)}, u32[]{:S(2)}) %collective-permute-start.21) | collective-permute-done | bytes 1572896 | tf_op jit(solution)/shard_map/ppermute | solution.py:44
  109.4 1.2 %shard_map.50 = bf16[16,48,4096]{2,1,0:T(8,128)(2,1)} custom-call(bf16[16,48,1024]{2,1,0:T(8,128)(2,1)S(1)} %collective-permute-done.21.refs_0_.refs_1_.refs_2_.refs_3_, bf16[16,48,1024]{2,1,0:T(8,128)(2,1)S(1)} %collective-permute-done.21.refs_0_.refs_1_.refs_2_.refs_3_, ...), custom_call_target="tpu_custom_call", output_to_operand_aliasing={{}: (4, {})} | custom-call | tf_op jit(solution)/shard_map/pallas_call | solution.py:257
  (19 shorter events, 0.1 us)
Async XLA Ops:
  25.1 3.2 %collective-permute-start = (bf16[768,256]{1,0:T(8,128)(2,1)S(1)}, bf16[768,256]{1,0:T(8,128)(2,1)S(1)}, u32[]{:S(2)}, u32[]{:S(2)}) collective-permute-start(bf16[768,256]{1,0:T(8,128)(2,1)S(1)} %get-tuple-element.22), channel_id=1, source_target_pairs={{0,16},{16,0},{32,48},{48,32},{64,80},{80,64},{96,112},{112,96},{1... | collective-permute-start | bytes 1179656 | tf_op jit(solution)/shard_map/ppermute | solution.py:44
  28.4 32.9 %copy-start.2 = (f32[8,2,48,512]{3,2,1,0:T(8,128)S(1)}, f32[8,2,48,512]{3,2,1,0:T(8,128)}, u32[]{:S(2)}) copy-start(f32[8,2,48,512]{3,2,1,0:T(8,128)} %param.3) | copy-start | bytes 4718596
  28.4 5.3 %collective-permute-start.1 = (bf16[192,256]{1,0:T(8,128)(2,1)S(1)}, bf16[192,256]{1,0:T(8,128)(2,1)S(1)}, u32[]{:S(2)}, u32[]{:S(2)}) collective-permute-start(bf16[192,256]{1,0:T(8,128)(2,1)S(1)} %get-tuple-element.24), channel_id=1, source_target_pairs={{0,32},{16,48},{32,64},{48,80},{64,96},{80,112},{96,0},{112,16},{1... | collective-permute-start | bytes 294920 | tf_op jit(solution)/shard_map/ppermute | solution.py:44
  29.7 4.0 %collective-permute-start.2 = (bf16[192,256]{1,0:T(8,128)(2,1)S(1)}, bf16[192,256]{1,0:T(8,128)(2,1)S(1)}, u32[]{:S(2)}, u32[]{:S(2)}) collective-permute-start(bf16[192,256]{1,0:T(8,128)(2,1)S(1)} %get-tuple-element.25), channel_id=1, source_target_pairs={{0,96},{16,112},{32,0},{48,16},{64,32},{80,48},{96,64},{112,80},{1... | collective-permute-start | bytes 294920 | tf_op jit(solution)/shard_map/ppermute | solution.py:44
  31.2 5.1 %collective-permute-start.3 = (bf16[192,256]{1,0:T(8,128)(2,1)S(1)}, bf16[192,256]{1,0:T(8,128)(2,1)S(1)}, u32[]{:S(2)}, u32[]{:S(2)}) collective-permute-start(bf16[192,256]{1,0:T(8,128)(2,1)S(1)} %get-tuple-element.26), channel_id=1, source_target_pairs={{0,64},{16,80},{32,96},{48,112},{64,0},{80,16},{96,32},{112,48},{1... | collective-permute-start | bytes 294920 | tf_op jit(solution)/shard_map/ppermute | solution.py:44
  36.3 7.1 %collective-permute-start.5 = (bf16[192,256]{1,0:T(8,128)(2,1)S(1)}, bf16[192,256]{1,0:T(8,128)(2,1)S(1)}, u32[]{:S(2)}, u32[]{:S(2)}) collective-permute-start(bf16[192,256]{1,0:T(8,128)(2,1)S(1)} %shard_map.43.refs_0_), channel_id=1, source_target_pairs={{0,64},{16,80},{32,96},{48,112},{64,0},{80,16},{96,32},{112,48},{1... | collective-permute-start | bytes 294920 | tf_op jit(solution)/shard_map/ppermute | solution.py:44
  37.8 6.8 %collective-permute-start.6 = (bf16[192,256]{1,0:T(8,128)(2,1)S(1)}, bf16[192,256]{1,0:T(8,128)(2,1)S(1)}, u32[]{:S(2)}, u32[]{:S(2)}) collective-permute-start(bf16[192,256]{1,0:T(8,128)(2,1)S(1)} %shard_map.43.refs_0_), channel_id=1, source_target_pairs={{0,32},{16,48},{32,64},{48,80},{64,96},{80,112},{96,0},{112,16},{1... | collective-permute-start | bytes 294920 | tf_op jit(solution)/shard_map/ppermute | solution.py:44
  38.5 7.5 %collective-permute-start.4 = (bf16[192,256]{1,0:T(8,128)(2,1)S(1)}, bf16[192,256]{1,0:T(8,128)(2,1)S(1)}, u32[]{:S(2)}, u32[]{:S(2)}) collective-permute-start(bf16[192,256]{1,0:T(8,128)(2,1)S(1)} %shard_map.43.refs_0_), channel_id=1, source_target_pairs={{0,96},{16,112},{32,0},{48,16},{64,32},{80,48},{96,64},{112,80},{1... | collective-permute-start | bytes 294920 | tf_op jit(solution)/shard_map/ppermute | solution.py:44
  40.5 8.5 %collective-permute-start.7 = (bf16[192,256]{1,0:T(8,128)(2,1)S(1)}, bf16[192,256]{1,0:T(8,128)(2,1)S(1)}, u32[]{:S(2)}, u32[]{:S(2)}) collective-permute-start(bf16[192,256]{1,0:T(8,128)(2,1)S(1)} %shard_map.43.refs_0_), channel_id=1, source_target_pairs={{0,16},{16,0},{32,48},{48,32},{64,80},{80,64},{96,112},{112,96},{1... | collective-permute-start | bytes 294920 | tf_op jit(solution)/shard_map/ppermute | solution.py:44
  43.4 5.6 %collective-permute-start.9 = (bf16[192,256]{1,0:T(8,128)(2,1)S(1)}, bf16[192,256]{1,0:T(8,128)(2,1)S(1)}, u32[]{:S(2)}, u32[]{:S(2)}) collective-permute-start(bf16[192,256]{1,0:T(8,128)(2,1)S(1)} %collective-permute-done.5.refs_2_), channel_id=1, source_target_pairs={{0,16},{16,0},{32,48},{48,32},{64,80},{80,64},{96,112},{112,96},{1... | collective-permute-start | bytes 294920 | tf_op jit(solution)/shard_map/ppermute | solution.py:44
  44.7 4.9 %collective-permute-start.10 = (bf16[192,256]{1,0:T(8,128)(2,1)S(1)}, bf16[192,256]{1,0:T(8,128)(2,1)S(1)}, u32[]{:S(2)}, u32[]{:S(2)}) collective-permute-start(bf16[192,256]{1,0:T(8,128)(2,1)S(1)} %collective-permute-done.6.refs_3_), channel_id=1, source_target_pairs={{0,16},{16,0},{32,48},{48,32},{64,80},{80,64},{96,112},{112,96},{1... | collective-permute-start | bytes 294920 | tf_op jit(solution)/shard_map/ppermute | solution.py:44
  46.0 3.6 %collective-permute-start.8 = (bf16[192,256]{1,0:T(8,128)(2,1)S(1)}, bf16[192,256]{1,0:T(8,128)(2,1)S(1)}, u32[]{:S(2)}, u32[]{:S(2)}) collective-permute-start(bf16[192,256]{1,0:T(8,128)(2,1)S(1)} %collective-permute-done.4.refs_1_), channel_id=1, source_target_pairs={{0,16},{16,0},{32,48},{48,32},{64,80},{80,64},{96,112},{112,96},{1... | collective-permute-start | bytes 294920 | tf_op jit(solution)/shard_map/ppermute | solution.py:44
  46.0 19.8 %collective-permute-start.11 = (bf16[768,256]{1,0:T(8,128)(2,1)S(1)}, bf16[768,256]{1,0:T(8,128)(2,1)S(1)}, u32[]{:S(2)}, u32[]{:S(2)}) collective-permute-start(bf16[768,256]{1,0:T(8,128)(2,1)S(1)} %get-tuple-element.32.refs_0_), channel_id=1, source_target_pairs={{0,96},{16,112},{32,0},{48,16},{64,32},{80,48},{96,64},{112,80},{1... | collective-permute-start | bytes 1179656 | tf_op jit(solution)/shard_map/ppermute | solution.py:44
  49.0 16.8 %collective-permute-start.12 = (bf16[768,256]{1,0:T(8,128)(2,1)S(1)}, bf16[768,256]{1,0:T(8,128)(2,1)S(1)}, u32[]{:S(2)}, u32[]{:S(2)}) collective-permute-start(bf16[768,256]{1,0:T(8,128)(2,1)S(1)} %get-tuple-element.32.refs_0_), channel_id=1, source_target_pairs={{0,64},{16,80},{32,96},{48,112},{64,0},{80,16},{96,32},{112,48},{1... | collective-permute-start | bytes 1179656 | tf_op jit(solution)/shard_map/ppermute | solution.py:44
  49.0 20.5 %collective-permute-start.13 = (bf16[768,256]{1,0:T(8,128)(2,1)S(1)}, bf16[768,256]{1,0:T(8,128)(2,1)S(1)}, u32[]{:S(2)}, u32[]{:S(2)}) collective-permute-start(bf16[768,256]{1,0:T(8,128)(2,1)S(1)} %get-tuple-element.32.refs_0_), channel_id=1, source_target_pairs={{0,32},{16,48},{32,64},{48,80},{64,96},{80,112},{96,0},{112,16},{1... | collective-permute-start | bytes 1179656 | tf_op jit(solution)/shard_map/ppermute | solution.py:44
  56.2 1.4 %copy-start = (bf16[2,768,768]{2,1,0:T(8,128)(2,1)}, bf16[2,768,768]{2,1,0:T(8,128)(2,1)S(1)}, u32[]{:S(2)}) copy-start(bf16[2,768,768]{2,1,0:T(8,128)(2,1)S(1)} %get-tuple-element.29.polys_in) | copy-start | bytes 7077892
  57.6 19.5 %all-to-all-start.1 = ((bf16[16,48,256]{2,1,0:T(8,128)(2,1)}), bf16[16,48,256]{2,1,0:T(8,128)(2,1)S(1)}, u32[]{:S(2)}, u32[]{:S(2)}) async-start(bf16[16,48,256]{2,1,0:T(8,128)(2,1)} %bitcast.2), calls=%async_computation.1 | async-start | bytes 786432 | tf_op jit(solution)/shard_map/all_to_all | solution.py:288
  61.3 8.2 %copy-start.1 = (bf16[2,768,768]{2,1,0:T(8,128)(2,1)S(1)}, bf16[2,768,768]{2,1,0:T(8,128)(2,1)}, u32[]{:S(2)}) copy-start(bf16[2,768,768]{2,1,0:T(8,128)(2,1)} %copy-done) | copy-start | bytes 7077892
  77.1 28.5 %all-to-all-start.2 = ((bf16[16,48,1024]{2,1,0:T(8,128)(2,1)}), bf16[16,48,1024]{2,1,0:T(8,128)(2,1)S(1)}, u32[]{:S(2)}, u32[]{:S(2)}) async-start(bf16[16,48,1024]{2,1,0:T(8,128)(2,1)} %bitcast.3), calls=%async_computation.2 | async-start | bytes 3145728 | tf_op jit(solution)/shard_map/all_to_all | solution.py:288
  80.8 10.0 %collective-permute-start.14 = (bf16[16,48,256]{2,1,0:T(8,128)(2,1)S(1)}, bf16[16,48,256]{2,1,0:T(8,128)(2,1)S(1)}, u32[]{:S(2)}, u32[]{:S(2)}) collective-permute-start(bf16[16,48,256]{2,1,0:T(8,128)(2,1)S(1)} %all-to-all-done.1.refs_0_), channel_id=1, source_target_pairs={{0,96},{16,112},{32,0},{48,16},{64,32},{80,48},{96,64},{112,80},{1... | collective-permute-start | bytes 1179656 | tf_op jit(solution)/shard_map/ppermute | solution.py:44
  81.0 12.6 %collective-permute-start.16 = (bf16[16,48,256]{2,1,0:T(8,128)(2,1)S(1)}, bf16[16,48,256]{2,1,0:T(8,128)(2,1)S(1)}, u32[]{:S(2)}, u32[]{:S(2)}) collective-permute-start(bf16[16,48,256]{2,1,0:T(8,128)(2,1)S(1)} %all-to-all-done.1.refs_0_), channel_id=1, source_target_pairs={{0,64},{16,80},{32,96},{48,112},{64,0},{80,16},{96,32},{112,48},{1... | collective-permute-start | bytes 1179656 | tf_op jit(solution)/shard_map/ppermute | solution.py:44
  82.1 19.9 %collective-permute-start.18 = (bf16[16,48,256]{2,1,0:T(8,128)(2,1)S(1)}, bf16[16,48,256]{2,1,0:T(8,128)(2,1)S(1)}, u32[]{:S(2)}, u32[]{:S(2)}) collective-permute-start(bf16[16,48,256]{2,1,0:T(8,128)(2,1)S(1)} %all-to-all-done.1.refs_0_), channel_id=1, source_target_pairs={{0,32},{16,48},{32,64},{48,80},{64,96},{80,112},{96,0},{112,16},{1... | collective-permute-start | bytes 1179656 | tf_op jit(solution)/shard_map/ppermute | solution.py:44
  82.4 20.2 %collective-permute-start.20 = (bf16[16,48,256]{2,1,0:T(8,128)(2,1)S(1)}, bf16[16,48,256]{2,1,0:T(8,128)(2,1)S(1)}, u32[]{:S(2)}, u32[]{:S(2)}) collective-permute-start(bf16[16,48,256]{2,1,0:T(8,128)(2,1)S(1)} %all-to-all-done.1.refs_0_), channel_id=1, source_target_pairs={{0,16},{16,0},{32,48},{48,32},{64,80},{80,64},{96,112},{112,96},{1... | collective-permute-start | bytes 1179656 | tf_op jit(solution)/shard_map/ppermute | solution.py:44
  90.8 13.7 %collective-permute-start.15 = (bf16[16,48,256]{2,1,0:T(8,128)(2,1)S(1)}, bf16[16,48,256]{2,1,0:T(8,128)(2,1)S(1)}, u32[]{:S(2)}, u32[]{:S(2)}) collective-permute-start(bf16[16,48,256]{2,1,0:T(8,128)(2,1)S(1)} %collective-permute-done.14.refs_0_), channel_id=1, source_target_pairs={{0,16},{16,0},{32,48},{48,32},{64,80},{80,64},{96,112},{112,96},{1... | collective-permute-start | bytes 1179656 | tf_op jit(solution)/shard_map/ppermute | solution.py:44
  93.6 10.9 %collective-permute-start.17 = (bf16[16,48,256]{2,1,0:T(8,128)(2,1)S(1)}, bf16[16,48,256]{2,1,0:T(8,128)(2,1)S(1)}, u32[]{:S(2)}, u32[]{:S(2)}) collective-permute-start(bf16[16,48,256]{2,1,0:T(8,128)(2,1)S(1)} %collective-permute-done.16.refs_1_), channel_id=1, source_target_pairs={{0,16},{16,0},{32,48},{48,32},{64,80},{80,64},{96,112},{112,96},{1... | collective-permute-start | bytes 1179656 | tf_op jit(solution)/shard_map/ppermute | solution.py:44
  102.0 2.5 %collective-permute-start.19 = (bf16[16,48,256]{2,1,0:T(8,128)(2,1)S(1)}, bf16[16,48,256]{2,1,0:T(8,128)(2,1)S(1)}, u32[]{:S(2)}, u32[]{:S(2)}) collective-permute-start(bf16[16,48,256]{2,1,0:T(8,128)(2,1)S(1)} %collective-permute-done.18.refs_2_), channel_id=1, source_target_pairs={{0,16},{16,0},{32,48},{48,32},{64,80},{80,64},{96,112},{112,96},{1... | collective-permute-start | bytes 1179656 | tf_op jit(solution)/shard_map/ppermute | solution.py:44
  105.6 3.8 %collective-permute-start.21 = (bf16[16,48,1024]{2,1,0:T(8,128)(2,1)S(1)}, bf16[16,48,1024]{2,1,0:T(8,128)(2,1)S(1)}, u32[]{:S(2)}, u32[]{:S(2)}) collective-permute-start(bf16[16,48,1024]{2,1,0:T(8,128)(2,1)S(1)} %all-to-all-done.2.refs_0_.refs_1_.refs_2_.refs_3_), channel_id=1, source_target_pairs={{0,16},{16,0},{32,48},{48,32},{64,80},{80,64},{96,112},{112,96},{1... | collective-permute-start | bytes 4718600 | tf_op jit(solution)/shard_map/ppermute | solution.py:44

commit v4 on v3

--- a/solution.py
+++ b/solution.py
@@ -130,7 +130,7 @@
 
 def chain_kernel(*refs):
     pieces, rows_ref = refs[:8], refs[8]
-    out_ref, polys_out, scale_ref, packed, gram, polys, sems = refs[9:]
+    out_ref, polys_out, scale_ref, packed, gram, polys, late, sems = refs[9:]
     index = lax.axis_index("replica")
     chip, core = index // 2, index % 2
     for steps in range(4):
@@ -155,24 +155,33 @@
         if row != col:
             gram[pl.ds(col * BLOCK, BLOCK), pl.ds(row * BLOCK, BLOCK)] = scaled.T.astype(BF16)
 
+    def keep(value, place):
+        polys[place] = value
+        copy = pltpu.make_async_copy(polys.at[place], polys_out.at[place], sems.at[place])
+        copy.start()
+        return copy
+
+    scale_ref[...] = jnp.broadcast_to(scale, scale_ref.shape)
     gram_0 = gram[...]
     poly_0 = (coef_gram * gram_0.astype(F32) + coef_square * dot(gram_0, gram_0)).astype(BF16)
+    copies = [keep(poly_0, 0)]
     half_way = (coef_linear * gram_0.astype(F32) + dot(poly_0, gram_0)).astype(BF16)
     gram_1 = (coef_linear * half_way.astype(F32) + dot(half_way, poly_0)).astype(BF16)
     poly_1 = (coef_gram * gram_1.astype(F32) + coef_square * dot(gram_1, gram_1)).astype(BF16)
-    polys[0] = poly_0
-    polys[1] = poly_1
-    scale_ref[...] = jnp.broadcast_to(scale, scale_ref.shape)
-    keep = pltpu.make_async_copy(polys, polys_out, sems.at[0])
-    keep.start()
-    out_ref[...] = both_steps(poly_0, poly_1, scale, rows_ref[:, :LATE])
-    keep.wait()
-
-
-def both_steps(poly_0, poly_1, scale, rows):
+    copies.append(keep(poly_1, 1))
+    rows = rows_ref[:, :LATE]
     first = ((coef_linear * rows.astype(F32) + dot(poly_0, rows)) * scale).astype(BF16)
-    second = coef_linear * first.astype(F32) + dot(poly_1, first)
-    return (scale_factor * second).astype(BF16)
+    for block in range(FF // BLOCK):
+        where = pl.ds(block * BLOCK, BLOCK)
+        cut = slice(block * BLOCK, (block + 1) * BLOCK)
+        second = coef_linear * first[cut].astype(F32) + dot(poly_1[cut], first)
+        late[where, :] = (scale_factor * second).astype(BF16)
+        copies.append(
+            pltpu.make_async_copy(late.at[where, :], out_ref.at[where, :], sems.at[2 + block])
+        )
+        copies[-1].start()
+    for copy in copies:
+        copy.wait()
 
 
 def chain(pieces, rows):
@@ -180,51 +189,88 @@
         chain_kernel,
         out_shape=(
             jax.ShapeDtypeStruct((FF, LATE), BF16),
-            jax.ShapeDtypeStruct((2, FF, FF), BF16),
+            pltpu.HBM((2, FF, FF), BF16),
             jax.ShapeDtypeStruct((8, 128), F32),
         ),
         in_specs=[VMEM] * 9,
-        out_specs=(VMEM, HBM, VMEM),
+        out_specs=(HBM, HBM, VMEM),
         scratch_shapes=[
             pltpu.VMEM((2, HALF, BLOCK), BF16),
             pltpu.VMEM((FF, FF), BF16),
             pltpu.VMEM((2, FF, FF), BF16),
-            pltpu.SemaphoreType.DMA((1,)),
+            pltpu.VMEM((FF, LATE), BF16),
+            pltpu.SemaphoreType.DMA((5,)),
         ],
+        cost_estimate=pl.CostEstimate(flops=0, bytes_accessed=0, transcendentals=0),
         compiler_params=LARGE,
     )(*pieces, rows)
 
 
-def early_kernel(polys_in, scale_ref, *refs):
-    early_in, out_ref, polys, early, sems = refs[:4], refs[4], refs[5], refs[6], refs[7]
-    copies = [pltpu.make_async_copy(polys_in, polys, sems.at[4])]
-    for steps in range(4):
-        copies.append(pltpu.make_async_copy(early_in[steps], early.at[steps], sems.at[steps]))
-    for copy in copies:
-        copy.start()
-    copies[0].wait()
-    for steps in range(4):
-        copies[1 + steps].wait()
-        out_ref[:, pl.ds(steps * EARLY, EARLY)] = both_steps(
-            polys[0], polys[1], scale_ref[:1, :1], early[steps]
+def both_steps_at_once(square, scale, rows):
+    total = coef_linear * coef_linear * rows.astype(F32) + dot(square, rows)
+    return ((scale_factor * scale) * total).astype(BF16)
+
+
+def own_kernel(polys_in, scale_ref, early_in, out_ref, square_out, polys, early, square, result, sems):
+    loads = [pltpu.make_async_copy(polys_in.at[i], polys.at[i], sems.at[i]) for i in range(2)]
+    loads.append(pltpu.make_async_copy(early_in, early, sems.at[2]))
+    for load in loads:
+        load.start()
+    for load in loads:
+        load.wait()
+    sums = polys[0].astype(F32) + polys[1].astype(F32)
+    square[...] = (coef_linear * sums + dot(polys[1], polys[0])).astype(BF16)
+    stores = [pltpu.make_async_copy(square, square_out, sems.at[3])]
+    stores[0].start()
+    result[...] = both_steps_at_once(square[...], scale_ref[:1, :1], early[...])
+    stores.append(pltpu.make_async_copy(result, out_ref.at[:, pl.ds(0, EARLY)], sems.at[4]))
+    stores[1].start()
+    for store in stores:
+        store.wait()
+
+
+def other_kernel(square_ref, scale_ref, *refs):
+    early_in, out_ref, result, sems = refs[:3], *refs[4:]
+    stores = []
+    for place in range(3):
+        result[place] = both_steps_at_once(
+            square_ref[...], scale_ref[:1, :1], early_in[place][...]
         )
+        where = out_ref.at[:, pl.ds((1 + place) * EARLY, EARLY)]
+        stores.append(pltpu.make_async_copy(result.at[place], where, sems.at[place]))
+        stores[-1].start()
+    for store in stores:
+        store.wait()
 
 
 def early_products(polys, scale, early):
-    flops = 2 * 2 * FF * FF * 4 * EARLY
-    return pl.pallas_call(
-        early_kernel,
-        out_shape=jax.ShapeDtypeStruct((FF, 4 * EARLY), BF16),
-        in_specs=[HBM, VMEM] + [HBM] * 4,
-        out_specs=VMEM,
+    out = jax.ShapeDtypeStruct((FF, 4 * EARLY), BF16)
+    flops = 2 * FF * FF * EARLY
+    result, square = pl.pallas_call(
+        own_kernel,
+        out_shape=(out, pltpu.HBM((FF, FF), BF16)),
+        in_specs=[HBM, VMEM, HBM],
+        out_specs=(HBM, HBM),
         scratch_shapes=[
             pltpu.VMEM((2, FF, FF), BF16),
-            pltpu.VMEM((4, FF, EARLY), BF16),
+            pltpu.VMEM((FF, EARLY), BF16),
+            pltpu.VMEM((FF, FF), BF16),
+            pltpu.VMEM((FF, EARLY), BF16),
             pltpu.SemaphoreType.DMA((5,)),
         ],
-        cost_estimate=pl.CostEstimate(flops=flops, bytes_accessed=0, transcendentals=0),
+        cost_estimate=pl.CostEstimate(flops=4 * flops, bytes_accessed=0, transcendentals=0),
         compiler_params=LARGE,
-    )(polys, scale, *early)
+    )(polys, scale, early[0])
+    return pl.pallas_call(
+        other_kernel,
+        out_shape=out,
+        in_specs=[VMEM] * 5 + [HBM],
+        out_specs=HBM,
+        scratch_shapes=[pltpu.VMEM((3, FF, EARLY), BF16), pltpu.SemaphoreType.DMA((3,))],
+        input_output_aliases={5: 0},
+        cost_estimate=pl.CostEstimate(flops=3 * flops, bytes_accessed=0, transcendentals=0),
+        compiler_params=LARGE,
+    )(square, scale, *early[1:], result)
 
 
 def place_kernel(where, aliased, *refs):
@@ -302,16 +348,22 @@
     def late_place(pieces, steps, cross):
         return (pieces[steps], steps, cross, 0, LATE, 0)
 
-    def early_place(value, cross):
-        return [(value, steps, cross, LATE, EARLY, steps * EARLY) for steps in range(4)]
-
-    late_across = {steps: shift(piece, 0, 1) for steps, piece in late_pieces.items()}
+    def early_place(value, steps, cross, source):
+        return (value, steps, cross, LATE, EARLY, source)
+
+    late_across = {0: shift(late, 0, 1)}
     update = place(None, shape, [late_place(late_pieces, 0, 0), late_place(late_across, 0, 1)])
-    update = place(update, shape, [late_place(late_pieces, steps, 0) for steps in (1, 2, 3)])
-    update = place(update, shape, [late_place(late_across, steps, 1) for steps in (1, 2, 3)])
+    for steps in (1, 3, 2):
+        late_pieces[steps], update = lax.optimization_barrier((late_pieces[steps], update))
+        late_across[steps] = shift(late_pieces[steps], 0, 1)
+    update = place(update, shape, [late_place(late_pieces, steps, 0) for steps in (1, 3, 2)])
+    update = place(update, shape, [late_place(late_across, steps, 1) for steps in (1, 3, 2)])
     early, update = lax.optimization_barrier((early, update))
-    update = place(update, shape, early_place(early, 0))
-    update = place(update, shape, early_place(shift(early, 0, 1), 1))
+    across = [shift(early[:, :, cut : cut + 2 * EARLY], 0, 1) for cut in (0, 2 * EARLY)]
+    update = place(update, shape, [early_place(early, steps, 0, steps * EARLY) for steps in range(4)])
+    for half in range(2):
+        places = [early_place(across[half], 2 * half + i, 1, i * EARLY) for i in range(2)]
+        update = place(update, shape, places)
     return (update.reshape(experts, pairs, row_count, 8 * WIDTH), new_momentum)
 
 

time: 111 us -> 107 us (0.964)
  Pallas kernels: 20.2 us -> 18.2 us
  other arithmetic: 4.75 us -> 3.37 us
  starting transfers between devices: 36.5 us -> 35.2 us
    ppermute x22 -> x23, starting transfers between devices: 29.1 us -> 26.3 us  [shift(): return lax.ppermute(value, 'replica', pairs)]
    pallas_call x1 -> x2, Pallas kernels: 7.57 us -> 5.55 us  [the longest x1 3.47 us: early_products(): pl.pallas_call(own_kernel, out_shape=(out, pltpu.HBM((FF, FF), BF16)), in...]
    all_to_all x2, starting transfers between devices: 7.45 us -> 8.91 us  [back(): lax.all_to_all(value, 'tensor', split_axis=0, concat_axis=0, tiled=True)]
    add x1, other arithmetic: 2.78 us -> 1.41 us  [stepped(): return momentum_decay * momentum + gradient.astype(F32)]
    pallas_call x5 -> x6, Pallas kernels: 5.34 us -> 5.9 us  [place(): pl.pallas_call(functools.partial(place_kernel, where, int(aliased)), out_...]
    ppermute x22 -> x23, waiting for transfers between devices: 25 us -> 24.6 us  [shift(): return lax.ppermute(value, 'replica', pairs)]
  transfers between devices with their start and end apart: 24 -> 25, of which waited for: 8 -> 11; matrix products, arithmetic and copies ran while one was open for 3% -> 1% of each run, Pallas kernels for 17% -> 16%
where the time goes in v4:
time: 107 us; the launch traced here: 106 us
  starting transfers between devices  35.2 us (33%)
  waiting for transfers between devices  24.6 us (23%)
  blocking collectives  21.9 us (20%)
  Pallas kernels  18.2 us (17%)
  other arithmetic  3.37 us (3%)
  local copies, waits for them, and re-layouts  1.88 us (2%)
    ppermute x23, starting transfers between devices, shift(): return lax.ppermute(value, 'replica', pairs)  26.3 us
    ppermute x23, waiting for transfers between devices, shift(): return lax.ppermute(value, 'replica', pairs)  24.6 us
    all_to_all x1, blocking collectives, local(): lax.all_to_all(flat_rows, 'tensor', split_axis=0, concat_axis=0, tiled=True)  21.9 us
    all_to_all x2, starting transfers between devices, back(): lax.all_to_all(value, 'tensor', split_axis=0, concat_axis=0, tiled=True)  8.91 us
    pallas_call x1, Pallas kernels, chain(): pl.pallas_call(chain_kernel, out_shape=(jax.ShapeDtypeStruct((FF, LATE),...  6.04 us
    pallas_call x6, Pallas kernels, place(): pl.pallas_call(functools.partial(place_kernel, where, int(aliased)), out_...  5.9 us
    pallas_call x1, Pallas kernels, early_products(): pl.pallas_call(own_kernel, out_shape=(out, pltpu.HBM((FF, FF), BF16)), in...  3.47 us
  transfers between devices with their start and end apart: 25, of which 11 were waited for; matrix products, arithmetic and copies ran while one was open for 1% of the time, Pallas kernels for 16%

profile of v4, /device:TPU:1, one launch (start us, length us, event | category | flops | bytes accessed | tf_op | source)
XLA Modules:
  0.0 106.2 jit_solution(7643708100278374513)
XLA Ops:
  0.6 2.0 %fusion.1 = bf16[8,2,48,512]{3,2,1,0:T(8,128)(2,1)S(1)} fusion(bf16[8,2,48,512]{3,2,1,0:T(8,128)(2,1)} %param.2, f32[8,2,48,512]{3,2,1,0:T(8,128)} %param.3), kind=kLoop, calls=%fused_computation.3 | loop fusion | flops 2359296 | bytes 3145728 | tf_op jit(solution)/shard_map/convert_element_type | solution.py:321
  2.6 21.9 %all_to_all.15 = bf16[16,48,512]{2,1,0:T(8,128)(2,1)S(1)} all-to-all(bf16[16,48,512]{2,1,0:T(8,128)(2,1)S(1)} %bitcast.8), channel_id=1, replica_groups=mesh['replica'=8,'tensor'=16] {'tensor'}, dimensions={0} | all-to-all | bytes 1572864 | tf_op jit(solution)/shard_map/all_to_all | solution.py:322
  24.5 0.6 shard_map.41
  25.1 1.9 %collective-permute-start = (bf16[768,256]{1,0:T(8,128)(2,1)S(1)}, bf16[768,256]{1,0:T(8,128)(2,1)S(1)}, u32[]{:S(2)}, u32[]{:S(2)}) collective-permute-start(bf16[768,256]{1,0:T(8,128)(2,1)S(1)} %get-tuple-element.30), channel_id=1, source_target_pairs={{0,16},{16,0},{32,48},{48,32},{64,80},{80,64},{96,112},{112,96},{1... | collective-permute-start | bytes 1179656 | tf_op jit(solution)/shard_map/ppermute | solution.py:44
  27.0 1.3 %collective-permute-done.got_ref = bf16[768,256]{1,0:T(8,128)(2,1)S(1)} collective-permute-done((bf16[768,256]{1,0:T(8,128)(2,1)S(1)}, bf16[768,256]{1,0:T(8,128)(2,1)S(1)}, u32[]{:S(2)}, u32[]{:S(2)}) %collective-permute-start) | collective-permute-done | bytes 393248 | tf_op jit(solution)/shard_map/ppermute | solution.py:44
  28.4 1.3 %collective-permute-start.1 = (bf16[192,256]{1,0:T(8,128)(2,1)S(1)}, bf16[192,256]{1,0:T(8,128)(2,1)S(1)}, u32[]{:S(2)}, u32[]{:S(2)}) collective-permute-start(bf16[192,256]{1,0:T(8,128)(2,1)S(1)} %get-tuple-element.32), channel_id=1, source_target_pairs={{0,32},{16,48},{32,64},{48,80},{64,96},{80,112},{96,0},{112,16},{1... | collective-permute-start | bytes 294920 | tf_op jit(solution)/shard_map/ppermute | solution.py:44
  29.7 1.5 %collective-permute-start.2 = (bf16[192,256]{1,0:T(8,128)(2,1)S(1)}, bf16[192,256]{1,0:T(8,128)(2,1)S(1)}, u32[]{:S(2)}, u32[]{:S(2)}) collective-permute-start(bf16[192,256]{1,0:T(8,128)(2,1)S(1)} %get-tuple-element.33), channel_id=1, source_target_pairs={{0,96},{16,112},{32,0},{48,16},{64,32},{80,48},{96,64},{112,80},{1... | collective-permute-start | bytes 294920 | tf_op jit(solution)/shard_map/ppermute | solution.py:44
  31.2 1.5 %collective-permute-start.3 = (bf16[192,256]{1,0:T(8,128)(2,1)S(1)}, bf16[192,256]{1,0:T(8,128)(2,1)S(1)}, u32[]{:S(2)}, u32[]{:S(2)}) collective-permute-start(bf16[192,256]{1,0:T(8,128)(2,1)S(1)} %get-tuple-element.34), channel_id=1, source_target_pairs={{0,64},{16,80},{32,96},{48,112},{64,0},{80,16},{96,32},{112,48},{1... | collective-permute-start | bytes 294920 | tf_op jit(solution)/shard_map/ppermute | solution.py:44
  32.7 1.0 collective-permute-done.1.a_ref
  33.7 2.6 %collective-permute-done.3.c_ref = bf16[192,256]{1,0:T(8,128)(2,1)S(1)} collective-permute-done((bf16[192,256]{1,0:T(8,128)(2,1)S(1)}, bf16[192,256]{1,0:T(8,128)(2,1)S(1)}, u32[]{:S(2)}, u32[]{:S(2)}) %collective-permute-start.3) | collective-permute-done | bytes 98336 | tf_op jit(solution)/shard_map/ppermute | solution.py:44
  36.3 1.0 collective-permute-start.6
  37.3 1.8 %collective-permute-start.5 = (bf16[192,256]{1,0:T(8,128)(2,1)S(1)}, bf16[192,256]{1,0:T(8,128)(2,1)S(1)}, u32[]{:S(2)}, u32[]{:S(2)}) collective-permute-start(bf16[192,256]{1,0:T(8,128)(2,1)S(1)} %shard_map.43.refs_0_), channel_id=1, source_target_pairs={{0,64},{16,80},{32,96},{48,112},{64,0},{80,16},{96,32},{112,48},{1... | collective-permute-start | bytes 294920 | tf_op jit(solution)/shard_map/ppermute | solution.py:44
  39.1 0.8 collective-permute-start.4
  39.9 2.9 %collective-permute-start.7 = (bf16[192,256]{1,0:T(8,128)(2,1)S(1)}, bf16[192,256]{1,0:T(8,128)(2,1)S(1)}, u32[]{:S(2)}, u32[]{:S(2)}) collective-permute-start(bf16[192,256]{1,0:T(8,128)(2,1)S(1)} %shard_map.43.refs_0_), channel_id=1, source_target_pairs={{0,16},{16,0},{32,48},{48,32},{64,80},{80,64},{96,112},{112,96},{1... | collective-permute-start | bytes 294920 | tf_op jit(solution)/shard_map/ppermute | solution.py:44
  42.8 1.4 %collective-permute-start.10 = (bf16[192,256]{1,0:T(8,128)(2,1)S(1)}, bf16[192,256]{1,0:T(8,128)(2,1)S(1)}, u32[]{:S(2)}, u32[]{:S(2)}) collective-permute-start(bf16[192,256]{1,0:T(8,128)(2,1)S(1)} %collective-permute-done.6.refs_3_), channel_id=1, source_target_pairs={{0,16},{16,0},{32,48},{48,32},{64,80},{80,64},{96,112},{112,96},{1... | collective-permute-start | bytes 294920 | tf_op jit(solution)/shard_map/ppermute | solution.py:44
  44.2 1.3 %collective-permute-start.9 = (bf16[192,256]{1,0:T(8,128)(2,1)S(1)}, bf16[192,256]{1,0:T(8,128)(2,1)S(1)}, u32[]{:S(2)}, u32[]{:S(2)}) collective-permute-start(bf16[192,256]{1,0:T(8,128)(2,1)S(1)} %collective-permute-done.5.refs_2_), channel_id=1, source_target_pairs={{0,16},{16,0},{32,48},{48,32},{64,80},{80,64},{96,112},{112,96},{1... | collective-permute-start | bytes 294920 | tf_op jit(solution)/shard_map/ppermute | solution.py:44
  45.5 0.8 collective-permute-start.8
  46.2 0.8 collective-permute-start.13
  47.0 2.7 %collective-permute-start.12 = (bf16[768,256]{1,0:T(8,128)(2,1)S(1)}, bf16[768,256]{1,0:T(8,128)(2,1)S(1)}, u32[]{:S(2)}, u32[]{:S(2)}) collective-permute-start(bf16[768,256]{1,0:T(8,128)(2,1)S(1)} %get-tuple-element.40.early_in), channel_id=1, source_target_pairs={{0,64},{16,80},{32,96},{48,112},{64,0},{80,16},{96,32},{112,48},{1... | collective-permute-start | bytes 1179656 | tf_op jit(solution)/shard_map/ppermute | solution.py:44
  49.7 6.0 %shard_map.44 = (bf16[768,256]{1,0:T(8,128)(2,1)}, bf16[2,768,768]{2,1,0:T(8,128)(2,1)}, f32[8,128]{1,0:T(8,128)S(1)}) custom-call(bf16[192,256]{1,0:T(8,128)(2,1)S(1)} %shard_map.43.refs_0_, bf16[192,256]{1,0:T(8,128)(2,1)S(1)} %collective-permute-done.4.refs_1_, bf16[192,256]{1,0:T(8,128)(2,1)S(1)} %collective-permute-done.5.refs_2_, ...), custom_call_target="tpu_custom_call" | custom-call | tf_op jit(solution)/shard_map/pallas_call | solution.py:188
  55.8 3.7 %all-to-all-start.1 = ((bf16[16,48,256]{2,1,0:T(8,128)(2,1)}), bf16[16,48,256]{2,1,0:T(8,128)(2,1)S(1)}, u32[]{:S(2)}, u32[]{:S(2)}) async-start(bf16[16,48,256]{2,1,0:T(8,128)(2,1)} %bitcast.2), calls=%async_computation.1 | async-start | bytes 786432 | tf_op jit(solution)/shard_map/all_to_all | solution.py:334
  59.5 1.7 %copy-done.1 = bf16[2,768,768]{2,1,0:T(8,128)(2,1)S(1)} copy-done((bf16[2,768,768]{2,1,0:T(8,128)(2,1)S(1)}, bf16[2,768,768]{2,1,0:T(8,128)(2,1)}, u32[]{:S(2)}) %copy-start.1) | copy-done | bytes 2359320
  61.2 3.5 %shard_map.45 = (bf16[768,1024]{1,0:T(8,128)(2,1)}, bf16[768,768]{1,0:T(8,128)(2,1)}) custom-call(bf16[2,768,768]{2,1,0:T(8,128)(2,1)S(1)} %copy-done.1, f32[8,128]{1,0:T(8,128)S(1)} %get-tuple-element.38.scale_ref, bf16[768,256]{1,0:T(8,128)(2,1)S(1)} %get-tuple-element.40.early_in), custom_call_target="tpu_custom_call" | custom-call | flops 1207959552 | tf_op jit(solution)/shard_map/pallas_call | solution.py:249
  64.7 1.4 %convert_add_fusion.2 = f32[8,2,48,512]{3,2,1,0:T(8,128)} fusion(bf16[8,2,48,512]{3,2,1,0:T(8,128)(2,1)S(1)} %copy-done.3, f32[8,2,48,512]{3,2,1,0:T(8,128)S(1)} %copy-done.2), kind=kLoop, calls=%fused_computation.4 | loop fusion | flops 1179648 | bytes 3932160 | tf_op jit(solution)/shard_map/add | solution.py:317
  66.1 1.3 %collective-permute-done.12.refs_1_ = bf16[768,256]{1,0:T(8,128)(2,1)S(1)} collective-permute-done((bf16[768,256]{1,0:T(8,128)(2,1)S(1)}, bf16[768,256]{1,0:T(8,128)(2,1)S(1)}, u32[]{:S(2)}, u32[]{:S(2)}) %collective-permute-start.12) | collective-permute-done | bytes 393248 | tf_op jit(solution)/shard_map/ppermute | solution.py:44
  67.4 2.1 %shard_map.46 = bf16[768,1024]{1,0:T(8,128)(2,1)} custom-call(bf16[768,768]{1,0:T(8,128)(2,1)S(1)} %copy-done, f32[8,128]{1,0:T(8,128)S(1)} %get-tuple-element.38.scale_ref, bf16[768,256]{1,0:T(8,128)(2,1)S(1)} %collective-permute-done.11.refs_0_, bf16[768,256]{1,0:T(8,128)(2,1)S(1)} %collective-permute-done.12.refs_1_, ...), custom_call_target="tpu_custom_call", output_to_operand_aliasing={{}: (5, {})} | custom-call | flops 905969664 | tf_op jit(solution)/shard_map/pallas_call | solution.py:264
  69.5 5.2 %all-to-all-start.2 = ((bf16[16,48,1024]{2,1,0:T(8,128)(2,1)}), bf16[16,48,1024]{2,1,0:T(8,128)(2,1)S(1)}, u32[]{:S(2)}, u32[]{:S(2)}) async-start(bf16[16,48,1024]{2,1,0:T(8,128)(2,1)} %bitcast.3), calls=%async_computation.2 | async-start | bytes 3145728 | tf_op jit(solution)/shard_map/all_to_all | solution.py:334
  74.7 1.8 %collective-permute-start.15 = (bf16[16,48,256]{2,1,0:T(8,128)(2,1)S(1)}, bf16[16,48,256]{2,1,0:T(8,128)(2,1)S(1)}, u32[]{:S(2)}, u32[]{:S(2)}) collective-permute-start(bf16[16,48,256]{2,1,0:T(8,128)(2,1)S(1)} %all-to-all-done.1.refs_0_), channel_id=1, source_target_pairs={{0,16},{16,0},{32,48},{48,32},{64,80},{80,64},{96,112},{112,96},{1... | collective-permute-start | bytes 1179656 | tf_op jit(solution)/shard_map/ppermute | solution.py:44
  76.5 0.2 collective-permute-start.14
  76.7 1.2 %collective-permute-start.17 = (bf16[16,48,256]{2,1,0:T(8,128)(2,1)S(1)}, bf16[16,48,256]{2,1,0:T(8,128)(2,1)S(1)}, u32[]{:S(2)}, u32[]{:S(2)}) collective-permute-start(bf16[16,48,256]{2,1,0:T(8,128)(2,1)S(1)} %all-to-all-done.1.refs_0_), channel_id=1, source_target_pairs={{0,32},{16,48},{32,64},{48,80},{64,96},{80,112},{96,0},{112,16},{1... | collective-permute-start | bytes 1179656 | tf_op jit(solution)/shard_map/ppermute | solution.py:44
  78.0 1.4 %collective-permute-start.19 = (bf16[16,48,256]{2,1,0:T(8,128)(2,1)S(1)}, bf16[16,48,256]{2,1,0:T(8,128)(2,1)S(1)}, u32[]{:S(2)}, u32[]{:S(2)}) collective-permute-start(bf16[16,48,256]{2,1,0:T(8,128)(2,1)S(1)} %all-to-all-done.1.refs_0_), channel_id=1, source_target_pairs={{0,64},{16,80},{32,96},{48,112},{64,0},{80,16},{96,32},{112,48},{1... | collective-permute-start | bytes 1179656 | tf_op jit(solution)/shard_map/ppermute | solution.py:44
  79.4 0.9 shard_map.47.refs_3_
  80.3 6.9 %collective-permute-done.14.refs_0_ = bf16[16,48,256]{2,1,0:T(8,128)(2,1)S(1)} collective-permute-done((bf16[16,48,256]{2,1,0:T(8,128)(2,1)S(1)}, bf16[16,48,256]{2,1,0:T(8,128)(2,1)S(1)}, u32[]{:S(2)}, u32[]{:S(2)}) %collective-permute-start.14) | collective-permute-done | bytes 393248 | tf_op jit(solution)/shard_map/ppermute | solution.py:44
  87.2 1.1 %collective-permute-done.17.refs_1_ = bf16[16,48,256]{2,1,0:T(8,128)(2,1)S(1)} collective-permute-done((bf16[16,48,256]{2,1,0:T(8,128)(2,1)S(1)}, bf16[16,48,256]{2,1,0:T(8,128)(2,1)S(1)}, u32[]{:S(2)}, u32[]{:S(2)}) %collective-permute-start.17) | collective-permute-done | bytes 393248 | tf_op jit(solution)/shard_map/ppermute | solution.py:44
  88.3 8.6 %collective-permute-done.19.refs_2_ = bf16[16,48,256]{2,1,0:T(8,128)(2,1)S(1)} collective-permute-done((bf16[16,48,256]{2,1,0:T(8,128)(2,1)S(1)}, bf16[16,48,256]{2,1,0:T(8,128)(2,1)S(1)}, u32[]{:S(2)}, u32[]{:S(2)}) %collective-permute-start.19) | collective-permute-done | bytes 393248 | tf_op jit(solution)/shard_map/ppermute | solution.py:44
  96.9 1.0 collective-permute-start.20
  97.9 0.5 collective-permute-start.16
  98.4 1.0 shard_map.48.refs_3_
  99.5 0.4 collective-permute-done.18.refs_1_
  99.8 0.6 collective-permute-done.16.refs_0_
  100.4 1.0 shard_map.49.refs_4_
  101.4 0.2 fusion.2
  101.6 0.5 collective-permute-start.22
  102.2 1.2 %shard_map.50.refs_2_ = bf16[16,48,4096]{2,1,0:T(8,128)(2,1)} custom-call(bf16[16,48,1024]{2,1,0:T(8,128)(2,1)S(1)} %all-to-all-done.2.refs_0_.refs_1_.refs_2_.refs_3_, bf16[16,48,1024]{2,1,0:T(8,128)(2,1)S(1)} %all-to-all-done.2.refs_0_.refs_1_.refs_2_.refs_3_, ...), custom_call_target="tpu_custom_call", output_to_operand_aliasing={{}: (4, {})} | custom-call | tf_op jit(solution)/shard_map/pallas_call | solution.py:303
  103.4 0.6 collective-permute-done.22.refs_0_.refs_1_
  104.0 0.9 shard_map.51.refs_2_
  104.9 0.2 collective-permute-done.21.refs_0_.refs_1_
  105.1 0.9 shard_map.52
  (26 shorter events, 0.3 us)
Async XLA Ops:
  25.1 3.2 %collective-permute-start = (bf16[768,256]{1,0:T(8,128)(2,1)S(1)}, bf16[768,256]{1,0:T(8,128)(2,1)S(1)}, u32[]{:S(2)}, u32[]{:S(2)}) collective-permute-start(bf16[768,256]{1,0:T(8,128)(2,1)S(1)} %get-tuple-element.30), channel_id=1, source_target_pairs={{0,16},{16,0},{32,48},{48,32},{64,80},{80,64},{96,112},{112,96},{1... | collective-permute-start | bytes 1179656 | tf_op jit(solution)/shard_map/ppermute | solution.py:44
  28.4 5.3 %collective-permute-start.1 = (bf16[192,256]{1,0:T(8,128)(2,1)S(1)}, bf16[192,256]{1,0:T(8,128)(2,1)S(1)}, u32[]{:S(2)}, u32[]{:S(2)}) collective-permute-start(bf16[192,256]{1,0:T(8,128)(2,1)S(1)} %get-tuple-element.32), channel_id=1, source_target_pairs={{0,32},{16,48},{32,64},{48,80},{64,96},{80,112},{96,0},{112,16},{1... | collective-permute-start | bytes 294920 | tf_op jit(solution)/shard_map/ppermute | solution.py:44
  29.7 4.0 %collective-permute-start.2 = (bf16[192,256]{1,0:T(8,128)(2,1)S(1)}, bf16[192,256]{1,0:T(8,128)(2,1)S(1)}, u32[]{:S(2)}, u32[]{:S(2)}) collective-permute-start(bf16[192,256]{1,0:T(8,128)(2,1)S(1)} %get-tuple-element.33), channel_id=1, source_target_pairs={{0,96},{16,112},{32,0},{48,16},{64,32},{80,48},{96,64},{112,80},{1... | collective-permute-start | bytes 294920 | tf_op jit(solution)/shard_map/ppermute | solution.py:44
  31.2 5.1 %collective-permute-start.3 = (bf16[192,256]{1,0:T(8,128)(2,1)S(1)}, bf16[192,256]{1,0:T(8,128)(2,1)S(1)}, u32[]{:S(2)}, u32[]{:S(2)}) collective-permute-start(bf16[192,256]{1,0:T(8,128)(2,1)S(1)} %get-tuple-element.34), channel_id=1, source_target_pairs={{0,64},{16,80},{32,96},{48,112},{64,0},{80,16},{96,32},{112,48},{1... | collective-permute-start | bytes 294920 | tf_op jit(solution)/shard_map/ppermute | solution.py:44
  36.3 6.5 %collective-permute-start.6 = (bf16[192,256]{1,0:T(8,128)(2,1)S(1)}, bf16[192,256]{1,0:T(8,128)(2,1)S(1)}, u32[]{:S(2)}, u32[]{:S(2)}) collective-permute-start(bf16[192,256]{1,0:T(8,128)(2,1)S(1)} %shard_map.43.refs_0_), channel_id=1, source_target_pairs={{0,32},{16,48},{32,64},{48,80},{64,96},{80,112},{96,0},{112,16},{1... | collective-permute-start | bytes 294920 | tf_op jit(solution)/shard_map/ppermute | solution.py:44
  37.3 6.9 %collective-permute-start.5 = (bf16[192,256]{1,0:T(8,128)(2,1)S(1)}, bf16[192,256]{1,0:T(8,128)(2,1)S(1)}, u32[]{:S(2)}, u32[]{:S(2)}) collective-permute-start(bf16[192,256]{1,0:T(8,128)(2,1)S(1)} %shard_map.43.refs_0_), channel_id=1, source_target_pairs={{0,64},{16,80},{32,96},{48,112},{64,0},{80,16},{96,32},{112,48},{1... | collective-permute-start | bytes 294920 | tf_op jit(solution)/shard_map/ppermute | solution.py:44
  39.1 6.4 %collective-permute-start.4 = (bf16[192,256]{1,0:T(8,128)(2,1)S(1)}, bf16[192,256]{1,0:T(8,128)(2,1)S(1)}, u32[]{:S(2)}, u32[]{:S(2)}) collective-permute-start(bf16[192,256]{1,0:T(8,128)(2,1)S(1)} %shard_map.43.refs_0_), channel_id=1, source_target_pairs={{0,96},{16,112},{32,0},{48,16},{64,32},{80,48},{96,64},{112,80},{1... | collective-permute-start | bytes 294920 | tf_op jit(solution)/shard_map/ppermute | solution.py:44
  39.9 7.1 %collective-permute-start.7 = (bf16[192,256]{1,0:T(8,128)(2,1)S(1)}, bf16[192,256]{1,0:T(8,128)(2,1)S(1)}, u32[]{:S(2)}, u32[]{:S(2)}) collective-permute-start(bf16[192,256]{1,0:T(8,128)(2,1)S(1)} %shard_map.43.refs_0_), channel_id=1, source_target_pairs={{0,16},{16,0},{32,48},{48,32},{64,80},{80,64},{96,112},{112,96},{1... | collective-permute-start | bytes 294920 | tf_op jit(solution)/shard_map/ppermute | solution.py:44
  42.8 6.9 %collective-permute-start.10 = (bf16[192,256]{1,0:T(8,128)(2,1)S(1)}, bf16[192,256]{1,0:T(8,128)(2,1)S(1)}, u32[]{:S(2)}, u32[]{:S(2)}) collective-permute-start(bf16[192,256]{1,0:T(8,128)(2,1)S(1)} %collective-permute-done.6.refs_3_), channel_id=1, source_target_pairs={{0,16},{16,0},{32,48},{48,32},{64,80},{80,64},{96,112},{112,96},{1... | collective-permute-start | bytes 294920 | tf_op jit(solution)/shard_map/ppermute | solution.py:44
  44.2 5.5 %collective-permute-start.9 = (bf16[192,256]{1,0:T(8,128)(2,1)S(1)}, bf16[192,256]{1,0:T(8,128)(2,1)S(1)}, u32[]{:S(2)}, u32[]{:S(2)}) collective-permute-start(bf16[192,256]{1,0:T(8,128)(2,1)S(1)} %collective-permute-done.5.refs_2_), channel_id=1, source_target_pairs={{0,16},{16,0},{32,48},{48,32},{64,80},{80,64},{96,112},{112,96},{1... | collective-permute-start | bytes 294920 | tf_op jit(solution)/shard_map/ppermute | solution.py:44
  45.5 4.2 %collective-permute-start.8 = (bf16[192,256]{1,0:T(8,128)(2,1)S(1)}, bf16[192,256]{1,0:T(8,128)(2,1)S(1)}, u32[]{:S(2)}, u32[]{:S(2)}) collective-permute-start(bf16[192,256]{1,0:T(8,128)(2,1)S(1)} %collective-permute-done.4.refs_1_), channel_id=1, source_target_pairs={{0,16},{16,0},{32,48},{48,32},{64,80},{80,64},{96,112},{112,96},{1... | collective-permute-start | bytes 294920 | tf_op jit(solution)/shard_map/ppermute | solution.py:44
  46.2 19.8 %collective-permute-start.13 = (bf16[768,256]{1,0:T(8,128)(2,1)S(1)}, bf16[768,256]{1,0:T(8,128)(2,1)S(1)}, u32[]{:S(2)}, u32[]{:S(2)}) collective-permute-start(bf16[768,256]{1,0:T(8,128)(2,1)S(1)} %get-tuple-element.40.early_in), channel_id=1, source_target_pairs={{0,32},{16,48},{32,64},{48,80},{64,96},{80,112},{96,0},{112,16},{1... | collective-permute-start | bytes 1179656 | tf_op jit(solution)/shard_map/ppermute | solution.py:44
  47.0 20.4 %collective-permute-start.12 = (bf16[768,256]{1,0:T(8,128)(2,1)S(1)}, bf16[768,256]{1,0:T(8,128)(2,1)S(1)}, u32[]{:S(2)}, u32[]{:S(2)}) collective-permute-start(bf16[768,256]{1,0:T(8,128)(2,1)S(1)} %get-tuple-element.40.early_in), channel_id=1, source_target_pairs={{0,64},{16,80},{32,96},{48,112},{64,0},{80,16},{96,32},{112,48},{1... | collective-permute-start | bytes 1179656 | tf_op jit(solution)/shard_map/ppermute | solution.py:44
  49.7 17.7 %collective-permute-start.11 = (bf16[768,256]{1,0:T(8,128)(2,1)S(1)}, bf16[768,256]{1,0:T(8,128)(2,1)S(1)}, u32[]{:S(2)}, u32[]{:S(2)}) collective-permute-start(bf16[768,256]{1,0:T(8,128)(2,1)S(1)} %get-tuple-element.40.early_in), channel_id=1, source_target_pairs={{0,96},{16,112},{32,0},{48,16},{64,32},{80,48},{96,64},{112,80},{1... | collective-permute-start | bytes 1179656 | tf_op jit(solution)/shard_map/ppermute | solution.py:44
  55.8 13.7 %all-to-all-start.1 = ((bf16[16,48,256]{2,1,0:T(8,128)(2,1)}), bf16[16,48,256]{2,1,0:T(8,128)(2,1)S(1)}, u32[]{:S(2)}, u32[]{:S(2)}) async-start(bf16[16,48,256]{2,1,0:T(8,128)(2,1)} %bitcast.2), calls=%async_computation.1 | async-start | bytes 786432 | tf_op jit(solution)/shard_map/all_to_all | solution.py:334
  59.5 1.7 %copy-start.1 = (bf16[2,768,768]{2,1,0:T(8,128)(2,1)S(1)}, bf16[2,768,768]{2,1,0:T(8,128)(2,1)}, u32[]{:S(2)}) copy-start(bf16[2,768,768]{2,1,0:T(8,128)(2,1)} %get-tuple-element.37.polys_in) | copy-start | bytes 7077892
  61.2 3.5 %copy-start.2 = (f32[8,2,48,512]{3,2,1,0:T(8,128)S(1)}, f32[8,2,48,512]{3,2,1,0:T(8,128)}, u32[]{:S(2)}) copy-start(f32[8,2,48,512]{3,2,1,0:T(8,128)} %param.3) | copy-start | bytes 4718596
  61.2 3.5 %copy-start.3 = (bf16[8,2,48,512]{3,2,1,0:T(8,128)(2,1)S(1)}, bf16[8,2,48,512]{3,2,1,0:T(8,128)(2,1)}, u32[]{:S(2)}) copy-start(bf16[8,2,48,512]{3,2,1,0:T(8,128)(2,1)} %param.2) | copy-start | bytes 2359300
  64.7 2.7 %copy-start = (bf16[768,768]{1,0:T(8,128)(2,1)S(1)}, bf16[768,768]{1,0:T(8,128)(2,1)}, u32[]{:S(2)}) copy-start(bf16[768,768]{1,0:T(8,128)(2,1)} %get-tuple-element.41.square_ref) | copy-start | bytes 3538948
  69.5 31.9 %all-to-all-start.2 = ((bf16[16,48,1024]{2,1,0:T(8,128)(2,1)}), bf16[16,48,1024]{2,1,0:T(8,128)(2,1)S(1)}, u32[]{:S(2)}, u32[]{:S(2)}) async-start(bf16[16,48,1024]{2,1,0:T(8,128)(2,1)} %bitcast.3), calls=%async_computation.2 | async-start | bytes 3145728 | tf_op jit(solution)/shard_map/all_to_all | solution.py:334
  74.7 4.7 %collective-permute-start.15 = (bf16[16,48,256]{2,1,0:T(8,128)(2,1)S(1)}, bf16[16,48,256]{2,1,0:T(8,128)(2,1)S(1)}, u32[]{:S(2)}, u32[]{:S(2)}) collective-permute-start(bf16[16,48,256]{2,1,0:T(8,128)(2,1)S(1)} %all-to-all-done.1.refs_0_), channel_id=1, source_target_pairs={{0,16},{16,0},{32,48},{48,32},{64,80},{80,64},{96,112},{112,96},{1... | collective-permute-start | bytes 1179656 | tf_op jit(solution)/shard_map/ppermute | solution.py:44
  76.5 10.7 %collective-permute-start.14 = (bf16[16,48,256]{2,1,0:T(8,128)(2,1)S(1)}, bf16[16,48,256]{2,1,0:T(8,128)(2,1)S(1)}, u32[]{:S(2)}, u32[]{:S(2)}) collective-permute-start(bf16[16,48,256]{2,1,0:T(8,128)(2,1)S(1)} %all-to-all-done.1.refs_0_), channel_id=1, source_target_pairs={{0,96},{16,112},{32,0},{48,16},{64,32},{80,48},{96,64},{112,80},{1... | collective-permute-start | bytes 1179656 | tf_op jit(solution)/shard_map/ppermute | solution.py:44
  76.7 11.6 %collective-permute-start.17 = (bf16[16,48,256]{2,1,0:T(8,128)(2,1)S(1)}, bf16[16,48,256]{2,1,0:T(8,128)(2,1)S(1)}, u32[]{:S(2)}, u32[]{:S(2)}) collective-permute-start(bf16[16,48,256]{2,1,0:T(8,128)(2,1)S(1)} %all-to-all-done.1.refs_0_), channel_id=1, source_target_pairs={{0,32},{16,48},{32,64},{48,80},{64,96},{80,112},{96,0},{112,16},{1... | collective-permute-start | bytes 1179656 | tf_op jit(solution)/shard_map/ppermute | solution.py:44
  78.0 18.9 %collective-permute-start.19 = (bf16[16,48,256]{2,1,0:T(8,128)(2,1)S(1)}, bf16[16,48,256]{2,1,0:T(8,128)(2,1)S(1)}, u32[]{:S(2)}, u32[]{:S(2)}) collective-permute-start(bf16[16,48,256]{2,1,0:T(8,128)(2,1)S(1)} %all-to-all-done.1.refs_0_), channel_id=1, source_target_pairs={{0,64},{16,80},{32,96},{48,112},{64,0},{80,16},{96,32},{112,48},{1... | collective-permute-start | bytes 1179656 | tf_op jit(solution)/shard_map/ppermute | solution.py:44
  96.9 2.6 %collective-permute-start.20 = (bf16[16,48,256]{2,1,0:T(8,128)(2,1)S(1)}, bf16[16,48,256]{2,1,0:T(8,128)(2,1)S(1)}, u32[]{:S(2)}, u32[]{:S(2)}) collective-permute-start(bf16[16,48,256]{2,1,0:T(8,128)(2,1)S(1)} %collective-permute-done.19.refs_2_), channel_id=1, source_target_pairs={{0,16},{16,0},{32,48},{48,32},{64,80},{80,64},{96,112},{112,96},{1... | collective-permute-start | bytes 1179656 | tf_op jit(solution)/shard_map/ppermute | solution.py:44
  97.9 1.9 %collective-permute-start.18 = (bf16[16,48,256]{2,1,0:T(8,128)(2,1)S(1)}, bf16[16,48,256]{2,1,0:T(8,128)(2,1)S(1)}, u32[]{:S(2)}, u32[]{:S(2)}) collective-permute-start(bf16[16,48,256]{2,1,0:T(8,128)(2,1)S(1)} %collective-permute-done.17.refs_1_), channel_id=1, source_target_pairs={{0,16},{16,0},{32,48},{48,32},{64,80},{80,64},{96,112},{112,96},{1... | collective-permute-start | bytes 1179656 | tf_op jit(solution)/shard_map/ppermute | solution.py:44
  97.9 2.5 %collective-permute-start.16 = (bf16[16,48,256]{2,1,0:T(8,128)(2,1)S(1)}, bf16[16,48,256]{2,1,0:T(8,128)(2,1)S(1)}, u32[]{:S(2)}, u32[]{:S(2)}) collective-permute-start(bf16[16,48,256]{2,1,0:T(8,128)(2,1)S(1)} %collective-permute-done.14.refs_0_), channel_id=1, source_target_pairs={{0,16},{16,0},{32,48},{48,32},{64,80},{80,64},{96,112},{112,96},{1... | collective-permute-start | bytes 1179656 | tf_op jit(solution)/shard_map/ppermute | solution.py:44
  101.6 2.4 %collective-permute-start.22 = (bf16[16,48,512]{2,1,0:T(8,128)(2,1)S(1)}, bf16[16,48,512]{2,1,0:T(8,128)(2,1)S(1)}, u32[]{:S(2)}, u32[]{:S(2)}) collective-permute-start(bf16[16,48,512]{2,1,0:T(8,128)(2,1)S(1)} %get-tuple-element.56), channel_id=1, source_target_pairs={{0,16},{16,0},{32,48},{48,32},{64,80},{80,64},{96,112},{112,96},{1... | collective-permute-start | bytes 2359304 | tf_op jit(solution)/shard_map/ppermute | solution.py:44
  102.1 3.0 %collective-permute-start.21 = (bf16[16,48,512]{2,1,0:T(8,128)(2,1)S(1)}, bf16[16,48,512]{2,1,0:T(8,128)(2,1)S(1)}, u32[]{:S(2)}, u32[]{:S(2)}) collective-permute-start(bf16[16,48,512]{2,1,0:T(8,128)(2,1)S(1)} %get-tuple-element.57), channel_id=1, source_target_pairs={{0,16},{16,0},{32,48},{48,32},{64,80},{80,64},{96,112},{112,96},{1... | collective-permute-start | bytes 2359304 | tf_op jit(solution)/shard_map/ppermute | solution.py:44

commit v5 on v4

--- a/solution.py
+++ b/solution.py
@@ -19,8 +19,10 @@
 scale_factor = 0.2 * math.sqrt(max(FF, D))
 
 WIDTH = 512
-EARLY = 256
-LATE = WIDTH - EARLY
+LATE, MIDDLE, EARLY = 256, 0, 256
+FIRST = LATE + MIDDLE
+NEAR = MIDDLE + EARLY
+SECOND = 2 * NEAR + 2 * EARLY
 BLOCK = 256
 HALF = FF
 VMEM = pl.BlockSpec(memory_space=pltpu.VMEM)
@@ -52,7 +54,7 @@
     return jnp.dot(left, right, preferred_element_type=F32)
 
 
-def gram_kernel(rows_ref, keep_ref, send_ref, early_ref):
+def gram_kernel(rows_ref, keep_ref, send_ref, near_ref, far_ref):
     core = lax.axis_index("replica") % 2
 
     def rows(index):
@@ -69,7 +71,8 @@
                 keep_ref[where, :] = dot_t(rows(kept[0]), rows(kept[1]))
                 send_ref[where, :] = dot_t(rows(sent[0]), rows(sent[1])).astype(BF16)
 
-    early_ref[...] = rows_ref[:, LATE:]
+    near_ref[...] = rows_ref[:, LATE:]
+    far_ref[...] = rows_ref[:, FIRST:]
 
 
 def partial_gram(rows):
@@ -78,10 +81,11 @@
         out_shape=(
             jax.ShapeDtypeStruct((HALF, BLOCK), F32),
             jax.ShapeDtypeStruct((HALF, BLOCK), BF16),
+            jax.ShapeDtypeStruct((FF, NEAR), BF16),
             jax.ShapeDtypeStruct((FF, EARLY), BF16),
         ),
         in_specs=[VMEM],
-        out_specs=(VMEM,) * 3,
+        out_specs=(VMEM,) * 4,
         compiler_params=PARAMS,
     )(rows)
 
@@ -169,7 +173,7 @@
     gram_1 = (coef_linear * half_way.astype(F32) + dot(half_way, poly_0)).astype(BF16)
     poly_1 = (coef_gram * gram_1.astype(F32) + coef_square * dot(gram_1, gram_1)).astype(BF16)
     copies.append(keep(poly_1, 1))
-    rows = rows_ref[:, :LATE]
+    rows = rows_ref[:, :FIRST]
     first = ((coef_linear * rows.astype(F32) + dot(poly_0, rows)) * scale).astype(BF16)
     for block in range(FF // BLOCK):
         where = pl.ds(block * BLOCK, BLOCK)
@@ -188,7 +192,7 @@
     return pl.pallas_call(
         chain_kernel,
         out_shape=(
-            jax.ShapeDtypeStruct((FF, LATE), BF16),
+            jax.ShapeDtypeStruct((FF, FIRST), BF16),
             pltpu.HBM((2, FF, FF), BF16),
             jax.ShapeDtypeStruct((8, 128), F32),
         ),
@@ -198,7 +202,7 @@
             pltpu.VMEM((2, HALF, BLOCK), BF16),
             pltpu.VMEM((FF, FF), BF16),
             pltpu.VMEM((2, FF, FF), BF16),
-            pltpu.VMEM((FF, LATE), BF16),
+            pltpu.VMEM((FF, FIRST), BF16),
             pltpu.SemaphoreType.DMA((5,)),
         ],
         cost_estimate=pl.CostEstimate(flops=0, bytes_accessed=0, transcendentals=0),
@@ -229,22 +233,27 @@
         store.wait()
 
 
+ORDER = 20_000_000_000
+OTHERS = ((EARLY, NEAR), (EARLY + NEAR, NEAR), (EARLY + 2 * NEAR, EARLY))
+
+
 def other_kernel(square_ref, scale_ref, *refs):
     early_in, out_ref, result, sems = refs[:3], *refs[4:]
     stores = []
-    for place in range(3):
-        result[place] = both_steps_at_once(
+    for place, (start, width) in enumerate(OTHERS):
+        cut = pl.ds(start - EARLY, width)
+        result[:, cut] = both_steps_at_once(
             square_ref[...], scale_ref[:1, :1], early_in[place][...]
         )
-        where = out_ref.at[:, pl.ds((1 + place) * EARLY, EARLY)]
-        stores.append(pltpu.make_async_copy(result.at[place], where, sems.at[place]))
+        where = out_ref.at[:, pl.ds(start, width)]
+        stores.append(pltpu.make_async_copy(result.at[:, cut], where, sems.at[place]))
         stores[-1].start()
     for store in stores:
         store.wait()
 
 
 def early_products(polys, scale, early):
-    out = jax.ShapeDtypeStruct((FF, 4 * EARLY), BF16)
+    out = jax.ShapeDtypeStruct((FF, SECOND), BF16)
     flops = 2 * FF * FF * EARLY
     result, square = pl.pallas_call(
         own_kernel,
@@ -258,7 +267,7 @@
             pltpu.VMEM((FF, EARLY), BF16),
             pltpu.SemaphoreType.DMA((5,)),
         ],
-        cost_estimate=pl.CostEstimate(flops=4 * flops, bytes_accessed=0, transcendentals=0),
+        cost_estimate=pl.CostEstimate(flops=7 * flops, bytes_accessed=0, transcendentals=0),
         compiler_params=LARGE,
     )(polys, scale, early[0])
     return pl.pallas_call(
@@ -266,9 +275,9 @@
         out_shape=out,
         in_specs=[VMEM] * 5 + [HBM],
         out_specs=HBM,
-        scratch_shapes=[pltpu.VMEM((3, FF, EARLY), BF16), pltpu.SemaphoreType.DMA((3,))],
+        scratch_shapes=[pltpu.VMEM((FF, SECOND - EARLY), BF16), pltpu.SemaphoreType.DMA((3,))],
         input_output_aliases={5: 0},
-        cost_estimate=pl.CostEstimate(flops=3 * flops, bytes_accessed=0, transcendentals=0),
+        cost_estimate=pl.CostEstimate(flops=ORDER, bytes_accessed=0, transcendentals=0),
         compiler_params=LARGE,
     )(square, scale, *early[1:], result)
 
@@ -322,7 +331,7 @@
     rows = lax.all_to_all(flat_rows, "tensor", split_axis=0, concat_axis=0, tiled=True)
     rows = rows.reshape(FF, col_count)
 
-    keep, send, early = partial_gram(rows)
+    keep, send, near, far = partial_gram(rows)
     own, to_next, to_last, to_far = chip_sum(keep, shift(send, 0, 1))
     mine = ring_sum(own, shift(to_next, 1), shift(to_last, -1), shift(to_far, 2))
     here = (mine, shift(mine, -1), shift(mine, 2), shift(mine, 1))
@@ -335,35 +344,41 @@
 
     gradient, momentum, late_rows = lax.optimization_barrier((gradient, momentum, late_rows))
     new_momentum = stepped(gradient, momentum)
-    early, _ = lax.optimization_barrier((early, here[2]))
-    early = (early, shift(early, -1), shift(early, 2), shift(early, 1))
-    early_rows = early_products(polys, scale, early)
+    near, far, _ = lax.optimization_barrier((near, far, here[2]))
+    early_rows = early_products(polys, scale, (far, shift(near, -1), shift(near, 1), shift(far, 2)))
     late = back(late_rows)
     late, early_rows, new_momentum = lax.optimization_barrier((late, early_rows, new_momentum))
-    late_pieces = {0: late, 1: shift(late, -1), 3: shift(late, 1), 2: shift(late, 2)}
-    early = back(early_rows)
+    cut = late[:, :, :LATE]
+    late_pieces = {0: late, 1: shift(cut, -1), 3: shift(cut, 1), 2: shift(late, 2)}
+    widths = {0: FIRST, 1: LATE, 3: LATE, 2: FIRST}
+    second = back(early_rows)
 
     shape = (experts * pairs, row_count, 8 * WIDTH)
 
     def late_place(pieces, steps, cross):
-        return (pieces[steps], steps, cross, 0, LATE, 0)
-
-    def early_place(value, steps, cross, source):
-        return (value, steps, cross, LATE, EARLY, source)
-
-    late_across = {0: shift(late, 0, 1)}
-    update = place(None, shape, [late_place(late_pieces, 0, 0), late_place(late_across, 0, 1)])
-    for steps in (1, 3, 2):
-        late_pieces[steps], update = lax.optimization_barrier((late_pieces[steps], update))
-        late_across[steps] = shift(late_pieces[steps], 0, 1)
-    update = place(update, shape, [late_place(late_pieces, steps, 0) for steps in (1, 3, 2)])
-    update = place(update, shape, [late_place(late_across, steps, 1) for steps in (1, 3, 2)])
-    early, update = lax.optimization_barrier((early, update))
-    across = [shift(early[:, :, cut : cut + 2 * EARLY], 0, 1) for cut in (0, 2 * EARLY)]
-    update = place(update, shape, [early_place(early, steps, 0, steps * EARLY) for steps in range(4)])
-    for half in range(2):
-        places = [early_place(across[half], 2 * half + i, 1, i * EARLY) for i in range(2)]
-        update = place(update, shape, places)
+        return (pieces[steps], steps, cross, 0, widths[steps], 0)
+
+    def early_places(value, cross, left, right):
+        starts = {0: (0, EARLY), 1: OTHERS[0], 3: OTHERS[1], 2: OTHERS[2]}
+        return [
+            (value, steps, cross, WIDTH - width, width, start - left)
+            for steps, (start, width) in starts.items()
+            if left <= start < right
+        ]
+
+    late_across = {steps: shift(late_pieces[steps], 0, 1) for steps in (0, 1, 3)}
+    places = [late_place(late_pieces, steps, 0) for steps in (0, 1, 3)]
+    update = place(None, shape, places + [late_place(late_across, 0, 1)])
+    late_pieces[2], update = lax.optimization_barrier((late_pieces[2], update))
+    late_across[2] = shift(late_pieces[2], 0, 1)
+    update = place(update, shape, [late_place(late_across, steps, 1) for steps in (1, 3)] + [late_place(late_pieces, 2, 0)])
+    update = place(update, shape, [late_place(late_across, steps, 1) for steps in (2,)])
+    second, update = lax.optimization_barrier((second, update))
+    update = place(update, shape, early_places(second, 0, 0, SECOND))
+    middle = EARLY + NEAR
+    for left, right in ((0, middle), (middle, SECOND)):
+        across = shift(second[:, :, left:right], 0, 1)
+        update = place(update, shape, early_places(across, 1, left, right))
     return (update.reshape(experts, pairs, row_count, 8 * WIDTH), new_momentum)
 
 

time: 107 us -> 105 us (0.981)
  waiting for transfers between devices: 24.6 us -> 13.1 us
  starting transfers between devices: 35.2 us -> 45.2 us
    ppermute x23, waiting for transfers between devices: 24.6 us -> 13.1 us  [shift(): return lax.ppermute(value, 'replica', pairs)]
    ppermute x23, starting transfers between devices: 26.3 us -> 36.2 us  [shift(): return lax.ppermute(value, 'replica', pairs)]
  transfers between devices with their start and end apart: 25 -> 25, of which waited for: 11 -> 9; matrix products, arithmetic and copies ran while one was open for 1% -> 1% of each run, Pallas kernels for 16% -> 16%
where the time goes in v5:
time: 105 us
  starting transfers between devices  45.2 us (43%)
  blocking collectives  21.9 us (21%)
  Pallas kernels  18.3 us (17%)
  waiting for transfers between devices  13.1 us (12%)
  other arithmetic  3.37 us (3%)
  local copies, waits for them, and re-layouts  1.88 us (2%)
    ppermute x23, starting transfers between devices, shift(): return lax.ppermute(value, 'replica', pairs)  36.2 us
    all_to_all x1, blocking collectives, local(): lax.all_to_all(flat_rows, 'tensor', split_axis=0, concat_axis=0, tiled=True)  21.9 us
    ppermute x23, waiting for transfers between devices, shift(): return lax.ppermute(value, 'replica', pairs)  13.1 us
    all_to_all x2, starting transfers between devices, back(): lax.all_to_all(value, 'tensor', split_axis=0, concat_axis=0, tiled=True)  8.96 us
    pallas_call x1, Pallas kernels, chain(): pl.pallas_call(chain_kernel, out_shape=(jax.ShapeDtypeStruct((FF, FIRST),...  6.04 us
    pallas_call x6, Pallas kernels, place(): pl.pallas_call(functools.partial(place_kernel, where, int(aliased)), out_...  5.92 us
    pallas_call x1, Pallas kernels, early_products(): pl.pallas_call(own_kernel, out_shape=(out, pltpu.HBM((FF, FF), BF16)), in...  3.47 us
  transfers between devices with their start and end apart: 25, of which 9 were waited for; matrix products, arithmetic and copies ran while one was open for 1% of the time, Pallas kernels for 16%

profile of v5, /device:TPU:1, one launch (start us, length us, event | category | flops | bytes accessed | tf_op | source)
XLA Modules:
  0.0 104.6 jit_solution(16782637327416338502)
XLA Ops:
  0.6 2.0 %fusion.1 = bf16[8,2,48,512]{3,2,1,0:T(8,128)(2,1)S(1)} fusion(bf16[8,2,48,512]{3,2,1,0:T(8,128)(2,1)} %param.2, f32[8,2,48,512]{3,2,1,0:T(8,128)} %param.3), kind=kLoop, calls=%fused_computation.3 | loop fusion | flops 2359296 | bytes 3145728 | tf_op jit(solution)/shard_map/convert_element_type | solution.py:330
  2.6 21.9 %all_to_all.15 = bf16[16,48,512]{2,1,0:T(8,128)(2,1)S(1)} all-to-all(bf16[16,48,512]{2,1,0:T(8,128)(2,1)S(1)} %bitcast.8), channel_id=1, replica_groups=mesh['replica'=8,'tensor'=16] {'tensor'}, dimensions={0} | all-to-all | bytes 1572864 | tf_op jit(solution)/shard_map/all_to_all | solution.py:331
  24.5 0.6 shard_map.41
  25.2 1.9 %collective-permute-start = (bf16[768,256]{1,0:T(8,128)(2,1)S(1)}, bf16[768,256]{1,0:T(8,128)(2,1)S(1)}, u32[]{:S(2)}, u32[]{:S(2)}) collective-permute-start(bf16[768,256]{1,0:T(8,128)(2,1)S(1)} %get-tuple-element.28), channel_id=1, source_target_pairs={{0,16},{16,0},{32,48},{48,32},{64,80},{80,64},{96,112},{112,96},{1... | collective-permute-start | bytes 1179656 | tf_op jit(solution)/shard_map/ppermute | solution.py:46
  27.0 1.3 %collective-permute-done.got_ref = bf16[768,256]{1,0:T(8,128)(2,1)S(1)} collective-permute-done((bf16[768,256]{1,0:T(8,128)(2,1)S(1)}, bf16[768,256]{1,0:T(8,128)(2,1)S(1)}, u32[]{:S(2)}, u32[]{:S(2)}) %collective-permute-start) | collective-permute-done | bytes 393248 | tf_op jit(solution)/shard_map/ppermute | solution.py:46
  28.5 1.3 %collective-permute-start.1 = (bf16[192,256]{1,0:T(8,128)(2,1)S(1)}, bf16[192,256]{1,0:T(8,128)(2,1)S(1)}, u32[]{:S(2)}, u32[]{:S(2)}) collective-permute-start(bf16[192,256]{1,0:T(8,128)(2,1)S(1)} %get-tuple-element.30), channel_id=1, source_target_pairs={{0,32},{16,48},{32,64},{48,80},{64,96},{80,112},{96,0},{112,16},{1... | collective-permute-start | bytes 294920 | tf_op jit(solution)/shard_map/ppermute | solution.py:46
  29.7 1.5 %collective-permute-start.2 = (bf16[192,256]{1,0:T(8,128)(2,1)S(1)}, bf16[192,256]{1,0:T(8,128)(2,1)S(1)}, u32[]{:S(2)}, u32[]{:S(2)}) collective-permute-start(bf16[192,256]{1,0:T(8,128)(2,1)S(1)} %get-tuple-element.31), channel_id=1, source_target_pairs={{0,96},{16,112},{32,0},{48,16},{64,32},{80,48},{96,64},{112,80},{1... | collective-permute-start | bytes 294920 | tf_op jit(solution)/shard_map/ppermute | solution.py:46
  31.2 1.5 %collective-permute-start.3 = (bf16[192,256]{1,0:T(8,128)(2,1)S(1)}, bf16[192,256]{1,0:T(8,128)(2,1)S(1)}, u32[]{:S(2)}, u32[]{:S(2)}) collective-permute-start(bf16[192,256]{1,0:T(8,128)(2,1)S(1)} %get-tuple-element.32), channel_id=1, source_target_pairs={{0,64},{16,80},{32,96},{48,112},{64,0},{80,16},{96,32},{112,48},{1... | collective-permute-start | bytes 294920 | tf_op jit(solution)/shard_map/ppermute | solution.py:46
  32.7 1.0 collective-permute-done.1.a_ref
  33.7 2.5 %collective-permute-done.3.c_ref = bf16[192,256]{1,0:T(8,128)(2,1)S(1)} collective-permute-done((bf16[192,256]{1,0:T(8,128)(2,1)S(1)}, bf16[192,256]{1,0:T(8,128)(2,1)S(1)}, u32[]{:S(2)}, u32[]{:S(2)}) %collective-permute-start.3) | collective-permute-done | bytes 98336 | tf_op jit(solution)/shard_map/ppermute | solution.py:46
  36.3 1.3 %collective-permute-start.6 = (bf16[192,256]{1,0:T(8,128)(2,1)S(1)}, bf16[192,256]{1,0:T(8,128)(2,1)S(1)}, u32[]{:S(2)}, u32[]{:S(2)}) collective-permute-start(bf16[192,256]{1,0:T(8,128)(2,1)S(1)} %shard_map.43.refs_0_), channel_id=1, source_target_pairs={{0,32},{16,48},{32,64},{48,80},{64,96},{80,112},{96,0},{112,16},{1... | collective-permute-start | bytes 294920 | tf_op jit(solution)/shard_map/ppermute | solution.py:46
  37.6 1.5 %collective-permute-start.5 = (bf16[192,256]{1,0:T(8,128)(2,1)S(1)}, bf16[192,256]{1,0:T(8,128)(2,1)S(1)}, u32[]{:S(2)}, u32[]{:S(2)}) collective-permute-start(bf16[192,256]{1,0:T(8,128)(2,1)S(1)} %shard_map.43.refs_0_), channel_id=1, source_target_pairs={{0,64},{16,80},{32,96},{48,112},{64,0},{80,16},{96,32},{112,48},{1... | collective-permute-start | bytes 294920 | tf_op jit(solution)/shard_map/ppermute | solution.py:46
  39.1 1.0 collective-permute-start.4
  40.1 2.7 %collective-permute-start.7 = (bf16[192,256]{1,0:T(8,128)(2,1)S(1)}, bf16[192,256]{1,0:T(8,128)(2,1)S(1)}, u32[]{:S(2)}, u32[]{:S(2)}) collective-permute-start(bf16[192,256]{1,0:T(8,128)(2,1)S(1)} %shard_map.43.refs_0_), channel_id=1, source_target_pairs={{0,16},{16,0},{32,48},{48,32},{64,80},{80,64},{96,112},{112,96},{1... | collective-permute-start | bytes 294920 | tf_op jit(solution)/shard_map/ppermute | solution.py:46
  42.8 1.5 %collective-permute-start.10 = (bf16[192,256]{1,0:T(8,128)(2,1)S(1)}, bf16[192,256]{1,0:T(8,128)(2,1)S(1)}, u32[]{:S(2)}, u32[]{:S(2)}) collective-permute-start(bf16[192,256]{1,0:T(8,128)(2,1)S(1)} %collective-permute-done.6.refs_3_), channel_id=1, source_target_pairs={{0,16},{16,0},{32,48},{48,32},{64,80},{80,64},{96,112},{112,96},{1... | collective-permute-start | bytes 294920 | tf_op jit(solution)/shard_map/ppermute | solution.py:46
  44.4 1.1 %collective-permute-start.9 = (bf16[192,256]{1,0:T(8,128)(2,1)S(1)}, bf16[192,256]{1,0:T(8,128)(2,1)S(1)}, u32[]{:S(2)}, u32[]{:S(2)}) collective-permute-start(bf16[192,256]{1,0:T(8,128)(2,1)S(1)} %collective-permute-done.5.refs_2_), channel_id=1, source_target_pairs={{0,16},{16,0},{32,48},{48,32},{64,80},{80,64},{96,112},{112,96},{1... | collective-permute-start | bytes 294920 | tf_op jit(solution)/shard_map/ppermute | solution.py:46
  45.5 0.8 collective-permute-start.8
  46.3 0.8 collective-permute-start.12
  47.0 1.9 %collective-permute-start.11 = (bf16[768,256]{1,0:T(8,128)(2,1)S(1)}, bf16[768,256]{1,0:T(8,128)(2,1)S(1)}, u32[]{:S(2)}, u32[]{:S(2)}) collective-permute-start(bf16[768,256]{1,0:T(8,128)(2,1)S(1)} %get-tuple-element.41), channel_id=1, source_target_pairs={{0,96},{16,112},{32,0},{48,16},{64,32},{80,48},{96,64},{112,80},{1... | collective-permute-start | bytes 1179656 | tf_op jit(solution)/shard_map/ppermute | solution.py:46
  49.0 0.8 collective-permute-start.13
  49.8 6.0 %shard_map.44 = (bf16[768,256]{1,0:T(8,128)(2,1)}, bf16[2,768,768]{2,1,0:T(8,128)(2,1)}, f32[8,128]{1,0:T(8,128)S(1)}) custom-call(bf16[192,256]{1,0:T(8,128)(2,1)S(1)} %shard_map.43.refs_0_, bf16[192,256]{1,0:T(8,128)(2,1)S(1)} %collective-permute-done.4.refs_1_, bf16[192,256]{1,0:T(8,128)(2,1)S(1)} %collective-permute-done.5.refs_2_, ...), custom_call_target="tpu_custom_call" | custom-call | tf_op jit(solution)/shard_map/pallas_call | solution.py:192
  55.8 3.7 %all-to-all-start.1 = ((bf16[16,48,256]{2,1,0:T(8,128)(2,1)}), bf16[16,48,256]{2,1,0:T(8,128)(2,1)S(1)}, u32[]{:S(2)}, u32[]{:S(2)}) async-start(bf16[16,48,256]{2,1,0:T(8,128)(2,1)} %bitcast.2), calls=%async_computation.1 | async-start | bytes 786432 | tf_op jit(solution)/shard_map/all_to_all | solution.py:343
  59.6 1.7 %copy-done = bf16[2,768,768]{2,1,0:T(8,128)(2,1)S(1)} copy-done((bf16[2,768,768]{2,1,0:T(8,128)(2,1)S(1)}, bf16[2,768,768]{2,1,0:T(8,128)(2,1)}, u32[]{:S(2)}) %copy-start) | copy-done | bytes 2359320
  61.3 3.5 %shard_map.45 = (bf16[768,1024]{1,0:T(8,128)(2,1)}, bf16[768,768]{1,0:T(8,128)(2,1)}) custom-call(bf16[2,768,768]{2,1,0:T(8,128)(2,1)S(1)} %copy-done, f32[8,128]{1,0:T(8,128)S(1)} %get-tuple-element.36.scale_ref, bf16[768,256]{1,0:T(8,128)(2,1)S(1)} %get-tuple-element.39.early_in), custom_call_target="tpu_custom_call" | custom-call | flops 2113929216 | tf_op jit(solution)/shard_map/pallas_call | solution.py:258
  64.8 1.4 %convert_add_fusion.2 = f32[8,2,48,512]{3,2,1,0:T(8,128)} fusion(bf16[8,2,48,512]{3,2,1,0:T(8,128)(2,1)S(1)} %copy-done.3, f32[8,2,48,512]{3,2,1,0:T(8,128)S(1)} %copy-done.2), kind=kLoop, calls=%fused_computation.4 | loop fusion | flops 1179648 | bytes 3932160 | tf_op jit(solution)/shard_map/add | solution.py:326
  66.2 1.2 %collective-permute-done.13.refs_2_ = bf16[768,256]{1,0:T(8,128)(2,1)S(1)} collective-permute-done((bf16[768,256]{1,0:T(8,128)(2,1)S(1)}, bf16[768,256]{1,0:T(8,128)(2,1)S(1)}, u32[]{:S(2)}, u32[]{:S(2)}) %collective-permute-start.13) | collective-permute-done | bytes 393248 | tf_op jit(solution)/shard_map/ppermute | solution.py:46
  67.4 2.1 %shard_map.46 = bf16[768,1024]{1,0:T(8,128)(2,1)} custom-call(bf16[768,768]{1,0:T(8,128)(2,1)S(1)} %copy-done.1, f32[8,128]{1,0:T(8,128)S(1)} %get-tuple-element.36.scale_ref, bf16[768,256]{1,0:T(8,128)(2,1)S(1)} %collective-permute-done.11.refs_0_, bf16[768,256]{1,0:T(8,128)(2,1)S(1)} %collective-permute-done.12.refs_1_, ...), custom_call_target="tpu_custom_call", output_to_operand_aliasing={{}: (5, {})} | custom-call | flops 20000000000 | tf_op jit(solution)/shard_map/pallas_call | solution.py:273
  69.5 5.2 %all-to-all-start.2 = ((bf16[16,48,1024]{2,1,0:T(8,128)(2,1)}), bf16[16,48,1024]{2,1,0:T(8,128)(2,1)S(1)}, u32[]{:S(2)}, u32[]{:S(2)}) async-start(bf16[16,48,1024]{2,1,0:T(8,128)(2,1)} %bitcast.3), calls=%async_computation.2 | async-start | bytes 3145728 | tf_op jit(solution)/shard_map/all_to_all | solution.py:343
  74.7 0.8 collective-permute-start.16
  75.6 1.9 %collective-permute-start.15 = (bf16[16,48,256]{2,1,0:T(8,128)(2,1)S(1)}, bf16[16,48,256]{2,1,0:T(8,128)(2,1)S(1)}, u32[]{:S(2)}, u32[]{:S(2)}) collective-permute-start(bf16[16,48,256]{2,1,0:T(8,128)(2,1)S(1)} %all-to-all-done.1.refs_0_), channel_id=1, source_target_pairs={{0,96},{16,112},{32,0},{48,16},{64,32},{80,48},{96,64},{112,80},{1... | collective-permute-start | bytes 1179656 | tf_op jit(solution)/shard_map/ppermute | solution.py:46
  77.5 1.7 %collective-permute-start.17 = (bf16[16,48,256]{2,1,0:T(8,128)(2,1)S(1)}, bf16[16,48,256]{2,1,0:T(8,128)(2,1)S(1)}, u32[]{:S(2)}, u32[]{:S(2)}) collective-permute-start(bf16[16,48,256]{2,1,0:T(8,128)(2,1)S(1)} %all-to-all-done.1.refs_0_), channel_id=1, source_target_pairs={{0,16},{16,0},{32,48},{48,32},{64,80},{80,64},{96,112},{112,96},{1... | collective-permute-start | bytes 1179656 | tf_op jit(solution)/shard_map/ppermute | solution.py:46
  79.2 1.2 %collective-permute-start.14 = (bf16[16,48,256]{2,1,0:T(8,128)(2,1)S(1)}, bf16[16,48,256]{2,1,0:T(8,128)(2,1)S(1)}, u32[]{:S(2)}, u32[]{:S(2)}) collective-permute-start(bf16[16,48,256]{2,1,0:T(8,128)(2,1)S(1)} %all-to-all-done.1.refs_0_), channel_id=1, source_target_pairs={{0,64},{16,80},{32,96},{48,112},{64,0},{80,16},{96,32},{112,48},{1... | collective-permute-start | bytes 1179656 | tf_op jit(solution)/shard_map/ppermute | solution.py:46
  80.4 5.8 %collective-permute-done.16.refs_2_ = bf16[16,48,256]{2,1,0:T(8,128)(2,1)S(1)} collective-permute-done((bf16[16,48,256]{2,1,0:T(8,128)(2,1)S(1)}, bf16[16,48,256]{2,1,0:T(8,128)(2,1)S(1)}, u32[]{:S(2)}, u32[]{:S(2)}) %collective-permute-start.16) | collective-permute-done | bytes 393248 | tf_op jit(solution)/shard_map/ppermute | solution.py:46
  86.2 9.8 %collective-permute-start.20 = (bf16[16,48,256]{2,1,0:T(8,128)(2,1)S(1)}, bf16[16,48,256]{2,1,0:T(8,128)(2,1)S(1)}, u32[]{:S(2)}, u32[]{:S(2)}) collective-permute-start(bf16[16,48,256]{2,1,0:T(8,128)(2,1)S(1)} %collective-permute-done.16.refs_2_), channel_id=1, source_target_pairs={{0,16},{16,0},{32,48},{48,32},{64,80},{80,64},{96,112},{112,96},{1... | collective-permute-start | bytes 1179656 | tf_op jit(solution)/shard_map/ppermute | solution.py:46
  96.0 1.2 %shard_map.47.refs_3_ = bf16[16,48,4096]{2,1,0:T(8,128)(2,1)} custom-call(bf16[16,48,256]{2,1,0:T(8,128)(2,1)S(1)} %all-to-all-done.1.refs_0_, bf16[16,48,256]{2,1,0:T(8,128)(2,1)S(1)} %collective-permute-done.15.refs_1_, bf16[16,48,256]{2,1,0:T(8,128)(2,1)S(1)} %collective-permute-done.16.refs_2_, bf16[16,48,256]{2,1,0:T(8,128)(2,1)S(1)} %collective-permute-done.17.refs_3_), custom_call_target="tpu_custom_call" | custom-call | tf_op jit(solution)/shard_map/pallas_call | solution.py:312
  97.2 0.6 collective-permute-start.18
  97.8 0.1 collective-permute-done.19.refs_0_
  97.9 1.0 shard_map.48.refs_1_
  98.9 0.2 collective-permute-done.18.refs_0_
  99.1 0.8 shard_map.49.refs_4_
  99.9 0.2 fusion.2
  100.1 0.5 collective-permute-start.22
  100.5 0.1 collective-permute-start.21
  100.7 1.2 %shard_map.50.refs_2_ = bf16[16,48,4096]{2,1,0:T(8,128)(2,1)} custom-call(bf16[16,48,1024]{2,1,0:T(8,128)(2,1)S(1)} %all-to-all-done.2.refs_0_.refs_1_.refs_2_.refs_3_, bf16[16,48,1024]{2,1,0:T(8,128)(2,1)S(1)} %all-to-all-done.2.refs_0_.refs_1_.refs_2_.refs_3_, ...), custom_call_target="tpu_custom_call", output_to_operand_aliasing={{}: (4, {})} | custom-call | tf_op jit(solution)/shard_map/pallas_call | solution.py:312
  101.9 0.6 collective-permute-done.22.refs_0_.refs_1_
  102.5 0.9 shard_map.51.refs_2_
  103.4 0.2 collective-permute-done.21.refs_0_.refs_1_
  103.6 0.9 shard_map.52
  (26 shorter events, 0.2 us)
Async XLA Ops:
  25.2 3.2 %collective-permute-start = (bf16[768,256]{1,0:T(8,128)(2,1)S(1)}, bf16[768,256]{1,0:T(8,128)(2,1)S(1)}, u32[]{:S(2)}, u32[]{:S(2)}) collective-permute-start(bf16[768,256]{1,0:T(8,128)(2,1)S(1)} %get-tuple-element.28), channel_id=1, source_target_pairs={{0,16},{16,0},{32,48},{48,32},{64,80},{80,64},{96,112},{112,96},{1... | collective-permute-start | bytes 1179656 | tf_op jit(solution)/shard_map/ppermute | solution.py:46
  28.5 5.3 %collective-permute-start.1 = (bf16[192,256]{1,0:T(8,128)(2,1)S(1)}, bf16[192,256]{1,0:T(8,128)(2,1)S(1)}, u32[]{:S(2)}, u32[]{:S(2)}) collective-permute-start(bf16[192,256]{1,0:T(8,128)(2,1)S(1)} %get-tuple-element.30), channel_id=1, source_target_pairs={{0,32},{16,48},{32,64},{48,80},{64,96},{80,112},{96,0},{112,16},{1... | collective-permute-start | bytes 294920 | tf_op jit(solution)/shard_map/ppermute | solution.py:46
  29.7 4.0 %collective-permute-start.2 = (bf16[192,256]{1,0:T(8,128)(2,1)S(1)}, bf16[192,256]{1,0:T(8,128)(2,1)S(1)}, u32[]{:S(2)}, u32[]{:S(2)}) collective-permute-start(bf16[192,256]{1,0:T(8,128)(2,1)S(1)} %get-tuple-element.31), channel_id=1, source_target_pairs={{0,96},{16,112},{32,0},{48,16},{64,32},{80,48},{96,64},{112,80},{1... | collective-permute-start | bytes 294920 | tf_op jit(solution)/shard_map/ppermute | solution.py:46
  31.2 5.1 %collective-permute-start.3 = (bf16[192,256]{1,0:T(8,128)(2,1)S(1)}, bf16[192,256]{1,0:T(8,128)(2,1)S(1)}, u32[]{:S(2)}, u32[]{:S(2)}) collective-permute-start(bf16[192,256]{1,0:T(8,128)(2,1)S(1)} %get-tuple-element.32), channel_id=1, source_target_pairs={{0,64},{16,80},{32,96},{48,112},{64,0},{80,16},{96,32},{112,48},{1... | collective-permute-start | bytes 294920 | tf_op jit(solution)/shard_map/ppermute | solution.py:46
  36.3 6.5 %collective-permute-start.6 = (bf16[192,256]{1,0:T(8,128)(2,1)S(1)}, bf16[192,256]{1,0:T(8,128)(2,1)S(1)}, u32[]{:S(2)}, u32[]{:S(2)}) collective-permute-start(bf16[192,256]{1,0:T(8,128)(2,1)S(1)} %shard_map.43.refs_0_), channel_id=1, source_target_pairs={{0,32},{16,48},{32,64},{48,80},{64,96},{80,112},{96,0},{112,16},{1... | collective-permute-start | bytes 294920 | tf_op jit(solution)/shard_map/ppermute | solution.py:46
  37.6 6.7 %collective-permute-start.5 = (bf16[192,256]{1,0:T(8,128)(2,1)S(1)}, bf16[192,256]{1,0:T(8,128)(2,1)S(1)}, u32[]{:S(2)}, u32[]{:S(2)}) collective-permute-start(bf16[192,256]{1,0:T(8,128)(2,1)S(1)} %shard_map.43.refs_0_), channel_id=1, source_target_pairs={{0,64},{16,80},{32,96},{48,112},{64,0},{80,16},{96,32},{112,48},{1... | collective-permute-start | bytes 294920 | tf_op jit(solution)/shard_map/ppermute | solution.py:46
  39.1 6.4 %collective-permute-start.4 = (bf16[192,256]{1,0:T(8,128)(2,1)S(1)}, bf16[192,256]{1,0:T(8,128)(2,1)S(1)}, u32[]{:S(2)}, u32[]{:S(2)}) collective-permute-start(bf16[192,256]{1,0:T(8,128)(2,1)S(1)} %shard_map.43.refs_0_), channel_id=1, source_target_pairs={{0,96},{16,112},{32,0},{48,16},{64,32},{80,48},{96,64},{112,80},{1... | collective-permute-start | bytes 294920 | tf_op jit(solution)/shard_map/ppermute | solution.py:46
  40.1 6.9 %collective-permute-start.7 = (bf16[192,256]{1,0:T(8,128)(2,1)S(1)}, bf16[192,256]{1,0:T(8,128)(2,1)S(1)}, u32[]{:S(2)}, u32[]{:S(2)}) collective-permute-start(bf16[192,256]{1,0:T(8,128)(2,1)S(1)} %shard_map.43.refs_0_), channel_id=1, source_target_pairs={{0,16},{16,0},{32,48},{48,32},{64,80},{80,64},{96,112},{112,96},{1... | collective-permute-start | bytes 294920 | tf_op jit(solution)/shard_map/ppermute | solution.py:46
  42.8 6.1 %collective-permute-start.10 = (bf16[192,256]{1,0:T(8,128)(2,1)S(1)}, bf16[192,256]{1,0:T(8,128)(2,1)S(1)}, u32[]{:S(2)}, u32[]{:S(2)}) collective-permute-start(bf16[192,256]{1,0:T(8,128)(2,1)S(1)} %collective-permute-done.6.refs_3_), channel_id=1, source_target_pairs={{0,16},{16,0},{32,48},{48,32},{64,80},{80,64},{96,112},{112,96},{1... | collective-permute-start | bytes 294920 | tf_op jit(solution)/shard_map/ppermute | solution.py:46
  44.4 5.4 %collective-permute-start.9 = (bf16[192,256]{1,0:T(8,128)(2,1)S(1)}, bf16[192,256]{1,0:T(8,128)(2,1)S(1)}, u32[]{:S(2)}, u32[]{:S(2)}) collective-permute-start(bf16[192,256]{1,0:T(8,128)(2,1)S(1)} %collective-permute-done.5.refs_2_), channel_id=1, source_target_pairs={{0,16},{16,0},{32,48},{48,32},{64,80},{80,64},{96,112},{112,96},{1... | collective-permute-start | bytes 294920 | tf_op jit(solution)/shard_map/ppermute | solution.py:46
  45.5 4.3 %collective-permute-start.8 = (bf16[192,256]{1,0:T(8,128)(2,1)S(1)}, bf16[192,256]{1,0:T(8,128)(2,1)S(1)}, u32[]{:S(2)}, u32[]{:S(2)}) collective-permute-start(bf16[192,256]{1,0:T(8,128)(2,1)S(1)} %collective-permute-done.4.refs_1_), channel_id=1, source_target_pairs={{0,16},{16,0},{32,48},{48,32},{64,80},{80,64},{96,112},{112,96},{1... | collective-permute-start | bytes 294920 | tf_op jit(solution)/shard_map/ppermute | solution.py:46
  46.3 21.1 %collective-permute-start.12 = (bf16[768,256]{1,0:T(8,128)(2,1)S(1)}, bf16[768,256]{1,0:T(8,128)(2,1)S(1)}, u32[]{:S(2)}, u32[]{:S(2)}) collective-permute-start(bf16[768,256]{1,0:T(8,128)(2,1)S(1)} %get-tuple-element.41), channel_id=1, source_target_pairs={{0,32},{16,48},{32,64},{48,80},{64,96},{80,112},{96,0},{112,16},{1... | collective-permute-start | bytes 1179656 | tf_op jit(solution)/shard_map/ppermute | solution.py:46
  47.0 20.4 %collective-permute-start.11 = (bf16[768,256]{1,0:T(8,128)(2,1)S(1)}, bf16[768,256]{1,0:T(8,128)(2,1)S(1)}, u32[]{:S(2)}, u32[]{:S(2)}) collective-permute-start(bf16[768,256]{1,0:T(8,128)(2,1)S(1)} %get-tuple-element.41), channel_id=1, source_target_pairs={{0,96},{16,112},{32,0},{48,16},{64,32},{80,48},{96,64},{112,80},{1... | collective-permute-start | bytes 1179656 | tf_op jit(solution)/shard_map/ppermute | solution.py:46
  49.0 18.4 %collective-permute-start.13 = (bf16[768,256]{1,0:T(8,128)(2,1)S(1)}, bf16[768,256]{1,0:T(8,128)(2,1)S(1)}, u32[]{:S(2)}, u32[]{:S(2)}) collective-permute-start(bf16[768,256]{1,0:T(8,128)(2,1)S(1)} %get-tuple-element.39.early_in), channel_id=1, source_target_pairs={{0,64},{16,80},{32,96},{48,112},{64,0},{80,16},{96,32},{112,48},{1... | collective-permute-start | bytes 1179656 | tf_op jit(solution)/shard_map/ppermute | solution.py:46
  55.8 13.7 %all-to-all-start.1 = ((bf16[16,48,256]{2,1,0:T(8,128)(2,1)}), bf16[16,48,256]{2,1,0:T(8,128)(2,1)S(1)}, u32[]{:S(2)}, u32[]{:S(2)}) async-start(bf16[16,48,256]{2,1,0:T(8,128)(2,1)} %bitcast.2), calls=%async_computation.1 | async-start | bytes 786432 | tf_op jit(solution)/shard_map/all_to_all | solution.py:343
  59.6 1.7 %copy-start = (bf16[2,768,768]{2,1,0:T(8,128)(2,1)S(1)}, bf16[2,768,768]{2,1,0:T(8,128)(2,1)}, u32[]{:S(2)}) copy-start(bf16[2,768,768]{2,1,0:T(8,128)(2,1)} %get-tuple-element.35.polys_in) | copy-start | bytes 7077892
  61.3 3.5 %copy-start.2 = (f32[8,2,48,512]{3,2,1,0:T(8,128)S(1)}, f32[8,2,48,512]{3,2,1,0:T(8,128)}, u32[]{:S(2)}) copy-start(f32[8,2,48,512]{3,2,1,0:T(8,128)} %param.3) | copy-start | bytes 4718596
  61.3 3.5 %copy-start.3 = (bf16[8,2,48,512]{3,2,1,0:T(8,128)(2,1)S(1)}, bf16[8,2,48,512]{3,2,1,0:T(8,128)(2,1)}, u32[]{:S(2)}) copy-start(bf16[8,2,48,512]{3,2,1,0:T(8,128)(2,1)} %param.2) | copy-start | bytes 2359300
  64.8 2.6 %copy-start.1 = (bf16[768,768]{1,0:T(8,128)(2,1)S(1)}, bf16[768,768]{1,0:T(8,128)(2,1)}, u32[]{:S(2)}) copy-start(bf16[768,768]{1,0:T(8,128)(2,1)} %get-tuple-element.40.square_ref) | copy-start | bytes 3538948
  69.5 30.4 %all-to-all-start.2 = ((bf16[16,48,1024]{2,1,0:T(8,128)(2,1)}), bf16[16,48,1024]{2,1,0:T(8,128)(2,1)S(1)}, u32[]{:S(2)}, u32[]{:S(2)}) async-start(bf16[16,48,1024]{2,1,0:T(8,128)(2,1)} %bitcast.3), calls=%async_computation.2 | async-start | bytes 3145728 | tf_op jit(solution)/shard_map/all_to_all | solution.py:343
  74.7 11.4 %collective-permute-start.16 = (bf16[16,48,256]{2,1,0:T(8,128)(2,1)S(1)}, bf16[16,48,256]{2,1,0:T(8,128)(2,1)S(1)}, u32[]{:S(2)}, u32[]{:S(2)}) collective-permute-start(bf16[16,48,256]{2,1,0:T(8,128)(2,1)S(1)} %all-to-all-done.1.refs_0_), channel_id=1, source_target_pairs={{0,32},{16,48},{32,64},{48,80},{64,96},{80,112},{96,0},{112,16},{1... | collective-permute-start | bytes 1179656 | tf_op jit(solution)/shard_map/ppermute | solution.py:46
  75.6 20.4 %collective-permute-start.15 = (bf16[16,48,256]{2,1,0:T(8,128)(2,1)S(1)}, bf16[16,48,256]{2,1,0:T(8,128)(2,1)S(1)}, u32[]{:S(2)}, u32[]{:S(2)}) collective-permute-start(bf16[16,48,256]{2,1,0:T(8,128)(2,1)S(1)} %all-to-all-done.1.refs_0_), channel_id=1, source_target_pairs={{0,96},{16,112},{32,0},{48,16},{64,32},{80,48},{96,64},{112,80},{1... | collective-permute-start | bytes 1179656 | tf_op jit(solution)/shard_map/ppermute | solution.py:46
  77.5 18.5 %collective-permute-start.17 = (bf16[16,48,256]{2,1,0:T(8,128)(2,1)S(1)}, bf16[16,48,256]{2,1,0:T(8,128)(2,1)S(1)}, u32[]{:S(2)}, u32[]{:S(2)}) collective-permute-start(bf16[16,48,256]{2,1,0:T(8,128)(2,1)S(1)} %all-to-all-done.1.refs_0_), channel_id=1, source_target_pairs={{0,16},{16,0},{32,48},{48,32},{64,80},{80,64},{96,112},{112,96},{1... | collective-permute-start | bytes 1179656 | tf_op jit(solution)/shard_map/ppermute | solution.py:46
  79.2 18.0 %collective-permute-start.14 = (bf16[16,48,256]{2,1,0:T(8,128)(2,1)S(1)}, bf16[16,48,256]{2,1,0:T(8,128)(2,1)S(1)}, u32[]{:S(2)}, u32[]{:S(2)}) collective-permute-start(bf16[16,48,256]{2,1,0:T(8,128)(2,1)S(1)} %all-to-all-done.1.refs_0_), channel_id=1, source_target_pairs={{0,64},{16,80},{32,96},{48,112},{64,0},{80,16},{96,32},{112,48},{1... | collective-permute-start | bytes 1179656 | tf_op jit(solution)/shard_map/ppermute | solution.py:46
  86.2 11.6 %collective-permute-start.20 = (bf16[16,48,256]{2,1,0:T(8,128)(2,1)S(1)}, bf16[16,48,256]{2,1,0:T(8,128)(2,1)S(1)}, u32[]{:S(2)}, u32[]{:S(2)}) collective-permute-start(bf16[16,48,256]{2,1,0:T(8,128)(2,1)S(1)} %collective-permute-done.16.refs_2_), channel_id=1, source_target_pairs={{0,16},{16,0},{32,48},{48,32},{64,80},{80,64},{96,112},{112,96},{1... | collective-permute-start | bytes 1179656 | tf_op jit(solution)/shard_map/ppermute | solution.py:46
  96.0 1.9 %collective-permute-start.19 = (bf16[16,48,256]{2,1,0:T(8,128)(2,1)S(1)}, bf16[16,48,256]{2,1,0:T(8,128)(2,1)S(1)}, u32[]{:S(2)}, u32[]{:S(2)}) collective-permute-start(bf16[16,48,256]{2,1,0:T(8,128)(2,1)S(1)} %collective-permute-done.15.refs_1_), channel_id=1, source_target_pairs={{0,16},{16,0},{32,48},{48,32},{64,80},{80,64},{96,112},{112,96},{1... | collective-permute-start | bytes 1179656 | tf_op jit(solution)/shard_map/ppermute | solution.py:46
  97.2 1.9 %collective-permute-start.18 = (bf16[16,48,256]{2,1,0:T(8,128)(2,1)S(1)}, bf16[16,48,256]{2,1,0:T(8,128)(2,1)S(1)}, u32[]{:S(2)}, u32[]{:S(2)}) collective-permute-start(bf16[16,48,256]{2,1,0:T(8,128)(2,1)S(1)} %collective-permute-done.14.refs_2_), channel_id=1, source_target_pairs={{0,16},{16,0},{32,48},{48,32},{64,80},{80,64},{96,112},{112,96},{1... | collective-permute-start | bytes 1179656 | tf_op jit(solution)/shard_map/ppermute | solution.py:46
  100.1 2.4 %collective-permute-start.22 = (bf16[16,48,512]{2,1,0:T(8,128)(2,1)S(1)}, bf16[16,48,512]{2,1,0:T(8,128)(2,1)S(1)}, u32[]{:S(2)}, u32[]{:S(2)}) collective-permute-start(bf16[16,48,512]{2,1,0:T(8,128)(2,1)S(1)} %get-tuple-element.52), channel_id=1, source_target_pairs={{0,16},{16,0},{32,48},{48,32},{64,80},{80,64},{96,112},{112,96},{1... | collective-permute-start | bytes 2359304 | tf_op jit(solution)/shard_map/ppermute | solution.py:46
  100.5 3.0 %collective-permute-start.21 = (bf16[16,48,512]{2,1,0:T(8,128)(2,1)S(1)}, bf16[16,48,512]{2,1,0:T(8,128)(2,1)S(1)}, u32[]{:S(2)}, u32[]{:S(2)}) collective-permute-start(bf16[16,48,512]{2,1,0:T(8,128)(2,1)S(1)} %get-tuple-element.53), channel_id=1, source_target_pairs={{0,16},{16,0},{32,48},{48,32},{64,80},{80,64},{96,112},{112,96},{1... | collective-permute-start | bytes 2359304 | tf_op jit(solution)/shard_map/ppermute | solution.py:46

commit v6 on v5

--- a/solution.py
+++ b/solution.py
@@ -133,14 +133,18 @@
 
 
 def chain_kernel(*refs):
-    pieces, rows_ref = refs[:8], refs[8]
-    out_ref, polys_out, scale_ref, packed, gram, polys, late, sems = refs[9:]
+    pieces, rows_ref = refs[:6], refs[6]
+    out_ref, polys_out, scale_ref, packed, gram, polys, late, sems = refs[7:]
     index = lax.axis_index("replica")
     chip, core = index // 2, index % 2
     for steps in range(4):
         start = pl.multiple_of(((chip + steps) % 4) * PIECE, PIECE)
         packed[core, pl.ds(start, PIECE), :] = pieces[steps][...]
-        packed[1 - core, pl.ds(start, PIECE), :] = pieces[4 + steps][...]
+        if steps == 0:
+            packed[1 - core, pl.ds(start, PIECE), :] = pieces[4][...]
+        else:
+            where = pl.ds((steps - 1) * PIECE, PIECE)
+            packed[1 - core, pl.ds(start, PIECE), :] = pieces[5][where, :]
     row_id = lax.broadcasted_iota(jnp.int32, (BLOCK, BLOCK), 0)
     col_id = lax.broadcasted_iota(jnp.int32, (BLOCK, BLOCK), 1)
     diagonal = row_id == col_id
@@ -159,31 +163,30 @@
         if row != col:
             gram[pl.ds(col * BLOCK, BLOCK), pl.ds(row * BLOCK, BLOCK)] = scaled.T.astype(BF16)
 
-    def keep(value, place):
-        polys[place] = value
-        copy = pltpu.make_async_copy(polys.at[place], polys_out.at[place], sems.at[place])
-        copy.start()
-        return copy
-
     scale_ref[...] = jnp.broadcast_to(scale, scale_ref.shape)
     gram_0 = gram[...]
     poly_0 = (coef_gram * gram_0.astype(F32) + coef_square * dot(gram_0, gram_0)).astype(BF16)
-    copies = [keep(poly_0, 0)]
+    polys[0] = poly_0
+    copies = [pltpu.make_async_copy(polys.at[0], polys_out.at[0], sems.at[0])]
+    copies[0].start()
+    rows = rows_ref[:, :FIRST]
+    first = ((coef_linear * rows.astype(F32) + dot(poly_0, rows)) * scale).astype(BF16)
     half_way = (coef_linear * gram_0.astype(F32) + dot(poly_0, gram_0)).astype(BF16)
     gram_1 = (coef_linear * half_way.astype(F32) + dot(half_way, poly_0)).astype(BF16)
-    poly_1 = (coef_gram * gram_1.astype(F32) + coef_square * dot(gram_1, gram_1)).astype(BF16)
-    copies.append(keep(poly_1, 1))
-    rows = rows_ref[:, :FIRST]
-    first = ((coef_linear * rows.astype(F32) + dot(poly_0, rows)) * scale).astype(BF16)
     for block in range(FF // BLOCK):
         where = pl.ds(block * BLOCK, BLOCK)
         cut = slice(block * BLOCK, (block + 1) * BLOCK)
-        second = coef_linear * first[cut].astype(F32) + dot(poly_1[cut], first)
+        square = dot(gram_1[cut], gram_1)
+        poly_1 = (coef_gram * gram_1[cut].astype(F32) + coef_square * square).astype(BF16)
+        polys[1, where, :] = poly_1
+        second = coef_linear * first[cut].astype(F32) + dot(poly_1, first)
         late[where, :] = (scale_factor * second).astype(BF16)
-        copies.append(
-            pltpu.make_async_copy(late.at[where, :], out_ref.at[where, :], sems.at[2 + block])
-        )
-        copies[-1].start()
+        for source, target, number in (
+            (polys.at[1, where, :], polys_out.at[1, where, :], 1 + 2 * block),
+            (late.at[where, :], out_ref.at[where, :], 2 + 2 * block),
+        ):
+            copies.append(pltpu.make_async_copy(source, target, sems.at[number]))
+            copies[-1].start()
     for copy in copies:
         copy.wait()
 
@@ -196,14 +199,14 @@
             pltpu.HBM((2, FF, FF), BF16),
             jax.ShapeDtypeStruct((8, 128), F32),
         ),
-        in_specs=[VMEM] * 9,
+        in_specs=[VMEM] * 7,
         out_specs=(HBM, HBM, VMEM),
         scratch_shapes=[
             pltpu.VMEM((2, HALF, BLOCK), BF16),
             pltpu.VMEM((FF, FF), BF16),
             pltpu.VMEM((2, FF, FF), BF16),
             pltpu.VMEM((FF, FIRST), BF16),
-            pltpu.SemaphoreType.DMA((5,)),
+            pltpu.SemaphoreType.DMA((7,)),
         ],
         cost_estimate=pl.CostEstimate(flops=0, bytes_accessed=0, transcendentals=0),
         compiler_params=LARGE,
@@ -215,22 +218,13 @@
     return ((scale_factor * scale) * total).astype(BF16)
 
 
-def own_kernel(polys_in, scale_ref, early_in, out_ref, square_out, polys, early, square, result, sems):
-    loads = [pltpu.make_async_copy(polys_in.at[i], polys.at[i], sems.at[i]) for i in range(2)]
-    loads.append(pltpu.make_async_copy(early_in, early, sems.at[2]))
-    for load in loads:
-        load.start()
-    for load in loads:
-        load.wait()
-    sums = polys[0].astype(F32) + polys[1].astype(F32)
-    square[...] = (coef_linear * sums + dot(polys[1], polys[0])).astype(BF16)
-    stores = [pltpu.make_async_copy(square, square_out, sems.at[3])]
-    stores[0].start()
-    result[...] = both_steps_at_once(square[...], scale_ref[:1, :1], early[...])
-    stores.append(pltpu.make_async_copy(result, out_ref.at[:, pl.ds(0, EARLY)], sems.at[4]))
-    stores[1].start()
-    for store in stores:
-        store.wait()
+def own_kernel(polys_ref, scale_ref, early_ref, out_ref, square_ref, result, sems):
+    sums = polys_ref[0].astype(F32) + polys_ref[1].astype(F32)
+    square_ref[...] = (coef_linear * sums + dot(polys_ref[1], polys_ref[0])).astype(BF16)
+    result[...] = both_steps_at_once(square_ref[...], scale_ref[:1, :1], early_ref[...])
+    store = pltpu.make_async_copy(result, out_ref.at[:, pl.ds(0, EARLY)], sems.at[0])
+    store.start()
+    store.wait()
 
 
 ORDER = 20_000_000_000
@@ -257,18 +251,12 @@
     flops = 2 * FF * FF * EARLY
     result, square = pl.pallas_call(
         own_kernel,
-        out_shape=(out, pltpu.HBM((FF, FF), BF16)),
-        in_specs=[HBM, VMEM, HBM],
-        out_specs=(HBM, HBM),
-        scratch_shapes=[
-            pltpu.VMEM((2, FF, FF), BF16),
-            pltpu.VMEM((FF, EARLY), BF16),
-            pltpu.VMEM((FF, FF), BF16),
-            pltpu.VMEM((FF, EARLY), BF16),
-            pltpu.SemaphoreType.DMA((5,)),
-        ],
-        cost_estimate=pl.CostEstimate(flops=7 * flops, bytes_accessed=0, transcendentals=0),
-        compiler_params=LARGE,
+        out_shape=(out, jax.ShapeDtypeStruct((FF, FF), BF16)),
+        in_specs=[VMEM] * 3,
+        out_specs=(HBM, VMEM),
+        scratch_shapes=[pltpu.VMEM((FF, EARLY), BF16), pltpu.SemaphoreType.DMA((1,))],
+        cost_estimate=pl.CostEstimate(flops=0, bytes_accessed=0, transcendentals=0),
+        compiler_params=PARAMS,
     )(polys, scale, early[0])
     return pl.pallas_call(
         other_kernel,
@@ -312,7 +300,7 @@
     return pl.pallas_call(
         functools.partial(place_kernel, where, int(aliased)),
         out_shape=jax.ShapeDtypeStruct(shape, BF16),
-        in_specs=[anywhere] * (len(arrays) + aliased),
+        in_specs=[VMEM] * len(arrays) + [anywhere] * aliased,
         out_specs=anywhere,
         scratch_shapes=[pltpu.SemaphoreType.DMA((len(arrays),))],
         input_output_aliases={len(arrays): 0} if aliased else {},
@@ -335,19 +323,19 @@
     own, to_next, to_last, to_far = chip_sum(keep, shift(send, 0, 1))
     mine = ring_sum(own, shift(to_next, 1), shift(to_last, -1), shift(to_far, 2))
     here = (mine, shift(mine, -1), shift(mine, 2), shift(mine, 1))
-    other = tuple(shift(piece, 0, 1) for piece in here)
-    late_rows, polys, scale = chain(here + other, rows)
+    other = shift(jnp.concatenate(here[1:]), 0, 1)
+    late_rows, polys, scale = chain((*here, shift(mine, 0, 1), other), rows)
 
     def back(value):
         value = value.reshape(experts * pairs, row_count, value.shape[1])
         return lax.all_to_all(value, "tensor", split_axis=0, concat_axis=0, tiled=True)
 
-    gradient, momentum, late_rows = lax.optimization_barrier((gradient, momentum, late_rows))
-    new_momentum = stepped(gradient, momentum)
     near, far, _ = lax.optimization_barrier((near, far, here[2]))
     early_rows = early_products(polys, scale, (far, shift(near, -1), shift(near, 1), shift(far, 2)))
     late = back(late_rows)
-    late, early_rows, new_momentum = lax.optimization_barrier((late, early_rows, new_momentum))
+    late, early_rows = lax.optimization_barrier((late, early_rows))
+    gradient, momentum, _ = lax.optimization_barrier((gradient, momentum, late))
+    new_momentum = stepped(gradient, momentum)
     cut = late[:, :, :LATE]
     late_pieces = {0: late, 1: shift(cut, -1), 3: shift(cut, 1), 2: shift(late, 2)}
     widths = {0: FIRST, 1: LATE, 3: LATE, 2: FIRST}
@@ -373,7 +361,7 @@
     late_across[2] = shift(late_pieces[2], 0, 1)
     update = place(update, shape, [late_place(late_across, steps, 1) for steps in (1, 3)] + [late_place(late_pieces, 2, 0)])
     update = place(update, shape, [late_place(late_across, steps, 1) for steps in (2,)])
-    second, update = lax.optimization_barrier((second, update))
+    second, update, new_momentum = lax.optimization_barrier((second, update, new_momentum))
     update = place(update, shape, early_places(second, 0, 0, SECOND))
     middle = EARLY + NEAR
     for left, right in ((0, middle), (middle, SECOND)):

time: 105 us -> 104 us (level)
  starting transfers between devices: 45.2 us -> 40.1 us
  waiting for transfers between devices: 13.1 us -> 18.1 us
  Pallas kernels: 18.3 us -> 16.8 us
    ppermute x23 -> x21, starting transfers between devices: 36.2 us -> 32.6 us  [shift(): return lax.ppermute(value, 'replica', pairs)]
    all_to_all x2, waiting for transfers between devices: 0.01 us -> 3.08 us  [back(): lax.all_to_all(value, 'tensor', split_axis=0, concat_axis=0, tiled=True)]
    ppermute x23 -> x21, waiting for transfers between devices: 13.1 us -> 15 us  [shift(): return lax.ppermute(value, 'replica', pairs)]
    all_to_all x2, starting transfers between devices: 8.96 us -> 7.45 us  [back(): lax.all_to_all(value, 'tensor', split_axis=0, concat_axis=0, tiled=True)]
  transfers between devices with their start and end apart: 25 -> 23, of which waited for: 9 -> 11; matrix products, arithmetic and copies ran while one was open for 1% -> 1% of each run, Pallas kernels for 16% -> 15%
where the time goes in v6:
time: 104 us; the launch traced here: 103 us
  starting transfers between devices  40.1 us (39%)
  blocking collectives  21.9 us (21%)
  waiting for transfers between devices  18.1 us (17%)
  Pallas kernels  16.8 us (16%)
  other arithmetic  3.4 us (3%)
  local copies, waits for them, and re-layouts  1.88 us (2%)
    ppermute x21, starting transfers between devices, shift(): return lax.ppermute(value, 'replica', pairs)  32.6 us
    all_to_all x1, blocking collectives, local(): lax.all_to_all(flat_rows, 'tensor', split_axis=0, concat_axis=0, tiled=True)  21.9 us
    ppermute x21, waiting for transfers between devices, shift(): return lax.ppermute(value, 'replica', pairs)  15 us
    all_to_all x2, starting transfers between devices, back(): lax.all_to_all(value, 'tensor', split_axis=0, concat_axis=0, tiled=True)  7.45 us
    pallas_call x6, Pallas kernels, place(): pl.pallas_call(functools.partial(place_kernel, where, int(aliased)), out_...  5.93 us
    pallas_call x1, Pallas kernels, chain(): pl.pallas_call(chain_kernel, out_shape=(jax.ShapeDtypeStruct((FF, FIRST),...  5.6 us
    all_to_all x2, waiting for transfers between devices, back(): lax.all_to_all(value, 'tensor', split_axis=0, concat_axis=0, tiled=True)  3.08 us
    pallas_call x1, Pallas kernels, early_products(): pl.pallas_call(own_kernel, out_shape=(out, jax.ShapeDtypeStruct((FF, FF),...  2.44 us
  transfers between devices with their start and end apart: 23, of which 11 were waited for; matrix products, arithmetic and copies ran while one was open for 1% of the time, Pallas kernels for 15%

profile of v6, /device:TPU:1, one launch (start us, length us, event | category | flops | bytes accessed | tf_op | source)
XLA Modules:
  0.0 103.2 jit_solution(2218356097506240275)
XLA Ops:
  0.6 2.0 %fusion.1 = bf16[8,2,48,512]{3,2,1,0:T(8,128)(2,1)S(1)} fusion(bf16[8,2,48,512]{3,2,1,0:T(8,128)(2,1)} %param.2, f32[8,2,48,512]{3,2,1,0:T(8,128)} %param.3), kind=kLoop, calls=%fused_computation.3 | loop fusion | flops 2359296 | bytes 3145728 | tf_op jit(solution)/shard_map/convert_element_type | solution.py:318
  2.6 21.9 %all_to_all.15 = bf16[16,48,512]{2,1,0:T(8,128)(2,1)S(1)} all-to-all(bf16[16,48,512]{2,1,0:T(8,128)(2,1)S(1)} %bitcast.8), channel_id=1, replica_groups=mesh['replica'=8,'tensor'=16] {'tensor'}, dimensions={0} | all-to-all | bytes 1572864 | tf_op jit(solution)/shard_map/all_to_all | solution.py:319
  24.5 0.7 shard_map.41
  25.2 1.9 %collective-permute-start = (bf16[768,256]{1,0:T(8,128)(2,1)S(1)}, bf16[768,256]{1,0:T(8,128)(2,1)S(1)}, u32[]{:S(2)}, u32[]{:S(2)}) collective-permute-start(bf16[768,256]{1,0:T(8,128)(2,1)S(1)} %get-tuple-element.27), channel_id=1, source_target_pairs={{0,16},{16,0},{32,48},{48,32},{64,80},{80,64},{96,112},{112,96},{1... | collective-permute-start | bytes 1179656 | tf_op jit(solution)/shard_map/ppermute | solution.py:46
  27.0 1.3 %collective-permute-done.got_ref = bf16[768,256]{1,0:T(8,128)(2,1)S(1)} collective-permute-done((bf16[768,256]{1,0:T(8,128)(2,1)S(1)}, bf16[768,256]{1,0:T(8,128)(2,1)S(1)}, u32[]{:S(2)}, u32[]{:S(2)}) %collective-permute-start) | collective-permute-done | bytes 393248 | tf_op jit(solution)/shard_map/ppermute | solution.py:46
  28.5 1.3 %collective-permute-start.1 = (bf16[192,256]{1,0:T(8,128)(2,1)S(1)}, bf16[192,256]{1,0:T(8,128)(2,1)S(1)}, u32[]{:S(2)}, u32[]{:S(2)}) collective-permute-start(bf16[192,256]{1,0:T(8,128)(2,1)S(1)} %get-tuple-element.29), channel_id=1, source_target_pairs={{0,32},{16,48},{32,64},{48,80},{64,96},{80,112},{96,0},{112,16},{1... | collective-permute-start | bytes 294920 | tf_op jit(solution)/shard_map/ppermute | solution.py:46
  29.7 1.5 %collective-permute-start.2 = (bf16[192,256]{1,0:T(8,128)(2,1)S(1)}, bf16[192,256]{1,0:T(8,128)(2,1)S(1)}, u32[]{:S(2)}, u32[]{:S(2)}) collective-permute-start(bf16[192,256]{1,0:T(8,128)(2,1)S(1)} %get-tuple-element.30), channel_id=1, source_target_pairs={{0,96},{16,112},{32,0},{48,16},{64,32},{80,48},{96,64},{112,80},{1... | collective-permute-start | bytes 294920 | tf_op jit(solution)/shard_map/ppermute | solution.py:46
  31.2 1.5 %collective-permute-start.3 = (bf16[192,256]{1,0:T(8,128)(2,1)S(1)}, bf16[192,256]{1,0:T(8,128)(2,1)S(1)}, u32[]{:S(2)}, u32[]{:S(2)}) collective-permute-start(bf16[192,256]{1,0:T(8,128)(2,1)S(1)} %get-tuple-element.31), channel_id=1, source_target_pairs={{0,64},{16,80},{32,96},{48,112},{64,0},{80,16},{96,32},{112,48},{1... | collective-permute-start | bytes 294920 | tf_op jit(solution)/shard_map/ppermute | solution.py:46
  32.7 1.0 collective-permute-done.1.a_ref
  33.7 2.6 %collective-permute-done.3.c_ref = bf16[192,256]{1,0:T(8,128)(2,1)S(1)} collective-permute-done((bf16[192,256]{1,0:T(8,128)(2,1)S(1)}, bf16[192,256]{1,0:T(8,128)(2,1)S(1)}, u32[]{:S(2)}, u32[]{:S(2)}) %collective-permute-start.3) | collective-permute-done | bytes 98336 | tf_op jit(solution)/shard_map/ppermute | solution.py:46
  36.4 1.5 %collective-permute-start.5 = (bf16[192,256]{1,0:T(8,128)(2,1)S(1)}, bf16[192,256]{1,0:T(8,128)(2,1)S(1)}, u32[]{:S(2)}, u32[]{:S(2)}) collective-permute-start(bf16[192,256]{1,0:T(8,128)(2,1)S(1)} %shard_map.43.refs_0_), channel_id=1, source_target_pairs={{0,64},{16,80},{32,96},{48,112},{64,0},{80,16},{96,32},{112,48},{1... | collective-permute-start | bytes 294920 | tf_op jit(solution)/shard_map/ppermute | solution.py:46
  37.8 1.9 %collective-permute-start.4 = (bf16[192,256]{1,0:T(8,128)(2,1)S(1)}, bf16[192,256]{1,0:T(8,128)(2,1)S(1)}, u32[]{:S(2)}, u32[]{:S(2)}) collective-permute-start(bf16[192,256]{1,0:T(8,128)(2,1)S(1)} %shard_map.43.refs_0_), channel_id=1, source_target_pairs={{0,96},{16,112},{32,0},{48,16},{64,32},{80,48},{96,64},{112,80},{1... | collective-permute-start | bytes 294920 | tf_op jit(solution)/shard_map/ppermute | solution.py:46
  39.8 1.7 %collective-permute-done.5.refs_2_ = bf16[192,256]{1,0:T(8,128)(2,1)S(1)} collective-permute-done((bf16[192,256]{1,0:T(8,128)(2,1)S(1)}, bf16[192,256]{1,0:T(8,128)(2,1)S(1)}, u32[]{:S(2)}, u32[]{:S(2)}) %collective-permute-start.5) | collective-permute-done | bytes 98336 | tf_op jit(solution)/shard_map/ppermute | solution.py:46
  41.4 1.0 collective-permute-start.10
  42.4 1.6 %collective-permute-start.9 = (bf16[768,256]{1,0:T(8,128)(2,1)S(1)}, bf16[768,256]{1,0:T(8,128)(2,1)S(1)}, u32[]{:S(2)}, u32[]{:S(2)}) collective-permute-start(bf16[768,256]{1,0:T(8,128)(2,1)S(1)} %get-tuple-element.39), channel_id=1, source_target_pairs={{0,96},{16,112},{32,0},{48,16},{64,32},{80,48},{96,64},{112,80},{1... | collective-permute-start | bytes 1179656 | tf_op jit(solution)/shard_map/ppermute | solution.py:46
  44.1 0.2 collective-permute-start.11
  44.3 0.8 collective-permute-done.6.refs_3_
  45.1 4.0 %collective-permute-start.8 = (bf16[576,256]{1,0:T(8,128)(2,1)S(1)}, bf16[576,256]{1,0:T(8,128)(2,1)S(1)}, u32[]{:S(2)}, u32[]{:S(2)}) collective-permute-start(bf16[576,256]{1,0:T(8,128)(2,1)S(1)} %pad_maximum_fusion), channel_id=1, source_target_pairs={{0,16},{16,0},{32,48},{48,32},{64,80},{80,64},{96,112},{112,96},{1... | collective-permute-start | bytes 884744 | tf_op jit(solution)/shard_map/ppermute | solution.py:46
  49.1 0.1 collective-permute-start.7
  49.2 1.3 %collective-permute-done.7.refs_4_ = bf16[192,256]{1,0:T(8,128)(2,1)S(1)} collective-permute-done((bf16[192,256]{1,0:T(8,128)(2,1)S(1)}, bf16[192,256]{1,0:T(8,128)(2,1)S(1)}, u32[]{:S(2)}, u32[]{:S(2)}) %collective-permute-start.7) | collective-permute-done | bytes 98336 | tf_op jit(solution)/shard_map/ppermute | solution.py:46
  50.5 5.6 %shard_map.44 = (bf16[768,256]{1,0:T(8,128)(2,1)}, bf16[2,768,768]{2,1,0:T(8,128)(2,1)}, f32[8,128]{1,0:T(8,128)S(1)}) custom-call(bf16[192,256]{1,0:T(8,128)(2,1)S(1)} %shard_map.43.refs_0_, bf16[192,256]{1,0:T(8,128)(2,1)S(1)} %collective-permute-done.4.refs_1_, bf16[192,256]{1,0:T(8,128)(2,1)S(1)} %collective-permute-done.5.refs_2_, ...), custom_call_target="tpu_custom_call" | custom-call | tf_op jit(solution)/shard_map/pallas_call | solution.py:195
  56.1 3.7 %all-to-all-start.1 = ((bf16[16,48,256]{2,1,0:T(8,128)(2,1)}), bf16[16,48,256]{2,1,0:T(8,128)(2,1)S(1)}, u32[]{:S(2)}, u32[]{:S(2)}) async-start(bf16[16,48,256]{2,1,0:T(8,128)(2,1)} %bitcast.2), calls=%async_computation.1 | async-start | bytes 786432 | tf_op jit(solution)/shard_map/all_to_all | solution.py:331
  59.8 1.7 %copy-done = bf16[2,768,768]{2,1,0:T(8,128)(2,1)S(1)} copy-done((bf16[2,768,768]{2,1,0:T(8,128)(2,1)S(1)}, bf16[2,768,768]{2,1,0:T(8,128)(2,1)}, u32[]{:S(2)}) %copy-start) | copy-done | bytes 2359320
  61.5 2.4 %shard_map.45 = (bf16[768,1024]{1,0:T(8,128)(2,1)}, bf16[768,768]{1,0:T(8,128)(2,1)S(1)}) custom-call(bf16[2,768,768]{2,1,0:T(8,128)(2,1)S(1)} %copy-done, f32[8,128]{1,0:T(8,128)S(1)} %get-tuple-element.34.scale_ref, bf16[768,256]{1,0:T(8,128)(2,1)S(1)} %get-tuple-element.37.early_ref), custom_call_target="tpu_custom_call" | custom-call | tf_op jit(solution)/shard_map/pallas_call | solution.py:252
  64.0 2.1 %shard_map.46 = bf16[768,1024]{1,0:T(8,128)(2,1)} custom-call(bf16[768,768]{1,0:T(8,128)(2,1)S(1)} %get-tuple-element.38.square_ref, f32[8,128]{1,0:T(8,128)S(1)} %get-tuple-element.34.scale_ref, bf16[768,256]{1,0:T(8,128)(2,1)S(1)} %collective-permute-done.9.refs_0_, ...), custom_call_target="tpu_custom_call", output_to_operand_aliasing={{}: (5, {})} | custom-call | flops 20000000000 | tf_op jit(solution)/shard_map/pallas_call | solution.py:261
  66.1 3.1 %all-to-all-done.1.refs_0_ = bf16[16,48,256]{2,1,0:T(8,128)(2,1)S(1)} async-done(((bf16[16,48,256]{2,1,0:T(8,128)(2,1)}), bf16[16,48,256]{2,1,0:T(8,128)(2,1)S(1)}, u32[]{:S(2)}, u32[]{:S(2)}) %all-to-all-start.1) | async-done | bytes 393248 | tf_op jit(solution)/shard_map/all_to_all | solution.py:331
  69.1 3.7 %all-to-all-start.2 = ((bf16[16,48,1024]{2,1,0:T(8,128)(2,1)}), bf16[16,48,1024]{2,1,0:T(8,128)(2,1)S(1)}, u32[]{:S(2)}, u32[]{:S(2)}) async-start(bf16[16,48,1024]{2,1,0:T(8,128)(2,1)} %bitcast.3), calls=%async_computation.2 | async-start | bytes 3145728 | tf_op jit(solution)/shard_map/all_to_all | solution.py:331
  72.9 1.1 %collective-permute-start.13 = (bf16[16,48,256]{2,1,0:T(8,128)(2,1)S(1)}, bf16[16,48,256]{2,1,0:T(8,128)(2,1)S(1)}, u32[]{:S(2)}, u32[]{:S(2)}) collective-permute-start(bf16[16,48,256]{2,1,0:T(8,128)(2,1)S(1)} %all-to-all-done.1.refs_0_), channel_id=1, source_target_pairs={{0,96},{16,112},{32,0},{48,16},{64,32},{80,48},{96,64},{112,80},{1... | collective-permute-start | bytes 1179656 | tf_op jit(solution)/shard_map/ppermute | solution.py:46
  74.0 0.4 collective-permute-start.14
  74.4 2.1 %collective-permute-start.15 = (bf16[16,48,256]{2,1,0:T(8,128)(2,1)S(1)}, bf16[16,48,256]{2,1,0:T(8,128)(2,1)S(1)}, u32[]{:S(2)}, u32[]{:S(2)}) collective-permute-start(bf16[16,48,256]{2,1,0:T(8,128)(2,1)S(1)} %all-to-all-done.1.refs_0_), channel_id=1, source_target_pairs={{0,16},{16,0},{32,48},{48,32},{64,80},{80,64},{96,112},{112,96},{1... | collective-permute-start | bytes 1179656 | tf_op jit(solution)/shard_map/ppermute | solution.py:46
  76.5 2.2 %collective-permute-start.12 = (bf16[16,48,256]{2,1,0:T(8,128)(2,1)S(1)}, bf16[16,48,256]{2,1,0:T(8,128)(2,1)S(1)}, u32[]{:S(2)}, u32[]{:S(2)}) collective-permute-start(bf16[16,48,256]{2,1,0:T(8,128)(2,1)S(1)} %all-to-all-done.1.refs_0_), channel_id=1, source_target_pairs={{0,64},{16,80},{32,96},{48,112},{64,0},{80,16},{96,32},{112,48},{1... | collective-permute-start | bytes 1179656 | tf_op jit(solution)/shard_map/ppermute | solution.py:46
  78.7 3.3 %collective-permute-done.13.refs_1_ = bf16[16,48,256]{2,1,0:T(8,128)(2,1)S(1)} collective-permute-done((bf16[16,48,256]{2,1,0:T(8,128)(2,1)S(1)}, bf16[16,48,256]{2,1,0:T(8,128)(2,1)S(1)}, u32[]{:S(2)}, u32[]{:S(2)}) %collective-permute-start.13) | collective-permute-done | bytes 393248 | tf_op jit(solution)/shard_map/ppermute | solution.py:46
  82.1 4.4 %collective-permute-start.17 = (bf16[16,48,256]{2,1,0:T(8,128)(2,1)S(1)}, bf16[16,48,256]{2,1,0:T(8,128)(2,1)S(1)}, u32[]{:S(2)}, u32[]{:S(2)}) collective-permute-start(bf16[16,48,256]{2,1,0:T(8,128)(2,1)S(1)} %collective-permute-done.13.refs_1_), channel_id=1, source_target_pairs={{0,16},{16,0},{32,48},{48,32},{64,80},{80,64},{96,112},{112,96},{1... | collective-permute-start | bytes 1179656 | tf_op jit(solution)/shard_map/ppermute | solution.py:46
  86.5 2.5 %collective-permute-start.18 = (bf16[16,48,256]{2,1,0:T(8,128)(2,1)S(1)}, bf16[16,48,256]{2,1,0:T(8,128)(2,1)S(1)}, u32[]{:S(2)}, u32[]{:S(2)}) collective-permute-start(bf16[16,48,256]{2,1,0:T(8,128)(2,1)S(1)} %collective-permute-done.14.refs_2_), channel_id=1, source_target_pairs={{0,16},{16,0},{32,48},{48,32},{64,80},{80,64},{96,112},{112,96},{1... | collective-permute-start | bytes 1179656 | tf_op jit(solution)/shard_map/ppermute | solution.py:46
  89.0 1.2 %shard_map.47.refs_3_ = bf16[16,48,4096]{2,1,0:T(8,128)(2,1)} custom-call(bf16[16,48,256]{2,1,0:T(8,128)(2,1)S(1)} %all-to-all-done.1.refs_0_, bf16[16,48,256]{2,1,0:T(8,128)(2,1)S(1)} %collective-permute-done.13.refs_1_, bf16[16,48,256]{2,1,0:T(8,128)(2,1)S(1)} %collective-permute-done.14.refs_2_, bf16[16,48,256]{2,1,0:T(8,128)(2,1)S(1)} %collective-permute-done.15.refs_3_), custom_call_target="tpu_custom_call" | custom-call | tf_op jit(solution)/shard_map/pallas_call | solution.py:300
  90.2 2.3 %collective-permute-done.12.refs_2_ = bf16[16,48,256]{2,1,0:T(8,128)(2,1)S(1)} collective-permute-done((bf16[16,48,256]{2,1,0:T(8,128)(2,1)S(1)}, bf16[16,48,256]{2,1,0:T(8,128)(2,1)S(1)}, u32[]{:S(2)}, u32[]{:S(2)}) %collective-permute-start.12) | collective-permute-done | bytes 393248 | tf_op jit(solution)/shard_map/ppermute | solution.py:46
  92.4 2.7 %collective-permute-start.16 = (bf16[16,48,256]{2,1,0:T(8,128)(2,1)S(1)}, bf16[16,48,256]{2,1,0:T(8,128)(2,1)S(1)}, u32[]{:S(2)}, u32[]{:S(2)}) collective-permute-start(bf16[16,48,256]{2,1,0:T(8,128)(2,1)S(1)} %collective-permute-done.12.refs_2_), channel_id=1, source_target_pairs={{0,16},{16,0},{32,48},{48,32},{64,80},{80,64},{96,112},{112,96},{1... | collective-permute-start | bytes 1179656 | tf_op jit(solution)/shard_map/ppermute | solution.py:46
  95.2 1.4 %convert_add_fusion.2 = f32[8,2,48,512]{3,2,1,0:T(8,128)} fusion(bf16[8,2,48,512]{3,2,1,0:T(8,128)(2,1)S(1)} %copy-done.2, f32[8,2,48,512]{3,2,1,0:T(8,128)S(1)} %copy-done.1), kind=kLoop, calls=%fused_computation.4 | loop fusion | flops 1179648 | bytes 3932160 | tf_op jit(solution)/shard_map/add | solution.py:314
  96.6 1.0 shard_map.48.refs_1_
  97.6 0.8 shard_map.49.refs_4_
  98.4 0.2 fusion.2
  98.6 0.1 collective-permute-start.20
  98.7 0.5 collective-permute-start.19
  99.2 1.2 %shard_map.50.refs_2_ = bf16[16,48,4096]{2,1,0:T(8,128)(2,1)} custom-call(bf16[16,48,1024]{2,1,0:T(8,128)(2,1)S(1)} %all-to-all-done.2.refs_0_.refs_1_.refs_2_.refs_3_, bf16[16,48,1024]{2,1,0:T(8,128)(2,1)S(1)} %all-to-all-done.2.refs_0_.refs_1_.refs_2_.refs_3_, ...), custom_call_target="tpu_custom_call", output_to_operand_aliasing={{}: (4, {})} | custom-call | tf_op jit(solution)/shard_map/pallas_call | solution.py:300
  100.4 0.6 collective-permute-done.20.refs_0_.refs_1_
  101.0 0.9 shard_map.51.refs_2_
  101.9 0.2 collective-permute-done.19.refs_0_.refs_1_
  102.1 0.9 shard_map.52
  (21 shorter events, 0.2 us)
Async XLA Ops:
  25.2 3.2 %collective-permute-start = (bf16[768,256]{1,0:T(8,128)(2,1)S(1)}, bf16[768,256]{1,0:T(8,128)(2,1)S(1)}, u32[]{:S(2)}, u32[]{:S(2)}) collective-permute-start(bf16[768,256]{1,0:T(8,128)(2,1)S(1)} %get-tuple-element.27), channel_id=1, source_target_pairs={{0,16},{16,0},{32,48},{48,32},{64,80},{80,64},{96,112},{112,96},{1... | collective-permute-start | bytes 1179656 | tf_op jit(solution)/shard_map/ppermute | solution.py:46
  28.5 5.3 %collective-permute-start.1 = (bf16[192,256]{1,0:T(8,128)(2,1)S(1)}, bf16[192,256]{1,0:T(8,128)(2,1)S(1)}, u32[]{:S(2)}, u32[]{:S(2)}) collective-permute-start(bf16[192,256]{1,0:T(8,128)(2,1)S(1)} %get-tuple-element.29), channel_id=1, source_target_pairs={{0,32},{16,48},{32,64},{48,80},{64,96},{80,112},{96,0},{112,16},{1... | collective-permute-start | bytes 294920 | tf_op jit(solution)/shard_map/ppermute | solution.py:46
  29.7 4.0 %collective-permute-start.2 = (bf16[192,256]{1,0:T(8,128)(2,1)S(1)}, bf16[192,256]{1,0:T(8,128)(2,1)S(1)}, u32[]{:S(2)}, u32[]{:S(2)}) collective-permute-start(bf16[192,256]{1,0:T(8,128)(2,1)S(1)} %get-tuple-element.30), channel_id=1, source_target_pairs={{0,96},{16,112},{32,0},{48,16},{64,32},{80,48},{96,64},{112,80},{1... | collective-permute-start | bytes 294920 | tf_op jit(solution)/shard_map/ppermute | solution.py:46
  31.2 5.1 %collective-permute-start.3 = (bf16[192,256]{1,0:T(8,128)(2,1)S(1)}, bf16[192,256]{1,0:T(8,128)(2,1)S(1)}, u32[]{:S(2)}, u32[]{:S(2)}) collective-permute-start(bf16[192,256]{1,0:T(8,128)(2,1)S(1)} %get-tuple-element.31), channel_id=1, source_target_pairs={{0,64},{16,80},{32,96},{48,112},{64,0},{80,16},{96,32},{112,48},{1... | collective-permute-start | bytes 294920 | tf_op jit(solution)/shard_map/ppermute | solution.py:46
  36.4 5.1 %collective-permute-start.5 = (bf16[192,256]{1,0:T(8,128)(2,1)S(1)}, bf16[192,256]{1,0:T(8,128)(2,1)S(1)}, u32[]{:S(2)}, u32[]{:S(2)}) collective-permute-start(bf16[192,256]{1,0:T(8,128)(2,1)S(1)} %shard_map.43.refs_0_), channel_id=1, source_target_pairs={{0,64},{16,80},{32,96},{48,112},{64,0},{80,16},{96,32},{112,48},{1... | collective-permute-start | bytes 294920 | tf_op jit(solution)/shard_map/ppermute | solution.py:46
  37.8 6.4 %collective-permute-start.4 = (bf16[192,256]{1,0:T(8,128)(2,1)S(1)}, bf16[192,256]{1,0:T(8,128)(2,1)S(1)}, u32[]{:S(2)}, u32[]{:S(2)}) collective-permute-start(bf16[192,256]{1,0:T(8,128)(2,1)S(1)} %shard_map.43.refs_0_), channel_id=1, source_target_pairs={{0,96},{16,112},{32,0},{48,16},{64,32},{80,48},{96,64},{112,80},{1... | collective-permute-start | bytes 294920 | tf_op jit(solution)/shard_map/ppermute | solution.py:46
  39.7 5.3 %collective-permute-start.6 = (bf16[192,256]{1,0:T(8,128)(2,1)S(1)}, bf16[192,256]{1,0:T(8,128)(2,1)S(1)}, u32[]{:S(2)}, u32[]{:S(2)}) collective-permute-start(bf16[192,256]{1,0:T(8,128)(2,1)S(1)} %shard_map.43.refs_0_), channel_id=1, source_target_pairs={{0,32},{16,48},{32,64},{48,80},{64,96},{80,112},{96,0},{112,16},{1... | collective-permute-start | bytes 294920 | tf_op jit(solution)/shard_map/ppermute | solution.py:46
  41.4 22.5 %collective-permute-start.10 = (bf16[768,256]{1,0:T(8,128)(2,1)S(1)}, bf16[768,256]{1,0:T(8,128)(2,1)S(1)}, u32[]{:S(2)}, u32[]{:S(2)}) collective-permute-start(bf16[768,256]{1,0:T(8,128)(2,1)S(1)} %get-tuple-element.39), channel_id=1, source_target_pairs={{0,32},{16,48},{32,64},{48,80},{64,96},{80,112},{96,0},{112,16},{1... | collective-permute-start | bytes 1179656 | tf_op jit(solution)/shard_map/ppermute | solution.py:46
  42.4 21.5 %collective-permute-start.9 = (bf16[768,256]{1,0:T(8,128)(2,1)S(1)}, bf16[768,256]{1,0:T(8,128)(2,1)S(1)}, u32[]{:S(2)}, u32[]{:S(2)}) collective-permute-start(bf16[768,256]{1,0:T(8,128)(2,1)S(1)} %get-tuple-element.39), channel_id=1, source_target_pairs={{0,96},{16,112},{32,0},{48,16},{64,32},{80,48},{96,64},{112,80},{1... | collective-permute-start | bytes 1179656 | tf_op jit(solution)/shard_map/ppermute | solution.py:46
  44.1 19.9 %collective-permute-start.11 = (bf16[768,256]{1,0:T(8,128)(2,1)S(1)}, bf16[768,256]{1,0:T(8,128)(2,1)S(1)}, u32[]{:S(2)}, u32[]{:S(2)}) collective-permute-start(bf16[768,256]{1,0:T(8,128)(2,1)S(1)} %get-tuple-element.37.early_ref), channel_id=1, source_target_pairs={{0,64},{16,80},{32,96},{48,112},{64,0},{80,16},{96,32},{112,48},{1... | collective-permute-start | bytes 1179656 | tf_op jit(solution)/shard_map/ppermute | solution.py:46
  45.1 5.4 %collective-permute-start.8 = (bf16[576,256]{1,0:T(8,128)(2,1)S(1)}, bf16[576,256]{1,0:T(8,128)(2,1)S(1)}, u32[]{:S(2)}, u32[]{:S(2)}) collective-permute-start(bf16[576,256]{1,0:T(8,128)(2,1)S(1)} %pad_maximum_fusion), channel_id=1, source_target_pairs={{0,16},{16,0},{32,48},{48,32},{64,80},{80,64},{96,112},{112,96},{1... | collective-permute-start | bytes 884744 | tf_op jit(solution)/shard_map/ppermute | solution.py:46
  49.1 1.3 %collective-permute-start.7 = (bf16[192,256]{1,0:T(8,128)(2,1)S(1)}, bf16[192,256]{1,0:T(8,128)(2,1)S(1)}, u32[]{:S(2)}, u32[]{:S(2)}) collective-permute-start(bf16[192,256]{1,0:T(8,128)(2,1)S(1)} %shard_map.43.refs_0_), channel_id=1, source_target_pairs={{0,16},{16,0},{32,48},{48,32},{64,80},{80,64},{96,112},{112,96},{1... | collective-permute-start | bytes 294920 | tf_op jit(solution)/shard_map/ppermute | solution.py:46
  56.1 13.1 %all-to-all-start.1 = ((bf16[16,48,256]{2,1,0:T(8,128)(2,1)}), bf16[16,48,256]{2,1,0:T(8,128)(2,1)S(1)}, u32[]{:S(2)}, u32[]{:S(2)}) async-start(bf16[16,48,256]{2,1,0:T(8,128)(2,1)} %bitcast.2), calls=%async_computation.1 | async-start | bytes 786432 | tf_op jit(solution)/shard_map/all_to_all | solution.py:331
  59.8 1.7 %copy-start = (bf16[2,768,768]{2,1,0:T(8,128)(2,1)S(1)}, bf16[2,768,768]{2,1,0:T(8,128)(2,1)}, u32[]{:S(2)}) copy-start(bf16[2,768,768]{2,1,0:T(8,128)(2,1)} %get-tuple-element.33.polys_ref) | copy-start | bytes 7077892
  69.1 29.3 %all-to-all-start.2 = ((bf16[16,48,1024]{2,1,0:T(8,128)(2,1)}), bf16[16,48,1024]{2,1,0:T(8,128)(2,1)S(1)}, u32[]{:S(2)}, u32[]{:S(2)}) async-start(bf16[16,48,1024]{2,1,0:T(8,128)(2,1)} %bitcast.3), calls=%async_computation.2 | async-start | bytes 3145728 | tf_op jit(solution)/shard_map/all_to_all | solution.py:331
  72.9 22.3 %copy-start.1 = (f32[8,2,48,512]{3,2,1,0:T(8,128)S(1)}, f32[8,2,48,512]{3,2,1,0:T(8,128)}, u32[]{:S(2)}) copy-start(f32[8,2,48,512]{3,2,1,0:T(8,128)} %param.3) | copy-start | bytes 4718596
  72.9 22.3 %copy-start.2 = (bf16[8,2,48,512]{3,2,1,0:T(8,128)(2,1)S(1)}, bf16[8,2,48,512]{3,2,1,0:T(8,128)(2,1)}, u32[]{:S(2)}) copy-start(bf16[8,2,48,512]{3,2,1,0:T(8,128)(2,1)} %param.2) | copy-start | bytes 2359300
  72.9 9.2 %collective-permute-start.13 = (bf16[16,48,256]{2,1,0:T(8,128)(2,1)S(1)}, bf16[16,48,256]{2,1,0:T(8,128)(2,1)S(1)}, u32[]{:S(2)}, u32[]{:S(2)}) collective-permute-start(bf16[16,48,256]{2,1,0:T(8,128)(2,1)S(1)} %all-to-all-done.1.refs_0_), channel_id=1, source_target_pairs={{0,96},{16,112},{32,0},{48,16},{64,32},{80,48},{96,64},{112,80},{1... | collective-permute-start | bytes 1179656 | tf_op jit(solution)/shard_map/ppermute | solution.py:46
  74.0 12.5 %collective-permute-start.14 = (bf16[16,48,256]{2,1,0:T(8,128)(2,1)S(1)}, bf16[16,48,256]{2,1,0:T(8,128)(2,1)S(1)}, u32[]{:S(2)}, u32[]{:S(2)}) collective-permute-start(bf16[16,48,256]{2,1,0:T(8,128)(2,1)S(1)} %all-to-all-done.1.refs_0_), channel_id=1, source_target_pairs={{0,32},{16,48},{32,64},{48,80},{64,96},{80,112},{96,0},{112,16},{1... | collective-permute-start | bytes 1179656 | tf_op jit(solution)/shard_map/ppermute | solution.py:46
  74.4 14.6 %collective-permute-start.15 = (bf16[16,48,256]{2,1,0:T(8,128)(2,1)S(1)}, bf16[16,48,256]{2,1,0:T(8,128)(2,1)S(1)}, u32[]{:S(2)}, u32[]{:S(2)}) collective-permute-start(bf16[16,48,256]{2,1,0:T(8,128)(2,1)S(1)} %all-to-all-done.1.refs_0_), channel_id=1, source_target_pairs={{0,16},{16,0},{32,48},{48,32},{64,80},{80,64},{96,112},{112,96},{1... | collective-permute-start | bytes 1179656 | tf_op jit(solution)/shard_map/ppermute | solution.py:46
  76.5 16.0 %collective-permute-start.12 = (bf16[16,48,256]{2,1,0:T(8,128)(2,1)S(1)}, bf16[16,48,256]{2,1,0:T(8,128)(2,1)S(1)}, u32[]{:S(2)}, u32[]{:S(2)}) collective-permute-start(bf16[16,48,256]{2,1,0:T(8,128)(2,1)S(1)} %all-to-all-done.1.refs_0_), channel_id=1, source_target_pairs={{0,64},{16,80},{32,96},{48,112},{64,0},{80,16},{96,32},{112,48},{1... | collective-permute-start | bytes 1179656 | tf_op jit(solution)/shard_map/ppermute | solution.py:46
  82.1 14.5 %collective-permute-start.17 = (bf16[16,48,256]{2,1,0:T(8,128)(2,1)S(1)}, bf16[16,48,256]{2,1,0:T(8,128)(2,1)S(1)}, u32[]{:S(2)}, u32[]{:S(2)}) collective-permute-start(bf16[16,48,256]{2,1,0:T(8,128)(2,1)S(1)} %collective-permute-done.13.refs_1_), channel_id=1, source_target_pairs={{0,16},{16,0},{32,48},{48,32},{64,80},{80,64},{96,112},{112,96},{1... | collective-permute-start | bytes 1179656 | tf_op jit(solution)/shard_map/ppermute | solution.py:46
  86.5 10.1 %collective-permute-start.18 = (bf16[16,48,256]{2,1,0:T(8,128)(2,1)S(1)}, bf16[16,48,256]{2,1,0:T(8,128)(2,1)S(1)}, u32[]{:S(2)}, u32[]{:S(2)}) collective-permute-start(bf16[16,48,256]{2,1,0:T(8,128)(2,1)S(1)} %collective-permute-done.14.refs_2_), channel_id=1, source_target_pairs={{0,16},{16,0},{32,48},{48,32},{64,80},{80,64},{96,112},{112,96},{1... | collective-permute-start | bytes 1179656 | tf_op jit(solution)/shard_map/ppermute | solution.py:46
  92.4 5.2 %collective-permute-start.16 = (bf16[16,48,256]{2,1,0:T(8,128)(2,1)S(1)}, bf16[16,48,256]{2,1,0:T(8,128)(2,1)S(1)}, u32[]{:S(2)}, u32[]{:S(2)}) collective-permute-start(bf16[16,48,256]{2,1,0:T(8,128)(2,1)S(1)} %collective-permute-done.12.refs_2_), channel_id=1, source_target_pairs={{0,16},{16,0},{32,48},{48,32},{64,80},{80,64},{96,112},{112,96},{1... | collective-permute-start | bytes 1179656 | tf_op jit(solution)/shard_map/ppermute | solution.py:46
  98.6 2.4 %collective-permute-start.20 = (bf16[16,48,512]{2,1,0:T(8,128)(2,1)S(1)}, bf16[16,48,512]{2,1,0:T(8,128)(2,1)S(1)}, u32[]{:S(2)}, u32[]{:S(2)}) collective-permute-start(bf16[16,48,512]{2,1,0:T(8,128)(2,1)S(1)} %get-tuple-element.50), channel_id=1, source_target_pairs={{0,16},{16,0},{32,48},{48,32},{64,80},{80,64},{96,112},{112,96},{1... | collective-permute-start | bytes 2359304 | tf_op jit(solution)/shard_map/ppermute | solution.py:46
  98.7 3.4 %collective-permute-start.19 = (bf16[16,48,512]{2,1,0:T(8,128)(2,1)S(1)}, bf16[16,48,512]{2,1,0:T(8,128)(2,1)S(1)}, u32[]{:S(2)}, u32[]{:S(2)}) collective-permute-start(bf16[16,48,512]{2,1,0:T(8,128)(2,1)S(1)} %get-tuple-element.51), channel_id=1, source_target_pairs={{0,16},{16,0},{32,48},{48,32},{64,80},{80,64},{96,112},{112,96},{1... | collective-permute-start | bytes 2359304 | tf_op jit(solution)/shard_map/ppermute | solution.py:46

commit v7 on v6

--- a/solution.py
+++ b/solution.py
@@ -213,15 +213,14 @@
     )(*pieces, rows)
 
 
-def both_steps_at_once(square, scale, rows):
-    total = coef_linear * coef_linear * rows.astype(F32) + dot(square, rows)
-    return ((scale_factor * scale) * total).astype(BF16)
-
-
-def own_kernel(polys_ref, scale_ref, early_ref, out_ref, square_ref, result, sems):
-    sums = polys_ref[0].astype(F32) + polys_ref[1].astype(F32)
-    square_ref[...] = (coef_linear * sums + dot(polys_ref[1], polys_ref[0])).astype(BF16)
-    result[...] = both_steps_at_once(square_ref[...], scale_ref[:1, :1], early_ref[...])
+def both_steps(poly_0, poly_1, scale, rows):
+    first = ((coef_linear * rows.astype(F32) + dot(poly_0, rows)) * scale).astype(BF16)
+    second = coef_linear * first.astype(F32) + dot(poly_1, first)
+    return (scale_factor * second).astype(BF16)
+
+
+def own_kernel(polys_ref, scale_ref, early_ref, out_ref, result, sems):
+    result[...] = both_steps(polys_ref[0], polys_ref[1], scale_ref[:1, :1], early_ref[...])
     store = pltpu.make_async_copy(result, out_ref.at[:, pl.ds(0, EARLY)], sems.at[0])
     store.start()
     store.wait()
@@ -231,16 +230,21 @@
 OTHERS = ((EARLY, NEAR), (EARLY + NEAR, NEAR), (EARLY + 2 * NEAR, EARLY))
 
 
-def other_kernel(square_ref, scale_ref, *refs):
-    early_in, out_ref, result, sems = refs[:3], *refs[4:]
+def other_kernel(polys_ref, scale_ref, *refs):
+    early_in, out_ref, early, result, sems = refs[:3], *refs[4:]
+    for place, (start, width) in enumerate(OTHERS):
+        early[:, pl.ds(start - EARLY, width)] = early_in[place][...]
+    rows = early[...]
+    total = coef_linear * rows.astype(F32) + dot(polys_ref[0], rows)
+    first = (total * scale_ref[:1, :1]).astype(BF16)
     stores = []
-    for place, (start, width) in enumerate(OTHERS):
-        cut = pl.ds(start - EARLY, width)
-        result[:, cut] = both_steps_at_once(
-            square_ref[...], scale_ref[:1, :1], early_in[place][...]
-        )
-        where = out_ref.at[:, pl.ds(start, width)]
-        stores.append(pltpu.make_async_copy(result.at[:, cut], where, sems.at[place]))
+    for block in range(FF // BLOCK):
+        where = pl.ds(block * BLOCK, BLOCK)
+        cut = slice(block * BLOCK, (block + 1) * BLOCK)
+        second = coef_linear * first[cut].astype(F32) + dot(polys_ref[1, where, :], first)
+        result[where, :] = (scale_factor * second).astype(BF16)
+        target = out_ref.at[where, pl.ds(EARLY, SECOND - EARLY)]
+        stores.append(pltpu.make_async_copy(result.at[where, :], target, sems.at[block]))
         stores[-1].start()
     for store in stores:
         store.wait()
@@ -249,11 +253,11 @@
 def early_products(polys, scale, early):
     out = jax.ShapeDtypeStruct((FF, SECOND), BF16)
     flops = 2 * FF * FF * EARLY
-    result, square = pl.pallas_call(
+    result = pl.pallas_call(
         own_kernel,
-        out_shape=(out, jax.ShapeDtypeStruct((FF, FF), BF16)),
+        out_shape=out,
         in_specs=[VMEM] * 3,
-        out_specs=(HBM, VMEM),
+        out_specs=HBM,
         scratch_shapes=[pltpu.VMEM((FF, EARLY), BF16), pltpu.SemaphoreType.DMA((1,))],
         cost_estimate=pl.CostEstimate(flops=0, bytes_accessed=0, transcendentals=0),
         compiler_params=PARAMS,
@@ -263,11 +267,15 @@
         out_shape=out,
         in_specs=[VMEM] * 5 + [HBM],
         out_specs=HBM,
-        scratch_shapes=[pltpu.VMEM((FF, SECOND - EARLY), BF16), pltpu.SemaphoreType.DMA((3,))],
+        scratch_shapes=[
+            pltpu.VMEM((FF, SECOND - EARLY), BF16),
+            pltpu.VMEM((FF, SECOND - EARLY), BF16),
+            pltpu.SemaphoreType.DMA((3,)),
+        ],
         input_output_aliases={5: 0},
         cost_estimate=pl.CostEstimate(flops=ORDER, bytes_accessed=0, transcendentals=0),
         compiler_params=LARGE,
-    )(square, scale, *early[1:], result)
+    )(polys, scale, *early[1:], result)
 
 
 def place_kernel(where, aliased, *refs):
@@ -321,6 +329,9 @@
 
     keep, send, near, far = partial_gram(rows)
     own, to_next, to_last, to_far = chip_sum(keep, shift(send, 0, 1))
+    gradient, momentum, own = lax.optimization_barrier((gradient, momentum, own))
+    new_momentum = stepped(gradient, momentum)
+    own, new_momentum = lax.optimization_barrier((own, new_momentum))
     mine = ring_sum(own, shift(to_next, 1), shift(to_last, -1), shift(to_far, 2))
     here = (mine, shift(mine, -1), shift(mine, 2), shift(mine, 1))
     other = shift(jnp.concatenate(here[1:]), 0, 1)
@@ -334,8 +345,6 @@
     early_rows = early_products(polys, scale, (far, shift(near, -1), shift(near, 1), shift(far, 2)))
     late = back(late_rows)
     late, early_rows = lax.optimization_barrier((late, early_rows))
-    gradient, momentum, _ = lax.optimization_barrier((gradient, momentum, late))
-    new_momentum = stepped(gradient, momentum)
     cut = late[:, :, :LATE]
     late_pieces = {0: late, 1: shift(cut, -1), 3: shift(cut, 1), 2: shift(late, 2)}
     widths = {0: FIRST, 1: LATE, 3: LATE, 2: FIRST}
@@ -361,7 +370,7 @@
     late_across[2] = shift(late_pieces[2], 0, 1)
     update = place(update, shape, [late_place(late_across, steps, 1) for steps in (1, 3)] + [late_place(late_pieces, 2, 0)])
     update = place(update, shape, [late_place(late_across, steps, 1) for steps in (2,)])
-    second, update, new_momentum = lax.optimization_barrier((second, update, new_momentum))
+    second, update = lax.optimization_barrier((second, update))
     update = place(update, shape, early_places(second, 0, 0, SECOND))
     middle = EARLY + NEAR
     for left, right in ((0, middle), (middle, SECOND)):

time: 104 us -> 103 us (level)
    ppermute x21, starting transfers between devices: 32.6 us -> 31.3 us  [shift(): return lax.ppermute(value, 'replica', pairs)]
  transfers between devices with their start and end apart: 23 -> 23, of which waited for: 11 -> 10; matrix products, arithmetic and copies ran while one was open for 1% -> 1% of each run, Pallas kernels for 15% -> 15%
where the time goes in v7:
time: 103 us; the launch traced here: 102 us
  starting transfers between devices  39.1 us (38%)
  blocking collectives  22 us (21%)
  waiting for transfers between devices  17.6 us (17%)
  Pallas kernels  17.5 us (17%)
  other arithmetic  3.4 us (3%)
  local copies, waits for them, and re-layouts  1.88 us (2%)
    ppermute x21, starting transfers between devices, shift(): return lax.ppermute(value, 'replica', pairs)  31.3 us
    all_to_all x1, blocking collectives, local(): lax.all_to_all(flat_rows, 'tensor', split_axis=0, concat_axis=0, tiled=True)  22 us
    ppermute x21, waiting for transfers between devices, shift(): return lax.ppermute(value, 'replica', pairs)  15.2 us
    all_to_all x2, starting transfers between devices, back(): lax.all_to_all(value, 'tensor', split_axis=0, concat_axis=0, tiled=True)  7.75 us
    pallas_call x6, Pallas kernels, place(): pl.pallas_call(functools.partial(place_kernel, where, int(aliased)), out_...  5.9 us
    pallas_call x1, Pallas kernels, chain(): pl.pallas_call(chain_kernel, out_shape=(jax.ShapeDtypeStruct((FF, FIRST),...  5.6 us
    pallas_call x1, Pallas kernels, early_products(): pl.pallas_call(other_kernel, out_shape=out, in_specs=[VMEM] * 5 + [HBM],...  3 us
    all_to_all x2, waiting for transfers between devices, back(): lax.all_to_all(value, 'tensor', split_axis=0, concat_axis=0, tiled=True)  2.44 us
  transfers between devices with their start and end apart: 23, of which 10 were waited for; matrix products, arithmetic and copies ran while one was open for 1% of the time, Pallas kernels for 15%

profile of v7, /device:TPU:1, one launch (start us, length us, event | category | flops | bytes accessed | tf_op | source)
XLA Modules:
  0.0 102.4 jit_solution(14584025802194445611)
XLA Ops:
  0.6 2.0 %fusion.1 = bf16[8,2,48,512]{3,2,1,0:T(8,128)(2,1)S(1)} fusion(bf16[8,2,48,512]{3,2,1,0:T(8,128)(2,1)} %param.2, f32[8,2,48,512]{3,2,1,0:T(8,128)} %param.3), kind=kLoop, calls=%fused_computation.3 | loop fusion | flops 2359296 | bytes 3145728 | tf_op jit(solution)/shard_map/convert_element_type | solution.py:326
  2.6 22.0 %all_to_all.15 = bf16[16,48,512]{2,1,0:T(8,128)(2,1)S(1)} all-to-all(bf16[16,48,512]{2,1,0:T(8,128)(2,1)S(1)} %bitcast.8), channel_id=1, replica_groups=mesh['replica'=8,'tensor'=16] {'tensor'}, dimensions={0} | all-to-all | bytes 1572864 | tf_op jit(solution)/shard_map/all_to_all | solution.py:327
  24.6 0.7 shard_map.41
  25.3 1.9 %collective-permute-start = (bf16[768,256]{1,0:T(8,128)(2,1)S(1)}, bf16[768,256]{1,0:T(8,128)(2,1)S(1)}, u32[]{:S(2)}, u32[]{:S(2)}) collective-permute-start(bf16[768,256]{1,0:T(8,128)(2,1)S(1)} %get-tuple-element.27), channel_id=1, source_target_pairs={{0,16},{16,0},{32,48},{48,32},{64,80},{80,64},{96,112},{112,96},{1... | collective-permute-start | bytes 1179656 | tf_op jit(solution)/shard_map/ppermute | solution.py:46
  27.2 1.3 %collective-permute-done.got_ref = bf16[768,256]{1,0:T(8,128)(2,1)S(1)} collective-permute-done((bf16[768,256]{1,0:T(8,128)(2,1)S(1)}, bf16[768,256]{1,0:T(8,128)(2,1)S(1)}, u32[]{:S(2)}, u32[]{:S(2)}) %collective-permute-start) | collective-permute-done | bytes 393248 | tf_op jit(solution)/shard_map/ppermute | solution.py:46
  28.5 0.1 shard_map.42
  28.6 1.3 %collective-permute-start.1 = (bf16[192,256]{1,0:T(8,128)(2,1)S(1)}, bf16[192,256]{1,0:T(8,128)(2,1)S(1)}, u32[]{:S(2)}, u32[]{:S(2)}) collective-permute-start(bf16[192,256]{1,0:T(8,128)(2,1)S(1)} %get-tuple-element.33), channel_id=1, source_target_pairs={{0,32},{16,48},{32,64},{48,80},{64,96},{80,112},{96,0},{112,16},{1... | collective-permute-start | bytes 294920 | tf_op jit(solution)/shard_map/ppermute | solution.py:46
  29.9 1.5 %collective-permute-start.2 = (bf16[192,256]{1,0:T(8,128)(2,1)S(1)}, bf16[192,256]{1,0:T(8,128)(2,1)S(1)}, u32[]{:S(2)}, u32[]{:S(2)}) collective-permute-start(bf16[192,256]{1,0:T(8,128)(2,1)S(1)} %get-tuple-element.34), channel_id=1, source_target_pairs={{0,96},{16,112},{32,0},{48,16},{64,32},{80,48},{96,64},{112,80},{1... | collective-permute-start | bytes 294920 | tf_op jit(solution)/shard_map/ppermute | solution.py:46
  31.4 1.5 %collective-permute-start.3 = (bf16[192,256]{1,0:T(8,128)(2,1)S(1)}, bf16[192,256]{1,0:T(8,128)(2,1)S(1)}, u32[]{:S(2)}, u32[]{:S(2)}) collective-permute-start(bf16[192,256]{1,0:T(8,128)(2,1)S(1)} %get-tuple-element.35), channel_id=1, source_target_pairs={{0,64},{16,80},{32,96},{48,112},{64,0},{80,16},{96,32},{112,48},{1... | collective-permute-start | bytes 294920 | tf_op jit(solution)/shard_map/ppermute | solution.py:46
  32.9 1.4 %convert_add_fusion.2 = f32[8,2,48,512]{3,2,1,0:T(8,128)} fusion(bf16[8,2,48,512]{3,2,1,0:T(8,128)(2,1)S(1)} %copy-done.3, f32[8,2,48,512]{3,2,1,0:T(8,128)S(1)} %copy-done.2), kind=kLoop, calls=%fused_computation.4 | loop fusion | flops 1179648 | bytes 3932160 | tf_op jit(solution)/shard_map/add | solution.py:322
  34.3 2.1 %collective-permute-done.3.c_ref = bf16[192,256]{1,0:T(8,128)(2,1)S(1)} collective-permute-done((bf16[192,256]{1,0:T(8,128)(2,1)S(1)}, bf16[192,256]{1,0:T(8,128)(2,1)S(1)}, u32[]{:S(2)}, u32[]{:S(2)}) %collective-permute-start.3) | collective-permute-done | bytes 98336 | tf_op jit(solution)/shard_map/ppermute | solution.py:46
  36.5 1.5 %collective-permute-start.5 = (bf16[192,256]{1,0:T(8,128)(2,1)S(1)}, bf16[192,256]{1,0:T(8,128)(2,1)S(1)}, u32[]{:S(2)}, u32[]{:S(2)}) collective-permute-start(bf16[192,256]{1,0:T(8,128)(2,1)S(1)} %shard_map.43.refs_0_), channel_id=1, source_target_pairs={{0,64},{16,80},{32,96},{48,112},{64,0},{80,16},{96,32},{112,48},{1... | collective-permute-start | bytes 294920 | tf_op jit(solution)/shard_map/ppermute | solution.py:46
  38.0 0.7 collective-permute-start.6
  38.7 2.0 %collective-permute-start.4 = (bf16[192,256]{1,0:T(8,128)(2,1)S(1)}, bf16[192,256]{1,0:T(8,128)(2,1)S(1)}, u32[]{:S(2)}, u32[]{:S(2)}) collective-permute-start(bf16[192,256]{1,0:T(8,128)(2,1)S(1)} %shard_map.43.refs_0_), channel_id=1, source_target_pairs={{0,96},{16,112},{32,0},{48,16},{64,32},{80,48},{96,64},{112,80},{1... | collective-permute-start | bytes 294920 | tf_op jit(solution)/shard_map/ppermute | solution.py:46
  40.7 0.9 collective-permute-done.5.refs_2_
  41.6 1.3 %collective-permute-start.10 = (bf16[768,256]{1,0:T(8,128)(2,1)S(1)}, bf16[768,256]{1,0:T(8,128)(2,1)S(1)}, u32[]{:S(2)}, u32[]{:S(2)}) collective-permute-start(bf16[768,256]{1,0:T(8,128)(2,1)S(1)} %get-tuple-element.41), channel_id=1, source_target_pairs={{0,32},{16,48},{32,64},{48,80},{64,96},{80,112},{96,0},{112,16},{1... | collective-permute-start | bytes 1179656 | tf_op jit(solution)/shard_map/ppermute | solution.py:46
  42.9 1.4 %collective-permute-start.9 = (bf16[768,256]{1,0:T(8,128)(2,1)S(1)}, bf16[768,256]{1,0:T(8,128)(2,1)S(1)}, u32[]{:S(2)}, u32[]{:S(2)}) collective-permute-start(bf16[768,256]{1,0:T(8,128)(2,1)S(1)} %get-tuple-element.41), channel_id=1, source_target_pairs={{0,96},{16,112},{32,0},{48,16},{64,32},{80,48},{96,64},{112,80},{1... | collective-permute-start | bytes 1179656 | tf_op jit(solution)/shard_map/ppermute | solution.py:46
  44.3 0.4 collective-permute-start.11
  44.7 4.0 %collective-permute-start.8 = (bf16[576,256]{1,0:T(8,128)(2,1)S(1)}, bf16[576,256]{1,0:T(8,128)(2,1)S(1)}, u32[]{:S(2)}, u32[]{:S(2)}) collective-permute-start(bf16[576,256]{1,0:T(8,128)(2,1)S(1)} %pad_maximum_fusion), channel_id=1, source_target_pairs={{0,16},{16,0},{32,48},{48,32},{64,80},{80,64},{96,112},{112,96},{1... | collective-permute-start | bytes 884744 | tf_op jit(solution)/shard_map/ppermute | solution.py:46
  48.8 1.3 %collective-permute-done.7.refs_4_ = bf16[192,256]{1,0:T(8,128)(2,1)S(1)} collective-permute-done((bf16[192,256]{1,0:T(8,128)(2,1)S(1)}, bf16[192,256]{1,0:T(8,128)(2,1)S(1)}, u32[]{:S(2)}, u32[]{:S(2)}) %collective-permute-start.7) | collective-permute-done | bytes 98336 | tf_op jit(solution)/shard_map/ppermute | solution.py:46
  50.1 5.6 %shard_map.44 = (bf16[768,256]{1,0:T(8,128)(2,1)}, bf16[2,768,768]{2,1,0:T(8,128)(2,1)}, f32[8,128]{1,0:T(8,128)S(1)}) custom-call(bf16[192,256]{1,0:T(8,128)(2,1)S(1)} %shard_map.43.refs_0_, bf16[192,256]{1,0:T(8,128)(2,1)S(1)} %collective-permute-done.4.refs_1_, bf16[192,256]{1,0:T(8,128)(2,1)S(1)} %collective-permute-done.5.refs_2_, ...), custom_call_target="tpu_custom_call" | custom-call | tf_op jit(solution)/shard_map/pallas_call | solution.py:195
  55.7 3.7 %all-to-all-start.1 = ((bf16[16,48,256]{2,1,0:T(8,128)(2,1)}), bf16[16,48,256]{2,1,0:T(8,128)(2,1)S(1)}, u32[]{:S(2)}, u32[]{:S(2)}) async-start(bf16[16,48,256]{2,1,0:T(8,128)(2,1)} %bitcast.2), calls=%async_computation.1 | async-start | bytes 786432 | tf_op jit(solution)/shard_map/all_to_all | solution.py:342
  59.5 1.7 %copy-done = bf16[2,768,768]{2,1,0:T(8,128)(2,1)S(1)} copy-done((bf16[2,768,768]{2,1,0:T(8,128)(2,1)S(1)}, bf16[2,768,768]{2,1,0:T(8,128)(2,1)}, u32[]{:S(2)}) %copy-start) | copy-done | bytes 2359320
  61.1 2.2 %shard_map.45.refs_3_ = bf16[768,1024]{1,0:T(8,128)(2,1)} custom-call(bf16[2,768,768]{2,1,0:T(8,128)(2,1)S(1)} %copy-done, f32[8,128]{1,0:T(8,128)S(1)} %get-tuple-element.38.scale_ref, bf16[768,256]{1,0:T(8,128)(2,1)S(1)} %get-tuple-element.42.early_ref), custom_call_target="tpu_custom_call" | custom-call | tf_op jit(solution)/shard_map/pallas_call | solution.py:256
  63.3 3.0 %shard_map.46 = bf16[768,1024]{1,0:T(8,128)(2,1)} custom-call(bf16[2,768,768]{2,1,0:T(8,128)(2,1)S(1)} %copy-done.1, f32[8,128]{1,0:T(8,128)S(1)} %get-tuple-element.38.scale_ref, bf16[768,256]{1,0:T(8,128)(2,1)S(1)} %collective-permute-done.9.refs_0_, bf16[768,256]{1,0:T(8,128)(2,1)S(1)} %collective-permute-done.10.refs_1_, ...), custom_call_target="tpu_custom_call", output_to_operand_aliasing={{}: (5, {})} | custom-call | flops 20000000000 | tf_op jit(solution)/shard_map/pallas_call | solution.py:265
  66.3 2.4 %all-to-all-done.1.refs_0_ = bf16[16,48,256]{2,1,0:T(8,128)(2,1)S(1)} async-done(((bf16[16,48,256]{2,1,0:T(8,128)(2,1)}), bf16[16,48,256]{2,1,0:T(8,128)(2,1)S(1)}, u32[]{:S(2)}, u32[]{:S(2)}) %all-to-all-start.1) | async-done | bytes 393248 | tf_op jit(solution)/shard_map/all_to_all | solution.py:342
  68.8 4.0 %all-to-all-start.2 = ((bf16[16,48,1024]{2,1,0:T(8,128)(2,1)}), bf16[16,48,1024]{2,1,0:T(8,128)(2,1)S(1)}, u32[]{:S(2)}, u32[]{:S(2)}) async-start(bf16[16,48,1024]{2,1,0:T(8,128)(2,1)} %bitcast.3), calls=%async_computation.2 | async-start | bytes 3145728 | tf_op jit(solution)/shard_map/all_to_all | solution.py:342
  72.8 0.7 collective-permute-start.14
  73.5 2.0 %collective-permute-start.13 = (bf16[16,48,256]{2,1,0:T(8,128)(2,1)S(1)}, bf16[16,48,256]{2,1,0:T(8,128)(2,1)S(1)}, u32[]{:S(2)}, u32[]{:S(2)}) collective-permute-start(bf16[16,48,256]{2,1,0:T(8,128)(2,1)S(1)} %all-to-all-done.1.refs_0_), channel_id=1, source_target_pairs={{0,96},{16,112},{32,0},{48,16},{64,32},{80,48},{96,64},{112,80},{1... | collective-permute-start | bytes 1179656 | tf_op jit(solution)/shard_map/ppermute | solution.py:46
  75.5 1.8 %collective-permute-start.15 = (bf16[16,48,256]{2,1,0:T(8,128)(2,1)S(1)}, bf16[16,48,256]{2,1,0:T(8,128)(2,1)S(1)}, u32[]{:S(2)}, u32[]{:S(2)}) collective-permute-start(bf16[16,48,256]{2,1,0:T(8,128)(2,1)S(1)} %all-to-all-done.1.refs_0_), channel_id=1, source_target_pairs={{0,16},{16,0},{32,48},{48,32},{64,80},{80,64},{96,112},{112,96},{1... | collective-permute-start | bytes 1179656 | tf_op jit(solution)/shard_map/ppermute | solution.py:46
  77.3 1.8 %collective-permute-start.12 = (bf16[16,48,256]{2,1,0:T(8,128)(2,1)S(1)}, bf16[16,48,256]{2,1,0:T(8,128)(2,1)S(1)}, u32[]{:S(2)}, u32[]{:S(2)}) collective-permute-start(bf16[16,48,256]{2,1,0:T(8,128)(2,1)S(1)} %all-to-all-done.1.refs_0_), channel_id=1, source_target_pairs={{0,64},{16,80},{32,96},{48,112},{64,0},{80,16},{96,32},{112,48},{1... | collective-permute-start | bytes 1179656 | tf_op jit(solution)/shard_map/ppermute | solution.py:46
  79.1 4.4 %collective-permute-done.14.refs_2_ = bf16[16,48,256]{2,1,0:T(8,128)(2,1)S(1)} collective-permute-done((bf16[16,48,256]{2,1,0:T(8,128)(2,1)S(1)}, bf16[16,48,256]{2,1,0:T(8,128)(2,1)S(1)}, u32[]{:S(2)}, u32[]{:S(2)}) %collective-permute-start.14) | collective-permute-done | bytes 393248 | tf_op jit(solution)/shard_map/ppermute | solution.py:46
  83.5 3.2 %collective-permute-start.18 = (bf16[16,48,256]{2,1,0:T(8,128)(2,1)S(1)}, bf16[16,48,256]{2,1,0:T(8,128)(2,1)S(1)}, u32[]{:S(2)}, u32[]{:S(2)}) collective-permute-start(bf16[16,48,256]{2,1,0:T(8,128)(2,1)S(1)} %collective-permute-done.14.refs_2_), channel_id=1, source_target_pairs={{0,16},{16,0},{32,48},{48,32},{64,80},{80,64},{96,112},{112,96},{1... | collective-permute-start | bytes 1179656 | tf_op jit(solution)/shard_map/ppermute | solution.py:46
  86.7 0.6 collective-permute-start.17
  87.3 1.2 %shard_map.47.refs_3_ = bf16[16,48,4096]{2,1,0:T(8,128)(2,1)} custom-call(bf16[16,48,256]{2,1,0:T(8,128)(2,1)S(1)} %all-to-all-done.1.refs_0_, bf16[16,48,256]{2,1,0:T(8,128)(2,1)S(1)} %collective-permute-done.13.refs_1_, bf16[16,48,256]{2,1,0:T(8,128)(2,1)S(1)} %collective-permute-done.14.refs_2_, bf16[16,48,256]{2,1,0:T(8,128)(2,1)S(1)} %collective-permute-done.15.refs_3_), custom_call_target="tpu_custom_call" | custom-call | tf_op jit(solution)/shard_map/pallas_call | solution.py:308
  88.5 4.0 %collective-permute-done.12.refs_2_ = bf16[16,48,256]{2,1,0:T(8,128)(2,1)S(1)} collective-permute-done((bf16[16,48,256]{2,1,0:T(8,128)(2,1)S(1)}, bf16[16,48,256]{2,1,0:T(8,128)(2,1)S(1)}, u32[]{:S(2)}, u32[]{:S(2)}) %collective-permute-start.12) | collective-permute-done | bytes 393248 | tf_op jit(solution)/shard_map/ppermute | solution.py:46
  92.5 2.1 %collective-permute-start.16 = (bf16[16,48,256]{2,1,0:T(8,128)(2,1)S(1)}, bf16[16,48,256]{2,1,0:T(8,128)(2,1)S(1)}, u32[]{:S(2)}, u32[]{:S(2)}) collective-permute-start(bf16[16,48,256]{2,1,0:T(8,128)(2,1)S(1)} %collective-permute-done.12.refs_2_), channel_id=1, source_target_pairs={{0,16},{16,0},{32,48},{48,32},{64,80},{80,64},{96,112},{112,96},{1... | collective-permute-start | bytes 1179656 | tf_op jit(solution)/shard_map/ppermute | solution.py:46
  94.7 1.0 %shard_map.48.refs_1_ = bf16[16,48,4096]{2,1,0:T(8,128)(2,1)} custom-call(bf16[16,48,256]{2,1,0:T(8,128)(2,1)S(1)} %collective-permute-done.17.refs_0_, bf16[16,48,256]{2,1,0:T(8,128)(2,1)S(1)} %collective-permute-done.18.refs_1_, bf16[16,48,256]{2,1,0:T(8,128)(2,1)S(1)} %collective-permute-done.12.refs_2_, ...), custom_call_target="tpu_custom_call", output_to_operand_aliasing={{}: (3, {})} | custom-call | tf_op jit(solution)/shard_map/pallas_call | solution.py:308
  95.7 0.3 collective-permute-done.16.refs_0_
  96.0 0.8 shard_map.49.refs_4_
  96.8 0.2 fusion.2
  97.0 1.4 %collective-permute-start.20 = (bf16[16,48,512]{2,1,0:T(8,128)(2,1)S(1)}, bf16[16,48,512]{2,1,0:T(8,128)(2,1)S(1)}, u32[]{:S(2)}, u32[]{:S(2)}) collective-permute-start(bf16[16,48,512]{2,1,0:T(8,128)(2,1)S(1)} %get-tuple-element.50), channel_id=1, source_target_pairs={{0,16},{16,0},{32,48},{48,32},{64,80},{80,64},{96,112},{112,96},{1... | collective-permute-start | bytes 2359304 | tf_op jit(solution)/shard_map/ppermute | solution.py:46
  98.4 0.1 collective-permute-start.19
  98.4 1.2 %shard_map.50.refs_2_ = bf16[16,48,4096]{2,1,0:T(8,128)(2,1)} custom-call(bf16[16,48,1024]{2,1,0:T(8,128)(2,1)S(1)} %all-to-all-done.2.refs_0_.refs_1_.refs_2_.refs_3_, bf16[16,48,1024]{2,1,0:T(8,128)(2,1)S(1)} %all-to-all-done.2.refs_0_.refs_1_.refs_2_.refs_3_, ...), custom_call_target="tpu_custom_call", output_to_operand_aliasing={{}: (4, {})} | custom-call | tf_op jit(solution)/shard_map/pallas_call | solution.py:308
  99.6 0.6 collective-permute-done.20.refs_0_.refs_1_
  100.3 0.9 shard_map.51.refs_2_
  101.2 0.2 collective-permute-done.19.refs_0_.refs_1_
  101.4 0.9 shard_map.52
  (23 shorter events, 0.2 us)
Async XLA Ops:
  2.6 30.3 %copy-start.2 = (f32[8,2,48,512]{3,2,1,0:T(8,128)S(1)}, f32[8,2,48,512]{3,2,1,0:T(8,128)}, u32[]{:S(2)}) copy-start(f32[8,2,48,512]{3,2,1,0:T(8,128)} %param.3) | copy-start | bytes 4718596
  2.6 30.3 %copy-start.3 = (bf16[8,2,48,512]{3,2,1,0:T(8,128)(2,1)S(1)}, bf16[8,2,48,512]{3,2,1,0:T(8,128)(2,1)}, u32[]{:S(2)}) copy-start(bf16[8,2,48,512]{3,2,1,0:T(8,128)(2,1)} %param.2) | copy-start | bytes 2359300
  25.3 3.2 %collective-permute-start = (bf16[768,256]{1,0:T(8,128)(2,1)S(1)}, bf16[768,256]{1,0:T(8,128)(2,1)S(1)}, u32[]{:S(2)}, u32[]{:S(2)}) collective-permute-start(bf16[768,256]{1,0:T(8,128)(2,1)S(1)} %get-tuple-element.27), channel_id=1, source_target_pairs={{0,16},{16,0},{32,48},{48,32},{64,80},{80,64},{96,112},{112,96},{1... | collective-permute-start | bytes 1179656 | tf_op jit(solution)/shard_map/ppermute | solution.py:46
  28.6 5.7 %collective-permute-start.1 = (bf16[192,256]{1,0:T(8,128)(2,1)S(1)}, bf16[192,256]{1,0:T(8,128)(2,1)S(1)}, u32[]{:S(2)}, u32[]{:S(2)}) collective-permute-start(bf16[192,256]{1,0:T(8,128)(2,1)S(1)} %get-tuple-element.33), channel_id=1, source_target_pairs={{0,32},{16,48},{32,64},{48,80},{64,96},{80,112},{96,0},{112,16},{1... | collective-permute-start | bytes 294920 | tf_op jit(solution)/shard_map/ppermute | solution.py:46
  29.9 4.4 %collective-permute-start.2 = (bf16[192,256]{1,0:T(8,128)(2,1)S(1)}, bf16[192,256]{1,0:T(8,128)(2,1)S(1)}, u32[]{:S(2)}, u32[]{:S(2)}) collective-permute-start(bf16[192,256]{1,0:T(8,128)(2,1)S(1)} %get-tuple-element.34), channel_id=1, source_target_pairs={{0,96},{16,112},{32,0},{48,16},{64,32},{80,48},{96,64},{112,80},{1... | collective-permute-start | bytes 294920 | tf_op jit(solution)/shard_map/ppermute | solution.py:46
  31.4 5.1 %collective-permute-start.3 = (bf16[192,256]{1,0:T(8,128)(2,1)S(1)}, bf16[192,256]{1,0:T(8,128)(2,1)S(1)}, u32[]{:S(2)}, u32[]{:S(2)}) collective-permute-start(bf16[192,256]{1,0:T(8,128)(2,1)S(1)} %get-tuple-element.35), channel_id=1, source_target_pairs={{0,64},{16,80},{32,96},{48,112},{64,0},{80,16},{96,32},{112,48},{1... | collective-permute-start | bytes 294920 | tf_op jit(solution)/shard_map/ppermute | solution.py:46
  36.5 5.1 %collective-permute-start.5 = (bf16[192,256]{1,0:T(8,128)(2,1)S(1)}, bf16[192,256]{1,0:T(8,128)(2,1)S(1)}, u32[]{:S(2)}, u32[]{:S(2)}) collective-permute-start(bf16[192,256]{1,0:T(8,128)(2,1)S(1)} %shard_map.43.refs_0_), channel_id=1, source_target_pairs={{0,64},{16,80},{32,96},{48,112},{64,0},{80,16},{96,32},{112,48},{1... | collective-permute-start | bytes 294920 | tf_op jit(solution)/shard_map/ppermute | solution.py:46
  38.0 6.7 %collective-permute-start.6 = (bf16[192,256]{1,0:T(8,128)(2,1)S(1)}, bf16[192,256]{1,0:T(8,128)(2,1)S(1)}, u32[]{:S(2)}, u32[]{:S(2)}) collective-permute-start(bf16[192,256]{1,0:T(8,128)(2,1)S(1)} %shard_map.43.refs_0_), channel_id=1, source_target_pairs={{0,32},{16,48},{32,64},{48,80},{64,96},{80,112},{96,0},{112,16},{1... | collective-permute-start | bytes 294920 | tf_op jit(solution)/shard_map/ppermute | solution.py:46
  38.7 6.0 %collective-permute-start.4 = (bf16[192,256]{1,0:T(8,128)(2,1)S(1)}, bf16[192,256]{1,0:T(8,128)(2,1)S(1)}, u32[]{:S(2)}, u32[]{:S(2)}) collective-permute-start(bf16[192,256]{1,0:T(8,128)(2,1)S(1)} %shard_map.43.refs_0_), channel_id=1, source_target_pairs={{0,96},{16,112},{32,0},{48,16},{64,32},{80,48},{96,64},{112,80},{1... | collective-permute-start | bytes 294920 | tf_op jit(solution)/shard_map/ppermute | solution.py:46
  41.6 21.7 %collective-permute-start.10 = (bf16[768,256]{1,0:T(8,128)(2,1)S(1)}, bf16[768,256]{1,0:T(8,128)(2,1)S(1)}, u32[]{:S(2)}, u32[]{:S(2)}) collective-permute-start(bf16[768,256]{1,0:T(8,128)(2,1)S(1)} %get-tuple-element.41), channel_id=1, source_target_pairs={{0,32},{16,48},{32,64},{48,80},{64,96},{80,112},{96,0},{112,16},{1... | collective-permute-start | bytes 1179656 | tf_op jit(solution)/shard_map/ppermute | solution.py:46
  42.9 20.4 %collective-permute-start.9 = (bf16[768,256]{1,0:T(8,128)(2,1)S(1)}, bf16[768,256]{1,0:T(8,128)(2,1)S(1)}, u32[]{:S(2)}, u32[]{:S(2)}) collective-permute-start(bf16[768,256]{1,0:T(8,128)(2,1)S(1)} %get-tuple-element.41), channel_id=1, source_target_pairs={{0,96},{16,112},{32,0},{48,16},{64,32},{80,48},{96,64},{112,80},{1... | collective-permute-start | bytes 1179656 | tf_op jit(solution)/shard_map/ppermute | solution.py:46
  44.3 19.1 %collective-permute-start.11 = (bf16[768,256]{1,0:T(8,128)(2,1)S(1)}, bf16[768,256]{1,0:T(8,128)(2,1)S(1)}, u32[]{:S(2)}, u32[]{:S(2)}) collective-permute-start(bf16[768,256]{1,0:T(8,128)(2,1)S(1)} %get-tuple-element.42.early_ref), channel_id=1, source_target_pairs={{0,64},{16,80},{32,96},{48,112},{64,0},{80,16},{96,32},{112,48},{1... | collective-permute-start | bytes 1179656 | tf_op jit(solution)/shard_map/ppermute | solution.py:46
  44.7 5.4 %collective-permute-start.8 = (bf16[576,256]{1,0:T(8,128)(2,1)S(1)}, bf16[576,256]{1,0:T(8,128)(2,1)S(1)}, u32[]{:S(2)}, u32[]{:S(2)}) collective-permute-start(bf16[576,256]{1,0:T(8,128)(2,1)S(1)} %pad_maximum_fusion), channel_id=1, source_target_pairs={{0,16},{16,0},{32,48},{48,32},{64,80},{80,64},{96,112},{112,96},{1... | collective-permute-start | bytes 884744 | tf_op jit(solution)/shard_map/ppermute | solution.py:46
  48.7 1.3 %collective-permute-start.7 = (bf16[192,256]{1,0:T(8,128)(2,1)S(1)}, bf16[192,256]{1,0:T(8,128)(2,1)S(1)}, u32[]{:S(2)}, u32[]{:S(2)}) collective-permute-start(bf16[192,256]{1,0:T(8,128)(2,1)S(1)} %shard_map.43.refs_0_), channel_id=1, source_target_pairs={{0,16},{16,0},{32,48},{48,32},{64,80},{80,64},{96,112},{112,96},{1... | collective-permute-start | bytes 294920 | tf_op jit(solution)/shard_map/ppermute | solution.py:46
  55.7 13.1 %all-to-all-start.1 = ((bf16[16,48,256]{2,1,0:T(8,128)(2,1)}), bf16[16,48,256]{2,1,0:T(8,128)(2,1)S(1)}, u32[]{:S(2)}, u32[]{:S(2)}) async-start(bf16[16,48,256]{2,1,0:T(8,128)(2,1)} %bitcast.2), calls=%async_computation.1 | async-start | bytes 786432 | tf_op jit(solution)/shard_map/all_to_all | solution.py:342
  59.4 1.7 %copy-start = (bf16[2,768,768]{2,1,0:T(8,128)(2,1)S(1)}, bf16[2,768,768]{2,1,0:T(8,128)(2,1)}, u32[]{:S(2)}) copy-start(bf16[2,768,768]{2,1,0:T(8,128)(2,1)} %get-tuple-element.37.polys_ref) | copy-start | bytes 7077892
  61.1 2.2 %copy-start.1 = (bf16[2,768,768]{2,1,0:T(8,128)(2,1)S(1)}, bf16[2,768,768]{2,1,0:T(8,128)(2,1)}, u32[]{:S(2)}) copy-start(bf16[2,768,768]{2,1,0:T(8,128)(2,1)} %get-tuple-element.37.polys_ref) | copy-start | bytes 7077892
  68.8 28.0 %all-to-all-start.2 = ((bf16[16,48,1024]{2,1,0:T(8,128)(2,1)}), bf16[16,48,1024]{2,1,0:T(8,128)(2,1)S(1)}, u32[]{:S(2)}, u32[]{:S(2)}) async-start(bf16[16,48,1024]{2,1,0:T(8,128)(2,1)} %bitcast.3), calls=%async_computation.2 | async-start | bytes 3145728 | tf_op jit(solution)/shard_map/all_to_all | solution.py:342
  72.8 10.7 %collective-permute-start.14 = (bf16[16,48,256]{2,1,0:T(8,128)(2,1)S(1)}, bf16[16,48,256]{2,1,0:T(8,128)(2,1)S(1)}, u32[]{:S(2)}, u32[]{:S(2)}) collective-permute-start(bf16[16,48,256]{2,1,0:T(8,128)(2,1)S(1)} %all-to-all-done.1.refs_0_), channel_id=1, source_target_pairs={{0,32},{16,48},{32,64},{48,80},{64,96},{80,112},{96,0},{112,16},{1... | collective-permute-start | bytes 1179656 | tf_op jit(solution)/shard_map/ppermute | solution.py:46
  73.5 13.2 %collective-permute-start.13 = (bf16[16,48,256]{2,1,0:T(8,128)(2,1)S(1)}, bf16[16,48,256]{2,1,0:T(8,128)(2,1)S(1)}, u32[]{:S(2)}, u32[]{:S(2)}) collective-permute-start(bf16[16,48,256]{2,1,0:T(8,128)(2,1)S(1)} %all-to-all-done.1.refs_0_), channel_id=1, source_target_pairs={{0,96},{16,112},{32,0},{48,16},{64,32},{80,48},{96,64},{112,80},{1... | collective-permute-start | bytes 1179656 | tf_op jit(solution)/shard_map/ppermute | solution.py:46
  75.5 11.8 %collective-permute-start.15 = (bf16[16,48,256]{2,1,0:T(8,128)(2,1)S(1)}, bf16[16,48,256]{2,1,0:T(8,128)(2,1)S(1)}, u32[]{:S(2)}, u32[]{:S(2)}) collective-permute-start(bf16[16,48,256]{2,1,0:T(8,128)(2,1)S(1)} %all-to-all-done.1.refs_0_), channel_id=1, source_target_pairs={{0,16},{16,0},{32,48},{48,32},{64,80},{80,64},{96,112},{112,96},{1... | collective-permute-start | bytes 1179656 | tf_op jit(solution)/shard_map/ppermute | solution.py:46
  77.3 15.2 %collective-permute-start.12 = (bf16[16,48,256]{2,1,0:T(8,128)(2,1)S(1)}, bf16[16,48,256]{2,1,0:T(8,128)(2,1)S(1)}, u32[]{:S(2)}, u32[]{:S(2)}) collective-permute-start(bf16[16,48,256]{2,1,0:T(8,128)(2,1)S(1)} %all-to-all-done.1.refs_0_), channel_id=1, source_target_pairs={{0,64},{16,80},{32,96},{48,112},{64,0},{80,16},{96,32},{112,48},{1... | collective-permute-start | bytes 1179656 | tf_op jit(solution)/shard_map/ppermute | solution.py:46
  83.5 11.2 %collective-permute-start.18 = (bf16[16,48,256]{2,1,0:T(8,128)(2,1)S(1)}, bf16[16,48,256]{2,1,0:T(8,128)(2,1)S(1)}, u32[]{:S(2)}, u32[]{:S(2)}) collective-permute-start(bf16[16,48,256]{2,1,0:T(8,128)(2,1)S(1)} %collective-permute-done.14.refs_2_), channel_id=1, source_target_pairs={{0,16},{16,0},{32,48},{48,32},{64,80},{80,64},{96,112},{112,96},{1... | collective-permute-start | bytes 1179656 | tf_op jit(solution)/shard_map/ppermute | solution.py:46
  86.7 8.0 %collective-permute-start.17 = (bf16[16,48,256]{2,1,0:T(8,128)(2,1)S(1)}, bf16[16,48,256]{2,1,0:T(8,128)(2,1)S(1)}, u32[]{:S(2)}, u32[]{:S(2)}) collective-permute-start(bf16[16,48,256]{2,1,0:T(8,128)(2,1)S(1)} %collective-permute-done.13.refs_1_), channel_id=1, source_target_pairs={{0,16},{16,0},{32,48},{48,32},{64,80},{80,64},{96,112},{112,96},{1... | collective-permute-start | bytes 1179656 | tf_op jit(solution)/shard_map/ppermute | solution.py:46
  92.5 3.5 %collective-permute-start.16 = (bf16[16,48,256]{2,1,0:T(8,128)(2,1)S(1)}, bf16[16,48,256]{2,1,0:T(8,128)(2,1)S(1)}, u32[]{:S(2)}, u32[]{:S(2)}) collective-permute-start(bf16[16,48,256]{2,1,0:T(8,128)(2,1)S(1)} %collective-permute-done.12.refs_2_), channel_id=1, source_target_pairs={{0,16},{16,0},{32,48},{48,32},{64,80},{80,64},{96,112},{112,96},{1... | collective-permute-start | bytes 1179656 | tf_op jit(solution)/shard_map/ppermute | solution.py:46
  97.0 3.3 %collective-permute-start.20 = (bf16[16,48,512]{2,1,0:T(8,128)(2,1)S(1)}, bf16[16,48,512]{2,1,0:T(8,128)(2,1)S(1)}, u32[]{:S(2)}, u32[]{:S(2)}) collective-permute-start(bf16[16,48,512]{2,1,0:T(8,128)(2,1)S(1)} %get-tuple-element.50), channel_id=1, source_target_pairs={{0,16},{16,0},{32,48},{48,32},{64,80},{80,64},{96,112},{112,96},{1... | collective-permute-start | bytes 2359304 | tf_op jit(solution)/shard_map/ppermute | solution.py:46
  98.4 3.0 %collective-permute-start.19 = (bf16[16,48,512]{2,1,0:T(8,128)(2,1)S(1)}, bf16[16,48,512]{2,1,0:T(8,128)(2,1)S(1)}, u32[]{:S(2)}, u32[]{:S(2)}) collective-permute-start(bf16[16,48,512]{2,1,0:T(8,128)(2,1)S(1)} %get-tuple-element.51), channel_id=1, source_target_pairs={{0,16},{16,0},{32,48},{48,32},{64,80},{80,64},{96,112},{112,96},{1... | collective-permute-start | bytes 2359304 | tf_op jit(solution)/shard_map/ppermute | solution.py:46

commit v8 on v7

--- a/solution.py
+++ b/solution.py
@@ -372,10 +372,7 @@
     update = place(update, shape, [late_place(late_across, steps, 1) for steps in (2,)])
     second, update = lax.optimization_barrier((second, update))
     update = place(update, shape, early_places(second, 0, 0, SECOND))
-    middle = EARLY + NEAR
-    for left, right in ((0, middle), (middle, SECOND)):
-        across = shift(second[:, :, left:right], 0, 1)
-        update = place(update, shape, early_places(across, 1, left, right))
+    update = place(update, shape, early_places(shift(second, 0, 1), 1, 0, SECOND))
     return (update.reshape(experts, pairs, row_count, 8 * WIDTH), new_momentum)
 
 

time: 103 us -> 103 us (level)
    ppermute x21 -> x20, waiting for transfers between devices: 15.2 us -> 16.2 us  [shift(): return lax.ppermute(value, 'replica', pairs)]
    pallas_call x6 -> x5, Pallas kernels: 5.9 us -> 5.28 us  [place(): pl.pallas_call(functools.partial(place_kernel, where, int(aliased)), out_...]
    ppermute x21 -> x20, starting transfers between devices: 31.3 us -> 31.1 us  [shift(): return lax.ppermute(value, 'replica', pairs)]
  transfers between devices with their start and end apart: 23 -> 22, of which waited for: 10 -> 9; matrix products, arithmetic and copies ran while one was open for 1% -> 1% of each run, Pallas kernels for 15% -> 15%
where the time goes in v8:
time: 103 us; the launch traced here: 102 us
  starting transfers between devices  38.9 us (38%)
  blocking collectives  22 us (21%)
  waiting for transfers between devices  18.6 us (18%)
  Pallas kernels  16.8 us (16%)
  other arithmetic  3.4 us (3%)
  local copies, waits for them, and re-layouts  1.68 us (2%)
    ppermute x20, starting transfers between devices, shift(): return lax.ppermute(value, 'replica', pairs)  31.1 us
    all_to_all x1, blocking collectives, local(): lax.all_to_all(flat_rows, 'tensor', split_axis=0, concat_axis=0, tiled=True)  22 us
    ppermute x20, waiting for transfers between devices, shift(): return lax.ppermute(value, 'replica', pairs)  16.2 us
    all_to_all x2, starting transfers between devices, back(): lax.all_to_all(value, 'tensor', split_axis=0, concat_axis=0, tiled=True)  7.76 us
    pallas_call x1, Pallas kernels, chain(): pl.pallas_call(chain_kernel, out_shape=(jax.ShapeDtypeStruct((FF, FIRST),...  5.59 us
    pallas_call x5, Pallas kernels, place(): pl.pallas_call(functools.partial(place_kernel, where, int(aliased)), out_...  5.28 us
    pallas_call x1, Pallas kernels, early_products(): pl.pallas_call(other_kernel, out_shape=out, in_specs=[VMEM] * 5 + [HBM],...  3 us
    all_to_all x2, waiting for transfers between devices, back(): lax.all_to_all(value, 'tensor', split_axis=0, concat_axis=0, tiled=True)  2.43 us
  transfers between devices with their start and end apart: 22, of which 9 were waited for; matrix products, arithmetic and copies ran while one was open for 1% of the time, Pallas kernels for 15%

profile of v8, /device:TPU:1, one launch (start us, length us, event | category | flops | bytes accessed | tf_op | source)
XLA Modules:
  0.0 102.4 jit_solution(7585909015186952982)
XLA Ops:
  0.6 2.0 %fusion.1 = bf16[8,2,48,512]{3,2,1,0:T(8,128)(2,1)S(1)} fusion(bf16[8,2,48,512]{3,2,1,0:T(8,128)(2,1)} %param.2, f32[8,2,48,512]{3,2,1,0:T(8,128)} %param.3), kind=kLoop, calls=%fused_computation.3 | loop fusion | flops 2359296 | bytes 3145728 | tf_op jit(solution)/shard_map/convert_element_type | solution.py:326
  2.6 0.0 copy-start.2
  2.6 0.0 copy-start.3
  2.6 22.0 %all_to_all.15 = bf16[16,48,512]{2,1,0:T(8,128)(2,1)S(1)} all-to-all(bf16[16,48,512]{2,1,0:T(8,128)(2,1)S(1)} %bitcast.8), channel_id=1, replica_groups=mesh['replica'=8,'tensor'=16] {'tensor'}, dimensions={0} | all-to-all | bytes 1572864 | tf_op jit(solution)/shard_map/all_to_all | solution.py:327
  24.7 0.7 shard_map.41
  25.3 1.9 %collective-permute-start = (bf16[768,256]{1,0:T(8,128)(2,1)S(1)}, bf16[768,256]{1,0:T(8,128)(2,1)S(1)}, u32[]{:S(2)}, u32[]{:S(2)}) collective-permute-start(bf16[768,256]{1,0:T(8,128)(2,1)S(1)} %get-tuple-element.27), channel_id=1, source_target_pairs={{0,16},{16,0},{32,48},{48,32},{64,80},{80,64},{96,112},{112,96},{1... | collective-permute-start | bytes 1179656 | tf_op jit(solution)/shard_map/ppermute | solution.py:46
  27.2 1.3 %collective-permute-done.got_ref = bf16[768,256]{1,0:T(8,128)(2,1)S(1)} collective-permute-done((bf16[768,256]{1,0:T(8,128)(2,1)S(1)}, bf16[768,256]{1,0:T(8,128)(2,1)S(1)}, u32[]{:S(2)}, u32[]{:S(2)}) %collective-permute-start) | collective-permute-done | bytes 393248 | tf_op jit(solution)/shard_map/ppermute | solution.py:46
  28.5 0.1 shard_map.42
  28.6 1.3 %collective-permute-start.1 = (bf16[192,256]{1,0:T(8,128)(2,1)S(1)}, bf16[192,256]{1,0:T(8,128)(2,1)S(1)}, u32[]{:S(2)}, u32[]{:S(2)}) collective-permute-start(bf16[192,256]{1,0:T(8,128)(2,1)S(1)} %get-tuple-element.33), channel_id=1, source_target_pairs={{0,32},{16,48},{32,64},{48,80},{64,96},{80,112},{96,0},{112,16},{1... | collective-permute-start | bytes 294920 | tf_op jit(solution)/shard_map/ppermute | solution.py:46
  29.9 1.5 %collective-permute-start.2 = (bf16[192,256]{1,0:T(8,128)(2,1)S(1)}, bf16[192,256]{1,0:T(8,128)(2,1)S(1)}, u32[]{:S(2)}, u32[]{:S(2)}) collective-permute-start(bf16[192,256]{1,0:T(8,128)(2,1)S(1)} %get-tuple-element.34), channel_id=1, source_target_pairs={{0,96},{16,112},{32,0},{48,16},{64,32},{80,48},{96,64},{112,80},{1... | collective-permute-start | bytes 294920 | tf_op jit(solution)/shard_map/ppermute | solution.py:46
  31.4 1.5 %collective-permute-start.3 = (bf16[192,256]{1,0:T(8,128)(2,1)S(1)}, bf16[192,256]{1,0:T(8,128)(2,1)S(1)}, u32[]{:S(2)}, u32[]{:S(2)}) collective-permute-start(bf16[192,256]{1,0:T(8,128)(2,1)S(1)} %get-tuple-element.35), channel_id=1, source_target_pairs={{0,64},{16,80},{32,96},{48,112},{64,0},{80,16},{96,32},{112,48},{1... | collective-permute-start | bytes 294920 | tf_op jit(solution)/shard_map/ppermute | solution.py:46
  32.9 1.4 %convert_add_fusion.2 = f32[8,2,48,512]{3,2,1,0:T(8,128)} fusion(bf16[8,2,48,512]{3,2,1,0:T(8,128)(2,1)S(1)} %copy-done.3, f32[8,2,48,512]{3,2,1,0:T(8,128)S(1)} %copy-done.2), kind=kLoop, calls=%fused_computation.4 | loop fusion | flops 1179648 | bytes 3932160 | tf_op jit(solution)/shard_map/add | solution.py:322
  34.3 2.1 %collective-permute-done.3.c_ref = bf16[192,256]{1,0:T(8,128)(2,1)S(1)} collective-permute-done((bf16[192,256]{1,0:T(8,128)(2,1)S(1)}, bf16[192,256]{1,0:T(8,128)(2,1)S(1)}, u32[]{:S(2)}, u32[]{:S(2)}) %collective-permute-start.3) | collective-permute-done | bytes 98336 | tf_op jit(solution)/shard_map/ppermute | solution.py:46
  36.5 1.5 %collective-permute-start.5 = (bf16[192,256]{1,0:T(8,128)(2,1)S(1)}, bf16[192,256]{1,0:T(8,128)(2,1)S(1)}, u32[]{:S(2)}, u32[]{:S(2)}) collective-permute-start(bf16[192,256]{1,0:T(8,128)(2,1)S(1)} %shard_map.43.refs_0_), channel_id=1, source_target_pairs={{0,64},{16,80},{32,96},{48,112},{64,0},{80,16},{96,32},{112,48},{1... | collective-permute-start | bytes 294920 | tf_op jit(solution)/shard_map/ppermute | solution.py:46
  38.0 0.7 collective-permute-start.6
  38.7 2.0 %collective-permute-start.4 = (bf16[192,256]{1,0:T(8,128)(2,1)S(1)}, bf16[192,256]{1,0:T(8,128)(2,1)S(1)}, u32[]{:S(2)}, u32[]{:S(2)}) collective-permute-start(bf16[192,256]{1,0:T(8,128)(2,1)S(1)} %shard_map.43.refs_0_), channel_id=1, source_target_pairs={{0,96},{16,112},{32,0},{48,16},{64,32},{80,48},{96,64},{112,80},{1... | collective-permute-start | bytes 294920 | tf_op jit(solution)/shard_map/ppermute | solution.py:46
  40.7 0.9 collective-permute-done.5.refs_2_
  41.6 1.3 %collective-permute-start.10 = (bf16[768,256]{1,0:T(8,128)(2,1)S(1)}, bf16[768,256]{1,0:T(8,128)(2,1)S(1)}, u32[]{:S(2)}, u32[]{:S(2)}) collective-permute-start(bf16[768,256]{1,0:T(8,128)(2,1)S(1)} %get-tuple-element.41), channel_id=1, source_target_pairs={{0,32},{16,48},{32,64},{48,80},{64,96},{80,112},{96,0},{112,16},{1... | collective-permute-start | bytes 1179656 | tf_op jit(solution)/shard_map/ppermute | solution.py:46
  42.9 1.4 %collective-permute-start.9 = (bf16[768,256]{1,0:T(8,128)(2,1)S(1)}, bf16[768,256]{1,0:T(8,128)(2,1)S(1)}, u32[]{:S(2)}, u32[]{:S(2)}) collective-permute-start(bf16[768,256]{1,0:T(8,128)(2,1)S(1)} %get-tuple-element.41), channel_id=1, source_target_pairs={{0,96},{16,112},{32,0},{48,16},{64,32},{80,48},{96,64},{112,80},{1... | collective-permute-start | bytes 1179656 | tf_op jit(solution)/shard_map/ppermute | solution.py:46
  44.3 0.4 collective-permute-start.11
  44.7 4.0 %collective-permute-start.8 = (bf16[576,256]{1,0:T(8,128)(2,1)S(1)}, bf16[576,256]{1,0:T(8,128)(2,1)S(1)}, u32[]{:S(2)}, u32[]{:S(2)}) collective-permute-start(bf16[576,256]{1,0:T(8,128)(2,1)S(1)} %pad_maximum_fusion), channel_id=1, source_target_pairs={{0,16},{16,0},{32,48},{48,32},{64,80},{80,64},{96,112},{112,96},{1... | collective-permute-start | bytes 884744 | tf_op jit(solution)/shard_map/ppermute | solution.py:46
  48.7 0.1 collective-permute-start.7
  48.8 1.3 %collective-permute-done.7.refs_4_ = bf16[192,256]{1,0:T(8,128)(2,1)S(1)} collective-permute-done((bf16[192,256]{1,0:T(8,128)(2,1)S(1)}, bf16[192,256]{1,0:T(8,128)(2,1)S(1)}, u32[]{:S(2)}, u32[]{:S(2)}) %collective-permute-start.7) | collective-permute-done | bytes 98336 | tf_op jit(solution)/shard_map/ppermute | solution.py:46
  50.1 5.6 %shard_map.44 = (bf16[768,256]{1,0:T(8,128)(2,1)}, bf16[2,768,768]{2,1,0:T(8,128)(2,1)}, f32[8,128]{1,0:T(8,128)S(1)}) custom-call(bf16[192,256]{1,0:T(8,128)(2,1)S(1)} %shard_map.43.refs_0_, bf16[192,256]{1,0:T(8,128)(2,1)S(1)} %collective-permute-done.4.refs_1_, bf16[192,256]{1,0:T(8,128)(2,1)S(1)} %collective-permute-done.5.refs_2_, ...), custom_call_target="tpu_custom_call" | custom-call | tf_op jit(solution)/shard_map/pallas_call | solution.py:195
  55.7 3.7 %all-to-all-start.1 = ((bf16[16,48,256]{2,1,0:T(8,128)(2,1)}), bf16[16,48,256]{2,1,0:T(8,128)(2,1)S(1)}, u32[]{:S(2)}, u32[]{:S(2)}) async-start(bf16[16,48,256]{2,1,0:T(8,128)(2,1)} %bitcast.2), calls=%async_computation.1 | async-start | bytes 786432 | tf_op jit(solution)/shard_map/all_to_all | solution.py:342
  59.4 0.0 copy-start
  59.4 1.7 %copy-done = bf16[2,768,768]{2,1,0:T(8,128)(2,1)S(1)} copy-done((bf16[2,768,768]{2,1,0:T(8,128)(2,1)S(1)}, bf16[2,768,768]{2,1,0:T(8,128)(2,1)}, u32[]{:S(2)}) %copy-start) | copy-done | bytes 2359320
  61.1 2.2 %shard_map.45.refs_3_ = bf16[768,1024]{1,0:T(8,128)(2,1)} custom-call(bf16[2,768,768]{2,1,0:T(8,128)(2,1)S(1)} %copy-done, f32[8,128]{1,0:T(8,128)S(1)} %get-tuple-element.38.scale_ref, bf16[768,256]{1,0:T(8,128)(2,1)S(1)} %get-tuple-element.42.early_ref), custom_call_target="tpu_custom_call" | custom-call | tf_op jit(solution)/shard_map/pallas_call | solution.py:256
  63.3 3.0 %shard_map.46 = bf16[768,1024]{1,0:T(8,128)(2,1)} custom-call(bf16[2,768,768]{2,1,0:T(8,128)(2,1)S(1)} %copy-done.1, f32[8,128]{1,0:T(8,128)S(1)} %get-tuple-element.38.scale_ref, bf16[768,256]{1,0:T(8,128)(2,1)S(1)} %collective-permute-done.9.refs_0_, bf16[768,256]{1,0:T(8,128)(2,1)S(1)} %collective-permute-done.10.refs_1_, ...), custom_call_target="tpu_custom_call", output_to_operand_aliasing={{}: (5, {})} | custom-call | flops 20000000000 | tf_op jit(solution)/shard_map/pallas_call | solution.py:265
  66.3 2.4 %all-to-all-done.1.refs_0_ = bf16[16,48,256]{2,1,0:T(8,128)(2,1)S(1)} async-done(((bf16[16,48,256]{2,1,0:T(8,128)(2,1)}), bf16[16,48,256]{2,1,0:T(8,128)(2,1)S(1)}, u32[]{:S(2)}, u32[]{:S(2)}) %all-to-all-start.1) | async-done | bytes 393248 | tf_op jit(solution)/shard_map/all_to_all | solution.py:342
  68.8 4.0 %all-to-all-start.2 = ((bf16[16,48,1024]{2,1,0:T(8,128)(2,1)}), bf16[16,48,1024]{2,1,0:T(8,128)(2,1)S(1)}, u32[]{:S(2)}, u32[]{:S(2)}) async-start(bf16[16,48,1024]{2,1,0:T(8,128)(2,1)} %bitcast.3), calls=%async_computation.2 | async-start | bytes 3145728 | tf_op jit(solution)/shard_map/all_to_all | solution.py:342
  72.8 0.7 collective-permute-start.14
  73.5 2.0 %collective-permute-start.13 = (bf16[16,48,256]{2,1,0:T(8,128)(2,1)S(1)}, bf16[16,48,256]{2,1,0:T(8,128)(2,1)S(1)}, u32[]{:S(2)}, u32[]{:S(2)}) collective-permute-start(bf16[16,48,256]{2,1,0:T(8,128)(2,1)S(1)} %all-to-all-done.1.refs_0_), channel_id=1, source_target_pairs={{0,96},{16,112},{32,0},{48,16},{64,32},{80,48},{96,64},{112,80},{1... | collective-permute-start | bytes 1179656 | tf_op jit(solution)/shard_map/ppermute | solution.py:46
  75.5 1.8 %collective-permute-start.15 = (bf16[16,48,256]{2,1,0:T(8,128)(2,1)S(1)}, bf16[16,48,256]{2,1,0:T(8,128)(2,1)S(1)}, u32[]{:S(2)}, u32[]{:S(2)}) collective-permute-start(bf16[16,48,256]{2,1,0:T(8,128)(2,1)S(1)} %all-to-all-done.1.refs_0_), channel_id=1, source_target_pairs={{0,16},{16,0},{32,48},{48,32},{64,80},{80,64},{96,112},{112,96},{1... | collective-permute-start | bytes 1179656 | tf_op jit(solution)/shard_map/ppermute | solution.py:46
  77.3 1.8 %collective-permute-start.12 = (bf16[16,48,256]{2,1,0:T(8,128)(2,1)S(1)}, bf16[16,48,256]{2,1,0:T(8,128)(2,1)S(1)}, u32[]{:S(2)}, u32[]{:S(2)}) collective-permute-start(bf16[16,48,256]{2,1,0:T(8,128)(2,1)S(1)} %all-to-all-done.1.refs_0_), channel_id=1, source_target_pairs={{0,64},{16,80},{32,96},{48,112},{64,0},{80,16},{96,32},{112,48},{1... | collective-permute-start | bytes 1179656 | tf_op jit(solution)/shard_map/ppermute | solution.py:46
  79.1 4.4 %collective-permute-done.14.refs_2_ = bf16[16,48,256]{2,1,0:T(8,128)(2,1)S(1)} collective-permute-done((bf16[16,48,256]{2,1,0:T(8,128)(2,1)S(1)}, bf16[16,48,256]{2,1,0:T(8,128)(2,1)S(1)}, u32[]{:S(2)}, u32[]{:S(2)}) %collective-permute-start.14) | collective-permute-done | bytes 393248 | tf_op jit(solution)/shard_map/ppermute | solution.py:46
  83.5 3.2 %collective-permute-start.18 = (bf16[16,48,256]{2,1,0:T(8,128)(2,1)S(1)}, bf16[16,48,256]{2,1,0:T(8,128)(2,1)S(1)}, u32[]{:S(2)}, u32[]{:S(2)}) collective-permute-start(bf16[16,48,256]{2,1,0:T(8,128)(2,1)S(1)} %collective-permute-done.14.refs_2_), channel_id=1, source_target_pairs={{0,16},{16,0},{32,48},{48,32},{64,80},{80,64},{96,112},{112,96},{1... | collective-permute-start | bytes 1179656 | tf_op jit(solution)/shard_map/ppermute | solution.py:46
  86.7 0.7 collective-permute-start.17
  87.3 1.2 %shard_map.47.refs_3_ = bf16[16,48,4096]{2,1,0:T(8,128)(2,1)} custom-call(bf16[16,48,256]{2,1,0:T(8,128)(2,1)S(1)} %all-to-all-done.1.refs_0_, bf16[16,48,256]{2,1,0:T(8,128)(2,1)S(1)} %collective-permute-done.13.refs_1_, bf16[16,48,256]{2,1,0:T(8,128)(2,1)S(1)} %collective-permute-done.14.refs_2_, bf16[16,48,256]{2,1,0:T(8,128)(2,1)S(1)} %collective-permute-done.15.refs_3_), custom_call_target="tpu_custom_call" | custom-call | tf_op jit(solution)/shard_map/pallas_call | solution.py:308
  88.5 4.0 %collective-permute-done.12.refs_2_ = bf16[16,48,256]{2,1,0:T(8,128)(2,1)S(1)} collective-permute-done((bf16[16,48,256]{2,1,0:T(8,128)(2,1)S(1)}, bf16[16,48,256]{2,1,0:T(8,128)(2,1)S(1)}, u32[]{:S(2)}, u32[]{:S(2)}) %collective-permute-start.12) | collective-permute-done | bytes 393248 | tf_op jit(solution)/shard_map/ppermute | solution.py:46
  92.5 2.1 %collective-permute-start.16 = (bf16[16,48,256]{2,1,0:T(8,128)(2,1)S(1)}, bf16[16,48,256]{2,1,0:T(8,128)(2,1)S(1)}, u32[]{:S(2)}, u32[]{:S(2)}) collective-permute-start(bf16[16,48,256]{2,1,0:T(8,128)(2,1)S(1)} %collective-permute-done.12.refs_2_), channel_id=1, source_target_pairs={{0,16},{16,0},{32,48},{48,32},{64,80},{80,64},{96,112},{112,96},{1... | collective-permute-start | bytes 1179656 | tf_op jit(solution)/shard_map/ppermute | solution.py:46
  94.7 1.0 %shard_map.48.refs_1_ = bf16[16,48,4096]{2,1,0:T(8,128)(2,1)} custom-call(bf16[16,48,256]{2,1,0:T(8,128)(2,1)S(1)} %collective-permute-done.17.refs_0_, bf16[16,48,256]{2,1,0:T(8,128)(2,1)S(1)} %collective-permute-done.18.refs_1_, bf16[16,48,256]{2,1,0:T(8,128)(2,1)S(1)} %collective-permute-done.12.refs_2_, ...), custom_call_target="tpu_custom_call", output_to_operand_aliasing={{}: (3, {})} | custom-call | tf_op jit(solution)/shard_map/pallas_call | solution.py:308
  95.7 0.3 collective-permute-done.16.refs_0_
  96.0 0.8 shard_map.49.refs_4_
  96.8 1.3 %collective-permute-start.19 = (bf16[16,48,1024]{2,1,0:T(8,128)(2,1)S(1)}, bf16[16,48,1024]{2,1,0:T(8,128)(2,1)S(1)}, u32[]{:S(2)}, u32[]{:S(2)}) collective-permute-start(bf16[16,48,1024]{2,1,0:T(8,128)(2,1)S(1)} %all-to-all-done.2.refs_0_.refs_1_.refs_2_.refs_3_), channel_id=1, source_target_pairs={{0,16},{16,0},{32,48},{48,32},{64,80},{80,64},{96,112},{112,96},{1... | collective-permute-start | bytes 4718600 | tf_op jit(solution)/shard_map/ppermute | solution.py:46
  98.1 1.2 %shard_map.50.refs_4_ = bf16[16,48,4096]{2,1,0:T(8,128)(2,1)} custom-call(bf16[16,48,1024]{2,1,0:T(8,128)(2,1)S(1)} %all-to-all-done.2.refs_0_.refs_1_.refs_2_.refs_3_, bf16[16,48,1024]{2,1,0:T(8,128)(2,1)S(1)} %all-to-all-done.2.refs_0_.refs_1_.refs_2_.refs_3_, ...), custom_call_target="tpu_custom_call", output_to_operand_aliasing={{}: (4, {})} | custom-call | tf_op jit(solution)/shard_map/pallas_call | solution.py:308
  99.3 1.9 %collective-permute-done.19.refs_0_.refs_1_.refs_2_.refs_3_ = bf16[16,48,1024]{2,1,0:T(8,128)(2,1)S(1)} collective-permute-done((bf16[16,48,1024]{2,1,0:T(8,128)(2,1)S(1)}, bf16[16,48,1024]{2,1,0:T(8,128)(2,1)S(1)}, u32[]{:S(2)}, u32[]{:S(2)}) %collective-permute-start.19) | collective-permute-done | bytes 1572896 | tf_op jit(solution)/shard_map/ppermute | solution.py:46
  101.1 1.2 %shard_map.51 = bf16[16,48,4096]{2,1,0:T(8,128)(2,1)} custom-call(bf16[16,48,1024]{2,1,0:T(8,128)(2,1)S(1)} %collective-permute-done.19.refs_0_.refs_1_.refs_2_.refs_3_, bf16[16,48,1024]{2,1,0:T(8,128)(2,1)S(1)} %collective-permute-done.19.refs_0_.refs_1_.refs_2_.refs_3_, ...), custom_call_target="tpu_custom_call", output_to_operand_aliasing={{}: (4, {})} | custom-call | tf_op jit(solution)/shard_map/pallas_call | solution.py:308
  (19 shorter events, 0.1 us)
Async XLA Ops:
  2.6 30.3 %copy-start.2 = (f32[8,2,48,512]{3,2,1,0:T(8,128)S(1)}, f32[8,2,48,512]{3,2,1,0:T(8,128)}, u32[]{:S(2)}) copy-start(f32[8,2,48,512]{3,2,1,0:T(8,128)} %param.3) | copy-start | bytes 4718596
  2.6 30.3 %copy-start.3 = (bf16[8,2,48,512]{3,2,1,0:T(8,128)(2,1)S(1)}, bf16[8,2,48,512]{3,2,1,0:T(8,128)(2,1)}, u32[]{:S(2)}) copy-start(bf16[8,2,48,512]{3,2,1,0:T(8,128)(2,1)} %param.2) | copy-start | bytes 2359300
  25.3 3.2 %collective-permute-start = (bf16[768,256]{1,0:T(8,128)(2,1)S(1)}, bf16[768,256]{1,0:T(8,128)(2,1)S(1)}, u32[]{:S(2)}, u32[]{:S(2)}) collective-permute-start(bf16[768,256]{1,0:T(8,128)(2,1)S(1)} %get-tuple-element.27), channel_id=1, source_target_pairs={{0,16},{16,0},{32,48},{48,32},{64,80},{80,64},{96,112},{112,96},{1... | collective-permute-start | bytes 1179656 | tf_op jit(solution)/shard_map/ppermute | solution.py:46
  28.6 5.7 %collective-permute-start.1 = (bf16[192,256]{1,0:T(8,128)(2,1)S(1)}, bf16[192,256]{1,0:T(8,128)(2,1)S(1)}, u32[]{:S(2)}, u32[]{:S(2)}) collective-permute-start(bf16[192,256]{1,0:T(8,128)(2,1)S(1)} %get-tuple-element.33), channel_id=1, source_target_pairs={{0,32},{16,48},{32,64},{48,80},{64,96},{80,112},{96,0},{112,16},{1... | collective-permute-start | bytes 294920 | tf_op jit(solution)/shard_map/ppermute | solution.py:46
  29.9 4.4 %collective-permute-start.2 = (bf16[192,256]{1,0:T(8,128)(2,1)S(1)}, bf16[192,256]{1,0:T(8,128)(2,1)S(1)}, u32[]{:S(2)}, u32[]{:S(2)}) collective-permute-start(bf16[192,256]{1,0:T(8,128)(2,1)S(1)} %get-tuple-element.34), channel_id=1, source_target_pairs={{0,96},{16,112},{32,0},{48,16},{64,32},{80,48},{96,64},{112,80},{1... | collective-permute-start | bytes 294920 | tf_op jit(solution)/shard_map/ppermute | solution.py:46
  31.4 5.1 %collective-permute-start.3 = (bf16[192,256]{1,0:T(8,128)(2,1)S(1)}, bf16[192,256]{1,0:T(8,128)(2,1)S(1)}, u32[]{:S(2)}, u32[]{:S(2)}) collective-permute-start(bf16[192,256]{1,0:T(8,128)(2,1)S(1)} %get-tuple-element.35), channel_id=1, source_target_pairs={{0,64},{16,80},{32,96},{48,112},{64,0},{80,16},{96,32},{112,48},{1... | collective-permute-start | bytes 294920 | tf_op jit(solution)/shard_map/ppermute | solution.py:46
  36.5 5.1 %collective-permute-start.5 = (bf16[192,256]{1,0:T(8,128)(2,1)S(1)}, bf16[192,256]{1,0:T(8,128)(2,1)S(1)}, u32[]{:S(2)}, u32[]{:S(2)}) collective-permute-start(bf16[192,256]{1,0:T(8,128)(2,1)S(1)} %shard_map.43.refs_0_), channel_id=1, source_target_pairs={{0,64},{16,80},{32,96},{48,112},{64,0},{80,16},{96,32},{112,48},{1... | collective-permute-start | bytes 294920 | tf_op jit(solution)/shard_map/ppermute | solution.py:46
  38.0 6.7 %collective-permute-start.6 = (bf16[192,256]{1,0:T(8,128)(2,1)S(1)}, bf16[192,256]{1,0:T(8,128)(2,1)S(1)}, u32[]{:S(2)}, u32[]{:S(2)}) collective-permute-start(bf16[192,256]{1,0:T(8,128)(2,1)S(1)} %shard_map.43.refs_0_), channel_id=1, source_target_pairs={{0,32},{16,48},{32,64},{48,80},{64,96},{80,112},{96,0},{112,16},{1... | collective-permute-start | bytes 294920 | tf_op jit(solution)/shard_map/ppermute | solution.py:46
  38.7 6.0 %collective-permute-start.4 = (bf16[192,256]{1,0:T(8,128)(2,1)S(1)}, bf16[192,256]{1,0:T(8,128)(2,1)S(1)}, u32[]{:S(2)}, u32[]{:S(2)}) collective-permute-start(bf16[192,256]{1,0:T(8,128)(2,1)S(1)} %shard_map.43.refs_0_), channel_id=1, source_target_pairs={{0,96},{16,112},{32,0},{48,16},{64,32},{80,48},{96,64},{112,80},{1... | collective-permute-start | bytes 294920 | tf_op jit(solution)/shard_map/ppermute | solution.py:46
  41.6 21.7 %collective-permute-start.10 = (bf16[768,256]{1,0:T(8,128)(2,1)S(1)}, bf16[768,256]{1,0:T(8,128)(2,1)S(1)}, u32[]{:S(2)}, u32[]{:S(2)}) collective-permute-start(bf16[768,256]{1,0:T(8,128)(2,1)S(1)} %get-tuple-element.41), channel_id=1, source_target_pairs={{0,32},{16,48},{32,64},{48,80},{64,96},{80,112},{96,0},{112,16},{1... | collective-permute-start | bytes 1179656 | tf_op jit(solution)/shard_map/ppermute | solution.py:46
  42.9 20.4 %collective-permute-start.9 = (bf16[768,256]{1,0:T(8,128)(2,1)S(1)}, bf16[768,256]{1,0:T(8,128)(2,1)S(1)}, u32[]{:S(2)}, u32[]{:S(2)}) collective-permute-start(bf16[768,256]{1,0:T(8,128)(2,1)S(1)} %get-tuple-element.41), channel_id=1, source_target_pairs={{0,96},{16,112},{32,0},{48,16},{64,32},{80,48},{96,64},{112,80},{1... | collective-permute-start | bytes 1179656 | tf_op jit(solution)/shard_map/ppermute | solution.py:46
  44.3 19.1 %collective-permute-start.11 = (bf16[768,256]{1,0:T(8,128)(2,1)S(1)}, bf16[768,256]{1,0:T(8,128)(2,1)S(1)}, u32[]{:S(2)}, u32[]{:S(2)}) collective-permute-start(bf16[768,256]{1,0:T(8,128)(2,1)S(1)} %get-tuple-element.42.early_ref), channel_id=1, source_target_pairs={{0,64},{16,80},{32,96},{48,112},{64,0},{80,16},{96,32},{112,48},{1... | collective-permute-start | bytes 1179656 | tf_op jit(solution)/shard_map/ppermute | solution.py:46
  44.7 5.4 %collective-permute-start.8 = (bf16[576,256]{1,0:T(8,128)(2,1)S(1)}, bf16[576,256]{1,0:T(8,128)(2,1)S(1)}, u32[]{:S(2)}, u32[]{:S(2)}) collective-permute-start(bf16[576,256]{1,0:T(8,128)(2,1)S(1)} %pad_maximum_fusion), channel_id=1, source_target_pairs={{0,16},{16,0},{32,48},{48,32},{64,80},{80,64},{96,112},{112,96},{1... | collective-permute-start | bytes 884744 | tf_op jit(solution)/shard_map/ppermute | solution.py:46
  48.7 1.3 %collective-permute-start.7 = (bf16[192,256]{1,0:T(8,128)(2,1)S(1)}, bf16[192,256]{1,0:T(8,128)(2,1)S(1)}, u32[]{:S(2)}, u32[]{:S(2)}) collective-permute-start(bf16[192,256]{1,0:T(8,128)(2,1)S(1)} %shard_map.43.refs_0_), channel_id=1, source_target_pairs={{0,16},{16,0},{32,48},{48,32},{64,80},{80,64},{96,112},{112,96},{1... | collective-permute-start | bytes 294920 | tf_op jit(solution)/shard_map/ppermute | solution.py:46
  55.7 13.1 %all-to-all-start.1 = ((bf16[16,48,256]{2,1,0:T(8,128)(2,1)}), bf16[16,48,256]{2,1,0:T(8,128)(2,1)S(1)}, u32[]{:S(2)}, u32[]{:S(2)}) async-start(bf16[16,48,256]{2,1,0:T(8,128)(2,1)} %bitcast.2), calls=%async_computation.1 | async-start | bytes 786432 | tf_op jit(solution)/shard_map/all_to_all | solution.py:342
  59.4 1.7 %copy-start = (bf16[2,768,768]{2,1,0:T(8,128)(2,1)S(1)}, bf16[2,768,768]{2,1,0:T(8,128)(2,1)}, u32[]{:S(2)}) copy-start(bf16[2,768,768]{2,1,0:T(8,128)(2,1)} %get-tuple-element.37.polys_ref) | copy-start | bytes 7077892
  61.1 2.2 %copy-start.1 = (bf16[2,768,768]{2,1,0:T(8,128)(2,1)S(1)}, bf16[2,768,768]{2,1,0:T(8,128)(2,1)}, u32[]{:S(2)}) copy-start(bf16[2,768,768]{2,1,0:T(8,128)(2,1)} %get-tuple-element.37.polys_ref) | copy-start | bytes 7077892
  68.8 28.0 %all-to-all-start.2 = ((bf16[16,48,1024]{2,1,0:T(8,128)(2,1)}), bf16[16,48,1024]{2,1,0:T(8,128)(2,1)S(1)}, u32[]{:S(2)}, u32[]{:S(2)}) async-start(bf16[16,48,1024]{2,1,0:T(8,128)(2,1)} %bitcast.3), calls=%async_computation.2 | async-start | bytes 3145728 | tf_op jit(solution)/shard_map/all_to_all | solution.py:342
  72.8 10.7 %collective-permute-start.14 = (bf16[16,48,256]{2,1,0:T(8,128)(2,1)S(1)}, bf16[16,48,256]{2,1,0:T(8,128)(2,1)S(1)}, u32[]{:S(2)}, u32[]{:S(2)}) collective-permute-start(bf16[16,48,256]{2,1,0:T(8,128)(2,1)S(1)} %all-to-all-done.1.refs_0_), channel_id=1, source_target_pairs={{0,32},{16,48},{32,64},{48,80},{64,96},{80,112},{96,0},{112,16},{1... | collective-permute-start | bytes 1179656 | tf_op jit(solution)/shard_map/ppermute | solution.py:46
  73.5 13.2 %collective-permute-start.13 = (bf16[16,48,256]{2,1,0:T(8,128)(2,1)S(1)}, bf16[16,48,256]{2,1,0:T(8,128)(2,1)S(1)}, u32[]{:S(2)}, u32[]{:S(2)}) collective-permute-start(bf16[16,48,256]{2,1,0:T(8,128)(2,1)S(1)} %all-to-all-done.1.refs_0_), channel_id=1, source_target_pairs={{0,96},{16,112},{32,0},{48,16},{64,32},{80,48},{96,64},{112,80},{1... | collective-permute-start | bytes 1179656 | tf_op jit(solution)/shard_map/ppermute | solution.py:46
  75.5 11.8 %collective-permute-start.15 = (bf16[16,48,256]{2,1,0:T(8,128)(2,1)S(1)}, bf16[16,48,256]{2,1,0:T(8,128)(2,1)S(1)}, u32[]{:S(2)}, u32[]{:S(2)}) collective-permute-start(bf16[16,48,256]{2,1,0:T(8,128)(2,1)S(1)} %all-to-all-done.1.refs_0_), channel_id=1, source_target_pairs={{0,16},{16,0},{32,48},{48,32},{64,80},{80,64},{96,112},{112,96},{1... | collective-permute-start | bytes 1179656 | tf_op jit(solution)/shard_map/ppermute | solution.py:46
  77.3 15.2 %collective-permute-start.12 = (bf16[16,48,256]{2,1,0:T(8,128)(2,1)S(1)}, bf16[16,48,256]{2,1,0:T(8,128)(2,1)S(1)}, u32[]{:S(2)}, u32[]{:S(2)}) collective-permute-start(bf16[16,48,256]{2,1,0:T(8,128)(2,1)S(1)} %all-to-all-done.1.refs_0_), channel_id=1, source_target_pairs={{0,64},{16,80},{32,96},{48,112},{64,0},{80,16},{96,32},{112,48},{1... | collective-permute-start | bytes 1179656 | tf_op jit(solution)/shard_map/ppermute | solution.py:46
  83.5 11.2 %collective-permute-start.18 = (bf16[16,48,256]{2,1,0:T(8,128)(2,1)S(1)}, bf16[16,48,256]{2,1,0:T(8,128)(2,1)S(1)}, u32[]{:S(2)}, u32[]{:S(2)}) collective-permute-start(bf16[16,48,256]{2,1,0:T(8,128)(2,1)S(1)} %collective-permute-done.14.refs_2_), channel_id=1, source_target_pairs={{0,16},{16,0},{32,48},{48,32},{64,80},{80,64},{96,112},{112,96},{1... | collective-permute-start | bytes 1179656 | tf_op jit(solution)/shard_map/ppermute | solution.py:46
  86.7 8.0 %collective-permute-start.17 = (bf16[16,48,256]{2,1,0:T(8,128)(2,1)S(1)}, bf16[16,48,256]{2,1,0:T(8,128)(2,1)S(1)}, u32[]{:S(2)}, u32[]{:S(2)}) collective-permute-start(bf16[16,48,256]{2,1,0:T(8,128)(2,1)S(1)} %collective-permute-done.13.refs_1_), channel_id=1, source_target_pairs={{0,16},{16,0},{32,48},{48,32},{64,80},{80,64},{96,112},{112,96},{1... | collective-permute-start | bytes 1179656 | tf_op jit(solution)/shard_map/ppermute | solution.py:46
  92.5 3.5 %collective-permute-start.16 = (bf16[16,48,256]{2,1,0:T(8,128)(2,1)S(1)}, bf16[16,48,256]{2,1,0:T(8,128)(2,1)S(1)}, u32[]{:S(2)}, u32[]{:S(2)}) collective-permute-start(bf16[16,48,256]{2,1,0:T(8,128)(2,1)S(1)} %collective-permute-done.12.refs_2_), channel_id=1, source_target_pairs={{0,16},{16,0},{32,48},{48,32},{64,80},{80,64},{96,112},{112,96},{1... | collective-permute-start | bytes 1179656 | tf_op jit(solution)/shard_map/ppermute | solution.py:46
  96.8 4.3 %collective-permute-start.19 = (bf16[16,48,1024]{2,1,0:T(8,128)(2,1)S(1)}, bf16[16,48,1024]{2,1,0:T(8,128)(2,1)S(1)}, u32[]{:S(2)}, u32[]{:S(2)}) collective-permute-start(bf16[16,48,1024]{2,1,0:T(8,128)(2,1)S(1)} %all-to-all-done.2.refs_0_.refs_1_.refs_2_.refs_3_), channel_id=1, source_target_pairs={{0,16},{16,0},{32,48},{48,32},{64,80},{80,64},{96,112},{112,96},{1... | collective-permute-start | bytes 4718600 | tf_op jit(solution)/shard_map/ppermute | solution.py:46

commit v9 on v7

--- a/solution.py
+++ b/solution.py
@@ -54,38 +54,52 @@
     return jnp.dot(left, right, preferred_element_type=F32)
 
 
-def gram_kernel(rows_ref, keep_ref, send_ref, near_ref, far_ref):
-    core = lax.axis_index("replica") % 2
-
+HALVES = (((0, 0), (1, 0), (1, 1)), ((2, 0), (2, 1), (2, 2)))
+
+
+def gram_blocks(rows_ref, out_ref, core):
     def rows(index):
         return rows_ref[pl.ds(index * BLOCK, BLOCK), :]
 
-    halves = (((0, 0), (1, 0), (1, 1)), ((2, 0), (2, 1), (2, 2)))
-    for mine in range(2):
-
-        @pl.when(core == mine)
+    for half in range(2):
+
+        @pl.when(core == half)
         def _():
-            for place in range(3):
-                kept, sent = halves[mine][place], halves[1 - mine][place]
+            for place, (row, col) in enumerate(HALVES[half]):
                 where = pl.ds(place * BLOCK, BLOCK)
-                keep_ref[where, :] = dot_t(rows(kept[0]), rows(kept[1]))
-                send_ref[where, :] = dot_t(rows(sent[0]), rows(sent[1])).astype(BF16)
-
+                out_ref[where, :] = dot_t(rows(row), rows(col)).astype(out_ref.dtype)
+
+
+def sent_kernel(rows_ref, send_ref):
+    gram_blocks(rows_ref, send_ref, 1 - lax.axis_index("replica") % 2)
+
+
+def kept_kernel(rows_ref, keep_ref, near_ref, far_ref):
+    gram_blocks(rows_ref, keep_ref, lax.axis_index("replica") % 2)
     near_ref[...] = rows_ref[:, LATE:]
     far_ref[...] = rows_ref[:, FIRST:]
 
 
-def partial_gram(rows):
-    return pl.pallas_call(
-        gram_kernel,
+def sent_gram(rows):
+    return pl.pallas_call(
+        sent_kernel,
+        out_shape=jax.ShapeDtypeStruct((HALF, BLOCK), BF16),
+        in_specs=[VMEM],
+        out_specs=VMEM,
+        compiler_params=PARAMS,
+    )(rows)
+
+
+def kept_gram(rows):
+    return pl.pallas_call(
+        kept_kernel,
         out_shape=(
             jax.ShapeDtypeStruct((HALF, BLOCK), F32),
-            jax.ShapeDtypeStruct((HALF, BLOCK), BF16),
             jax.ShapeDtypeStruct((FF, NEAR), BF16),
             jax.ShapeDtypeStruct((FF, EARLY), BF16),
         ),
         in_specs=[VMEM],
-        out_specs=(VMEM,) * 4,
+        out_specs=(VMEM,) * 3,
         compiler_params=PARAMS,
     )(rows)
 
@@ -327,7 +341,8 @@
     rows = lax.all_to_all(flat_rows, "tensor", split_axis=0, concat_axis=0, tiled=True)
     rows = rows.reshape(FF, col_count)
 
-    keep, send, near, far = partial_gram(rows)
+    send = sent_gram(rows)
+    keep, near, far = kept_gram(rows)
     own, to_next, to_last, to_far = chip_sum(keep, shift(send, 0, 1))
     gradient, momentum, own = lax.optimization_barrier((gradient, momentum, own))
     new_momentum = stepped(gradient, momentum)

time: 103 us -> 102 us (level)
  transfers between devices with their start and end apart: 23 -> 23, of which waited for: 10 -> 10; matrix products, arithmetic and copies ran while one was open for 1% -> 1% of each run, Pallas kernels for 15% -> 16%
where the time goes in v9:
time: 102 us
  starting transfers between devices  39.1 us (38%)
  blocking collectives  21.9 us (21%)
  Pallas kernels  17.6 us (17%)
  waiting for transfers between devices  17.2 us (17%)
  other arithmetic  3.4 us (3%)
  local copies, waits for them, and re-layouts  1.88 us (2%)
    ppermute x21, starting transfers between devices, shift(): return lax.ppermute(value, 'replica', pairs)  31.3 us
    all_to_all x1, blocking collectives, local(): lax.all_to_all(flat_rows, 'tensor', split_axis=0, concat_axis=0, tiled=True)  21.9 us
    ppermute x21, waiting for transfers between devices, shift(): return lax.ppermute(value, 'replica', pairs)  14.7 us
    all_to_all x2, starting transfers between devices, back(): lax.all_to_all(value, 'tensor', split_axis=0, concat_axis=0, tiled=True)  7.74 us
    pallas_call x6, Pallas kernels, place(): pl.pallas_call(functools.partial(place_kernel, where, int(aliased)), out_...  5.9 us
    pallas_call x1, Pallas kernels, chain(): pl.pallas_call(chain_kernel, out_shape=(jax.ShapeDtypeStruct((FF, FIRST),...  5.6 us
    pallas_call x1, Pallas kernels, early_products(): pl.pallas_call(other_kernel, out_shape=out, in_specs=[VMEM] * 5 + [HBM],...  3 us
    all_to_all x2, waiting for transfers between devices, back(): lax.all_to_all(value, 'tensor', split_axis=0, concat_axis=0, tiled=True)  2.44 us
  transfers between devices with their start and end apart: 23, of which 10 were waited for; matrix products, arithmetic and copies ran while one was open for 1% of the time, Pallas kernels for 16%

profile of v9, /device:TPU:1, one launch (start us, length us, event | category | flops | bytes accessed | tf_op | source)
XLA Modules:
  0.0 102.0 jit_solution(1839318187587785202)
XLA Ops:
  0.6 2.0 %fusion.1 = bf16[8,2,48,512]{3,2,1,0:T(8,128)(2,1)S(1)} fusion(bf16[8,2,48,512]{3,2,1,0:T(8,128)(2,1)} %param.2, f32[8,2,48,512]{3,2,1,0:T(8,128)} %param.3), kind=kLoop, calls=%fused_computation.3 | loop fusion | flops 2359296 | bytes 3145728 | tf_op jit(solution)/shard_map/convert_element_type | solution.py:340
  2.6 21.9 %all_to_all.15 = bf16[16,48,512]{2,1,0:T(8,128)(2,1)S(1)} all-to-all(bf16[16,48,512]{2,1,0:T(8,128)(2,1)S(1)} %bitcast.9), channel_id=1, replica_groups=mesh['replica'=8,'tensor'=16] {'tensor'}, dimensions={0} | all-to-all | bytes 1572864 | tf_op jit(solution)/shard_map/all_to_all | solution.py:341
  24.5 0.4 shard_map.42
  24.9 1.9 %collective-permute-start = (bf16[768,256]{1,0:T(8,128)(2,1)S(1)}, bf16[768,256]{1,0:T(8,128)(2,1)S(1)}, u32[]{:S(2)}, u32[]{:S(2)}) collective-permute-start(bf16[768,256]{1,0:T(8,128)(2,1)S(1)} %shard_map.42), channel_id=1, source_target_pairs={{0,16},{16,0},{32,48},{48,32},{64,80},{80,64},{96,112},{112,96},{1... | collective-permute-start | bytes 1179656 | tf_op jit(solution)/shard_map/ppermute | solution.py:46
  26.8 0.4 shard_map.41
  27.2 0.9 collective-permute-done.got_ref
  28.1 0.1 shard_map.43
  28.2 1.3 %collective-permute-start.1 = (bf16[192,256]{1,0:T(8,128)(2,1)S(1)}, bf16[192,256]{1,0:T(8,128)(2,1)S(1)}, u32[]{:S(2)}, u32[]{:S(2)}) collective-permute-start(bf16[192,256]{1,0:T(8,128)(2,1)S(1)} %get-tuple-element.31), channel_id=1, source_target_pairs={{0,32},{16,48},{32,64},{48,80},{64,96},{80,112},{96,0},{112,16},{1... | collective-permute-start | bytes 294920 | tf_op jit(solution)/shard_map/ppermute | solution.py:46
  29.5 1.5 %collective-permute-start.2 = (bf16[192,256]{1,0:T(8,128)(2,1)S(1)}, bf16[192,256]{1,0:T(8,128)(2,1)S(1)}, u32[]{:S(2)}, u32[]{:S(2)}) collective-permute-start(bf16[192,256]{1,0:T(8,128)(2,1)S(1)} %get-tuple-element.32), channel_id=1, source_target_pairs={{0,96},{16,112},{32,0},{48,16},{64,32},{80,48},{96,64},{112,80},{1... | collective-permute-start | bytes 294920 | tf_op jit(solution)/shard_map/ppermute | solution.py:46
  31.0 1.5 %collective-permute-start.3 = (bf16[192,256]{1,0:T(8,128)(2,1)S(1)}, bf16[192,256]{1,0:T(8,128)(2,1)S(1)}, u32[]{:S(2)}, u32[]{:S(2)}) collective-permute-start(bf16[192,256]{1,0:T(8,128)(2,1)S(1)} %get-tuple-element.33), channel_id=1, source_target_pairs={{0,64},{16,80},{32,96},{48,112},{64,0},{80,16},{96,32},{112,48},{1... | collective-permute-start | bytes 294920 | tf_op jit(solution)/shard_map/ppermute | solution.py:46
  32.5 1.4 %convert_add_fusion.2 = f32[8,2,48,512]{3,2,1,0:T(8,128)} fusion(bf16[8,2,48,512]{3,2,1,0:T(8,128)(2,1)S(1)} %copy-done.3, f32[8,2,48,512]{3,2,1,0:T(8,128)S(1)} %copy-done.2), kind=kLoop, calls=%fused_computation.4 | loop fusion | flops 1179648 | bytes 3932160 | tf_op jit(solution)/shard_map/add | solution.py:336
  33.9 2.1 %collective-permute-done.3.c_ref = bf16[192,256]{1,0:T(8,128)(2,1)S(1)} collective-permute-done((bf16[192,256]{1,0:T(8,128)(2,1)S(1)}, bf16[192,256]{1,0:T(8,128)(2,1)S(1)}, u32[]{:S(2)}, u32[]{:S(2)}) %collective-permute-start.3) | collective-permute-done | bytes 98336 | tf_op jit(solution)/shard_map/ppermute | solution.py:46
  36.1 1.5 %collective-permute-start.5 = (bf16[192,256]{1,0:T(8,128)(2,1)S(1)}, bf16[192,256]{1,0:T(8,128)(2,1)S(1)}, u32[]{:S(2)}, u32[]{:S(2)}) collective-permute-start(bf16[192,256]{1,0:T(8,128)(2,1)S(1)} %shard_map.44.refs_0_), channel_id=1, source_target_pairs={{0,64},{16,80},{32,96},{48,112},{64,0},{80,16},{96,32},{112,48},{1... | collective-permute-start | bytes 294920 | tf_op jit(solution)/shard_map/ppermute | solution.py:46
  37.6 0.7 collective-permute-start.6
  38.3 2.0 %collective-permute-start.4 = (bf16[192,256]{1,0:T(8,128)(2,1)S(1)}, bf16[192,256]{1,0:T(8,128)(2,1)S(1)}, u32[]{:S(2)}, u32[]{:S(2)}) collective-permute-start(bf16[192,256]{1,0:T(8,128)(2,1)S(1)} %shard_map.44.refs_0_), channel_id=1, source_target_pairs={{0,96},{16,112},{32,0},{48,16},{64,32},{80,48},{96,64},{112,80},{1... | collective-permute-start | bytes 294920 | tf_op jit(solution)/shard_map/ppermute | solution.py:46
  40.3 0.9 collective-permute-done.5.refs_2_
  41.2 1.3 %collective-permute-start.10 = (bf16[768,256]{1,0:T(8,128)(2,1)S(1)}, bf16[768,256]{1,0:T(8,128)(2,1)S(1)}, u32[]{:S(2)}, u32[]{:S(2)}) collective-permute-start(bf16[768,256]{1,0:T(8,128)(2,1)S(1)} %get-tuple-element.39), channel_id=1, source_target_pairs={{0,32},{16,48},{32,64},{48,80},{64,96},{80,112},{96,0},{112,16},{1... | collective-permute-start | bytes 1179656 | tf_op jit(solution)/shard_map/ppermute | solution.py:46
  42.5 1.4 %collective-permute-start.9 = (bf16[768,256]{1,0:T(8,128)(2,1)S(1)}, bf16[768,256]{1,0:T(8,128)(2,1)S(1)}, u32[]{:S(2)}, u32[]{:S(2)}) collective-permute-start(bf16[768,256]{1,0:T(8,128)(2,1)S(1)} %get-tuple-element.39), channel_id=1, source_target_pairs={{0,96},{16,112},{32,0},{48,16},{64,32},{80,48},{96,64},{112,80},{1... | collective-permute-start | bytes 1179656 | tf_op jit(solution)/shard_map/ppermute | solution.py:46
  43.8 0.4 collective-permute-start.11
  44.3 4.0 %collective-permute-start.8 = (bf16[576,256]{1,0:T(8,128)(2,1)S(1)}, bf16[576,256]{1,0:T(8,128)(2,1)S(1)}, u32[]{:S(2)}, u32[]{:S(2)}) collective-permute-start(bf16[576,256]{1,0:T(8,128)(2,1)S(1)} %pad_maximum_fusion), channel_id=1, source_target_pairs={{0,16},{16,0},{32,48},{48,32},{64,80},{80,64},{96,112},{112,96},{1... | collective-permute-start | bytes 884744 | tf_op jit(solution)/shard_map/ppermute | solution.py:46
  48.4 1.3 %collective-permute-done.7.refs_4_ = bf16[192,256]{1,0:T(8,128)(2,1)S(1)} collective-permute-done((bf16[192,256]{1,0:T(8,128)(2,1)S(1)}, bf16[192,256]{1,0:T(8,128)(2,1)S(1)}, u32[]{:S(2)}, u32[]{:S(2)}) %collective-permute-start.7) | collective-permute-done | bytes 98336 | tf_op jit(solution)/shard_map/ppermute | solution.py:46
  49.7 5.6 %shard_map.45 = (bf16[768,256]{1,0:T(8,128)(2,1)}, bf16[2,768,768]{2,1,0:T(8,128)(2,1)}, f32[8,128]{1,0:T(8,128)S(1)}) custom-call(bf16[192,256]{1,0:T(8,128)(2,1)S(1)} %shard_map.44.refs_0_, bf16[192,256]{1,0:T(8,128)(2,1)S(1)} %collective-permute-done.4.refs_1_, bf16[192,256]{1,0:T(8,128)(2,1)S(1)} %collective-permute-done.5.refs_2_, ...), custom_call_target="tpu_custom_call" | custom-call | tf_op jit(solution)/shard_map/pallas_call | solution.py:209
  55.3 3.7 %all-to-all-start.1 = ((bf16[16,48,256]{2,1,0:T(8,128)(2,1)}), bf16[16,48,256]{2,1,0:T(8,128)(2,1)S(1)}, u32[]{:S(2)}, u32[]{:S(2)}) async-start(bf16[16,48,256]{2,1,0:T(8,128)(2,1)} %bitcast.2), calls=%async_computation.1 | async-start | bytes 786432 | tf_op jit(solution)/shard_map/all_to_all | solution.py:357
  59.0 1.7 %copy-done = bf16[2,768,768]{2,1,0:T(8,128)(2,1)S(1)} copy-done((bf16[2,768,768]{2,1,0:T(8,128)(2,1)S(1)}, bf16[2,768,768]{2,1,0:T(8,128)(2,1)}, u32[]{:S(2)}) %copy-start) | copy-done | bytes 2359320
  60.7 2.2 %shard_map.46.refs_3_ = bf16[768,1024]{1,0:T(8,128)(2,1)} custom-call(bf16[2,768,768]{2,1,0:T(8,128)(2,1)S(1)} %copy-done, f32[8,128]{1,0:T(8,128)S(1)} %get-tuple-element.36.scale_ref, bf16[768,256]{1,0:T(8,128)(2,1)S(1)} %get-tuple-element.40.early_ref), custom_call_target="tpu_custom_call" | custom-call | tf_op jit(solution)/shard_map/pallas_call | solution.py:270
  62.9 3.0 %shard_map.47 = bf16[768,1024]{1,0:T(8,128)(2,1)} custom-call(bf16[2,768,768]{2,1,0:T(8,128)(2,1)S(1)} %copy-done.1, f32[8,128]{1,0:T(8,128)S(1)} %get-tuple-element.36.scale_ref, bf16[768,256]{1,0:T(8,128)(2,1)S(1)} %collective-permute-done.9.refs_0_, bf16[768,256]{1,0:T(8,128)(2,1)S(1)} %collective-permute-done.10.refs_1_, ...), custom_call_target="tpu_custom_call", output_to_operand_aliasing={{}: (5, {})} | custom-call | flops 20000000000 | tf_op jit(solution)/shard_map/pallas_call | solution.py:279
  65.9 2.4 %all-to-all-done.1.refs_0_ = bf16[16,48,256]{2,1,0:T(8,128)(2,1)S(1)} async-done(((bf16[16,48,256]{2,1,0:T(8,128)(2,1)}), bf16[16,48,256]{2,1,0:T(8,128)(2,1)S(1)}, u32[]{:S(2)}, u32[]{:S(2)}) %all-to-all-start.1) | async-done | bytes 393248 | tf_op jit(solution)/shard_map/all_to_all | solution.py:357
  68.4 4.0 %all-to-all-start.2 = ((bf16[16,48,1024]{2,1,0:T(8,128)(2,1)}), bf16[16,48,1024]{2,1,0:T(8,128)(2,1)S(1)}, u32[]{:S(2)}, u32[]{:S(2)}) async-start(bf16[16,48,1024]{2,1,0:T(8,128)(2,1)} %bitcast.3), calls=%async_computation.2 | async-start | bytes 3145728 | tf_op jit(solution)/shard_map/all_to_all | solution.py:357
  72.4 0.7 collective-permute-start.14
  73.1 2.0 %collective-permute-start.13 = (bf16[16,48,256]{2,1,0:T(8,128)(2,1)S(1)}, bf16[16,48,256]{2,1,0:T(8,128)(2,1)S(1)}, u32[]{:S(2)}, u32[]{:S(2)}) collective-permute-start(bf16[16,48,256]{2,1,0:T(8,128)(2,1)S(1)} %all-to-all-done.1.refs_0_), channel_id=1, source_target_pairs={{0,96},{16,112},{32,0},{48,16},{64,32},{80,48},{96,64},{112,80},{1... | collective-permute-start | bytes 1179656 | tf_op jit(solution)/shard_map/ppermute | solution.py:46
  75.1 1.8 %collective-permute-start.15 = (bf16[16,48,256]{2,1,0:T(8,128)(2,1)S(1)}, bf16[16,48,256]{2,1,0:T(8,128)(2,1)S(1)}, u32[]{:S(2)}, u32[]{:S(2)}) collective-permute-start(bf16[16,48,256]{2,1,0:T(8,128)(2,1)S(1)} %all-to-all-done.1.refs_0_), channel_id=1, source_target_pairs={{0,16},{16,0},{32,48},{48,32},{64,80},{80,64},{96,112},{112,96},{1... | collective-permute-start | bytes 1179656 | tf_op jit(solution)/shard_map/ppermute | solution.py:46
  76.9 1.8 %collective-permute-start.12 = (bf16[16,48,256]{2,1,0:T(8,128)(2,1)S(1)}, bf16[16,48,256]{2,1,0:T(8,128)(2,1)S(1)}, u32[]{:S(2)}, u32[]{:S(2)}) collective-permute-start(bf16[16,48,256]{2,1,0:T(8,128)(2,1)S(1)} %all-to-all-done.1.refs_0_), channel_id=1, source_target_pairs={{0,64},{16,80},{32,96},{48,112},{64,0},{80,16},{96,32},{112,48},{1... | collective-permute-start | bytes 1179656 | tf_op jit(solution)/shard_map/ppermute | solution.py:46
  78.7 4.4 %collective-permute-done.14.refs_2_ = bf16[16,48,256]{2,1,0:T(8,128)(2,1)S(1)} collective-permute-done((bf16[16,48,256]{2,1,0:T(8,128)(2,1)S(1)}, bf16[16,48,256]{2,1,0:T(8,128)(2,1)S(1)}, u32[]{:S(2)}, u32[]{:S(2)}) %collective-permute-start.14) | collective-permute-done | bytes 393248 | tf_op jit(solution)/shard_map/ppermute | solution.py:46
  83.0 3.2 %collective-permute-start.18 = (bf16[16,48,256]{2,1,0:T(8,128)(2,1)S(1)}, bf16[16,48,256]{2,1,0:T(8,128)(2,1)S(1)}, u32[]{:S(2)}, u32[]{:S(2)}) collective-permute-start(bf16[16,48,256]{2,1,0:T(8,128)(2,1)S(1)} %collective-permute-done.14.refs_2_), channel_id=1, source_target_pairs={{0,16},{16,0},{32,48},{48,32},{64,80},{80,64},{96,112},{112,96},{1... | collective-permute-start | bytes 1179656 | tf_op jit(solution)/shard_map/ppermute | solution.py:46
  86.3 0.6 collective-permute-start.17
  86.9 1.2 %shard_map.48.refs_3_ = bf16[16,48,4096]{2,1,0:T(8,128)(2,1)} custom-call(bf16[16,48,256]{2,1,0:T(8,128)(2,1)S(1)} %all-to-all-done.1.refs_0_, bf16[16,48,256]{2,1,0:T(8,128)(2,1)S(1)} %collective-permute-done.13.refs_1_, bf16[16,48,256]{2,1,0:T(8,128)(2,1)S(1)} %collective-permute-done.14.refs_2_, bf16[16,48,256]{2,1,0:T(8,128)(2,1)S(1)} %collective-permute-done.15.refs_3_), custom_call_target="tpu_custom_call" | custom-call | tf_op jit(solution)/shard_map/pallas_call | solution.py:322
  88.1 4.0 %collective-permute-done.12.refs_2_ = bf16[16,48,256]{2,1,0:T(8,128)(2,1)S(1)} collective-permute-done((bf16[16,48,256]{2,1,0:T(8,128)(2,1)S(1)}, bf16[16,48,256]{2,1,0:T(8,128)(2,1)S(1)}, u32[]{:S(2)}, u32[]{:S(2)}) %collective-permute-start.12) | collective-permute-done | bytes 393248 | tf_op jit(solution)/shard_map/ppermute | solution.py:46
  92.1 2.1 %collective-permute-start.16 = (bf16[16,48,256]{2,1,0:T(8,128)(2,1)S(1)}, bf16[16,48,256]{2,1,0:T(8,128)(2,1)S(1)}, u32[]{:S(2)}, u32[]{:S(2)}) collective-permute-start(bf16[16,48,256]{2,1,0:T(8,128)(2,1)S(1)} %collective-permute-done.12.refs_2_), channel_id=1, source_target_pairs={{0,16},{16,0},{32,48},{48,32},{64,80},{80,64},{96,112},{112,96},{1... | collective-permute-start | bytes 1179656 | tf_op jit(solution)/shard_map/ppermute | solution.py:46
  94.2 1.0 %shard_map.49.refs_1_ = bf16[16,48,4096]{2,1,0:T(8,128)(2,1)} custom-call(bf16[16,48,256]{2,1,0:T(8,128)(2,1)S(1)} %collective-permute-done.17.refs_0_, bf16[16,48,256]{2,1,0:T(8,128)(2,1)S(1)} %collective-permute-done.18.refs_1_, bf16[16,48,256]{2,1,0:T(8,128)(2,1)S(1)} %collective-permute-done.12.refs_2_, ...), custom_call_target="tpu_custom_call", output_to_operand_aliasing={{}: (3, {})} | custom-call | tf_op jit(solution)/shard_map/pallas_call | solution.py:322
  95.3 0.3 collective-permute-done.16.refs_0_
  95.6 0.8 shard_map.50.refs_4_
  96.4 0.2 fusion.2
  96.6 1.4 %collective-permute-start.20 = (bf16[16,48,512]{2,1,0:T(8,128)(2,1)S(1)}, bf16[16,48,512]{2,1,0:T(8,128)(2,1)S(1)}, u32[]{:S(2)}, u32[]{:S(2)}) collective-permute-start(bf16[16,48,512]{2,1,0:T(8,128)(2,1)S(1)} %get-tuple-element.48), channel_id=1, source_target_pairs={{0,16},{16,0},{32,48},{48,32},{64,80},{80,64},{96,112},{112,96},{1... | collective-permute-start | bytes 2359304 | tf_op jit(solution)/shard_map/ppermute | solution.py:46
  98.0 1.2 %shard_map.51.refs_2_ = bf16[16,48,4096]{2,1,0:T(8,128)(2,1)} custom-call(bf16[16,48,1024]{2,1,0:T(8,128)(2,1)S(1)} %all-to-all-done.2.refs_0_.refs_1_.refs_2_.refs_3_, bf16[16,48,1024]{2,1,0:T(8,128)(2,1)S(1)} %all-to-all-done.2.refs_0_.refs_1_.refs_2_.refs_3_, ...), custom_call_target="tpu_custom_call", output_to_operand_aliasing={{}: (4, {})} | custom-call | tf_op jit(solution)/shard_map/pallas_call | solution.py:322
  99.2 0.6 collective-permute-done.20.refs_0_.refs_1_
  99.9 0.9 shard_map.52.refs_2_
  100.8 0.2 collective-permute-done.19.refs_0_.refs_1_
  101.0 0.9 shard_map.53
  (24 shorter events, 0.3 us)
Async XLA Ops:
  24.5 8.0 %copy-start.2 = (f32[8,2,48,512]{3,2,1,0:T(8,128)S(1)}, f32[8,2,48,512]{3,2,1,0:T(8,128)}, u32[]{:S(2)}) copy-start(f32[8,2,48,512]{3,2,1,0:T(8,128)} %param.3) | copy-start | bytes 4718596
  24.5 8.0 %copy-start.3 = (bf16[8,2,48,512]{3,2,1,0:T(8,128)(2,1)S(1)}, bf16[8,2,48,512]{3,2,1,0:T(8,128)(2,1)}, u32[]{:S(2)}) copy-start(bf16[8,2,48,512]{3,2,1,0:T(8,128)(2,1)} %param.2) | copy-start | bytes 2359300
  24.9 3.2 %collective-permute-start = (bf16[768,256]{1,0:T(8,128)(2,1)S(1)}, bf16[768,256]{1,0:T(8,128)(2,1)S(1)}, u32[]{:S(2)}, u32[]{:S(2)}) collective-permute-start(bf16[768,256]{1,0:T(8,128)(2,1)S(1)} %shard_map.42), channel_id=1, source_target_pairs={{0,16},{16,0},{32,48},{48,32},{64,80},{80,64},{96,112},{112,96},{1... | collective-permute-start | bytes 1179656 | tf_op jit(solution)/shard_map/ppermute | solution.py:46
  28.2 5.7 %collective-permute-start.1 = (bf16[192,256]{1,0:T(8,128)(2,1)S(1)}, bf16[192,256]{1,0:T(8,128)(2,1)S(1)}, u32[]{:S(2)}, u32[]{:S(2)}) collective-permute-start(bf16[192,256]{1,0:T(8,128)(2,1)S(1)} %get-tuple-element.31), channel_id=1, source_target_pairs={{0,32},{16,48},{32,64},{48,80},{64,96},{80,112},{96,0},{112,16},{1... | collective-permute-start | bytes 294920 | tf_op jit(solution)/shard_map/ppermute | solution.py:46
  29.5 4.4 %collective-permute-start.2 = (bf16[192,256]{1,0:T(8,128)(2,1)S(1)}, bf16[192,256]{1,0:T(8,128)(2,1)S(1)}, u32[]{:S(2)}, u32[]{:S(2)}) collective-permute-start(bf16[192,256]{1,0:T(8,128)(2,1)S(1)} %get-tuple-element.32), channel_id=1, source_target_pairs={{0,96},{16,112},{32,0},{48,16},{64,32},{80,48},{96,64},{112,80},{1... | collective-permute-start | bytes 294920 | tf_op jit(solution)/shard_map/ppermute | solution.py:46
  31.0 5.1 %collective-permute-start.3 = (bf16[192,256]{1,0:T(8,128)(2,1)S(1)}, bf16[192,256]{1,0:T(8,128)(2,1)S(1)}, u32[]{:S(2)}, u32[]{:S(2)}) collective-permute-start(bf16[192,256]{1,0:T(8,128)(2,1)S(1)} %get-tuple-element.33), channel_id=1, source_target_pairs={{0,64},{16,80},{32,96},{48,112},{64,0},{80,16},{96,32},{112,48},{1... | collective-permute-start | bytes 294920 | tf_op jit(solution)/shard_map/ppermute | solution.py:46
  36.1 5.1 %collective-permute-start.5 = (bf16[192,256]{1,0:T(8,128)(2,1)S(1)}, bf16[192,256]{1,0:T(8,128)(2,1)S(1)}, u32[]{:S(2)}, u32[]{:S(2)}) collective-permute-start(bf16[192,256]{1,0:T(8,128)(2,1)S(1)} %shard_map.44.refs_0_), channel_id=1, source_target_pairs={{0,64},{16,80},{32,96},{48,112},{64,0},{80,16},{96,32},{112,48},{1... | collective-permute-start | bytes 294920 | tf_op jit(solution)/shard_map/ppermute | solution.py:46
  37.6 6.7 %collective-permute-start.6 = (bf16[192,256]{1,0:T(8,128)(2,1)S(1)}, bf16[192,256]{1,0:T(8,128)(2,1)S(1)}, u32[]{:S(2)}, u32[]{:S(2)}) collective-permute-start(bf16[192,256]{1,0:T(8,128)(2,1)S(1)} %shard_map.44.refs_0_), channel_id=1, source_target_pairs={{0,32},{16,48},{32,64},{48,80},{64,96},{80,112},{96,0},{112,16},{1... | collective-permute-start | bytes 294920 | tf_op jit(solution)/shard_map/ppermute | solution.py:46
  38.3 6.0 %collective-permute-start.4 = (bf16[192,256]{1,0:T(8,128)(2,1)S(1)}, bf16[192,256]{1,0:T(8,128)(2,1)S(1)}, u32[]{:S(2)}, u32[]{:S(2)}) collective-permute-start(bf16[192,256]{1,0:T(8,128)(2,1)S(1)} %shard_map.44.refs_0_), channel_id=1, source_target_pairs={{0,96},{16,112},{32,0},{48,16},{64,32},{80,48},{96,64},{112,80},{1... | collective-permute-start | bytes 294920 | tf_op jit(solution)/shard_map/ppermute | solution.py:46
  41.2 21.7 %collective-permute-start.10 = (bf16[768,256]{1,0:T(8,128)(2,1)S(1)}, bf16[768,256]{1,0:T(8,128)(2,1)S(1)}, u32[]{:S(2)}, u32[]{:S(2)}) collective-permute-start(bf16[768,256]{1,0:T(8,128)(2,1)S(1)} %get-tuple-element.39), channel_id=1, source_target_pairs={{0,32},{16,48},{32,64},{48,80},{64,96},{80,112},{96,0},{112,16},{1... | collective-permute-start | bytes 1179656 | tf_op jit(solution)/shard_map/ppermute | solution.py:46
  42.5 20.4 %collective-permute-start.9 = (bf16[768,256]{1,0:T(8,128)(2,1)S(1)}, bf16[768,256]{1,0:T(8,128)(2,1)S(1)}, u32[]{:S(2)}, u32[]{:S(2)}) collective-permute-start(bf16[768,256]{1,0:T(8,128)(2,1)S(1)} %get-tuple-element.39), channel_id=1, source_target_pairs={{0,96},{16,112},{32,0},{48,16},{64,32},{80,48},{96,64},{112,80},{1... | collective-permute-start | bytes 1179656 | tf_op jit(solution)/shard_map/ppermute | solution.py:46
  43.8 19.1 %collective-permute-start.11 = (bf16[768,256]{1,0:T(8,128)(2,1)S(1)}, bf16[768,256]{1,0:T(8,128)(2,1)S(1)}, u32[]{:S(2)}, u32[]{:S(2)}) collective-permute-start(bf16[768,256]{1,0:T(8,128)(2,1)S(1)} %get-tuple-element.40.early_ref), channel_id=1, source_target_pairs={{0,64},{16,80},{32,96},{48,112},{64,0},{80,16},{96,32},{112,48},{1... | collective-permute-start | bytes 1179656 | tf_op jit(solution)/shard_map/ppermute | solution.py:46
  44.3 5.4 %collective-permute-start.8 = (bf16[576,256]{1,0:T(8,128)(2,1)S(1)}, bf16[576,256]{1,0:T(8,128)(2,1)S(1)}, u32[]{:S(2)}, u32[]{:S(2)}) collective-permute-start(bf16[576,256]{1,0:T(8,128)(2,1)S(1)} %pad_maximum_fusion), channel_id=1, source_target_pairs={{0,16},{16,0},{32,48},{48,32},{64,80},{80,64},{96,112},{112,96},{1... | collective-permute-start | bytes 884744 | tf_op jit(solution)/shard_map/ppermute | solution.py:46
  48.3 1.3 %collective-permute-start.7 = (bf16[192,256]{1,0:T(8,128)(2,1)S(1)}, bf16[192,256]{1,0:T(8,128)(2,1)S(1)}, u32[]{:S(2)}, u32[]{:S(2)}) collective-permute-start(bf16[192,256]{1,0:T(8,128)(2,1)S(1)} %shard_map.44.refs_0_), channel_id=1, source_target_pairs={{0,16},{16,0},{32,48},{48,32},{64,80},{80,64},{96,112},{112,96},{1... | collective-permute-start | bytes 294920 | tf_op jit(solution)/shard_map/ppermute | solution.py:46
  55.3 13.1 %all-to-all-start.1 = ((bf16[16,48,256]{2,1,0:T(8,128)(2,1)}), bf16[16,48,256]{2,1,0:T(8,128)(2,1)S(1)}, u32[]{:S(2)}, u32[]{:S(2)}) async-start(bf16[16,48,256]{2,1,0:T(8,128)(2,1)} %bitcast.2), calls=%async_computation.1 | async-start | bytes 786432 | tf_op jit(solution)/shard_map/all_to_all | solution.py:357
  59.0 1.7 %copy-start = (bf16[2,768,768]{2,1,0:T(8,128)(2,1)S(1)}, bf16[2,768,768]{2,1,0:T(8,128)(2,1)}, u32[]{:S(2)}) copy-start(bf16[2,768,768]{2,1,0:T(8,128)(2,1)} %get-tuple-element.35.polys_ref) | copy-start | bytes 7077892
  60.7 2.2 %copy-start.1 = (bf16[2,768,768]{2,1,0:T(8,128)(2,1)S(1)}, bf16[2,768,768]{2,1,0:T(8,128)(2,1)}, u32[]{:S(2)}) copy-start(bf16[2,768,768]{2,1,0:T(8,128)(2,1)} %get-tuple-element.35.polys_ref) | copy-start | bytes 7077892
  68.4 28.0 %all-to-all-start.2 = ((bf16[16,48,1024]{2,1,0:T(8,128)(2,1)}), bf16[16,48,1024]{2,1,0:T(8,128)(2,1)S(1)}, u32[]{:S(2)}, u32[]{:S(2)}) async-start(bf16[16,48,1024]{2,1,0:T(8,128)(2,1)} %bitcast.3), calls=%async_computation.2 | async-start | bytes 3145728 | tf_op jit(solution)/shard_map/all_to_all | solution.py:357
  72.4 10.7 %collective-permute-start.14 = (bf16[16,48,256]{2,1,0:T(8,128)(2,1)S(1)}, bf16[16,48,256]{2,1,0:T(8,128)(2,1)S(1)}, u32[]{:S(2)}, u32[]{:S(2)}) collective-permute-start(bf16[16,48,256]{2,1,0:T(8,128)(2,1)S(1)} %all-to-all-done.1.refs_0_), channel_id=1, source_target_pairs={{0,32},{16,48},{32,64},{48,80},{64,96},{80,112},{96,0},{112,16},{1... | collective-permute-start | bytes 1179656 | tf_op jit(solution)/shard_map/ppermute | solution.py:46
  73.1 13.2 %collective-permute-start.13 = (bf16[16,48,256]{2,1,0:T(8,128)(2,1)S(1)}, bf16[16,48,256]{2,1,0:T(8,128)(2,1)S(1)}, u32[]{:S(2)}, u32[]{:S(2)}) collective-permute-start(bf16[16,48,256]{2,1,0:T(8,128)(2,1)S(1)} %all-to-all-done.1.refs_0_), channel_id=1, source_target_pairs={{0,96},{16,112},{32,0},{48,16},{64,32},{80,48},{96,64},{112,80},{1... | collective-permute-start | bytes 1179656 | tf_op jit(solution)/shard_map/ppermute | solution.py:46
  75.1 11.8 %collective-permute-start.15 = (bf16[16,48,256]{2,1,0:T(8,128)(2,1)S(1)}, bf16[16,48,256]{2,1,0:T(8,128)(2,1)S(1)}, u32[]{:S(2)}, u32[]{:S(2)}) collective-permute-start(bf16[16,48,256]{2,1,0:T(8,128)(2,1)S(1)} %all-to-all-done.1.refs_0_), channel_id=1, source_target_pairs={{0,16},{16,0},{32,48},{48,32},{64,80},{80,64},{96,112},{112,96},{1... | collective-permute-start | bytes 1179656 | tf_op jit(solution)/shard_map/ppermute | solution.py:46
  76.9 15.2 %collective-permute-start.12 = (bf16[16,48,256]{2,1,0:T(8,128)(2,1)S(1)}, bf16[16,48,256]{2,1,0:T(8,128)(2,1)S(1)}, u32[]{:S(2)}, u32[]{:S(2)}) collective-permute-start(bf16[16,48,256]{2,1,0:T(8,128)(2,1)S(1)} %all-to-all-done.1.refs_0_), channel_id=1, source_target_pairs={{0,64},{16,80},{32,96},{48,112},{64,0},{80,16},{96,32},{112,48},{1... | collective-permute-start | bytes 1179656 | tf_op jit(solution)/shard_map/ppermute | solution.py:46
  83.0 11.2 %collective-permute-start.18 = (bf16[16,48,256]{2,1,0:T(8,128)(2,1)S(1)}, bf16[16,48,256]{2,1,0:T(8,128)(2,1)S(1)}, u32[]{:S(2)}, u32[]{:S(2)}) collective-permute-start(bf16[16,48,256]{2,1,0:T(8,128)(2,1)S(1)} %collective-permute-done.14.refs_2_), channel_id=1, source_target_pairs={{0,16},{16,0},{32,48},{48,32},{64,80},{80,64},{96,112},{112,96},{1... | collective-permute-start | bytes 1179656 | tf_op jit(solution)/shard_map/ppermute | solution.py:46
  86.3 8.0 %collective-permute-start.17 = (bf16[16,48,256]{2,1,0:T(8,128)(2,1)S(1)}, bf16[16,48,256]{2,1,0:T(8,128)(2,1)S(1)}, u32[]{:S(2)}, u32[]{:S(2)}) collective-permute-start(bf16[16,48,256]{2,1,0:T(8,128)(2,1)S(1)} %collective-permute-done.13.refs_1_), channel_id=1, source_target_pairs={{0,16},{16,0},{32,48},{48,32},{64,80},{80,64},{96,112},{112,96},{1... | collective-permute-start | bytes 1179656 | tf_op jit(solution)/shard_map/ppermute | solution.py:46
  92.1 3.5 %collective-permute-start.16 = (bf16[16,48,256]{2,1,0:T(8,128)(2,1)S(1)}, bf16[16,48,256]{2,1,0:T(8,128)(2,1)S(1)}, u32[]{:S(2)}, u32[]{:S(2)}) collective-permute-start(bf16[16,48,256]{2,1,0:T(8,128)(2,1)S(1)} %collective-permute-done.12.refs_2_), channel_id=1, source_target_pairs={{0,16},{16,0},{32,48},{48,32},{64,80},{80,64},{96,112},{112,96},{1... | collective-permute-start | bytes 1179656 | tf_op jit(solution)/shard_map/ppermute | solution.py:46
  96.6 3.3 %collective-permute-start.20 = (bf16[16,48,512]{2,1,0:T(8,128)(2,1)S(1)}, bf16[16,48,512]{2,1,0:T(8,128)(2,1)S(1)}, u32[]{:S(2)}, u32[]{:S(2)}) collective-permute-start(bf16[16,48,512]{2,1,0:T(8,128)(2,1)S(1)} %get-tuple-element.48), channel_id=1, source_target_pairs={{0,16},{16,0},{32,48},{48,32},{64,80},{80,64},{96,112},{112,96},{1... | collective-permute-start | bytes 2359304 | tf_op jit(solution)/shard_map/ppermute | solution.py:46
  97.9 3.0 %collective-permute-start.19 = (bf16[16,48,512]{2,1,0:T(8,128)(2,1)S(1)}, bf16[16,48,512]{2,1,0:T(8,128)(2,1)S(1)}, u32[]{:S(2)}, u32[]{:S(2)}) collective-permute-start(bf16[16,48,512]{2,1,0:T(8,128)(2,1)S(1)} %get-tuple-element.49), channel_id=1, source_target_pairs={{0,16},{16,0},{32,48},{48,32},{64,80},{80,64},{96,112},{112,96},{1... | collective-permute-start | bytes 2359304 | tf_op jit(solution)/shard_map/ppermute | solution.py:46

commit v10 on v9

--- a/solution.py
+++ b/solution.py
@@ -164,28 +164,30 @@
     diagonal = row_id == col_id
     places = ((0, 0), (1, 0), (1, 1), (2, 0), (2, 1), (2, 2))
     blocks = [packed[place // 3, pl.ds((place % 3) * BLOCK, BLOCK), :] for place in range(6)]
+    for block, (row, col) in zip(blocks, places):
+        gram[pl.ds(row * BLOCK, BLOCK), pl.ds(col * BLOCK, BLOCK)] = block
+        if row != col:
+            flipped = block.astype(F32).T.astype(BF16)
+            gram[pl.ds(col * BLOCK, BLOCK), pl.ds(row * BLOCK, BLOCK)] = flipped
     squares = sum(
         jnp.sum(jnp.where(diagonal, block.astype(F32), 0.0))
         for block, (row, col) in zip(blocks, places)
         if row == col
     )
-    squares = jnp.full((1, 1), squares, F32)
-    scale = 1.0 / (jnp.sqrt(squares) + epsilon)
-    for block, (row, col) in zip(blocks, places):
-        scaled = (block.astype(F32) * scale) * scale
-        gram[pl.ds(row * BLOCK, BLOCK), pl.ds(col * BLOCK, BLOCK)] = scaled.astype(BF16)
-        if row != col:
-            gram[pl.ds(col * BLOCK, BLOCK), pl.ds(row * BLOCK, BLOCK)] = scaled.T.astype(BF16)
-
+    scale = 1.0 / (jnp.sqrt(jnp.full((1, 1), squares, F32)) + epsilon)
     scale_ref[...] = jnp.broadcast_to(scale, scale_ref.shape)
-    gram_0 = gram[...]
-    poly_0 = (coef_gram * gram_0.astype(F32) + coef_square * dot(gram_0, gram_0)).astype(BF16)
+    second_power = scale * scale
+    fourth_power = second_power * second_power
+    raw = gram[...]
+    poly_0 = (coef_gram * second_power) * raw.astype(F32)
+    poly_0 = (poly_0 + (coef_square * fourth_power) * dot(raw, raw)).astype(BF16)
     polys[0] = poly_0
     copies = [pltpu.make_async_copy(polys.at[0], polys_out.at[0], sems.at[0])]
     copies[0].start()
     rows = rows_ref[:, :FIRST]
     first = ((coef_linear * rows.astype(F32) + dot(poly_0, rows)) * scale).astype(BF16)
-    half_way = (coef_linear * gram_0.astype(F32) + dot(poly_0, gram_0)).astype(BF16)
+    half_way = coef_linear * raw.astype(F32) + dot(poly_0, raw)
+    half_way = (second_power * half_way).astype(BF16)
     gram_1 = (coef_linear * half_way.astype(F32) + dot(half_way, poly_0)).astype(BF16)
     for block in range(FF // BLOCK):
         where = pl.ds(block * BLOCK, BLOCK)

time: 102 us -> 102 us (level)
  no operation moved by 1% of the time
where the time goes in v10:
time: 102 us
  starting transfers between devices  39.1 us (38%)
  blocking collectives  21.9 us (21%)
  Pallas kernels  17.5 us (17%)
  waiting for transfers between devices  17.2 us (17%)
  other arithmetic  3.4 us (3%)
  local copies, waits for them, and re-layouts  1.88 us (2%)
    ppermute x21, starting transfers between devices, shift(): return lax.ppermute(value, 'replica', pairs)  31.3 us
    all_to_all x1, blocking collectives, local(): lax.all_to_all(flat_rows, 'tensor', split_axis=0, concat_axis=0, tiled=True)  21.9 us
    ppermute x21, waiting for transfers between devices, shift(): return lax.ppermute(value, 'replica', pairs)  14.7 us
    all_to_all x2, starting transfers between devices, back(): lax.all_to_all(value, 'tensor', split_axis=0, concat_axis=0, tiled=True)  7.74 us
    pallas_call x6, Pallas kernels, place(): pl.pallas_call(functools.partial(place_kernel, where, int(aliased)), out_...  5.9 us
    pallas_call x1, Pallas kernels, chain(): pl.pallas_call(chain_kernel, out_shape=(jax.ShapeDtypeStruct((FF, FIRST),...  5.48 us
    pallas_call x1, Pallas kernels, early_products(): pl.pallas_call(other_kernel, out_shape=out, in_specs=[VMEM] * 5 + [HBM],...  3 us
    all_to_all x2, waiting for transfers between devices, back(): lax.all_to_all(value, 'tensor', split_axis=0, concat_axis=0, tiled=True)  2.44 us
  transfers between devices with their start and end apart: 23, of which 10 were waited for; matrix products, arithmetic and copies ran while one was open for 1% of the time, Pallas kernels for 16%

profile of v10, /device:TPU:1, one launch (start us, length us, event | category | flops | bytes accessed | tf_op | source)
XLA Modules:
  0.0 101.9 jit_solution(9850442356001588027)
XLA Ops:
  0.6 2.0 %fusion.1 = bf16[8,2,48,512]{3,2,1,0:T(8,128)(2,1)S(1)} fusion(bf16[8,2,48,512]{3,2,1,0:T(8,128)(2,1)} %param.2, f32[8,2,48,512]{3,2,1,0:T(8,128)} %param.3), kind=kLoop, calls=%fused_computation.3 | loop fusion | flops 2359296 | bytes 3145728 | tf_op jit(solution)/shard_map/convert_element_type | solution.py:342
  2.6 21.9 %all_to_all.15 = bf16[16,48,512]{2,1,0:T(8,128)(2,1)S(1)} all-to-all(bf16[16,48,512]{2,1,0:T(8,128)(2,1)S(1)} %bitcast.9), channel_id=1, replica_groups=mesh['replica'=8,'tensor'=16] {'tensor'}, dimensions={0} | all-to-all | bytes 1572864 | tf_op jit(solution)/shard_map/all_to_all | solution.py:343
  24.5 0.4 shard_map.42
  24.9 1.9 %collective-permute-start = (bf16[768,256]{1,0:T(8,128)(2,1)S(1)}, bf16[768,256]{1,0:T(8,128)(2,1)S(1)}, u32[]{:S(2)}, u32[]{:S(2)}) collective-permute-start(bf16[768,256]{1,0:T(8,128)(2,1)S(1)} %shard_map.42), channel_id=1, source_target_pairs={{0,16},{16,0},{32,48},{48,32},{64,80},{80,64},{96,112},{112,96},{1... | collective-permute-start | bytes 1179656 | tf_op jit(solution)/shard_map/ppermute | solution.py:46
  26.8 0.4 shard_map.41
  27.2 0.9 collective-permute-done.got_ref
  28.1 0.1 shard_map.43
  28.2 1.3 %collective-permute-start.1 = (bf16[192,256]{1,0:T(8,128)(2,1)S(1)}, bf16[192,256]{1,0:T(8,128)(2,1)S(1)}, u32[]{:S(2)}, u32[]{:S(2)}) collective-permute-start(bf16[192,256]{1,0:T(8,128)(2,1)S(1)} %get-tuple-element.31), channel_id=1, source_target_pairs={{0,32},{16,48},{32,64},{48,80},{64,96},{80,112},{96,0},{112,16},{1... | collective-permute-start | bytes 294920 | tf_op jit(solution)/shard_map/ppermute | solution.py:46
  29.5 1.5 %collective-permute-start.2 = (bf16[192,256]{1,0:T(8,128)(2,1)S(1)}, bf16[192,256]{1,0:T(8,128)(2,1)S(1)}, u32[]{:S(2)}, u32[]{:S(2)}) collective-permute-start(bf16[192,256]{1,0:T(8,128)(2,1)S(1)} %get-tuple-element.32), channel_id=1, source_target_pairs={{0,96},{16,112},{32,0},{48,16},{64,32},{80,48},{96,64},{112,80},{1... | collective-permute-start | bytes 294920 | tf_op jit(solution)/shard_map/ppermute | solution.py:46
  31.0 1.5 %collective-permute-start.3 = (bf16[192,256]{1,0:T(8,128)(2,1)S(1)}, bf16[192,256]{1,0:T(8,128)(2,1)S(1)}, u32[]{:S(2)}, u32[]{:S(2)}) collective-permute-start(bf16[192,256]{1,0:T(8,128)(2,1)S(1)} %get-tuple-element.33), channel_id=1, source_target_pairs={{0,64},{16,80},{32,96},{48,112},{64,0},{80,16},{96,32},{112,48},{1... | collective-permute-start | bytes 294920 | tf_op jit(solution)/shard_map/ppermute | solution.py:46
  32.5 1.4 %convert_add_fusion.2 = f32[8,2,48,512]{3,2,1,0:T(8,128)} fusion(bf16[8,2,48,512]{3,2,1,0:T(8,128)(2,1)S(1)} %copy-done.3, f32[8,2,48,512]{3,2,1,0:T(8,128)S(1)} %copy-done.2), kind=kLoop, calls=%fused_computation.4 | loop fusion | flops 1179648 | bytes 3932160 | tf_op jit(solution)/shard_map/add | solution.py:338
  33.9 2.1 %collective-permute-done.3.c_ref = bf16[192,256]{1,0:T(8,128)(2,1)S(1)} collective-permute-done((bf16[192,256]{1,0:T(8,128)(2,1)S(1)}, bf16[192,256]{1,0:T(8,128)(2,1)S(1)}, u32[]{:S(2)}, u32[]{:S(2)}) %collective-permute-start.3) | collective-permute-done | bytes 98336 | tf_op jit(solution)/shard_map/ppermute | solution.py:46
  36.1 1.5 %collective-permute-start.5 = (bf16[192,256]{1,0:T(8,128)(2,1)S(1)}, bf16[192,256]{1,0:T(8,128)(2,1)S(1)}, u32[]{:S(2)}, u32[]{:S(2)}) collective-permute-start(bf16[192,256]{1,0:T(8,128)(2,1)S(1)} %shard_map.44.refs_0_), channel_id=1, source_target_pairs={{0,64},{16,80},{32,96},{48,112},{64,0},{80,16},{96,32},{112,48},{1... | collective-permute-start | bytes 294920 | tf_op jit(solution)/shard_map/ppermute | solution.py:46
  37.6 0.7 collective-permute-start.6
  38.3 2.0 %collective-permute-start.4 = (bf16[192,256]{1,0:T(8,128)(2,1)S(1)}, bf16[192,256]{1,0:T(8,128)(2,1)S(1)}, u32[]{:S(2)}, u32[]{:S(2)}) collective-permute-start(bf16[192,256]{1,0:T(8,128)(2,1)S(1)} %shard_map.44.refs_0_), channel_id=1, source_target_pairs={{0,96},{16,112},{32,0},{48,16},{64,32},{80,48},{96,64},{112,80},{1... | collective-permute-start | bytes 294920 | tf_op jit(solution)/shard_map/ppermute | solution.py:46
  40.3 0.9 collective-permute-done.5.refs_2_
  41.2 1.3 %collective-permute-start.10 = (bf16[768,256]{1,0:T(8,128)(2,1)S(1)}, bf16[768,256]{1,0:T(8,128)(2,1)S(1)}, u32[]{:S(2)}, u32[]{:S(2)}) collective-permute-start(bf16[768,256]{1,0:T(8,128)(2,1)S(1)} %get-tuple-element.39), channel_id=1, source_target_pairs={{0,32},{16,48},{32,64},{48,80},{64,96},{80,112},{96,0},{112,16},{1... | collective-permute-start | bytes 1179656 | tf_op jit(solution)/shard_map/ppermute | solution.py:46
  42.5 1.4 %collective-permute-start.9 = (bf16[768,256]{1,0:T(8,128)(2,1)S(1)}, bf16[768,256]{1,0:T(8,128)(2,1)S(1)}, u32[]{:S(2)}, u32[]{:S(2)}) collective-permute-start(bf16[768,256]{1,0:T(8,128)(2,1)S(1)} %get-tuple-element.39), channel_id=1, source_target_pairs={{0,96},{16,112},{32,0},{48,16},{64,32},{80,48},{96,64},{112,80},{1... | collective-permute-start | bytes 1179656 | tf_op jit(solution)/shard_map/ppermute | solution.py:46
  43.8 0.4 collective-permute-start.11
  44.3 4.0 %collective-permute-start.8 = (bf16[576,256]{1,0:T(8,128)(2,1)S(1)}, bf16[576,256]{1,0:T(8,128)(2,1)S(1)}, u32[]{:S(2)}, u32[]{:S(2)}) collective-permute-start(bf16[576,256]{1,0:T(8,128)(2,1)S(1)} %pad_maximum_fusion), channel_id=1, source_target_pairs={{0,16},{16,0},{32,48},{48,32},{64,80},{80,64},{96,112},{112,96},{1... | collective-permute-start | bytes 884744 | tf_op jit(solution)/shard_map/ppermute | solution.py:46
  48.4 1.3 %collective-permute-done.7.refs_4_ = bf16[192,256]{1,0:T(8,128)(2,1)S(1)} collective-permute-done((bf16[192,256]{1,0:T(8,128)(2,1)S(1)}, bf16[192,256]{1,0:T(8,128)(2,1)S(1)}, u32[]{:S(2)}, u32[]{:S(2)}) %collective-permute-start.7) | collective-permute-done | bytes 98336 | tf_op jit(solution)/shard_map/ppermute | solution.py:46
  49.7 5.5 %shard_map.45 = (bf16[768,256]{1,0:T(8,128)(2,1)}, bf16[2,768,768]{2,1,0:T(8,128)(2,1)}, f32[8,128]{1,0:T(8,128)S(1)}) custom-call(bf16[192,256]{1,0:T(8,128)(2,1)S(1)} %shard_map.44.refs_0_, bf16[192,256]{1,0:T(8,128)(2,1)S(1)} %collective-permute-done.4.refs_1_, bf16[192,256]{1,0:T(8,128)(2,1)S(1)} %collective-permute-done.5.refs_2_, ...), custom_call_target="tpu_custom_call" | custom-call | tf_op jit(solution)/shard_map/pallas_call | solution.py:211
  55.2 3.7 %all-to-all-start.1 = ((bf16[16,48,256]{2,1,0:T(8,128)(2,1)}), bf16[16,48,256]{2,1,0:T(8,128)(2,1)S(1)}, u32[]{:S(2)}, u32[]{:S(2)}) async-start(bf16[16,48,256]{2,1,0:T(8,128)(2,1)} %bitcast.2), calls=%async_computation.1 | async-start | bytes 786432 | tf_op jit(solution)/shard_map/all_to_all | solution.py:359
  58.9 1.7 %copy-done = bf16[2,768,768]{2,1,0:T(8,128)(2,1)S(1)} copy-done((bf16[2,768,768]{2,1,0:T(8,128)(2,1)S(1)}, bf16[2,768,768]{2,1,0:T(8,128)(2,1)}, u32[]{:S(2)}) %copy-start) | copy-done | bytes 2359320
  60.6 2.2 %shard_map.46.refs_3_ = bf16[768,1024]{1,0:T(8,128)(2,1)} custom-call(bf16[2,768,768]{2,1,0:T(8,128)(2,1)S(1)} %copy-done, f32[8,128]{1,0:T(8,128)S(1)} %get-tuple-element.36.scale_ref, bf16[768,256]{1,0:T(8,128)(2,1)S(1)} %get-tuple-element.40.early_ref), custom_call_target="tpu_custom_call" | custom-call | tf_op jit(solution)/shard_map/pallas_call | solution.py:272
  62.8 3.0 %shard_map.47 = bf16[768,1024]{1,0:T(8,128)(2,1)} custom-call(bf16[2,768,768]{2,1,0:T(8,128)(2,1)S(1)} %copy-done.1, f32[8,128]{1,0:T(8,128)S(1)} %get-tuple-element.36.scale_ref, bf16[768,256]{1,0:T(8,128)(2,1)S(1)} %collective-permute-done.9.refs_0_, bf16[768,256]{1,0:T(8,128)(2,1)S(1)} %collective-permute-done.10.refs_1_, ...), custom_call_target="tpu_custom_call", output_to_operand_aliasing={{}: (5, {})} | custom-call | flops 20000000000 | tf_op jit(solution)/shard_map/pallas_call | solution.py:281
  65.8 2.4 %all-to-all-done.1.refs_0_ = bf16[16,48,256]{2,1,0:T(8,128)(2,1)S(1)} async-done(((bf16[16,48,256]{2,1,0:T(8,128)(2,1)}), bf16[16,48,256]{2,1,0:T(8,128)(2,1)S(1)}, u32[]{:S(2)}, u32[]{:S(2)}) %all-to-all-start.1) | async-done | bytes 393248 | tf_op jit(solution)/shard_map/all_to_all | solution.py:359
  68.2 4.0 %all-to-all-start.2 = ((bf16[16,48,1024]{2,1,0:T(8,128)(2,1)}), bf16[16,48,1024]{2,1,0:T(8,128)(2,1)S(1)}, u32[]{:S(2)}, u32[]{:S(2)}) async-start(bf16[16,48,1024]{2,1,0:T(8,128)(2,1)} %bitcast.3), calls=%async_computation.2 | async-start | bytes 3145728 | tf_op jit(solution)/shard_map/all_to_all | solution.py:359
  72.2 0.7 collective-permute-start.14
  72.9 2.0 %collective-permute-start.13 = (bf16[16,48,256]{2,1,0:T(8,128)(2,1)S(1)}, bf16[16,48,256]{2,1,0:T(8,128)(2,1)S(1)}, u32[]{:S(2)}, u32[]{:S(2)}) collective-permute-start(bf16[16,48,256]{2,1,0:T(8,128)(2,1)S(1)} %all-to-all-done.1.refs_0_), channel_id=1, source_target_pairs={{0,96},{16,112},{32,0},{48,16},{64,32},{80,48},{96,64},{112,80},{1... | collective-permute-start | bytes 1179656 | tf_op jit(solution)/shard_map/ppermute | solution.py:46
  75.0 1.8 %collective-permute-start.15 = (bf16[16,48,256]{2,1,0:T(8,128)(2,1)S(1)}, bf16[16,48,256]{2,1,0:T(8,128)(2,1)S(1)}, u32[]{:S(2)}, u32[]{:S(2)}) collective-permute-start(bf16[16,48,256]{2,1,0:T(8,128)(2,1)S(1)} %all-to-all-done.1.refs_0_), channel_id=1, source_target_pairs={{0,16},{16,0},{32,48},{48,32},{64,80},{80,64},{96,112},{112,96},{1... | collective-permute-start | bytes 1179656 | tf_op jit(solution)/shard_map/ppermute | solution.py:46
  76.8 1.8 %collective-permute-start.12 = (bf16[16,48,256]{2,1,0:T(8,128)(2,1)S(1)}, bf16[16,48,256]{2,1,0:T(8,128)(2,1)S(1)}, u32[]{:S(2)}, u32[]{:S(2)}) collective-permute-start(bf16[16,48,256]{2,1,0:T(8,128)(2,1)S(1)} %all-to-all-done.1.refs_0_), channel_id=1, source_target_pairs={{0,64},{16,80},{32,96},{48,112},{64,0},{80,16},{96,32},{112,48},{1... | collective-permute-start | bytes 1179656 | tf_op jit(solution)/shard_map/ppermute | solution.py:46
  78.6 4.4 %collective-permute-done.14.refs_2_ = bf16[16,48,256]{2,1,0:T(8,128)(2,1)S(1)} collective-permute-done((bf16[16,48,256]{2,1,0:T(8,128)(2,1)S(1)}, bf16[16,48,256]{2,1,0:T(8,128)(2,1)S(1)}, u32[]{:S(2)}, u32[]{:S(2)}) %collective-permute-start.14) | collective-permute-done | bytes 393248 | tf_op jit(solution)/shard_map/ppermute | solution.py:46
  82.9 3.2 %collective-permute-start.18 = (bf16[16,48,256]{2,1,0:T(8,128)(2,1)S(1)}, bf16[16,48,256]{2,1,0:T(8,128)(2,1)S(1)}, u32[]{:S(2)}, u32[]{:S(2)}) collective-permute-start(bf16[16,48,256]{2,1,0:T(8,128)(2,1)S(1)} %collective-permute-done.14.refs_2_), channel_id=1, source_target_pairs={{0,16},{16,0},{32,48},{48,32},{64,80},{80,64},{96,112},{112,96},{1... | collective-permute-start | bytes 1179656 | tf_op jit(solution)/shard_map/ppermute | solution.py:46
  86.1 0.7 collective-permute-start.17
  86.8 1.2 %shard_map.48.refs_3_ = bf16[16,48,4096]{2,1,0:T(8,128)(2,1)} custom-call(bf16[16,48,256]{2,1,0:T(8,128)(2,1)S(1)} %all-to-all-done.1.refs_0_, bf16[16,48,256]{2,1,0:T(8,128)(2,1)S(1)} %collective-permute-done.13.refs_1_, bf16[16,48,256]{2,1,0:T(8,128)(2,1)S(1)} %collective-permute-done.14.refs_2_, bf16[16,48,256]{2,1,0:T(8,128)(2,1)S(1)} %collective-permute-done.15.refs_3_), custom_call_target="tpu_custom_call" | custom-call | tf_op jit(solution)/shard_map/pallas_call | solution.py:324
  88.0 4.0 %collective-permute-done.12.refs_2_ = bf16[16,48,256]{2,1,0:T(8,128)(2,1)S(1)} collective-permute-done((bf16[16,48,256]{2,1,0:T(8,128)(2,1)S(1)}, bf16[16,48,256]{2,1,0:T(8,128)(2,1)S(1)}, u32[]{:S(2)}, u32[]{:S(2)}) %collective-permute-start.12) | collective-permute-done | bytes 393248 | tf_op jit(solution)/shard_map/ppermute | solution.py:46
  92.0 2.1 %collective-permute-start.16 = (bf16[16,48,256]{2,1,0:T(8,128)(2,1)S(1)}, bf16[16,48,256]{2,1,0:T(8,128)(2,1)S(1)}, u32[]{:S(2)}, u32[]{:S(2)}) collective-permute-start(bf16[16,48,256]{2,1,0:T(8,128)(2,1)S(1)} %collective-permute-done.12.refs_2_), channel_id=1, source_target_pairs={{0,16},{16,0},{32,48},{48,32},{64,80},{80,64},{96,112},{112,96},{1... | collective-permute-start | bytes 1179656 | tf_op jit(solution)/shard_map/ppermute | solution.py:46
  94.1 1.0 %shard_map.49.refs_1_ = bf16[16,48,4096]{2,1,0:T(8,128)(2,1)} custom-call(bf16[16,48,256]{2,1,0:T(8,128)(2,1)S(1)} %collective-permute-done.17.refs_0_, bf16[16,48,256]{2,1,0:T(8,128)(2,1)S(1)} %collective-permute-done.18.refs_1_, bf16[16,48,256]{2,1,0:T(8,128)(2,1)S(1)} %collective-permute-done.12.refs_2_, ...), custom_call_target="tpu_custom_call", output_to_operand_aliasing={{}: (3, {})} | custom-call | tf_op jit(solution)/shard_map/pallas_call | solution.py:324
  95.2 0.3 collective-permute-done.16.refs_0_
  95.5 0.8 shard_map.50.refs_4_
  96.2 0.2 fusion.2
  96.5 1.4 %collective-permute-start.20 = (bf16[16,48,512]{2,1,0:T(8,128)(2,1)S(1)}, bf16[16,48,512]{2,1,0:T(8,128)(2,1)S(1)}, u32[]{:S(2)}, u32[]{:S(2)}) collective-permute-start(bf16[16,48,512]{2,1,0:T(8,128)(2,1)S(1)} %get-tuple-element.48), channel_id=1, source_target_pairs={{0,16},{16,0},{32,48},{48,32},{64,80},{80,64},{96,112},{112,96},{1... | collective-permute-start | bytes 2359304 | tf_op jit(solution)/shard_map/ppermute | solution.py:46
  97.9 1.2 %shard_map.51.refs_2_ = bf16[16,48,4096]{2,1,0:T(8,128)(2,1)} custom-call(bf16[16,48,1024]{2,1,0:T(8,128)(2,1)S(1)} %all-to-all-done.2.refs_0_.refs_1_.refs_2_.refs_3_, bf16[16,48,1024]{2,1,0:T(8,128)(2,1)S(1)} %all-to-all-done.2.refs_0_.refs_1_.refs_2_.refs_3_, ...), custom_call_target="tpu_custom_call", output_to_operand_aliasing={{}: (4, {})} | custom-call | tf_op jit(solution)/shard_map/pallas_call | solution.py:324
  99.1 0.6 collective-permute-done.20.refs_0_.refs_1_
  99.7 0.9 shard_map.52.refs_2_
  100.6 0.2 collective-permute-done.19.refs_0_.refs_1_
  100.9 0.9 shard_map.53
  (24 shorter events, 0.3 us)
Async XLA Ops:
  24.5 8.0 %copy-start.2 = (f32[8,2,48,512]{3,2,1,0:T(8,128)S(1)}, f32[8,2,48,512]{3,2,1,0:T(8,128)}, u32[]{:S(2)}) copy-start(f32[8,2,48,512]{3,2,1,0:T(8,128)} %param.3) | copy-start | bytes 4718596
  24.5 8.0 %copy-start.3 = (bf16[8,2,48,512]{3,2,1,0:T(8,128)(2,1)S(1)}, bf16[8,2,48,512]{3,2,1,0:T(8,128)(2,1)}, u32[]{:S(2)}) copy-start(bf16[8,2,48,512]{3,2,1,0:T(8,128)(2,1)} %param.2) | copy-start | bytes 2359300
  24.9 3.2 %collective-permute-start = (bf16[768,256]{1,0:T(8,128)(2,1)S(1)}, bf16[768,256]{1,0:T(8,128)(2,1)S(1)}, u32[]{:S(2)}, u32[]{:S(2)}) collective-permute-start(bf16[768,256]{1,0:T(8,128)(2,1)S(1)} %shard_map.42), channel_id=1, source_target_pairs={{0,16},{16,0},{32,48},{48,32},{64,80},{80,64},{96,112},{112,96},{1... | collective-permute-start | bytes 1179656 | tf_op jit(solution)/shard_map/ppermute | solution.py:46
  28.2 5.7 %collective-permute-start.1 = (bf16[192,256]{1,0:T(8,128)(2,1)S(1)}, bf16[192,256]{1,0:T(8,128)(2,1)S(1)}, u32[]{:S(2)}, u32[]{:S(2)}) collective-permute-start(bf16[192,256]{1,0:T(8,128)(2,1)S(1)} %get-tuple-element.31), channel_id=1, source_target_pairs={{0,32},{16,48},{32,64},{48,80},{64,96},{80,112},{96,0},{112,16},{1... | collective-permute-start | bytes 294920 | tf_op jit(solution)/shard_map/ppermute | solution.py:46
  29.5 4.4 %collective-permute-start.2 = (bf16[192,256]{1,0:T(8,128)(2,1)S(1)}, bf16[192,256]{1,0:T(8,128)(2,1)S(1)}, u32[]{:S(2)}, u32[]{:S(2)}) collective-permute-start(bf16[192,256]{1,0:T(8,128)(2,1)S(1)} %get-tuple-element.32), channel_id=1, source_target_pairs={{0,96},{16,112},{32,0},{48,16},{64,32},{80,48},{96,64},{112,80},{1... | collective-permute-start | bytes 294920 | tf_op jit(solution)/shard_map/ppermute | solution.py:46
  31.0 5.1 %collective-permute-start.3 = (bf16[192,256]{1,0:T(8,128)(2,1)S(1)}, bf16[192,256]{1,0:T(8,128)(2,1)S(1)}, u32[]{:S(2)}, u32[]{:S(2)}) collective-permute-start(bf16[192,256]{1,0:T(8,128)(2,1)S(1)} %get-tuple-element.33), channel_id=1, source_target_pairs={{0,64},{16,80},{32,96},{48,112},{64,0},{80,16},{96,32},{112,48},{1... | collective-permute-start | bytes 294920 | tf_op jit(solution)/shard_map/ppermute | solution.py:46
  36.1 5.1 %collective-permute-start.5 = (bf16[192,256]{1,0:T(8,128)(2,1)S(1)}, bf16[192,256]{1,0:T(8,128)(2,1)S(1)}, u32[]{:S(2)}, u32[]{:S(2)}) collective-permute-start(bf16[192,256]{1,0:T(8,128)(2,1)S(1)} %shard_map.44.refs_0_), channel_id=1, source_target_pairs={{0,64},{16,80},{32,96},{48,112},{64,0},{80,16},{96,32},{112,48},{1... | collective-permute-start | bytes 294920 | tf_op jit(solution)/shard_map/ppermute | solution.py:46
  37.6 6.7 %collective-permute-start.6 = (bf16[192,256]{1,0:T(8,128)(2,1)S(1)}, bf16[192,256]{1,0:T(8,128)(2,1)S(1)}, u32[]{:S(2)}, u32[]{:S(2)}) collective-permute-start(bf16[192,256]{1,0:T(8,128)(2,1)S(1)} %shard_map.44.refs_0_), channel_id=1, source_target_pairs={{0,32},{16,48},{32,64},{48,80},{64,96},{80,112},{96,0},{112,16},{1... | collective-permute-start | bytes 294920 | tf_op jit(solution)/shard_map/ppermute | solution.py:46
  38.3 6.0 %collective-permute-start.4 = (bf16[192,256]{1,0:T(8,128)(2,1)S(1)}, bf16[192,256]{1,0:T(8,128)(2,1)S(1)}, u32[]{:S(2)}, u32[]{:S(2)}) collective-permute-start(bf16[192,256]{1,0:T(8,128)(2,1)S(1)} %shard_map.44.refs_0_), channel_id=1, source_target_pairs={{0,96},{16,112},{32,0},{48,16},{64,32},{80,48},{96,64},{112,80},{1... | collective-permute-start | bytes 294920 | tf_op jit(solution)/shard_map/ppermute | solution.py:46
  41.2 21.6 %collective-permute-start.10 = (bf16[768,256]{1,0:T(8,128)(2,1)S(1)}, bf16[768,256]{1,0:T(8,128)(2,1)S(1)}, u32[]{:S(2)}, u32[]{:S(2)}) collective-permute-start(bf16[768,256]{1,0:T(8,128)(2,1)S(1)} %get-tuple-element.39), channel_id=1, source_target_pairs={{0,32},{16,48},{32,64},{48,80},{64,96},{80,112},{96,0},{112,16},{1... | collective-permute-start | bytes 1179656 | tf_op jit(solution)/shard_map/ppermute | solution.py:46
  42.5 20.3 %collective-permute-start.9 = (bf16[768,256]{1,0:T(8,128)(2,1)S(1)}, bf16[768,256]{1,0:T(8,128)(2,1)S(1)}, u32[]{:S(2)}, u32[]{:S(2)}) collective-permute-start(bf16[768,256]{1,0:T(8,128)(2,1)S(1)} %get-tuple-element.39), channel_id=1, source_target_pairs={{0,96},{16,112},{32,0},{48,16},{64,32},{80,48},{96,64},{112,80},{1... | collective-permute-start | bytes 1179656 | tf_op jit(solution)/shard_map/ppermute | solution.py:46
  43.8 18.9 %collective-permute-start.11 = (bf16[768,256]{1,0:T(8,128)(2,1)S(1)}, bf16[768,256]{1,0:T(8,128)(2,1)S(1)}, u32[]{:S(2)}, u32[]{:S(2)}) collective-permute-start(bf16[768,256]{1,0:T(8,128)(2,1)S(1)} %get-tuple-element.40.early_ref), channel_id=1, source_target_pairs={{0,64},{16,80},{32,96},{48,112},{64,0},{80,16},{96,32},{112,48},{1... | collective-permute-start | bytes 1179656 | tf_op jit(solution)/shard_map/ppermute | solution.py:46
  44.3 5.4 %collective-permute-start.8 = (bf16[576,256]{1,0:T(8,128)(2,1)S(1)}, bf16[576,256]{1,0:T(8,128)(2,1)S(1)}, u32[]{:S(2)}, u32[]{:S(2)}) collective-permute-start(bf16[576,256]{1,0:T(8,128)(2,1)S(1)} %pad_maximum_fusion), channel_id=1, source_target_pairs={{0,16},{16,0},{32,48},{48,32},{64,80},{80,64},{96,112},{112,96},{1... | collective-permute-start | bytes 884744 | tf_op jit(solution)/shard_map/ppermute | solution.py:46
  48.3 1.3 %collective-permute-start.7 = (bf16[192,256]{1,0:T(8,128)(2,1)S(1)}, bf16[192,256]{1,0:T(8,128)(2,1)S(1)}, u32[]{:S(2)}, u32[]{:S(2)}) collective-permute-start(bf16[192,256]{1,0:T(8,128)(2,1)S(1)} %shard_map.44.refs_0_), channel_id=1, source_target_pairs={{0,16},{16,0},{32,48},{48,32},{64,80},{80,64},{96,112},{112,96},{1... | collective-permute-start | bytes 294920 | tf_op jit(solution)/shard_map/ppermute | solution.py:46
  55.2 13.1 %all-to-all-start.1 = ((bf16[16,48,256]{2,1,0:T(8,128)(2,1)}), bf16[16,48,256]{2,1,0:T(8,128)(2,1)S(1)}, u32[]{:S(2)}, u32[]{:S(2)}) async-start(bf16[16,48,256]{2,1,0:T(8,128)(2,1)} %bitcast.2), calls=%async_computation.1 | async-start | bytes 786432 | tf_op jit(solution)/shard_map/all_to_all | solution.py:359
  58.9 1.7 %copy-start = (bf16[2,768,768]{2,1,0:T(8,128)(2,1)S(1)}, bf16[2,768,768]{2,1,0:T(8,128)(2,1)}, u32[]{:S(2)}) copy-start(bf16[2,768,768]{2,1,0:T(8,128)(2,1)} %get-tuple-element.35.polys_ref) | copy-start | bytes 7077892
  60.6 2.2 %copy-start.1 = (bf16[2,768,768]{2,1,0:T(8,128)(2,1)S(1)}, bf16[2,768,768]{2,1,0:T(8,128)(2,1)}, u32[]{:S(2)}) copy-start(bf16[2,768,768]{2,1,0:T(8,128)(2,1)} %get-tuple-element.35.polys_ref) | copy-start | bytes 7077892
  68.2 28.0 %all-to-all-start.2 = ((bf16[16,48,1024]{2,1,0:T(8,128)(2,1)}), bf16[16,48,1024]{2,1,0:T(8,128)(2,1)S(1)}, u32[]{:S(2)}, u32[]{:S(2)}) async-start(bf16[16,48,1024]{2,1,0:T(8,128)(2,1)} %bitcast.3), calls=%async_computation.2 | async-start | bytes 3145728 | tf_op jit(solution)/shard_map/all_to_all | solution.py:359
  72.2 10.7 %collective-permute-start.14 = (bf16[16,48,256]{2,1,0:T(8,128)(2,1)S(1)}, bf16[16,48,256]{2,1,0:T(8,128)(2,1)S(1)}, u32[]{:S(2)}, u32[]{:S(2)}) collective-permute-start(bf16[16,48,256]{2,1,0:T(8,128)(2,1)S(1)} %all-to-all-done.1.refs_0_), channel_id=1, source_target_pairs={{0,32},{16,48},{32,64},{48,80},{64,96},{80,112},{96,0},{112,16},{1... | collective-permute-start | bytes 1179656 | tf_op jit(solution)/shard_map/ppermute | solution.py:46
  72.9 13.2 %collective-permute-start.13 = (bf16[16,48,256]{2,1,0:T(8,128)(2,1)S(1)}, bf16[16,48,256]{2,1,0:T(8,128)(2,1)S(1)}, u32[]{:S(2)}, u32[]{:S(2)}) collective-permute-start(bf16[16,48,256]{2,1,0:T(8,128)(2,1)S(1)} %all-to-all-done.1.refs_0_), channel_id=1, source_target_pairs={{0,96},{16,112},{32,0},{48,16},{64,32},{80,48},{96,64},{112,80},{1... | collective-permute-start | bytes 1179656 | tf_op jit(solution)/shard_map/ppermute | solution.py:46
  75.0 11.8 %collective-permute-start.15 = (bf16[16,48,256]{2,1,0:T(8,128)(2,1)S(1)}, bf16[16,48,256]{2,1,0:T(8,128)(2,1)S(1)}, u32[]{:S(2)}, u32[]{:S(2)}) collective-permute-start(bf16[16,48,256]{2,1,0:T(8,128)(2,1)S(1)} %all-to-all-done.1.refs_0_), channel_id=1, source_target_pairs={{0,16},{16,0},{32,48},{48,32},{64,80},{80,64},{96,112},{112,96},{1... | collective-permute-start | bytes 1179656 | tf_op jit(solution)/shard_map/ppermute | solution.py:46
  76.8 15.2 %collective-permute-start.12 = (bf16[16,48,256]{2,1,0:T(8,128)(2,1)S(1)}, bf16[16,48,256]{2,1,0:T(8,128)(2,1)S(1)}, u32[]{:S(2)}, u32[]{:S(2)}) collective-permute-start(bf16[16,48,256]{2,1,0:T(8,128)(2,1)S(1)} %all-to-all-done.1.refs_0_), channel_id=1, source_target_pairs={{0,64},{16,80},{32,96},{48,112},{64,0},{80,16},{96,32},{112,48},{1... | collective-permute-start | bytes 1179656 | tf_op jit(solution)/shard_map/ppermute | solution.py:46
  82.9 11.2 %collective-permute-start.18 = (bf16[16,48,256]{2,1,0:T(8,128)(2,1)S(1)}, bf16[16,48,256]{2,1,0:T(8,128)(2,1)S(1)}, u32[]{:S(2)}, u32[]{:S(2)}) collective-permute-start(bf16[16,48,256]{2,1,0:T(8,128)(2,1)S(1)} %collective-permute-done.14.refs_2_), channel_id=1, source_target_pairs={{0,16},{16,0},{32,48},{48,32},{64,80},{80,64},{96,112},{112,96},{1... | collective-permute-start | bytes 1179656 | tf_op jit(solution)/shard_map/ppermute | solution.py:46
  86.1 8.0 %collective-permute-start.17 = (bf16[16,48,256]{2,1,0:T(8,128)(2,1)S(1)}, bf16[16,48,256]{2,1,0:T(8,128)(2,1)S(1)}, u32[]{:S(2)}, u32[]{:S(2)}) collective-permute-start(bf16[16,48,256]{2,1,0:T(8,128)(2,1)S(1)} %collective-permute-done.13.refs_1_), channel_id=1, source_target_pairs={{0,16},{16,0},{32,48},{48,32},{64,80},{80,64},{96,112},{112,96},{1... | collective-permute-start | bytes 1179656 | tf_op jit(solution)/shard_map/ppermute | solution.py:46
  92.0 3.5 %collective-permute-start.16 = (bf16[16,48,256]{2,1,0:T(8,128)(2,1)S(1)}, bf16[16,48,256]{2,1,0:T(8,128)(2,1)S(1)}, u32[]{:S(2)}, u32[]{:S(2)}) collective-permute-start(bf16[16,48,256]{2,1,0:T(8,128)(2,1)S(1)} %collective-permute-done.12.refs_2_), channel_id=1, source_target_pairs={{0,16},{16,0},{32,48},{48,32},{64,80},{80,64},{96,112},{112,96},{1... | collective-permute-start | bytes 1179656 | tf_op jit(solution)/shard_map/ppermute | solution.py:46
  96.5 3.3 %collective-permute-start.20 = (bf16[16,48,512]{2,1,0:T(8,128)(2,1)S(1)}, bf16[16,48,512]{2,1,0:T(8,128)(2,1)S(1)}, u32[]{:S(2)}, u32[]{:S(2)}) collective-permute-start(bf16[16,48,512]{2,1,0:T(8,128)(2,1)S(1)} %get-tuple-element.48), channel_id=1, source_target_pairs={{0,16},{16,0},{32,48},{48,32},{64,80},{80,64},{96,112},{112,96},{1... | collective-permute-start | bytes 2359304 | tf_op jit(solution)/shard_map/ppermute | solution.py:46
  97.8 3.0 %collective-permute-start.19 = (bf16[16,48,512]{2,1,0:T(8,128)(2,1)S(1)}, bf16[16,48,512]{2,1,0:T(8,128)(2,1)S(1)}, u32[]{:S(2)}, u32[]{:S(2)}) collective-permute-start(bf16[16,48,512]{2,1,0:T(8,128)(2,1)S(1)} %get-tuple-element.49), channel_id=1, source_target_pairs={{0,16},{16,0},{32,48},{48,32},{64,80},{80,64},{96,112},{112,96},{1... | collective-permute-start | bytes 2359304 | tf_op jit(solution)/shard_map/ppermute | solution.py:46
